TPU v7x, 32 devices: a whole 2x2x4 slice. The times are simulated.
32 devices in a mesh: groups: 2 (over x), fsdp: 16 (over z, y, core).
Axes of the slice: x: 2, y: 2, z: 4, core: 2. Of those that a mesh axis runs over, the one named last changes fastest.
Arguments:
- hidden: bfloat16 [256, 8192], P('groups', 'fsdp'), parts along dimension 0
- parent_gain: float32 [16384], P('groups'), parts along dimension 0, may hold values from 0.1 to 1.9
- child_gain: float32 [16384], P('groups'), parts along dimension 0, may hold values from 0.1 to 1.9
- gate_weight: bfloat16 [4096, 8192], P(('groups', 'fsdp')), parts along dimension 0, may hold values from -0.0625 to 0.0625
- up_weight: bfloat16 [4096, 8192], P(('groups', 'fsdp')), parts along dimension 0, may hold values from -0.0625 to 0.0625
- down_weight: bfloat16 [4096, 8192], P(('groups', 'fsdp')), parts along dimension 0, may hold values from -0.125 to 0.125
- kept_index: int32 [4096], P('groups'), parts along dimension 0, may hold values from -1 to 2047, as said below
- tile_owner: int32 [32], P('groups'), parts along dimension 0, may hold values from 0 to 15, each once
Outputs:
- grad_gate: bfloat16 [4096, 8192], P(('groups', 'fsdp')), parts along dimension 0
- grad_up: bfloat16 [4096, 8192], P(('groups', 'fsdp')), parts along dimension 0
- grad_down: bfloat16 [4096, 8192], P(('groups', 'fsdp')), parts along dimension 0
- gain_grad: float32 [16384], P(('groups', 'fsdp')), parts along dimension 0
- loss_value: float32 [2], P('groups'), parts along dimension 0
There are 2 independent parts, one for each index of `groups`. A program takes and returns all parts, laid end to end along the dimension named above; each array names one. Nothing has to cross between parts.
Inputs may be any that keep to these rules, and one draw needn't show every extreme that they name: `kept_index`: entry i is the parent channel placed in row i of the padded child, or -1 for an empty row; no channel appears twice; a tile takes at most 8 rows from the 128 channels of one device, and some tile has no empty row. `tile_owner`: each device along fsdp owns exactly one tile.
All inputs are finite; a program needn't handle non-finite values.
Results may differ from a plain program's by a relative error of at most 0.0045.
The roundings to bfloat16 on the way count: a program that leaves them out, or rounds other values in their place, can miss the bound.
Values may be sent and summed in bfloat16 or wider, within the bound.
No kernel may reach another device: no remote copies, remote signals or barrier semaphores. Data moves between devices by JAX's collectives and lax.ppermute only.
A program may use at most 128 MiB of HBM per device.

v0:
```python
import jax
import jax.numpy as jnp
from jax import lax
from jax.sharding import PartitionSpec as P


def matmul(left_side, right_side):
    return jnp.dot(left_side, right_side, preferred_element_type=jnp.float32)


def contract_rows(left_side, right_side):
    return lax.dot_general(
        left_side, right_side, (((0,), (0,)), ((), ())), preferred_element_type=jnp.float32
    )


def routing(kept_index, tile_owner, device, devices, parent_rows):
    tile_count = tile_owner.shape[0]
    tile_rows = kept_index.shape[0] // tile_count
    per_pair = tile_rows // devices
    layout = kept_index.reshape(tile_count, tile_rows)
    source = jnp.where(layout >= 0, layout // parent_rows, -1)
    from_each = (source[:, :, None] == jnp.arange(devices)[None, None, :]).astype(jnp.int32)
    earlier = jnp.cumsum(from_each, axis=1) - from_each
    position = jnp.sum(earlier * from_each, axis=2)
    local_row = layout - device * parent_rows
    picked = (source == device)[:, :, None] & (
        position[:, :, None] == jnp.arange(per_pair)[None, None, :]
    )
    chosen = jnp.sum(jnp.where(picked, local_row[:, :, None], 0), axis=1)
    present = jnp.any(picked, axis=1).astype(jnp.int32)
    owned_by = (tile_owner[None, :] == jnp.arange(devices)[:, None]).astype(jnp.int32)
    send_rows = jnp.sum(owned_by[:, :, None] * chosen[None, :, :], axis=1).reshape(-1)
    send_live = jnp.sum(owned_by[:, :, None] * present[None, :, :], axis=1).reshape(-1) > 0
    my_tile = jnp.sum(jnp.arange(tile_count) * (tile_owner == device).astype(jnp.int32))
    my_source = lax.dynamic_index_in_dim(source, my_tile, 0, keepdims=False)
    my_position = lax.dynamic_index_in_dim(position, my_tile, 0, keepdims=False)
    my_live = my_source >= 0
    recv_rows = jnp.where(my_live, my_source * per_pair + my_position, 0)
    return (send_rows, send_live, recv_rows, my_live)


def outgoing(weights, send_rows, send_live):
    picked = jnp.take(weights, send_rows, axis=0)
    return jnp.where(send_live[:, None], picked, jnp.zeros((), weights.dtype))


def assemble(received, recv_rows, my_live):
    picked = jnp.take(received, recv_rows, axis=0)
    return jnp.where(my_live[:, None], picked, jnp.zeros((), received.dtype))


def shards(
    hidden, parent_gain, child_gain, gate_weight, up_weight, down_weight, kept_index, tile_owner
):
    devices = lax.axis_size("fsdp")
    device = lax.axis_index("fsdp")
    parent_rows = gate_weight.shape[0]
    full_rows = lax.all_gather(hidden, "fsdp", axis=1, tiled=True)
    token_count = full_rows.shape[0]
    feat_width = full_rows.shape[1]
    inputs_f = full_rows.astype(jnp.float32)
    normed = inputs_f / jnp.sqrt(jnp.mean(inputs_f * inputs_f, axis=1, keepdims=True) + 1e-05)
    parent_in = (normed * parent_gain).astype(jnp.bfloat16)
    child_in = (normed * child_gain).astype(jnp.bfloat16)
    send_rows, send_live, recv_rows, my_live = routing(
        kept_index, tile_owner, device, devices, parent_rows
    )
    kept_here = jnp.any(
        send_live[:, None] & (send_rows[:, None] == jnp.arange(parent_rows)[None, :]), axis=0
    )
    both_in = jnp.concatenate([parent_in, child_in], axis=0)
    gate_both = matmul(both_in, gate_weight.T)
    up_both = matmul(both_in, up_weight.T)
    parent_gate = gate_both[:token_count]
    parent_up = up_both[:token_count]
    child_gate = gate_both[token_count:]
    child_up = up_both[token_count:]
    parent_hid = (parent_gate * jax.nn.sigmoid(parent_gate) * parent_up).astype(jnp.bfloat16)
    child_sig = jax.nn.sigmoid(child_gate)
    child_hid = jnp.where(kept_here[None, :], child_gate * child_sig * child_up, 0.0).astype(
        jnp.bfloat16
    )
    difference = lax.psum(matmul(child_hid, down_weight) - matmul(parent_hid, down_weight), "fsdp")
    loss_value = 0.5 * jnp.sum(difference * difference) / (token_count * feat_width)
    out_slope = difference.astype(jnp.bfloat16)
    child_slope = matmul(out_slope, down_weight.T)
    down_rows = contract_rows(child_hid, out_slope).astype(jnp.bfloat16)
    gate_back = child_slope * child_up * child_sig * (1.0 + child_gate * (1.0 - child_sig))
    up_back = child_slope * child_gate * child_sig
    gate_back = jnp.where(kept_here[None, :], gate_back, 0.0).astype(jnp.bfloat16)
    up_back = jnp.where(kept_here[None, :], up_back, 0.0).astype(jnp.bfloat16)
    gate_rows = contract_rows(gate_back, child_in).astype(jnp.bfloat16)
    up_rows = contract_rows(up_back, child_in).astype(jnp.bfloat16)
    input_slope = matmul(gate_back, gate_weight) + matmul(up_back, up_weight)
    gain_part = jnp.sum(input_slope * normed, axis=0)
    gain_grad = lax.psum_scatter(gain_part, "fsdp", scatter_dimension=0, tiled=True)
    returned = (
        lax.all_to_all(
            outgoing(gate_rows, send_rows, send_live),
            "fsdp",
            split_axis=0,
            concat_axis=0,
            tiled=True,
        ),
        lax.all_to_all(
            outgoing(up_rows, send_rows, send_live), "fsdp", split_axis=0, concat_axis=0, tiled=True
        ),
        lax.all_to_all(
            outgoing(down_rows, send_rows, send_live),
            "fsdp",
            split_axis=0,
            concat_axis=0,
            tiled=True,
        ),
    )
    grad_gate = assemble(returned[0], recv_rows, my_live)
    grad_up = assemble(returned[1], recv_rows, my_live)
    grad_down = assemble(returned[2], recv_rows, my_live)
    return (grad_gate, grad_up, grad_down, gain_grad, loss_value.reshape(1))


def solution(mesh):
    placed = (
        P("groups", "fsdp"),
        P("groups"),
        P("groups"),
        P(("groups", "fsdp"), None),
        P(("groups", "fsdp"), None),
        P(("groups", "fsdp"), None),
        P("groups"),
        P("groups"),
    )
    return jax.shard_map(
        shards,
        mesh=mesh,
        in_specs=placed,
        out_specs=(
            P(("groups", "fsdp"), None),
            P(("groups", "fsdp"), None),
            P(("groups", "fsdp"), None),
            P(("groups", "fsdp")),
            P("groups"),
        ),
        check_vma=False,
    )
```

profile of v0, /device:TPU:0, one launch (start us, length us, event | category | flops | bytes accessed | tf_op | source)
XLA Modules:
  0.0 436.5 jit_solution(17024450051360334318)
XLA Ops:
  7.2 0.7 all-gather.2.cloned.1.call-update
  8.0 0.7 bitcast_subtract_fusion
  8.7 0.1 copy.34
  8.8 2.8 select_reduce_fusion
  11.6 0.7 broadcast_compare_fusion.1
  12.4 0.3 select_reduce_fusion.1
  12.7 0.1 copy.38
  12.8 0.4 fusion.18
  13.2 0.1 copy.37
  13.3 0.7 fusion.26
  13.9 0.6 multiply_reduce_fusion.2
  14.6 0.1 gt.11
  14.7 0.1 eq.87
  14.7 0.1 fusion.20
  14.9 39.3 %all-gather.2.cloned.1.call-done = bf16[128,8192]{1,0:T(8,128)(2,1)} async-done(((bf16[128,512]{1,0:T(8,128)(2,1)}), bf16[128,8192]{1,0:T(8,128)(2,1)}) %all-gather.2.cloned.1.call-update) | async-done | bytes 2097168 | tf_op jit(solution)/shard_map/all_gather | solution.py:59
  54.1 2.2 fusion.1
  56.4 0.9 multiply_convert_fusion.1
  57.3 0.6 copy-done.11
  58.0 1.2 fusion.2
  59.2 0.4 copy-done.7
  59.6 1.2 fusion.3
  60.9 0.7 fusion.32
  61.6 2.7 convolution_subtract_fusion
  64.4 110.5 %all-reduce.3.cloned.1.call-done = f32[128,8192]{1,0:T(8,128)} async-done(((f32[128,8192]{1,0:T(8,128)}), f32[128,8192]{1,0:T(8,128)}) %all-reduce.3.cloned.1.call-update) | async-done | bytes 4194320 | tf_op jit(solution)/shard_map/psum | solution.py:84
  174.9 3.1 select_convert_fusion
  178.0 0.7 convolution_convert_fusion.1
  178.8 2.1 convolution_convert_fusion.2
  180.8 0.9 copy-done.2
  181.7 2.1 convolution_convert_fusion
  183.8 7.1 %gather_fusion.4 = bf16[128,8192]{1,0:T(8,128)(2,1)} fusion(bf16[128,8192]{1,0:T(8,128)(2,1)} %convolution_convert_fusion, s32[1024]{0:T(1024)S(1)} %pad_clamp_fusion.1), kind=kCustom, calls=%fused_computation.4.clone | custom fusion | bytes 4194816 | tf_op jit(solution)/shard_map/jit(_take)/gather | solution.py:44
  190.9 7.0 %gather_fusion = bf16[128,8192]{1,0:T(8,128)(2,1)} fusion(bf16[128,8192]{1,0:T(8,128)(2,1)} %convolution_convert_fusion.2, s32[1024]{0:T(1024)S(1)} %pad_clamp_fusion.1), kind=kCustom, calls=%fused_computation.clone | custom fusion | bytes 4194816 | tf_op jit(solution)/shard_map/jit(_take)/gather | solution.py:44
  197.8 3.2 gather_fusion.2
  201.0 4.9 %fusion.4 = (bf16[16,8,8192]{2,1,0:T(8,128)(2,1)S(1)}, bf16[16,8,8192]{2,1,0:T(8,128)(2,1)S(1)}, bf16[16,8,8192]{2,1,0:T(8,128)(2,1)}) fusion(bf16[128,8192]{1,0:T(8,128)(2,1)} %gather_fusion.4, pred[128]{0:T(512)(128)(4,1)S(1)} %compare_and_fusion.1, pred[128]{0:T(512)(128)(4,1)S(1)} %gt.11, bf16[128,8192]{1,0:T(8,128)(2,1)} %gather_fusion.2, ...), kind=kLoop, calls=%fused_computation.23 | loop fusion | flops 6291456 | bytes 12583168 | tf_op jit(solution)/shard_map/all_to_all | solution.py:109
  205.9 50.8 %all_to_all.36 = bf16[16,8,8192]{2,1,0:T(8,128)(2,1)} all-to-all(bf16[16,8,8192]{2,1,0:T(8,128)(2,1)S(1)} %get-tuple-element.19), channel_id=1, replica_groups=mesh['groups'=2,'fsdp'=16] {'fsdp'}, dimensions={0} | all-to-all | bytes 4194304 | tf_op jit(solution)/shard_map/all_to_all | solution.py:109
  256.8 52.3 %all_to_all.37 = bf16[16,8,8192]{2,1,0:T(8,128)(2,1)} all-to-all(bf16[16,8,8192]{2,1,0:T(8,128)(2,1)S(1)} %get-tuple-element.20), channel_id=1, replica_groups=mesh['groups'=2,'fsdp'=16] {'fsdp'}, dimensions={0} | all-to-all | bytes 4194304 | tf_op jit(solution)/shard_map/all_to_all | solution.py:106
  309.1 5.2 %all-to-all-start = ((bf16[16,8,8192]{2,1,0:T(8,128)(2,1)}), bf16[16,8,8192]{2,1,0:T(8,128)(2,1)S(1)}, u32[]{:S(2)}, u32[]{:S(2)}) async-start(bf16[16,8,8192]{2,1,0:T(8,128)(2,1)} %get-tuple-element.21), calls=%async_computation | async-start | bytes 4194304 | tf_op jit(solution)/shard_map/all_to_all | solution.py:99
  314.4 0.6 fusion.28
  317.0 0.6 dynamic-slice
  318.3 3.9 multiply_reduce_fusion
  322.8 2.4 fusion.33
  325.3 0.4 copy-done.12
  325.6 1.2 fusion.7
  326.9 77.9 %all-reduce = f32[8192]{0:T(1024)S(1)} all-reduce(f32[8192]{0:T(1024)S(1)} %fusion.7), channel_id=2, replica_groups=mesh['groups'=2,'fsdp'=16] {'fsdp'}, use_global_device_ids=true, to_apply=%region_11.13.clone | all-reduce | flops 8192 | bytes 65536
  404.8 0.7 dynamic-slice.1
  405.4 6.9 %gather_fusion.5 = bf16[128,8192]{1,0:T(8,128)(2,1)} fusion(bf16[128,8192]{1,0:T(8,128)(2,1)} %bitcast.59, s32[1024]{0:T(1024)S(1)} %pad_clamp_fusion), kind=kCustom, calls=%fused_computation.5.clone | custom fusion | bytes 4194816 | tf_op jit(solution)/shard_map/jit(_take)/gather | solution.py:49
  412.4 6.9 %gather_fusion.3 = bf16[128,8192]{1,0:T(8,128)(2,1)} fusion(bf16[128,8192]{1,0:T(8,128)(2,1)} %bitcast.60, s32[1024]{0:T(1024)S(1)} %pad_clamp_fusion), kind=kCustom, calls=%fused_computation.3.clone | custom fusion | bytes 4194816 | tf_op jit(solution)/shard_map/jit(_take)/gather | solution.py:49
  419.3 3.2 gather_fusion.1
  422.5 6.1 %select_select_fusion = (bf16[128,8192]{1,0:T(8,128)(2,1)}, bf16[128,8192]{1,0:T(8,128)(2,1)}, bf16[128,8192]{1,0:T(8,128)(2,1)}) fusion(bf16[128,8192]{1,0:T(8,128)(2,1)} %gather_fusion.5, pred[128]{0:T(512)(128)(4,1)S(1)} %get-tuple-element.8, pred[128]{0:T(512)(128)(4,1)S(1)} %compare_bitcast_fusion, bf16[128,8192]{1,0:T(8,128)(2,1)} %gather_fusion.3, ...), kind=kLoop, calls=%fused_computation.21 | loop fusion | flops 6291456 | bytes 12583168 | tf_op jit(solution)/shard_map/jit(_where)/select_n | solution.py:50
  (39 shorter events, 0.3 us)
Async XLA Ops:
  7.2 53.8 %copy-start = (bf16[128,8192]{1,0:T(8,128)(2,1)S(1)}, bf16[128,8192]{1,0:T(8,128)(2,1)}, u32[]{:S(2)}) copy-start(bf16[128,8192]{1,0:T(8,128)(2,1)} %param.15) | copy-start | bytes 6291460
  7.2 49.2 %copy-start.9 = (f32[8192]{0:T(1024)S(1)}, f32[8192]{0:T(1024)}, u32[]{:S(2)}) copy-start(f32[8192]{0:T(1024)} %param.12) | copy-start | bytes 98308
  7.2 49.2 %copy-start.8 = (f32[8192]{0:T(1024)S(1)}, f32[8192]{0:T(1024)}, u32[]{:S(2)}) copy-start(f32[8192]{0:T(1024)} %param.11) | copy-start | bytes 98308
  7.2 46.9 %all-gather.2.cloned.1.call-start = ((), (), s32[]{:S(2)}) async-start(), calls=%async_computation.3 | async-start | bytes 2228224 | tf_op jit(solution)/shard_map/all_gather | solution.py:59
  7.9 167.0 %all-reduce.3.cloned.1.call-start = ((), (), s32[]{:S(2)}) async-start(), calls=%async_computation.4 | async-start | bytes 8388608 | tf_op jit(solution)/shard_map/psum | solution.py:84
  54.1 2.3 copy-start.5
  56.4 1.6 copy-start.11
  57.3 1.9 copy-start.3
  58.0 1.7 copy-start.7
  174.9 3.1 copy-start.4
  178.8 2.9 copy-start.2
  309.1 5.3 %copy-start.10 = (s32[16]{0:T(128)S(1)}, s32[16]{0:T(128)}, u32[]{:S(2)}) copy-start(s32[16]{0:T(128)} %param.17) | copy-start | bytes 196
  309.1 7.9 %copy-start.13 = (u32[32]{0:T(128)S(1)}, u32[32]{0:T(128)}, u32[]{:S(2)}) copy-start(u32[32]{0:T(128)} %constant.69) | copy-start | bytes 388
  309.1 110.2 %all-to-all-start = ((bf16[16,8,8192]{2,1,0:T(8,128)(2,1)}), bf16[16,8,8192]{2,1,0:T(8,128)(2,1)S(1)}, u32[]{:S(2)}, u32[]{:S(2)}) async-start(bf16[16,8,8192]{2,1,0:T(8,128)(2,1)} %get-tuple-element.21), calls=%async_computation | async-start | bytes 4194304 | tf_op jit(solution)/shard_map/all_to_all | solution.py:99
  322.8 2.5 copy-start.6
  322.8 2.8 copy-start.12
  422.5 6.1 %copy-start.1 = (bf16[128,8192]{1,0:T(8,128)(2,1)S(1)}, bf16[128,8192]{1,0:T(8,128)(2,1)}, u32[]{:S(2)}) copy-start(bf16[128,8192]{1,0:T(8,128)(2,1)} %param.15) | copy-start | bytes 6291460
Sparse Core Ops, SparseCore 0:
  10.2 43.8 all-gather.1
  64.5 110.3 all-reduce.2
where the time goes:
time: 437 us
  blocking collectives  181 us (41%)
  waiting for transfers between devices  150 us (34%)
  local copies, waits for them, and re-layouts  38.4 us (9%)
  other arithmetic  25.1 us (6%)
  between operations  18.7 us (4%)
  matrix products  17.5 us (4%)
  starting transfers between devices  5.32 us (1%)
    psum x1, waiting for transfers between devices, shards(): lax.psum(matmul(child_hid, down_weight) - matmul(parent_hid, down_weight)...  111 us
    unnamed x1, blocking collectives  77.9 us
    all_to_all x1, blocking collectives, shards(): lax.all_to_all(outgoing(up_rows, send_rows, send_live), 'fsdp', split_axi...  52.3 us
    all_to_all x1, blocking collectives, shards(): lax.all_to_all(outgoing(down_rows, send_rows, send_live), 'fsdp', split_a...  50.8 us
    all_gather x1, waiting for transfers between devices, shards(): full_rows = lax.all_gather(hidden, 'fsdp', axis=1, tiled=True)  39.3 us
    gather x3, local copies, waits for them, and re-layouts, outgoing(): picked = jnp.take(weights, send_rows, axis=0)  17.3 us
    gather x3, local copies, waits for them, and re-layouts, assemble(): picked = jnp.take(received, recv_rows, axis=0)  17.1 us
    dot_general x7, matrix products, matmul(): return jnp.dot(left_side, right_side, preferred_element_type=jnp.float32)  12.6 us
  transfers between devices with their start and end apart: 3, of which 2 were waited for; matrix products, arithmetic and copies ran while one was open for 7% of the time, Pallas kernels for 0%

commit v1 on v0

--- a/solution.py
+++ b/solution.py
@@ -6,12 +6,6 @@
 
 def matmul(left_side, right_side):
     return jnp.dot(left_side, right_side, preferred_element_type=jnp.float32)
-
-
-def contract_rows(left_side, right_side):
-    return lax.dot_general(
-        left_side, right_side, (((0,), (0,)), ((), ())), preferred_element_type=jnp.float32
-    )
 
 
 def routing(kept_index, tile_owner, device, devices, parent_rows):
@@ -40,14 +34,16 @@
     return (send_rows, send_live, recv_rows, my_live)
 
 
-def outgoing(weights, send_rows, send_live):
-    picked = jnp.take(weights, send_rows, axis=0)
-    return jnp.where(send_live[:, None], picked, jnp.zeros((), weights.dtype))
+def select_rows(row_of_slot, live, back):
+    hot = (row_of_slot[:, None] == jnp.arange(back.shape[1])[None, :]) & live[:, None]
+    return lax.dot_general(
+        hot.astype(jnp.bfloat16), back, (((1,), (1,)), ((), ())), preferred_element_type=jnp.float32
+    ).astype(jnp.bfloat16)
 
 
-def assemble(received, recv_rows, my_live):
-    picked = jnp.take(received, recv_rows, axis=0)
-    return jnp.where(my_live[:, None], picked, jnp.zeros((), received.dtype))
+def place_rows(slot_of_row, live, received):
+    hot = (slot_of_row[:, None] == jnp.arange(received.shape[0])[None, :]) & live[:, None]
+    return matmul(hot.astype(jnp.bfloat16), received).astype(jnp.bfloat16)
 
 
 def shards(
@@ -81,42 +77,34 @@
     child_hid = jnp.where(kept_here[None, :], child_gate * child_sig * child_up, 0.0).astype(
         jnp.bfloat16
     )
+    hid_sent = select_rows(send_rows, send_live, child_hid).reshape(devices, -1, token_count)
+    hid_sent = lax.all_to_all(hid_sent, "fsdp", split_axis=0, concat_axis=0, tiled=True)
+    hid_tile = place_rows(recv_rows, my_live, hid_sent.reshape(-1, token_count))
     difference = lax.psum(matmul(child_hid, down_weight) - matmul(parent_hid, down_weight), "fsdp")
     loss_value = 0.5 * jnp.sum(difference * difference) / (token_count * feat_width)
     out_slope = difference.astype(jnp.bfloat16)
     child_slope = matmul(out_slope, down_weight.T)
-    down_rows = contract_rows(child_hid, out_slope).astype(jnp.bfloat16)
     gate_back = child_slope * child_up * child_sig * (1.0 + child_gate * (1.0 - child_sig))
     up_back = child_slope * child_gate * child_sig
     gate_back = jnp.where(kept_here[None, :], gate_back, 0.0).astype(jnp.bfloat16)
     up_back = jnp.where(kept_here[None, :], up_back, 0.0).astype(jnp.bfloat16)
-    gate_rows = contract_rows(gate_back, child_in).astype(jnp.bfloat16)
-    up_rows = contract_rows(up_back, child_in).astype(jnp.bfloat16)
     input_slope = matmul(gate_back, gate_weight) + matmul(up_back, up_weight)
     gain_part = jnp.sum(input_slope * normed, axis=0)
     gain_grad = lax.psum_scatter(gain_part, "fsdp", scatter_dimension=0, tiled=True)
-    returned = (
-        lax.all_to_all(
-            outgoing(gate_rows, send_rows, send_live),
-            "fsdp",
-            split_axis=0,
-            concat_axis=0,
-            tiled=True,
-        ),
-        lax.all_to_all(
-            outgoing(up_rows, send_rows, send_live), "fsdp", split_axis=0, concat_axis=0, tiled=True
-        ),
-        lax.all_to_all(
-            outgoing(down_rows, send_rows, send_live),
-            "fsdp",
-            split_axis=0,
-            concat_axis=0,
-            tiled=True,
-        ),
+    per_pair = send_rows.shape[0] // devices
+    both = jnp.stack(
+        [
+            select_rows(send_rows, send_live, gate_back).reshape(devices, per_pair, token_count),
+            select_rows(send_rows, send_live, up_back).reshape(devices, per_pair, token_count),
+        ],
+        axis=1,
     )
-    grad_gate = assemble(returned[0], recv_rows, my_live)
-    grad_up = assemble(returned[1], recv_rows, my_live)
-    grad_down = assemble(returned[2], recv_rows, my_live)
+    both = lax.all_to_all(both, "fsdp", split_axis=0, concat_axis=0, tiled=True)
+    gate_tile = place_rows(recv_rows, my_live, both[:, 0].reshape(-1, token_count))
+    up_tile = place_rows(recv_rows, my_live, both[:, 1].reshape(-1, token_count))
+    grad_gate = matmul(gate_tile, child_in).astype(jnp.bfloat16)
+    grad_up = matmul(up_tile, child_in).astype(jnp.bfloat16)
+    grad_down = matmul(hid_tile, out_slope).astype(jnp.bfloat16)
     return (grad_gate, grad_up, grad_down, gain_grad, loss_value.reshape(1))
 
 

time: 437 us -> 274 us (0.63)
  blocking collectives: 181 us -> 61.8 us
  local copies, waits for them, and re-layouts: 38.4 us -> 4.72 us
  other arithmetic: 25.1 us -> 14.7 us
  waiting for transfers between devices: 150 us -> 142 us
  matrix products: 17.5 us -> 24.1 us
    all_to_all x2 -> x0, blocking collectives: 103 us -> none  [the longest x1 52.3 us: shards(): lax.all_to_all(outgoing(up_rows, send_rows, send_live), 'fsdp', split_axi...]
    gather x6 -> x0, local copies, waits for them, and re-layouts: 34.3 us -> none  [the longest x3 17.3 us: outgoing(): picked = jnp.take(weights, send_rows, axis=0)]
    unnamed x1, blocking collectives: 77.9 us -> 61.8 us
    dot_general x7 -> x10, matrix products: 12.6 us -> 22.8 us  [matmul(): return jnp.dot(left_side, right_side, preferred_element_type=jnp.float32)]
    psum x1, waiting for transfers between devices: 111 us -> 102 us  [shards(): lax.psum(matmul(child_hid, down_weight) - matmul(parent_hid, down_weight)...]
    select_n x2 -> x1, other arithmetic: 6.06 us -> 0.01 us  [routing(): recv_rows = jnp.where(my_live, my_source * per_pair + my_position, 0)]
    all_to_all x1 -> x0, other arithmetic: 4.93 us -> none  [shards(): lax.all_to_all(outgoing(down_rows, send_rows, send_live), 'fsdp', split_a...]
  transfers between devices with their start and end apart: 3 -> 4, of which waited for: 2 -> 2; matrix products, arithmetic and copies ran while one was open for 7% -> 9% of each run, Pallas kernels for 0% -> 0%
where the time goes in v1:
time: 274 us; the launch traced here: 273 us
  waiting for transfers between devices  142 us (52%)
  blocking collectives  61.8 us (23%)
  matrix products  24.1 us (9%)
  between operations  18.7 us (7%)
  other arithmetic  14.7 us (5%)
  starting transfers between devices  7.41 us (3%)
  local copies, waits for them, and re-layouts  4.72 us (2%)
    psum x1, waiting for transfers between devices, shards(): lax.psum(matmul(child_hid, down_weight) - matmul(parent_hid, down_weight)...  102 us
    unnamed x1, blocking collectives  61.8 us
    all_gather x1, waiting for transfers between devices, shards(): full_rows = lax.all_gather(hidden, 'fsdp', axis=1, tiled=True)  39.3 us
    dot_general x10, matrix products, matmul(): return jnp.dot(left_side, right_side, preferred_element_type=jnp.float32)  22.8 us
  transfers between devices with their start and end apart: 4, of which 2 were waited for; matrix products, arithmetic and copies ran while one was open for 9% of the time, Pallas kernels for 0%

profile of v1, /device:TPU:0, one launch (start us, length us, event | category | flops | bytes accessed | tf_op | source)
XLA Modules:
  0.0 273.3 jit_solution(4467588743268536304)
XLA Ops:
  7.2 0.0 all-gather.2.cloned.1.call-start
  7.2 0.7 all-gather.2.cloned.1.call-update
  7.9 0.0 all-reduce.3.cloned.1.call-start
  8.0 0.7 bitcast_subtract_fusion
  8.7 0.1 copy.40
  8.8 2.8 %select_reduce_fusion = s32[16,128]{0,1:T(8,128)S(1)} fusion(s32[16,128]{0,1:T(8,128)S(1)} %copy.40), kind=kOutput, calls=%fused_computation.31 | output fusion | flops 4388864 | bytes 16384 | tf_op jit(solution)/shard_map/jit(cumsum)/reduce_window_sum | solution.py:18
  11.6 0.1 copy.41
  11.6 0.7 broadcast_compare_fusion.1
  12.4 0.3 select_reduce_fusion.1
  12.7 0.1 copy.43
  12.8 0.4 fusion.25
  13.2 0.1 copy.44
  13.3 0.7 fusion.56
  13.9 0.6 multiply_reduce_fusion.1
  14.6 0.1 gt.11
  14.6 0.1 eq.64
  14.7 0.1 fusion.30
  14.9 39.3 %all-gather.2.cloned.1.call-done = bf16[128,8192]{1,0:T(8,128)(2,1)} async-done(((bf16[128,512]{1,0:T(8,128)(2,1)}), bf16[128,8192]{1,0:T(8,128)(2,1)}) %all-gather.2.cloned.1.call-update) | async-done | bytes 2097168 | tf_op jit(solution)/shard_map/all_gather | solution.py:55
  54.1 2.2 fusion.1
  56.4 0.9 multiply_convert_fusion.1
  57.3 0.6 copy-done.9
  58.0 1.2 fusion.2
  59.2 0.4 copy-done.4
  59.6 1.2 fusion.3
  60.9 0.7 fusion.62
  61.6 2.7 convolution_subtract_fusion
  64.4 0.0 all-reduce.3.cloned.1.call-update
  64.4 0.6 copy-done.8
  65.0 0.6 fusion.58
  67.6 0.6 dynamic-slice
  68.9 0.8 fusion.11
  69.7 3.6 %all-to-all-start.1 = ((bf16[16,8,128]{2,1,0:T(8,128)(2,1)}), bf16[16,8,128]{2,1,0:T(8,128)(2,1)S(1)}, u32[]{:S(2)}, u32[]{:S(2)}) async-start(bf16[16,8,128]{2,1,0:T(8,128)(2,1)} %fusion.11), calls=%async_computation.1 | async-start | bytes 65536 | tf_op jit(solution)/shard_map/all_to_all | solution.py:81
  73.4 102.0 %all-reduce.3.cloned.1.call-done = f32[128,8192]{1,0:T(8,128)} async-done(((f32[128,8192]{1,0:T(8,128)}), f32[128,8192]{1,0:T(8,128)}) %all-reduce.3.cloned.1.call-update) | async-done | bytes 4194320 | tf_op jit(solution)/shard_map/psum | solution.py:83
  175.3 3.1 %select_convert_fusion.1 = (bf16[128,128]{1,0:T(8,128)(2,1)S(1)}, bf16[128,128]{1,0:T(8,128)(2,1)S(1)}) fusion(f32[256,128]{1,0:T(8,128)S(1)} %fusion.2, f32[256,128]{1,0:T(8,128)S(1)} %fusion.3, pred[128]{0:T(512)(128)(4,1)S(1)} %fusion.30, bf16[128,8192]{1,0:T(8,128)(2,1)S(1)} %copy-done, f32[128,8192]{1,0:T(8,128)} %all-reduce.3.cloned.1.call-done), kind=kOutput, calls=%fused_computation.38 | convolution fusion | flops 269729792 | bytes 6488192 | tf_op jit(solution)/shard_map/dot_general | solution.py:8
  178.4 0.2 fusion.9
  178.6 0.7 fusion.63
  179.3 0.2 fusion.10
  179.5 0.7 copy-done.3
  180.2 0.6 copy-done.10
  180.8 1.2 fusion.4
  182.1 0.6 pad_maximum_fusion.3
  182.7 3.7 %all-to-all-start = ((bf16[16,2,8,128]{3,2,1,0:T(8,128)(2,1)}), bf16[16,2,8,128]{3,2,1,0:T(8,128)(2,1)S(1)}, u32[]{:S(2)}, u32[]{:S(2)}) async-start(bf16[16,2,8,128]{3,2,1,0:T(8,128)(2,1)} %pad_maximum_fusion.3), calls=%async_computation | async-start | bytes 131072 | tf_op jit(solution)/shard_map/all_to_all | solution.py:102
  186.4 4.4 %convolution_convert_fusion = bf16[128,8192]{1,0:T(8,128)(2,1)} fusion(f32[128,8192]{1,0:T(8,128)} %all-reduce.3.cloned.1.call-done, bf16[16,8,128]{2,1,0:T(8,128)(2,1)S(1)} %all-to-all-done.1, s32[128]{0:T(128)S(1)} %bitcast_select_fusion, pred[128]{0:T(512)(128)(4,1)S(1)} %compare_bitcast_fusion), kind=kOutput, calls=%fused_computation.3 | convolution fusion | flops 274776064 | bytes 6324864 | tf_op jit(solution)/shard_map/dot_general | solution.py:8
  190.8 3.9 %multiply_reduce_fusion = f32[]{:T(128)} fusion(f32[128,8192]{1,0:T(8,128)} %all-reduce.3.cloned.1.call-done), kind=kLoop, calls=%fused_computation.10 | loop fusion | flops 2097151 | bytes 4194308 | tf_op jit(solution)/shard_map/reduce_sum | solution.py:84
  195.3 61.8 %all-reduce = f32[8192]{0:T(1024)S(1)} all-reduce(f32[8192]{0:T(1024)S(1)} %fusion.4), channel_id=2, replica_groups=mesh['groups'=2,'fsdp'=16] {'fsdp'}, use_global_device_ids=true, to_apply=%region_11.12.clone | all-reduce | flops 8192 | bytes 65536
  257.1 0.7 dynamic-slice.1
  257.8 3.8 %convolution_convert_fusion.1 = bf16[128,8192]{1,0:T(8,128)(2,1)} fusion(bf16[128,8192]{1,0:T(8,128)(2,1)} %copy-done.1, bf16[16,2,8,128]{3,2,1,0:T(8,128)(2,1)S(1)} %all-to-all-done, s32[128]{0:T(128)S(1)} %bitcast_select_fusion, pred[128]{0:T(512)(128)(4,1)S(1)} %compare_bitcast_fusion), kind=kOutput, calls=%fused_computation.4 | convolution fusion | flops 273727488 | bytes 4228096 | tf_op jit(solution)/shard_map/dot_general | solution.py:8
  261.6 3.8 %convolution_convert_fusion.2 = bf16[128,8192]{1,0:T(8,128)(2,1)} fusion(bf16[128,8192]{1,0:T(8,128)(2,1)} %copy-done.1, bf16[16,2,8,128]{3,2,1,0:T(8,128)(2,1)S(1)} %all-to-all-done, s32[128]{0:T(128)S(1)} %bitcast_select_fusion, pred[128]{0:T(512)(128)(4,1)S(1)} %compare_bitcast_fusion), kind=kOutput, calls=%fused_computation.5 | convolution fusion | flops 273727488 | bytes 4228096 | tf_op jit(solution)/shard_map/dot_general | solution.py:8
  (27 shorter events, 0.1 us)
Async XLA Ops:
  7.2 53.8 %copy-start = (bf16[128,8192]{1,0:T(8,128)(2,1)S(1)}, bf16[128,8192]{1,0:T(8,128)(2,1)}, u32[]{:S(2)}) copy-start(bf16[128,8192]{1,0:T(8,128)(2,1)} %param.13) | copy-start | bytes 6291460
  7.2 49.2 %copy-start.7 = (f32[8192]{0:T(1024)S(1)}, f32[8192]{0:T(1024)}, u32[]{:S(2)}) copy-start(f32[8192]{0:T(1024)} %param.10) | copy-start | bytes 98308
  7.2 49.2 %copy-start.6 = (f32[8192]{0:T(1024)S(1)}, f32[8192]{0:T(1024)}, u32[]{:S(2)}) copy-start(f32[8192]{0:T(1024)} %param.9) | copy-start | bytes 98308
  7.2 46.9 %all-gather.2.cloned.1.call-start = ((), (), s32[]{:S(2)}) async-start(), calls=%async_computation.2 | async-start | bytes 2228224 | tf_op jit(solution)/shard_map/all_gather | solution.py:55
  7.9 167.4 %all-reduce.3.cloned.1.call-start = ((), (), s32[]{:S(2)}) async-start(), calls=%async_computation.3 | async-start | bytes 8388608 | tf_op jit(solution)/shard_map/psum | solution.py:83
  54.1 2.3 copy-start.2
  56.4 1.6 copy-start.9
  57.3 1.9 copy-start.1
  58.0 1.7 copy-start.4
  64.4 0.7 copy-start.8
  64.4 3.2 %copy-start.11 = (u32[32]{0:T(128)S(1)}, u32[32]{0:T(128)}, u32[]{:S(2)}) copy-start(u32[32]{0:T(128)} %constant.57) | copy-start | bytes 388
  69.7 113.0 %all-to-all-start.1 = ((bf16[16,8,128]{2,1,0:T(8,128)(2,1)}), bf16[16,8,128]{2,1,0:T(8,128)(2,1)S(1)}, u32[]{:S(2)}, u32[]{:S(2)}) async-start(bf16[16,8,128]{2,1,0:T(8,128)(2,1)} %fusion.11), calls=%async_computation.1 | async-start | bytes 65536 | tf_op jit(solution)/shard_map/all_to_all | solution.py:81
  175.3 3.3 %copy-start.5 = (bf16[128,8192]{1,0:T(8,128)(2,1)S(1)}, bf16[128,8192]{1,0:T(8,128)(2,1)}, u32[]{:S(2)}) copy-start(bf16[128,8192]{1,0:T(8,128)(2,1)} %param.11) | copy-start | bytes 6291460
  178.6 1.6 copy-start.3
  178.6 2.2 copy-start.10
  182.7 75.1 %all-to-all-start = ((bf16[16,2,8,128]{3,2,1,0:T(8,128)(2,1)}), bf16[16,2,8,128]{3,2,1,0:T(8,128)(2,1)S(1)}, u32[]{:S(2)}, u32[]{:S(2)}) async-start(bf16[16,2,8,128]{3,2,1,0:T(8,128)(2,1)} %pad_maximum_fusion.3), calls=%async_computation | async-start | bytes 131072 | tf_op jit(solution)/shard_map/all_to_all | solution.py:102
Sparse Core Ops, SparseCore 0:
  10.2 43.8 all-gather.1
  64.5 110.7 all-reduce.2

commit v2 on v1

v2 whole, which is shorter than its diff:
```python
import functools

import jax
import jax.numpy as jnp
from jax import lax
from jax.experimental import pallas as pl
from jax.experimental.pallas import tpu as pltpu
from jax.sharding import PartitionSpec as P

BF16 = jnp.bfloat16
F32 = jnp.float32
NT = (((1,), (1,)), ((), ()))


def dot(left, right):
    return jnp.dot(left, right, preferred_element_type=F32)


def dot_nt(left, right):
    return lax.dot_general(left, right, NT, preferred_element_type=F32)


class Ring:
    def __init__(self, devices):
        self.chips = devices // 2
        self.snake = self.chips == 8
        self.devices = devices
        self.up_steps = self.chips // 2
        self.down_steps = self.chips - 1 - self.up_steps
        self.sibling = [(i, i ^ 1) for i in range(devices)]

    def chip_at(self, place):
        if not self.snake:
            return place
        return jnp.where(
            place < self.chips // 2, 2 * place, 2 * (self.chips - 1 - place) + 1
        )

    def place_of(self, chip):
        if not self.snake:
            return chip
        return jnp.where(chip % 2 == 0, chip // 2, self.chips - 1 - chip // 2)

    def owner(self, device, distance, core):
        chip = self.chip_at((self.place_of(device // 2) + distance) % self.chips)
        return 2 * chip + (device % 2 + core) % 2

    def shift(self, step):
        pairs = []
        for i in range(self.devices):
            place = i // 2
            if self.snake:
                place = i // 4 if place % 2 == 0 else self.chips - 1 - place // 2
            place = (place + step) % self.chips
            chip = place
            if self.snake:
                half = self.chips // 2
                chip = 2 * place if place < half else 2 * (self.chips - 1 - place) + 1
            pairs.append((i, 2 * chip + i % 2))
        return pairs

    def gather(self, block, device):
        tokens, width = block.shape
        whole = jnp.zeros((tokens, width * self.devices), block.dtype)

        def put(whole, part, distance, core):
            owner = self.owner(device, distance, core)
            return lax.dynamic_update_slice(whole, part, (0, owner * width))

        whole = put(whole, block, 0, 0)
        whole = put(whole, lax.ppermute(block, "fsdp", self.sibling), 0, 1)
        up = down = block
        for step in range(1, self.up_steps + 1):
            both = step <= self.down_steps
            up = lax.ppermute(up, "fsdp", self.shift(1))
            if both:
                down = lax.ppermute(down, "fsdp", self.shift(-1))
            whole = put(whole, up, self.chips - step, 0)
            whole = put(whole, lax.ppermute(up, "fsdp", self.sibling), self.chips - step, 1)
            if both:
                whole = put(whole, down, step, 0)
                whole = put(whole, lax.ppermute(down, "fsdp", self.sibling), step, 1)
        return whole

    def scatter_sum(self, term):
        up = term(self.up_steps)
        down = term(self.up_steps + 1) if self.down_steps else None
        for step in range(1, self.up_steps + 1):
            up = lax.ppermute(up.astype(BF16), "fsdp", self.shift(1)).astype(F32)
            if step <= self.down_steps:
                down = lax.ppermute(down.astype(BF16), "fsdp", self.shift(-1)).astype(F32)
            if step < self.up_steps:
                up = up + term(self.up_steps - step)
            if step < self.down_steps:
                down = down + term(self.up_steps + 1 + step)
        total = term(0) + up
        return total + down if self.down_steps else total


def routing(kept_index, tile_owner, device, devices, parent_rows):
    tile_count = tile_owner.shape[0]
    tile_rows = kept_index.shape[0] // tile_count
    per_pair = tile_rows // devices
    kinds = 3
    slots = devices * kinds * per_pair
    layout = kept_index.reshape(tile_count, tile_rows)
    local = layout - device * parent_rows
    mine = (local >= 0) & (local < parent_rows)
    earlier = jnp.arange(tile_rows)[:, None] < jnp.arange(tile_rows)[None, :]
    position = dot(mine.astype(BF16), earlier.astype(BF16)).astype(jnp.int32)
    slot = jnp.where(mine, tile_owner[:, None] * (kinds * per_pair) + position, -1).reshape(-1)
    at_slot = (slot[None, :] == jnp.arange(slots)[:, None]).astype(BF16)
    at_row = (local.reshape(-1)[:, None] == jnp.arange(parent_rows)[None, :]).astype(BF16)
    send = dot(at_slot, at_row).astype(BF16)
    kept = jnp.any(local.reshape(-1)[:, None] == jnp.arange(parent_rows)[None, :], axis=0)
    mine_row = jnp.sum(jnp.where((tile_owner == device)[:, None], layout, 0), axis=0)
    source = jnp.where(mine_row >= 0, mine_row // parent_rows, -1)
    same = (source[:, None] == source[None, :]) & earlier.T
    rank = jnp.sum(same.astype(jnp.int32), axis=1)
    from_slot = jnp.where(mine_row >= 0, source * (kinds * per_pair) + rank, -slots)
    place = (from_slot[:, None] == jnp.arange(slots)[None, :]).astype(BF16)
    return send, place, kept.astype(F32).reshape(1, parent_rows), per_pair


def forward_kernel(
    ring,
    hidden,
    parent_gain,
    child_gain,
    gate,
    up,
    down,
    kept,
    child_in,
    scale,
    child_gate,
    child_up,
    child_hid,
    keep,
    send,
):
    tokens, features = hidden.shape
    width = features // ring.devices
    pieces = 16
    piece = features // pieces
    cuts = [slice(k * piece, (k + 1) * piece) for k in range(pieces)]
    squares = jnp.zeros((tokens, piece), F32)
    for cols in cuts:
        h = hidden[:, cols].astype(F32)
        squares = squares + h * h
    mean = jnp.sum(squares, axis=1, keepdims=True) / features
    inverse = 1.0 / jnp.sqrt(mean + 1e-05)
    scale[...] = jnp.broadcast_to(inverse, scale.shape)
    gate_both = jnp.zeros((2 * tokens, gate.shape[0]), F32)
    up_both = jnp.zeros((2 * tokens, gate.shape[0]), F32)
    for cols in cuts:
        normed = hidden[:, cols].astype(F32) * inverse
        parent = (normed * parent_gain[:, cols]).astype(BF16)
        child = (normed * child_gain[:, cols]).astype(BF16)
        child_in[:, cols] = child
        both = jnp.concatenate([parent, child], axis=0)
        gate_both = gate_both + dot_nt(both, gate[:, cols])
        up_both = up_both + dot_nt(both, up[:, cols])
    hid = gate_both * jax.nn.sigmoid(gate_both) * up_both
    child_gate[...] = gate_both[tokens:]
    child_up[...] = up_both[tokens:]
    child = jnp.where(kept[...] > 0, hid[tokens:], 0.0).astype(BF16)
    child_hid[...] = child
    both_hid = jnp.concatenate([child, -hid[:tokens].astype(BF16)], axis=0)
    device = lax.axis_index("fsdp")
    for core, target in ((1, send), (0, keep)):
        for distance in range(ring.chips):
            start = ring.owner(device, distance, core) * width
            out = dot(both_hid, down[:, pl.ds(pl.multiple_of(start, width), width)])
            target[distance] = out[:tokens] + out[tokens:]


def slope_kernel(
    slope, down, kept, child_gate, child_up, child_hid, select, gate_back, up_back, sent
):
    child_slope = dot_nt(slope[...], down[...])
    g, u = child_gate[...], child_up[...]
    sig = jax.nn.sigmoid(g)
    live = kept[...] > 0
    for_gate = child_slope * u * sig * (1.0 + g * (1.0 - sig))
    for_gate = jnp.where(live, for_gate, 0.0).astype(BF16)
    for_up = jnp.where(live, child_slope * g * sig, 0.0).astype(BF16)
    gate_back[...] = for_gate
    up_back[...] = for_up
    sent[...] = (
        dot_nt(select[0], for_gate) + dot_nt(select[1], for_up) + dot_nt(select[2], child_hid[...])
    ).astype(BF16)


def gain_kernel(gate_back, up_back, gate, up, hidden, scale, difference, lanes):
    devices, rows, _ = lanes.shape
    width = hidden.shape[1] // devices
    inverse = scale[...][:, :1]
    loss = jnp.sum(difference[...] * difference[...], axis=0, keepdims=True)
    loss = jnp.broadcast_to(jnp.sum(loss, axis=1, keepdims=True), (1, 128))
    for k in range(devices):
        cols = slice(k * width, (k + 1) * width)
        input_slope = dot(gate_back[...], gate[:, cols]) + dot(up_back[...], up[:, cols])
        normed = hidden[:, cols].astype(F32) * inverse
        part = jnp.sum(input_slope * normed, axis=0, keepdims=True)
        for r in range(width // 128):
            lanes[k, r : r + 1, :] = part[:, r * 128 : (r + 1) * 128]
        lanes[k, width // 128 : width // 128 + 1, :] = loss


def rows_kernel(received, place, child_in, slope, grad_gate, grad_up, grad_down, tiles):
    rows = grad_gate.shape[0]

    @pl.when(pl.program_id(0) == 0)
    def _():
        for kind in range(3):
            tiles[kind * rows : (kind + 1) * rows, :] = dot(place[kind], received[...]).astype(BF16)

    out = dot(tiles[: 2 * rows, :], child_in[...]).astype(BF16)
    grad_gate[...] = out[:rows]
    grad_up[...] = out[rows:]
    grad_down[...] = dot(tiles[2 * rows :, :], slope[...]).astype(BF16)


VMEM = pl.BlockSpec(memory_space=pltpu.VMEM)
MIB = 1024 * 1024


def call(kernel, outs, operands, limit, name):
    return pl.pallas_call(
        kernel,
        out_shape=[jax.ShapeDtypeStruct(shape, dtype) for shape, dtype in outs],
        in_specs=[VMEM] * len(operands),
        out_specs=[VMEM] * len(outs),
        compiler_params=pltpu.CompilerParams(vmem_limit_bytes=limit * MIB),
        name=name,
    )(*operands)


def shards(
    hidden, parent_gain, child_gain, gate_weight, up_weight, down_weight, kept_index, tile_owner
):
    devices = lax.axis_size("fsdp")
    device = lax.axis_index("fsdp")
    ring = Ring(devices)
    chips = ring.chips
    parent_rows = gate_weight.shape[0]
    tokens, width = hidden.shape
    features = width * devices
    send, place, kept, per_pair = routing(kept_index, tile_owner, device, devices, parent_rows)
    select = jnp.stack([jnp.roll(send, kind * per_pair, axis=0) for kind in range(3)])
    places = jnp.stack([jnp.roll(place, kind * per_pair, axis=1) for kind in range(3)])

    square = ((tokens, parent_rows), F32)
    wide = ((tokens, features), BF16)
    hidden_all = ring.gather(hidden, device)
    child_in, scale, child_gate, child_up, child_hid, keep, other = call(
        functools.partial(forward_kernel, ring),
        [
            wide,
            ((tokens, 128), F32),
            square,
            square,
            ((tokens, parent_rows), BF16),
            ((chips, tokens, width), F32),
            ((chips, tokens, width), F32),
        ],
        [
            hidden_all,
            parent_gain.reshape(1, features),
            child_gain.reshape(1, features),
            gate_weight,
            up_weight,
            down_weight,
            kept,
        ],
        limit=20,
        name="forward",
    )
    first = list(range(ring.up_steps, min(ring.up_steps + 2, chips)))
    rest = [j for j in range(chips) if j not in first]
    swapped = {}
    lead = lax.ppermute(other[first[0] : first[-1] + 1], "fsdp", ring.sibling)
    for i, j in enumerate(first):
        swapped[j] = lead[i]
    for run in ([j for j in rest if j < first[0]], [j for j in rest if j > first[-1]]):
        if run:
            part = lax.ppermute(other[run[0] : run[-1] + 1], "fsdp", ring.sibling)
            for i, j in enumerate(run):
                swapped[j] = part[i]
    difference = ring.scatter_sum(lambda j: keep[j] + swapped[j])
    slope_all = ring.gather(difference.astype(BF16), device)

    slots = send.shape[0]
    gate_back, up_back, sent = call(
        slope_kernel,
        [((tokens, parent_rows), BF16), ((tokens, parent_rows), BF16), ((slots, tokens), BF16)],
        [slope_all, down_weight, kept, child_gate, child_up, child_hid, select],
        limit=8,
        name="slope",
    )
    received = lax.all_to_all(
        sent.reshape(devices, slots // devices, tokens), "fsdp", 0, 0, tiled=True
    ).reshape(slots, tokens)
    gain_rows = width // 128
    (lanes,) = call(
        gain_kernel,
        [((devices, -(-(gain_rows + 1) // 8) * 8, 128), F32)],
        [gate_back, up_back, gate_weight, up_weight, hidden_all, scale, difference],
        limit=8,
        name="gain",
    )
    received, lanes = lax.optimization_barrier((received, lanes))
    lanes = jnp.sum(lax.all_to_all(lanes, "fsdp", 0, 0, tiled=True), axis=0)
    gain_grad = lanes[:gain_rows].reshape(width)
    loss_value = 0.5 * lanes[gain_rows, :1] / (tokens * features)

    cut = min(features, 1024)
    column = pl.BlockSpec((tokens, cut), lambda i: (0, i))
    grad = pl.BlockSpec((parent_rows, cut), lambda i: (0, i))
    grad_gate, grad_up, grad_down = pl.pallas_call(
        rows_kernel,
        out_shape=[jax.ShapeDtypeStruct((parent_rows, features), BF16)] * 3,
        grid=(features // cut,),
        in_specs=[
            pl.BlockSpec((slots, tokens), lambda i: (0, 0)),
            pl.BlockSpec(places.shape, lambda i: (0, 0, 0)),
            column,
            column,
        ],
        out_specs=[grad] * 3,
        scratch_shapes=[pltpu.VMEM((3 * parent_rows, tokens), BF16)],
        compiler_params=pltpu.CompilerParams(vmem_limit_bytes=8 * MIB),
        name="rows",
    )(received, places, child_in, slope_all)
    return (grad_gate, grad_up, grad_down, gain_grad, loss_value)


def solution(mesh):
    placed = (
        P("groups", "fsdp"),
        P("groups"),
        P("groups"),
        P(("groups", "fsdp"), None),
        P(("groups", "fsdp"), None),
        P(("groups", "fsdp"), None),
        P("groups"),
        P("groups"),
    )
    return jax.shard_map(
        shards,
        mesh=mesh,
        in_specs=placed,
        out_specs=(
            P(("groups", "fsdp"), None),
            P(("groups", "fsdp"), None),
            P(("groups", "fsdp"), None),
            P(("groups", "fsdp")),
            P("groups"),
        ),
        check_vma=False,
    )
```

time: 274 us -> 114 us (0.42)
  waiting for transfers between devices: 142 us -> 47.3 us
  blocking collectives: 61.8 us -> 0 us
  starting transfers between devices: 7.41 us -> 36.3 us
  matrix products: 24.1 us -> 0.94 us
  between operations: 18.7 us -> 3.42 us
  Pallas kernels: 0 us -> 13 us
  other arithmetic: 14.7 us -> 2.3 us
  local copies, waits for them, and re-layouts: 4.72 us -> 9.83 us
    psum x1 -> x0, waiting for transfers between devices: 102 us -> none  [shards(): lax.psum(matmul(child_hid, down_weight) - matmul(parent_hid, down_weight)...]
    unnamed x1 -> x0, blocking collectives: 61.8 us -> none
    ppermute x0 -> x40, waiting for transfers between devices: none -> 46.6 us  [the longest x8 28.2 us: gather(): up = lax.ppermute(up, 'fsdp', self.shift(1))]
    all_gather x1 -> x0, waiting for transfers between devices: 39.3 us -> none  [shards(): full_rows = lax.all_gather(hidden, 'fsdp', axis=1, tiled=True)]
    ppermute x0 -> x40, starting transfers between devices: none -> 26.9 us  [the longest x8 14.4 us: gather(): up = lax.ppermute(up, 'fsdp', self.shift(1))]
    dot_general x13 -> x2, matrix products: 24.1 us -> 0.94 us  [dot(): return jnp.dot(left, right, preferred_element_type=F32)]
    pallas_call x0 -> x4, Pallas kernels: none -> 13 us  [the longest x3 7.67 us: call(): pl.pallas_call(kernel, out_shape=[jax.ShapeDtypeStruct(shape, dtype) for...]
    reduce_sum x5 -> x3, other arithmetic: 7.69 us -> 0.28 us  [the longest x1 0.17 us: routing(): rank = jnp.sum(same.astype(jnp.int32), axis=1)]
  transfers between devices with their start and end apart: 4 -> 42, of which waited for: 2 -> 19; matrix products, arithmetic and copies ran while one was open for 9% -> 3% of each run, Pallas kernels for 0% -> 6%
where the time goes in v2:
time: 114 us; the launch traced here: 113 us
  waiting for transfers between devices  47.3 us (41%)
  starting transfers between devices  36.3 us (32%)
  Pallas kernels  13 us (11%)
  local copies, waits for them, and re-layouts  9.83 us (9%)
  between operations  3.42 us (3%)
  other arithmetic  2.3 us (2%)
    ppermute x8, waiting for transfers between devices, gather(): up = lax.ppermute(up, 'fsdp', self.shift(1))  28.2 us
    ppermute x8, starting transfers between devices, gather(): up = lax.ppermute(up, 'fsdp', self.shift(1))  14.4 us
    ppermute x4, waiting for transfers between devices, scatter_sum(): up = lax.ppermute(up.astype(BF16), 'fsdp', self.shift(1)).astype(F32)  11.9 us
    pallas_call x3, Pallas kernels, call(): pl.pallas_call(kernel, out_shape=[jax.ShapeDtypeStruct(shape, dtype) for...  7.67 us
    unnamed x32, local copies, waits for them, and re-layouts  7.51 us
    ppermute x4, starting transfers between devices, scatter_sum(): up = lax.ppermute(up.astype(BF16), 'fsdp', self.shift(1)).astype(F32)  7.16 us
    all_to_all x1, starting transfers between devices, shards(): lanes = jnp.sum(lax.all_to_all(lanes, 'fsdp', 0, 0, tiled=True), axis=0)  5.34 us
    pallas_call x1, Pallas kernels, shards(): pl.pallas_call(rows_kernel, out_shape=[jax.ShapeDtypeStruct((parent_rows,...  5.3 us
  transfers between devices with their start and end apart: 42, of which 19 were waited for; matrix products, arithmetic and copies ran while one was open for 3% of the time, Pallas kernels for 6%

profile of v2, /device:TPU:0, one launch (start us, length us, event | category | flops | bytes accessed | tf_op | source)
XLA Modules:
  0.0 113.1 jit_solution(5334264425551088198)
XLA Ops:
  0.6 0.5 collective-permute-start
  1.2 2.6 %collective-permute-start.1 = (bf16[128,512]{1,0:T(8,128)(2,1)}, bf16[128,512]{1,0:T(8,128)(2,1)S(1)}, u32[]{:S(2)}, u32[]{:S(2)}) collective-permute-start(bf16[128,512]{1,0:T(8,128)(2,1)} %param.8), channel_id=1, source_target_pairs={{0,4},{1,5},{2,0},{3,1},{4,8},{5,9},{6,2},{7,3},{8,12},{9,13},{10,... | collective-permute-start | bytes 393224 | tf_op jit(solution)/shard_map/ppermute | solution.py:75
  3.8 0.7 broadcast_subtract_fusion
  5.5 2.5 %collective-permute-done.1 = bf16[128,512]{1,0:T(8,128)(2,1)S(1)} collective-permute-done((bf16[128,512]{1,0:T(8,128)(2,1)}, bf16[128,512]{1,0:T(8,128)(2,1)S(1)}, u32[]{:S(2)}, u32[]{:S(2)}) %collective-permute-start.1) | collective-permute-done | bytes 131104 | tf_op jit(solution)/shard_map/ppermute | solution.py:75
  8.1 1.8 %collective-permute-start.5 = (bf16[128,512]{1,0:T(8,128)(2,1)S(1)}, bf16[128,512]{1,0:T(8,128)(2,1)S(1)}, u32[]{:S(2)}, u32[]{:S(2)}) collective-permute-start(bf16[128,512]{1,0:T(8,128)(2,1)S(1)} %collective-permute-done.1), channel_id=1, source_target_pairs={{0,4},{1,5},{2,0},{3,1},{4,8},{5,9},{6,2},{7,3},{8,12},{9,13},{10,... | collective-permute-start | bytes 393224 | tf_op jit(solution)/shard_map/ppermute | solution.py:75
  10.4 3.6 %collective-permute-done.5 = bf16[128,512]{1,0:T(8,128)(2,1)S(1)} collective-permute-done((bf16[128,512]{1,0:T(8,128)(2,1)S(1)}, bf16[128,512]{1,0:T(8,128)(2,1)S(1)}, u32[]{:S(2)}, u32[]{:S(2)}) %collective-permute-start.5) | collective-permute-done | bytes 131104 | tf_op jit(solution)/shard_map/ppermute | solution.py:75
  14.0 1.8 %collective-permute-start.9 = (bf16[128,512]{1,0:T(8,128)(2,1)S(1)}, bf16[128,512]{1,0:T(8,128)(2,1)S(1)}, u32[]{:S(2)}, u32[]{:S(2)}) collective-permute-start(bf16[128,512]{1,0:T(8,128)(2,1)S(1)} %collective-permute-done.5), channel_id=1, source_target_pairs={{0,4},{1,5},{2,0},{3,1},{4,8},{5,9},{6,2},{7,3},{8,12},{9,13},{10,... | collective-permute-start | bytes 393224 | tf_op jit(solution)/shard_map/ppermute | solution.py:75
  16.3 3.5 %collective-permute-done.9 = bf16[128,512]{1,0:T(8,128)(2,1)S(1)} collective-permute-done((bf16[128,512]{1,0:T(8,128)(2,1)S(1)}, bf16[128,512]{1,0:T(8,128)(2,1)S(1)}, u32[]{:S(2)}, u32[]{:S(2)}) %collective-permute-start.9) | collective-permute-done | bytes 131104 | tf_op jit(solution)/shard_map/ppermute | solution.py:75
  19.9 1.8 %collective-permute-start.13 = (bf16[128,512]{1,0:T(8,128)(2,1)S(1)}, bf16[128,512]{1,0:T(8,128)(2,1)S(1)}, u32[]{:S(2)}, u32[]{:S(2)}) collective-permute-start(bf16[128,512]{1,0:T(8,128)(2,1)S(1)} %collective-permute-done.9), channel_id=1, source_target_pairs={{0,4},{1,5},{2,0},{3,1},{4,8},{5,9},{6,2},{7,3},{8,12},{9,13},{10,... | collective-permute-start | bytes 393224 | tf_op jit(solution)/shard_map/ppermute | solution.py:75
  22.0 3.8 %collective-permute-done.13 = bf16[128,512]{1,0:T(8,128)(2,1)S(1)} collective-permute-done((bf16[128,512]{1,0:T(8,128)(2,1)S(1)}, bf16[128,512]{1,0:T(8,128)(2,1)S(1)}, u32[]{:S(2)}, u32[]{:S(2)}) %collective-permute-start.13) | collective-permute-done | bytes 131104 | tf_op jit(solution)/shard_map/ppermute | solution.py:75
  25.9 1.2 %collective-permute-done.14 = bf16[128,512]{1,0:T(8,128)(2,1)S(1)} collective-permute-done((bf16[128,512]{1,0:T(8,128)(2,1)S(1)}, bf16[128,512]{1,0:T(8,128)(2,1)S(1)}, u32[]{:S(2)}, u32[]{:S(2)}) %collective-permute-start.14) | collective-permute-done | bytes 131104 | tf_op jit(solution)/shard_map/ppermute | solution.py:79
  27.2 4.1 %forward.1 = (bf16[128,8192]{1,0:T(8,128)(2,1)S(1)}, f32[128,128]{1,0:T(8,128)S(1)}, f32[128,128]{1,0:T(8,128)S(1)}, f32[128,128]{1,0:T(8,128)S(1)}, bf16[128,12...) custom-call(bf16[128,8192]{1,0:T(8,128)(2,1)S(1)} %constant_dynamic-update-slice_fusion.16.hidden, ...), custom_call_target="tpu_custom_call" | custom-call | tf_op jit(solution)/shard_map/forward/pallas_call | solution.py:230
  31.6 1.1 copy-done.7
  33.3 0.8 fusion.2
  34.7 1.8 %collective-permute-start.17 = (bf16[128,512]{1,0:T(8,128)(2,1)S(1)}, bf16[128,512]{1,0:T(8,128)(2,1)S(1)}, u32[]{:S(2)}, u32[]{:S(2)}) collective-permute-start(bf16[128,512]{1,0:T(8,128)(2,1)S(1)} %get-tuple-element.38), channel_id=1, source_target_pairs={{0,4},{1,5},{2,0},{3,1},{4,8},{5,9},{6,2},{7,3},{8,12},{9,13},{10,... | collective-permute-start | bytes 393224 | tf_op jit(solution)/shard_map/ppermute | solution.py:89
  37.0 3.3 %collective-permute-done.17 = bf16[128,512]{1,0:T(8,128)(2,1)S(1)} collective-permute-done((bf16[128,512]{1,0:T(8,128)(2,1)S(1)}, bf16[128,512]{1,0:T(8,128)(2,1)S(1)}, u32[]{:S(2)}, u32[]{:S(2)}) %collective-permute-start.17) | collective-permute-done | bytes 131104 | tf_op jit(solution)/shard_map/ppermute | solution.py:89
  40.4 1.8 %collective-permute-start.18 = (bf16[128,512]{1,0:T(8,128)(2,1)S(1)}, bf16[128,512]{1,0:T(8,128)(2,1)S(1)}, u32[]{:S(2)}, u32[]{:S(2)}) collective-permute-start(bf16[128,512]{1,0:T(8,128)(2,1)S(1)} %fusion.23), channel_id=1, source_target_pairs={{0,4},{1,5},{2,0},{3,1},{4,8},{5,9},{6,2},{7,3},{8,12},{9,13},{10,... | collective-permute-start | bytes 393224 | tf_op jit(solution)/shard_map/ppermute | solution.py:89
  42.6 2.8 %collective-permute-done.18 = bf16[128,512]{1,0:T(8,128)(2,1)S(1)} collective-permute-done((bf16[128,512]{1,0:T(8,128)(2,1)S(1)}, bf16[128,512]{1,0:T(8,128)(2,1)S(1)}, u32[]{:S(2)}, u32[]{:S(2)}) %collective-permute-start.18) | collective-permute-done | bytes 131104 | tf_op jit(solution)/shard_map/ppermute | solution.py:89
  45.5 1.8 %collective-permute-start.19 = (bf16[128,512]{1,0:T(8,128)(2,1)S(1)}, bf16[128,512]{1,0:T(8,128)(2,1)S(1)}, u32[]{:S(2)}, u32[]{:S(2)}) collective-permute-start(bf16[128,512]{1,0:T(8,128)(2,1)S(1)} %get-tuple-element.42), channel_id=1, source_target_pairs={{0,4},{1,5},{2,0},{3,1},{4,8},{5,9},{6,2},{7,3},{8,12},{9,13},{10,... | collective-permute-start | bytes 393224 | tf_op jit(solution)/shard_map/ppermute | solution.py:89
  47.6 2.9 %collective-permute-done.19 = bf16[128,512]{1,0:T(8,128)(2,1)S(1)} collective-permute-done((bf16[128,512]{1,0:T(8,128)(2,1)S(1)}, bf16[128,512]{1,0:T(8,128)(2,1)S(1)}, u32[]{:S(2)}, u32[]{:S(2)}) %collective-permute-start.19) | collective-permute-done | bytes 131104 | tf_op jit(solution)/shard_map/ppermute | solution.py:89
  50.5 1.8 %collective-permute-done.23 = bf16[128,512]{1,0:T(8,128)(2,1)S(1)} collective-permute-done((bf16[128,512]{1,0:T(8,128)(2,1)S(1)}, bf16[128,512]{1,0:T(8,128)(2,1)S(1)}, u32[]{:S(2)}, u32[]{:S(2)}) %collective-permute-start.23) | collective-permute-done | bytes 131104 | tf_op jit(solution)/shard_map/ppermute | solution.py:91
  52.5 1.6 %collective-permute-start.20 = (bf16[128,512]{1,0:T(8,128)(2,1)S(1)}, bf16[128,512]{1,0:T(8,128)(2,1)S(1)}, u32[]{:S(2)}, u32[]{:S(2)}) collective-permute-start(bf16[128,512]{1,0:T(8,128)(2,1)S(1)} %get-tuple-element.40), channel_id=1, source_target_pairs={{0,4},{1,5},{2,0},{3,1},{4,8},{5,9},{6,2},{7,3},{8,12},{9,13},{10,... | collective-permute-start | bytes 393224 | tf_op jit(solution)/shard_map/ppermute | solution.py:89
  54.7 2.9 %collective-permute-done.20 = bf16[128,512]{1,0:T(8,128)(2,1)S(1)} collective-permute-done((bf16[128,512]{1,0:T(8,128)(2,1)S(1)}, bf16[128,512]{1,0:T(8,128)(2,1)S(1)}, u32[]{:S(2)}, u32[]{:S(2)}) %collective-permute-start.20) | collective-permute-done | bytes 131104 | tf_op jit(solution)/shard_map/ppermute | solution.py:89
  57.6 1.6 %collective-permute-done.24 = bf16[128,512]{1,0:T(8,128)(2,1)S(1)} collective-permute-done((bf16[128,512]{1,0:T(8,128)(2,1)S(1)}, bf16[128,512]{1,0:T(8,128)(2,1)S(1)}, u32[]{:S(2)}, u32[]{:S(2)}) %collective-permute-start.24) | collective-permute-done | bytes 131104 | tf_op jit(solution)/shard_map/ppermute | solution.py:91
  59.5 1.6 %collective-permute-start.26 = (bf16[128,512]{1,0:T(8,128)(2,1)S(1)}, bf16[128,512]{1,0:T(8,128)(2,1)S(1)}, u32[]{:S(2)}, u32[]{:S(2)}) collective-permute-start(bf16[128,512]{1,0:T(8,128)(2,1)S(1)} %get-tuple-element.36), channel_id=1, source_target_pairs={{0,4},{1,5},{2,0},{3,1},{4,8},{5,9},{6,2},{7,3},{8,12},{9,13},{10,... | collective-permute-start | bytes 393224 | tf_op jit(solution)/shard_map/ppermute | solution.py:75
  61.2 0.4 collective-permute-start.28
  61.8 3.6 %collective-permute-done.26 = bf16[128,512]{1,0:T(8,128)(2,1)S(1)} collective-permute-done((bf16[128,512]{1,0:T(8,128)(2,1)S(1)}, bf16[128,512]{1,0:T(8,128)(2,1)S(1)}, u32[]{:S(2)}, u32[]{:S(2)}) %collective-permute-start.26) | collective-permute-done | bytes 131104 | tf_op jit(solution)/shard_map/ppermute | solution.py:75
  65.4 1.6 %collective-permute-start.30 = (bf16[128,512]{1,0:T(8,128)(2,1)S(1)}, bf16[128,512]{1,0:T(8,128)(2,1)S(1)}, u32[]{:S(2)}, u32[]{:S(2)}) collective-permute-start(bf16[128,512]{1,0:T(8,128)(2,1)S(1)} %collective-permute-done.26), channel_id=1, source_target_pairs={{0,4},{1,5},{2,0},{3,1},{4,8},{5,9},{6,2},{7,3},{8,12},{9,13},{10,... | collective-permute-start | bytes 393224 | tf_op jit(solution)/shard_map/ppermute | solution.py:75
  67.2 0.4 collective-permute-start.32
  67.7 3.6 %collective-permute-done.30 = bf16[128,512]{1,0:T(8,128)(2,1)S(1)} collective-permute-done((bf16[128,512]{1,0:T(8,128)(2,1)S(1)}, bf16[128,512]{1,0:T(8,128)(2,1)S(1)}, u32[]{:S(2)}, u32[]{:S(2)}) %collective-permute-start.30) | collective-permute-done | bytes 131104 | tf_op jit(solution)/shard_map/ppermute | solution.py:75
  71.3 1.6 %collective-permute-start.34 = (bf16[128,512]{1,0:T(8,128)(2,1)S(1)}, bf16[128,512]{1,0:T(8,128)(2,1)S(1)}, u32[]{:S(2)}, u32[]{:S(2)}) collective-permute-start(bf16[128,512]{1,0:T(8,128)(2,1)S(1)} %collective-permute-done.30), channel_id=1, source_target_pairs={{0,4},{1,5},{2,0},{3,1},{4,8},{5,9},{6,2},{7,3},{8,12},{9,13},{10,... | collective-permute-start | bytes 393224 | tf_op jit(solution)/shard_map/ppermute | solution.py:75
  73.2 0.4 collective-permute-start.36
  73.7 3.5 %collective-permute-done.34 = bf16[128,512]{1,0:T(8,128)(2,1)S(1)} collective-permute-done((bf16[128,512]{1,0:T(8,128)(2,1)S(1)}, bf16[128,512]{1,0:T(8,128)(2,1)S(1)}, u32[]{:S(2)}, u32[]{:S(2)}) %collective-permute-start.34) | collective-permute-done | bytes 131104 | tf_op jit(solution)/shard_map/ppermute | solution.py:75
  77.3 1.6 %collective-permute-start.38 = (bf16[128,512]{1,0:T(8,128)(2,1)S(1)}, bf16[128,512]{1,0:T(8,128)(2,1)S(1)}, u32[]{:S(2)}, u32[]{:S(2)}) collective-permute-start(bf16[128,512]{1,0:T(8,128)(2,1)S(1)} %collective-permute-done.34), channel_id=1, source_target_pairs={{0,4},{1,5},{2,0},{3,1},{4,8},{5,9},{6,2},{7,3},{8,12},{9,13},{10,... | collective-permute-start | bytes 393224 | tf_op jit(solution)/shard_map/ppermute | solution.py:75
  79.2 4.0 %collective-permute-done.38 = bf16[128,512]{1,0:T(8,128)(2,1)S(1)} collective-permute-done((bf16[128,512]{1,0:T(8,128)(2,1)S(1)}, bf16[128,512]{1,0:T(8,128)(2,1)S(1)}, u32[]{:S(2)}, u32[]{:S(2)}) %collective-permute-start.38) | collective-permute-done | bytes 131104 | tf_op jit(solution)/shard_map/ppermute | solution.py:75
  83.3 1.2 %collective-permute-done.39 = bf16[128,512]{1,0:T(8,128)(2,1)S(1)} collective-permute-done((bf16[128,512]{1,0:T(8,128)(2,1)S(1)}, bf16[128,512]{1,0:T(8,128)(2,1)S(1)}, u32[]{:S(2)}, u32[]{:S(2)}) %collective-permute-start.39) | collective-permute-done | bytes 131104 | tf_op jit(solution)/shard_map/ppermute | solution.py:79
  84.5 1.7 %slope.1 = (bf16[128,128]{1,0:T(8,128)(2,1)S(1)}, bf16[128,128]{1,0:T(8,128)(2,1)S(1)}, bf16[384,128]{1,0:T(8,128)(2,1)}) custom-call(bf16[128,8192]{1,0:T(8,128)(2,1)S(1)} %constant_dynamic-update-slice_fusion.slope, bf16[128,8192]{1,0:T(8,128)(2,1)S(1)} %copy-done.2, f32[1,128]{1,0:T(1,128)S(1)} %convert_bitcast_fusion.kept, ...), custom_call_target="tpu_custom_call" | custom-call | tf_op jit(solution)/shard_map/slope/pallas_call | solution.py:230
  86.2 4.1 %all-to-all-start = ((bf16[16,24,128]{2,1,0:T(8,128)(2,1)}), bf16[16,24,128]{2,1,0:T(8,128)(2,1)S(1)}, u32[]{:S(2)}, u32[]{:S(2)}) async-start(bf16[16,24,128]{2,1,0:T(8,128)(2,1)} %bitcast.16), calls=%async_computation | async-start | bytes 196608 | tf_op jit(solution)/shard_map/all_to_all | solution.py:302
  90.5 1.6 %copy-done.1 = bf16[128,8192]{1,0:T(8,128)(2,1)S(1)} copy-done((bf16[128,8192]{1,0:T(8,128)(2,1)S(1)}, bf16[128,8192]{1,0:T(8,128)(2,1)}, u32[]{:S(2)}) %copy-start.1) | copy-done | bytes 2097176
  92.0 1.6 %copy-done.4 = bf16[128,8192]{1,0:T(8,128)(2,1)S(1)} copy-done((bf16[128,8192]{1,0:T(8,128)(2,1)S(1)}, bf16[128,8192]{1,0:T(8,128)(2,1)}, u32[]{:S(2)}) %copy-start.4) | copy-done | bytes 2097176
  93.6 1.6 %copy-done.6 = bf16[128,8192]{1,0:T(8,128)(2,1)S(1)} copy-done((bf16[128,8192]{1,0:T(8,128)(2,1)S(1)}, bf16[128,8192]{1,0:T(8,128)(2,1)}, u32[]{:S(2)}) %copy-start.6) | copy-done | bytes 2097176
  95.2 1.9 %gain.1 = f32[16,8,128]{2,1,0:T(8,128)} custom-call(bf16[128,128]{1,0:T(8,128)(2,1)S(1)} %get-tuple-element.26.gate_back, bf16[128,128]{1,0:T(8,128)(2,1)S(1)} %get-tuple-element.27.up_back, bf16[128,8192]{1,0:T(8,128)(2,1)S(1)} %copy-done.4, bf16[128,8192]{1,0:T(8,128)(2,1)S(1)} %copy-done.6, bf16[128,8192]{1,0:T(8,128)(2,1)S(1)} %copy-done.1, ...), custom_call_target="tpu_custom_call" | custom-call | tf_op jit(solution)/shard_map/gain/pallas_call | solution.py:230
  97.1 0.7 all-to-all-done
  97.8 5.3 %all-to-all-start.1 = ((f32[16,8,128]{2,1,0:T(8,128)}), f32[16,8,128]{2,1,0:T(8,128)S(1)}, u32[]{:S(2)}, u32[]{:S(2)}) async-start(f32[16,8,128]{2,1,0:T(8,128)} %gain.1), calls=%async_computation.1 | async-start | bytes 131072 | tf_op jit(solution)/shard_map/all_to_all | solution.py:314
  103.3 1.6 %copy-done.8 = bf16[128,8192]{1,0:T(8,128)(2,1)S(1)} copy-done((bf16[128,8192]{1,0:T(8,128)(2,1)S(1)}, bf16[128,8192]{1,0:T(8,128)(2,1)}, u32[]{:S(2)}) %copy-start.8) | copy-done | bytes 2097176
  104.9 5.3 %rows.1 = (bf16[128,8192]{1,0:T(8,128)(2,1)}, bf16[128,8192]{1,0:T(8,128)(2,1)}, bf16[128,8192]{1,0:T(8,128)(2,1)}) custom-call(bf16[384,128]{1,0:T(8,128)(2,1)S(1)} %bitcast.74, bf16[3,128,384]{2,1,0:T(8,128)(2,1)S(1)} %pad_maximum_fusion.1.place, bf16[128,8192]{1,0:T(8,128)(2,1)S(1)} %copy-done.8, bf16[128,8192]{1,0:T(8,128)(2,1)S(1)} %constant_dynamic-update-slice_fusion.slope), custom_call_target="tpu_custom_call" | custom-call | tf_op jit(solution)/shard_map/rows/pallas_call | solution.py:321
  110.2 0.6 slice_bitcast_fusion
  110.8 0.5 slice.123
  (142 shorter events, 7.1 us)
Async XLA Ops:
  0.6 9.7 %collective-permute-start = (bf16[128,512]{1,0:T(8,128)(2,1)}, bf16[128,512]{1,0:T(8,128)(2,1)S(1)}, u32[]{:S(2)}, u32[]{:S(2)}) collective-permute-start(bf16[128,512]{1,0:T(8,128)(2,1)} %param.8), channel_id=1, source_target_pairs={{0,1},{1,0},{2,3},{3,2},{4,5},{5,4},{6,7},{7,6},{8,9},{9,8},{10,11... | collective-permute-start | bytes 393224 | tf_op jit(solution)/shard_map/ppermute | solution.py:71
  1.2 6.9 %collective-permute-start.1 = (bf16[128,512]{1,0:T(8,128)(2,1)}, bf16[128,512]{1,0:T(8,128)(2,1)S(1)}, u32[]{:S(2)}, u32[]{:S(2)}) collective-permute-start(bf16[128,512]{1,0:T(8,128)(2,1)} %param.8), channel_id=1, source_target_pairs={{0,4},{1,5},{2,0},{3,1},{4,8},{5,9},{6,2},{7,3},{8,12},{9,13},{10,... | collective-permute-start | bytes 393224 | tf_op jit(solution)/shard_map/ppermute | solution.py:75
  3.8 6.1 %collective-permute-start.3 = (bf16[128,512]{1,0:T(8,128)(2,1)}, bf16[128,512]{1,0:T(8,128)(2,1)S(1)}, u32[]{:S(2)}, u32[]{:S(2)}) collective-permute-start(bf16[128,512]{1,0:T(8,128)(2,1)} %param.8), channel_id=1, source_target_pairs={{0,2},{1,3},{2,6},{3,7},{4,0},{5,1},{6,10},{7,11},{8,4},{9,5},{10,... | collective-permute-start | bytes 393224 | tf_op jit(solution)/shard_map/ppermute | solution.py:77
  5.2 22.0 %copy-start.10 = (f32[8192]{0:T(1024)S(1)}, f32[8192]{0:T(1024)}, u32[]{:S(2)}) copy-start(f32[8192]{0:T(1024)} %param.10) | copy-start | bytes 98308
  5.2 22.0 %copy-start.9 = (f32[8192]{0:T(1024)S(1)}, f32[8192]{0:T(1024)}, u32[]{:S(2)}) copy-start(f32[8192]{0:T(1024)} %param.9) | copy-start | bytes 98308
  5.3 21.9 %copy-start.5 = (bf16[128,8192]{1,0:T(8,128)(2,1)S(1)}, bf16[128,8192]{1,0:T(8,128)(2,1)}, u32[]{:S(2)}) copy-start(bf16[128,8192]{1,0:T(8,128)(2,1)} %up.3) | copy-start | bytes 6291460
  5.5 21.7 %copy-start.2 = (bf16[128,8192]{1,0:T(8,128)(2,1)S(1)}, bf16[128,8192]{1,0:T(8,128)(2,1)}, u32[]{:S(2)}) copy-start(bf16[128,8192]{1,0:T(8,128)(2,1)} %down.3) | copy-start | bytes 6291460
  5.5 21.7 %copy-start.3 = (bf16[128,8192]{1,0:T(8,128)(2,1)S(1)}, bf16[128,8192]{1,0:T(8,128)(2,1)}, u32[]{:S(2)}) copy-start(bf16[128,8192]{1,0:T(8,128)(2,1)} %gate.3) | copy-start | bytes 6291460
  8.1 8.0 %collective-permute-start.2 = (bf16[128,512]{1,0:T(8,128)(2,1)S(1)}, bf16[128,512]{1,0:T(8,128)(2,1)S(1)}, u32[]{:S(2)}, u32[]{:S(2)}) collective-permute-start(bf16[128,512]{1,0:T(8,128)(2,1)S(1)} %collective-permute-done.1), channel_id=1, source_target_pairs={{0,1},{1,0},{2,3},{3,2},{4,5},{5,4},{6,7},{7,6},{8,9},{9,8},{10,11... | collective-permute-start | bytes 393224 | tf_op jit(solution)/shard_map/ppermute | solution.py:79
  8.1 5.9 %collective-permute-start.5 = (bf16[128,512]{1,0:T(8,128)(2,1)S(1)}, bf16[128,512]{1,0:T(8,128)(2,1)S(1)}, u32[]{:S(2)}, u32[]{:S(2)}) collective-permute-start(bf16[128,512]{1,0:T(8,128)(2,1)S(1)} %collective-permute-done.1), channel_id=1, source_target_pairs={{0,4},{1,5},{2,0},{3,1},{4,8},{5,9},{6,2},{7,3},{8,12},{9,13},{10,... | collective-permute-start | bytes 393224 | tf_op jit(solution)/shard_map/ppermute | solution.py:75
  9.9 6.4 %collective-permute-start.4 = (bf16[128,512]{1,0:T(8,128)(2,1)S(1)}, bf16[128,512]{1,0:T(8,128)(2,1)S(1)}, u32[]{:S(2)}, u32[]{:S(2)}) collective-permute-start(bf16[128,512]{1,0:T(8,128)(2,1)S(1)} %collective-permute-done.3), channel_id=1, source_target_pairs={{0,1},{1,0},{2,3},{3,2},{4,5},{5,4},{6,7},{7,6},{8,9},{9,8},{10,11... | collective-permute-start | bytes 393224 | tf_op jit(solution)/shard_map/ppermute | solution.py:82
  10.1 5.7 %collective-permute-start.7 = (bf16[128,512]{1,0:T(8,128)(2,1)S(1)}, bf16[128,512]{1,0:T(8,128)(2,1)S(1)}, u32[]{:S(2)}, u32[]{:S(2)}) collective-permute-start(bf16[128,512]{1,0:T(8,128)(2,1)S(1)} %collective-permute-done.3), channel_id=1, source_target_pairs={{0,2},{1,3},{2,6},{3,7},{4,0},{5,1},{6,10},{7,11},{8,4},{9,5},{10,... | collective-permute-start | bytes 393224 | tf_op jit(solution)/shard_map/ppermute | solution.py:77
  14.0 8.0 %collective-permute-start.6 = (bf16[128,512]{1,0:T(8,128)(2,1)S(1)}, bf16[128,512]{1,0:T(8,128)(2,1)S(1)}, u32[]{:S(2)}, u32[]{:S(2)}) collective-permute-start(bf16[128,512]{1,0:T(8,128)(2,1)S(1)} %collective-permute-done.5), channel_id=1, source_target_pairs={{0,1},{1,0},{2,3},{3,2},{4,5},{5,4},{6,7},{7,6},{8,9},{9,8},{10,11... | collective-permute-start | bytes 393224 | tf_op jit(solution)/shard_map/ppermute | solution.py:79
  14.0 5.9 %collective-permute-start.9 = (bf16[128,512]{1,0:T(8,128)(2,1)S(1)}, bf16[128,512]{1,0:T(8,128)(2,1)S(1)}, u32[]{:S(2)}, u32[]{:S(2)}) collective-permute-start(bf16[128,512]{1,0:T(8,128)(2,1)S(1)} %collective-permute-done.5), channel_id=1, source_target_pairs={{0,4},{1,5},{2,0},{3,1},{4,8},{5,9},{6,2},{7,3},{8,12},{9,13},{10,... | collective-permute-start | bytes 393224 | tf_op jit(solution)/shard_map/ppermute | solution.py:75
  15.8 6.2 %collective-permute-start.8 = (bf16[128,512]{1,0:T(8,128)(2,1)S(1)}, bf16[128,512]{1,0:T(8,128)(2,1)S(1)}, u32[]{:S(2)}, u32[]{:S(2)}) collective-permute-start(bf16[128,512]{1,0:T(8,128)(2,1)S(1)} %collective-permute-done.7), channel_id=1, source_target_pairs={{0,1},{1,0},{2,3},{3,2},{4,5},{5,4},{6,7},{7,6},{8,9},{9,8},{10,11... | collective-permute-start | bytes 393224 | tf_op jit(solution)/shard_map/ppermute | solution.py:82
  16.0 5.7 %collective-permute-start.11 = (bf16[128,512]{1,0:T(8,128)(2,1)S(1)}, bf16[128,512]{1,0:T(8,128)(2,1)S(1)}, u32[]{:S(2)}, u32[]{:S(2)}) collective-permute-start(bf16[128,512]{1,0:T(8,128)(2,1)S(1)} %collective-permute-done.7), channel_id=1, source_target_pairs={{0,2},{1,3},{2,6},{3,7},{4,0},{5,1},{6,10},{7,11},{8,4},{9,5},{10,... | collective-permute-start | bytes 393224 | tf_op jit(solution)/shard_map/ppermute | solution.py:77
  19.9 5.9 %collective-permute-start.10 = (bf16[128,512]{1,0:T(8,128)(2,1)S(1)}, bf16[128,512]{1,0:T(8,128)(2,1)S(1)}, u32[]{:S(2)}, u32[]{:S(2)}) collective-permute-start(bf16[128,512]{1,0:T(8,128)(2,1)S(1)} %collective-permute-done.9), channel_id=1, source_target_pairs={{0,1},{1,0},{2,3},{3,2},{4,5},{5,4},{6,7},{7,6},{8,9},{9,8},{10,11... | collective-permute-start | bytes 393224 | tf_op jit(solution)/shard_map/ppermute | solution.py:79
  19.9 5.9 %collective-permute-start.13 = (bf16[128,512]{1,0:T(8,128)(2,1)S(1)}, bf16[128,512]{1,0:T(8,128)(2,1)S(1)}, u32[]{:S(2)}, u32[]{:S(2)}) collective-permute-start(bf16[128,512]{1,0:T(8,128)(2,1)S(1)} %collective-permute-done.9), channel_id=1, source_target_pairs={{0,4},{1,5},{2,0},{3,1},{4,8},{5,9},{6,2},{7,3},{8,12},{9,13},{10,... | collective-permute-start | bytes 393224 | tf_op jit(solution)/shard_map/ppermute | solution.py:75
  21.7 4.2 %collective-permute-start.12 = (bf16[128,512]{1,0:T(8,128)(2,1)S(1)}, bf16[128,512]{1,0:T(8,128)(2,1)S(1)}, u32[]{:S(2)}, u32[]{:S(2)}) collective-permute-start(bf16[128,512]{1,0:T(8,128)(2,1)S(1)} %collective-permute-done.11), channel_id=1, source_target_pairs={{0,1},{1,0},{2,3},{3,2},{4,5},{5,4},{6,7},{7,6},{8,9},{9,8},{10,11... | collective-permute-start | bytes 393224 | tf_op jit(solution)/shard_map/ppermute | solution.py:82
  25.8 1.3 %collective-permute-start.14 = (bf16[128,512]{1,0:T(8,128)(2,1)S(1)}, bf16[128,512]{1,0:T(8,128)(2,1)S(1)}, u32[]{:S(2)}, u32[]{:S(2)}) collective-permute-start(bf16[128,512]{1,0:T(8,128)(2,1)S(1)} %collective-permute-done.13), channel_id=1, source_target_pairs={{0,1},{1,0},{2,3},{3,2},{4,5},{5,4},{6,7},{7,6},{8,9},{9,8},{10,11... | collective-permute-start | bytes 393224 | tf_op jit(solution)/shard_map/ppermute | solution.py:79
  32.7 1.9 %collective-permute-start.16 = (f32[2,128,512]{2,1,0:T(8,128)S(1)}, f32[2,128,512]{2,1,0:T(8,128)S(1)}, u32[]{:S(2)}, u32[]{:S(2)}) collective-permute-start(f32[2,128,512]{2,1,0:T(8,128)S(1)} %get-tuple-element.44), channel_id=1, source_target_pairs={{0,1},{1,0},{2,3},{3,2},{4,5},{5,4},{6,7},{7,6},{8,9},{9,8},{10,11... | collective-permute-start | bytes 1572872 | tf_op jit(solution)/shard_map/ppermute | solution.py:283
  32.8 7.5 %collective-permute-start.15 = (f32[4,128,512]{2,1,0:T(8,128)S(1)}, f32[4,128,512]{2,1,0:T(8,128)S(1)}, u32[]{:S(2)}, u32[]{:S(2)}) collective-permute-start(f32[4,128,512]{2,1,0:T(8,128)S(1)} %slice.96), channel_id=1, source_target_pairs={{0,1},{1,0},{2,3},{3,2},{4,5},{5,4},{6,7},{7,6},{8,9},{9,8},{10,11... | collective-permute-start | bytes 3145736 | tf_op jit(solution)/shard_map/ppermute | solution.py:288
  34.1 18.3 %copy-start.11 = (bf16[384,128]{1,0:T(8,128)(2,1)}, bf16[384,128]{1,0:T(8,128)(2,1)S(1)}, u32[]{:S(2)}) copy-start(bf16[384,128]{1,0:T(8,128)(2,1)S(1)} %fusion.2) | copy-start | bytes 294916
  34.7 5.6 %collective-permute-start.17 = (bf16[128,512]{1,0:T(8,128)(2,1)S(1)}, bf16[128,512]{1,0:T(8,128)(2,1)S(1)}, u32[]{:S(2)}, u32[]{:S(2)}) collective-permute-start(bf16[128,512]{1,0:T(8,128)(2,1)S(1)} %get-tuple-element.38), channel_id=1, source_target_pairs={{0,4},{1,5},{2,0},{3,1},{4,8},{5,9},{6,2},{7,3},{8,12},{9,13},{10,... | collective-permute-start | bytes 393224 | tf_op jit(solution)/shard_map/ppermute | solution.py:89
  36.6 5.8 %collective-permute-start.22 = (f32[2,128,512]{2,1,0:T(8,128)S(1)}, f32[2,128,512]{2,1,0:T(8,128)S(1)}, u32[]{:S(2)}, u32[]{:S(2)}) collective-permute-start(f32[2,128,512]{2,1,0:T(8,128)S(1)} %get-tuple-element.45), channel_id=1, source_target_pairs={{0,1},{1,0},{2,3},{3,2},{4,5},{5,4},{6,7},{7,6},{8,9},{9,8},{10,11... | collective-permute-start | bytes 1572872 | tf_op jit(solution)/shard_map/ppermute | solution.py:288
  36.7 5.9 %collective-permute-start.21 = (bf16[128,512]{1,0:T(8,128)(2,1)S(1)}, bf16[128,512]{1,0:T(8,128)(2,1)S(1)}, u32[]{:S(2)}, u32[]{:S(2)}) collective-permute-start(bf16[128,512]{1,0:T(8,128)(2,1)S(1)} %get-tuple-element.39), channel_id=1, source_target_pairs={{0,2},{1,3},{2,6},{3,7},{4,0},{5,1},{6,10},{7,11},{8,4},{9,5},{10,... | collective-permute-start | bytes 393224 | tf_op jit(solution)/shard_map/ppermute | solution.py:91
  40.4 5.0 %collective-permute-start.18 = (bf16[128,512]{1,0:T(8,128)(2,1)S(1)}, bf16[128,512]{1,0:T(8,128)(2,1)S(1)}, u32[]{:S(2)}, u32[]{:S(2)}) collective-permute-start(bf16[128,512]{1,0:T(8,128)(2,1)S(1)} %fusion.23), channel_id=1, source_target_pairs={{0,4},{1,5},{2,0},{3,1},{4,8},{5,9},{6,2},{7,3},{8,12},{9,13},{10,... | collective-permute-start | bytes 393224 | tf_op jit(solution)/shard_map/ppermute | solution.py:89
  45.5 5.0 %collective-permute-start.19 = (bf16[128,512]{1,0:T(8,128)(2,1)S(1)}, bf16[128,512]{1,0:T(8,128)(2,1)S(1)}, u32[]{:S(2)}, u32[]{:S(2)}) collective-permute-start(bf16[128,512]{1,0:T(8,128)(2,1)S(1)} %get-tuple-element.42), channel_id=1, source_target_pairs={{0,4},{1,5},{2,0},{3,1},{4,8},{5,9},{6,2},{7,3},{8,12},{9,13},{10,... | collective-permute-start | bytes 393224 | tf_op jit(solution)/shard_map/ppermute | solution.py:89
  47.4 5.0 %collective-permute-start.23 = (bf16[128,512]{1,0:T(8,128)(2,1)S(1)}, bf16[128,512]{1,0:T(8,128)(2,1)S(1)}, u32[]{:S(2)}, u32[]{:S(2)}) collective-permute-start(bf16[128,512]{1,0:T(8,128)(2,1)S(1)} %get-tuple-element.43), channel_id=1, source_target_pairs={{0,2},{1,3},{2,6},{3,7},{4,0},{5,1},{6,10},{7,11},{8,4},{9,5},{10,... | collective-permute-start | bytes 393224 | tf_op jit(solution)/shard_map/ppermute | solution.py:91
  52.5 5.0 %collective-permute-start.20 = (bf16[128,512]{1,0:T(8,128)(2,1)S(1)}, bf16[128,512]{1,0:T(8,128)(2,1)S(1)}, u32[]{:S(2)}, u32[]{:S(2)}) collective-permute-start(bf16[128,512]{1,0:T(8,128)(2,1)S(1)} %get-tuple-element.40), channel_id=1, source_target_pairs={{0,4},{1,5},{2,0},{3,1},{4,8},{5,9},{6,2},{7,3},{8,12},{9,13},{10,... | collective-permute-start | bytes 393224 | tf_op jit(solution)/shard_map/ppermute | solution.py:89
  54.2 5.0 %collective-permute-start.24 = (bf16[128,512]{1,0:T(8,128)(2,1)S(1)}, bf16[128,512]{1,0:T(8,128)(2,1)S(1)}, u32[]{:S(2)}, u32[]{:S(2)}) collective-permute-start(bf16[128,512]{1,0:T(8,128)(2,1)S(1)} %get-tuple-element.41), channel_id=1, source_target_pairs={{0,2},{1,3},{2,6},{3,7},{4,0},{5,1},{6,10},{7,11},{8,4},{9,5},{10,... | collective-permute-start | bytes 393224 | tf_op jit(solution)/shard_map/ppermute | solution.py:91
  59.4 8.2 %collective-permute-start.25 = (bf16[128,512]{1,0:T(8,128)(2,1)S(1)}, bf16[128,512]{1,0:T(8,128)(2,1)S(1)}, u32[]{:S(2)}, u32[]{:S(2)}) collective-permute-start(bf16[128,512]{1,0:T(8,128)(2,1)S(1)} %get-tuple-element.36), channel_id=1, source_target_pairs={{0,1},{1,0},{2,3},{3,2},{4,5},{5,4},{6,7},{7,6},{8,9},{9,8},{10,11... | collective-permute-start | bytes 393224 | tf_op jit(solution)/shard_map/ppermute | solution.py:71
  59.5 5.9 %collective-permute-start.26 = (bf16[128,512]{1,0:T(8,128)(2,1)S(1)}, bf16[128,512]{1,0:T(8,128)(2,1)S(1)}, u32[]{:S(2)}, u32[]{:S(2)}) collective-permute-start(bf16[128,512]{1,0:T(8,128)(2,1)S(1)} %get-tuple-element.36), channel_id=1, source_target_pairs={{0,4},{1,5},{2,0},{3,1},{4,8},{5,9},{6,2},{7,3},{8,12},{9,13},{10,... | collective-permute-start | bytes 393224 | tf_op jit(solution)/shard_map/ppermute | solution.py:75
  61.2 5.9 %collective-permute-start.28 = (bf16[128,512]{1,0:T(8,128)(2,1)S(1)}, bf16[128,512]{1,0:T(8,128)(2,1)S(1)}, u32[]{:S(2)}, u32[]{:S(2)}) collective-permute-start(bf16[128,512]{1,0:T(8,128)(2,1)S(1)} %get-tuple-element.36), channel_id=1, source_target_pairs={{0,2},{1,3},{2,6},{3,7},{4,0},{5,1},{6,10},{7,11},{8,4},{9,5},{10,... | collective-permute-start | bytes 393224 | tf_op jit(solution)/shard_map/ppermute | solution.py:77
  65.4 7.7 %collective-permute-start.27 = (bf16[128,512]{1,0:T(8,128)(2,1)S(1)}, bf16[128,512]{1,0:T(8,128)(2,1)S(1)}, u32[]{:S(2)}, u32[]{:S(2)}) collective-permute-start(bf16[128,512]{1,0:T(8,128)(2,1)S(1)} %collective-permute-done.26), channel_id=1, source_target_pairs={{0,1},{1,0},{2,3},{3,2},{4,5},{5,4},{6,7},{7,6},{8,9},{9,8},{10,11... | collective-permute-start | bytes 393224 | tf_op jit(solution)/shard_map/ppermute | solution.py:79
  65.4 5.9 %collective-permute-start.30 = (bf16[128,512]{1,0:T(8,128)(2,1)S(1)}, bf16[128,512]{1,0:T(8,128)(2,1)S(1)}, u32[]{:S(2)}, u32[]{:S(2)}) collective-permute-start(bf16[128,512]{1,0:T(8,128)(2,1)S(1)} %collective-permute-done.26), channel_id=1, source_target_pairs={{0,4},{1,5},{2,0},{3,1},{4,8},{5,9},{6,2},{7,3},{8,12},{9,13},{10,... | collective-permute-start | bytes 393224 | tf_op jit(solution)/shard_map/ppermute | solution.py:75
  67.0 6.6 %collective-permute-start.29 = (bf16[128,512]{1,0:T(8,128)(2,1)S(1)}, bf16[128,512]{1,0:T(8,128)(2,1)S(1)}, u32[]{:S(2)}, u32[]{:S(2)}) collective-permute-start(bf16[128,512]{1,0:T(8,128)(2,1)S(1)} %collective-permute-done.28), channel_id=1, source_target_pairs={{0,1},{1,0},{2,3},{3,2},{4,5},{5,4},{6,7},{7,6},{8,9},{9,8},{10,11... | collective-permute-start | bytes 393224 | tf_op jit(solution)/shard_map/ppermute | solution.py:82
  67.2 5.7 %collective-permute-start.32 = (bf16[128,512]{1,0:T(8,128)(2,1)S(1)}, bf16[128,512]{1,0:T(8,128)(2,1)S(1)}, u32[]{:S(2)}, u32[]{:S(2)}) collective-permute-start(bf16[128,512]{1,0:T(8,128)(2,1)S(1)} %collective-permute-done.28), channel_id=1, source_target_pairs={{0,2},{1,3},{2,6},{3,7},{4,0},{5,1},{6,10},{7,11},{8,4},{9,5},{10,... | collective-permute-start | bytes 393224 | tf_op jit(solution)/shard_map/ppermute | solution.py:77
  71.3 7.7 %collective-permute-start.31 = (bf16[128,512]{1,0:T(8,128)(2,1)S(1)}, bf16[128,512]{1,0:T(8,128)(2,1)S(1)}, u32[]{:S(2)}, u32[]{:S(2)}) collective-permute-start(bf16[128,512]{1,0:T(8,128)(2,1)S(1)} %collective-permute-done.30), channel_id=1, source_target_pairs={{0,1},{1,0},{2,3},{3,2},{4,5},{5,4},{6,7},{7,6},{8,9},{9,8},{10,11... | collective-permute-start | bytes 393224 | tf_op jit(solution)/shard_map/ppermute | solution.py:79
  71.3 5.9 %collective-permute-start.34 = (bf16[128,512]{1,0:T(8,128)(2,1)S(1)}, bf16[128,512]{1,0:T(8,128)(2,1)S(1)}, u32[]{:S(2)}, u32[]{:S(2)}) collective-permute-start(bf16[128,512]{1,0:T(8,128)(2,1)S(1)} %collective-permute-done.30), channel_id=1, source_target_pairs={{0,4},{1,5},{2,0},{3,1},{4,8},{5,9},{6,2},{7,3},{8,12},{9,13},{10,... | collective-permute-start | bytes 393224 | tf_op jit(solution)/shard_map/ppermute | solution.py:75
  72.9 6.2 %collective-permute-start.33 = (bf16[128,512]{1,0:T(8,128)(2,1)S(1)}, bf16[128,512]{1,0:T(8,128)(2,1)S(1)}, u32[]{:S(2)}, u32[]{:S(2)}) collective-permute-start(bf16[128,512]{1,0:T(8,128)(2,1)S(1)} %collective-permute-done.32), channel_id=1, source_target_pairs={{0,1},{1,0},{2,3},{3,2},{4,5},{5,4},{6,7},{7,6},{8,9},{9,8},{10,11... | collective-permute-start | bytes 393224 | tf_op jit(solution)/shard_map/ppermute | solution.py:82
  73.2 5.7 %collective-permute-start.36 = (bf16[128,512]{1,0:T(8,128)(2,1)S(1)}, bf16[128,512]{1,0:T(8,128)(2,1)S(1)}, u32[]{:S(2)}, u32[]{:S(2)}) collective-permute-start(bf16[128,512]{1,0:T(8,128)(2,1)S(1)} %collective-permute-done.32), channel_id=1, source_target_pairs={{0,2},{1,3},{2,6},{3,7},{4,0},{5,1},{6,10},{7,11},{8,4},{9,5},{10,... | collective-permute-start | bytes 393224 | tf_op jit(solution)/shard_map/ppermute | solution.py:77
  77.3 5.9 %collective-permute-start.35 = (bf16[128,512]{1,0:T(8,128)(2,1)S(1)}, bf16[128,512]{1,0:T(8,128)(2,1)S(1)}, u32[]{:S(2)}, u32[]{:S(2)}) collective-permute-start(bf16[128,512]{1,0:T(8,128)(2,1)S(1)} %collective-permute-done.34), channel_id=1, source_target_pairs={{0,1},{1,0},{2,3},{3,2},{4,5},{5,4},{6,7},{7,6},{8,9},{9,8},{10,11... | collective-permute-start | bytes 393224 | tf_op jit(solution)/shard_map/ppermute | solution.py:79
  77.3 5.9 %collective-permute-start.38 = (bf16[128,512]{1,0:T(8,128)(2,1)S(1)}, bf16[128,512]{1,0:T(8,128)(2,1)S(1)}, u32[]{:S(2)}, u32[]{:S(2)}) collective-permute-start(bf16[128,512]{1,0:T(8,128)(2,1)S(1)} %collective-permute-done.34), channel_id=1, source_target_pairs={{0,4},{1,5},{2,0},{3,1},{4,8},{5,9},{6,2},{7,3},{8,12},{9,13},{10,... | collective-permute-start | bytes 393224 | tf_op jit(solution)/shard_map/ppermute | solution.py:75
  78.8 4.4 %collective-permute-start.37 = (bf16[128,512]{1,0:T(8,128)(2,1)S(1)}, bf16[128,512]{1,0:T(8,128)(2,1)S(1)}, u32[]{:S(2)}, u32[]{:S(2)}) collective-permute-start(bf16[128,512]{1,0:T(8,128)(2,1)S(1)} %collective-permute-done.36), channel_id=1, source_target_pairs={{0,1},{1,0},{2,3},{3,2},{4,5},{5,4},{6,7},{7,6},{8,9},{9,8},{10,11... | collective-permute-start | bytes 393224 | tf_op jit(solution)/shard_map/ppermute | solution.py:82
  83.2 1.3 %collective-permute-start.39 = (bf16[128,512]{1,0:T(8,128)(2,1)S(1)}, bf16[128,512]{1,0:T(8,128)(2,1)S(1)}, u32[]{:S(2)}, u32[]{:S(2)}) collective-permute-start(bf16[128,512]{1,0:T(8,128)(2,1)S(1)} %collective-permute-done.38), channel_id=1, source_target_pairs={{0,1},{1,0},{2,3},{3,2},{4,5},{5,4},{6,7},{7,6},{8,9},{9,8},{10,11... | collective-permute-start | bytes 393224 | tf_op jit(solution)/shard_map/ppermute | solution.py:79
  86.2 11.5 %all-to-all-start = ((bf16[16,24,128]{2,1,0:T(8,128)(2,1)}), bf16[16,24,128]{2,1,0:T(8,128)(2,1)S(1)}, u32[]{:S(2)}, u32[]{:S(2)}) async-start(bf16[16,24,128]{2,1,0:T(8,128)(2,1)} %bitcast.16), calls=%async_computation | async-start | bytes 196608 | tf_op jit(solution)/shard_map/all_to_all | solution.py:302
  97.8 12.4 %all-to-all-start.1 = ((f32[16,8,128]{2,1,0:T(8,128)}), f32[16,8,128]{2,1,0:T(8,128)S(1)}, u32[]{:S(2)}, u32[]{:S(2)}) async-start(f32[16,8,128]{2,1,0:T(8,128)} %gain.1), calls=%async_computation.1 | async-start | bytes 131072 | tf_op jit(solution)/shard_map/all_to_all | solution.py:314
  (14 other events, 66.0 us)

commit v3 on v2

v3 whole, which is shorter than its diff:
```python
import functools

import jax
import jax.numpy as jnp
from jax import lax
from jax.experimental import pallas as pl
from jax.experimental.pallas import tpu as pltpu
from jax.sharding import PartitionSpec as P

BF16 = jnp.bfloat16
F32 = jnp.float32
NT = (((1,), (1,)), ((), ()))


def dot(left, right):
    return jnp.dot(left, right, preferred_element_type=F32)


def dot_nt(left, right):
    return lax.dot_general(left, right, NT, preferred_element_type=F32)


def after(value, other):
    return lax.optimization_barrier((value, other))[0]


def place(whole, part, owner):
    return lax.dynamic_update_slice(whole, part, (0, owner * part.shape[1]))


class Ring:
    def __init__(self, devices):
        self.devices = devices
        self.chips = devices // 2
        self.up_steps = self.chips // 2
        self.down_steps = self.chips - 1 - self.up_steps
        self.sibling = [(i, i ^ 1) for i in range(devices)]

    def owner(self, device, distance, core):
        return 2 * ((device // 2 + distance) % self.chips) + (device % 2 + core) % 2

    def shift(self, step):
        return [(i, (i + 2 * step) % self.devices) for i in range(self.devices)]

    def gather(self, block, device):
        tokens, width = block.shape
        whole = jnp.zeros((tokens, width * self.devices), block.dtype)

        def put(whole, part, distance):
            whole = place(whole, part, self.owner(device, distance, 0))
            other = lax.ppermute(part, "fsdp", self.sibling)
            return place(whole, other, self.owner(device, distance, 1))

        whole = put(whole, block, 0)
        up = down = block
        for step in range(1, self.up_steps + 1):
            up = lax.ppermute(up, "fsdp", self.shift(1))
            if step <= self.down_steps:
                down = lax.ppermute(down, "fsdp", self.shift(-1))
            whole = put(whole, up, self.chips - step)
            if step <= self.down_steps:
                whole = put(whole, down, step)
        return whole

    def scatter_sum(self, keep, other):
        swapped = lax.ppermute(other, "fsdp", self.sibling)

        def term(distance):
            return keep[distance] + swapped[distance]

        up = term(self.up_steps)
        down = term(self.up_steps + 1) if self.down_steps else None
        for step in range(1, self.up_steps + 1):
            up = lax.ppermute(up.astype(BF16), "fsdp", self.shift(1)).astype(F32)
            if step <= self.down_steps:
                down = lax.ppermute(down.astype(BF16), "fsdp", self.shift(-1)).astype(F32)
            if step < self.up_steps:
                up = up + term(self.up_steps - step)
            if step < self.down_steps:
                down = down + term(self.up_steps + 1 + step)
        total = term(0) + up
        return total + down if self.down_steps else total


class Grid(Ring):
    FAR_FIRST = (3, 2, 1, 0)

    def across(self, bits):
        return [(i, i ^ bits) for i in range(self.devices)]

    def owner(self, device, distance, core):
        return jnp.bitwise_xor(device, 2 * distance + core)

    def gather(self, block, device):
        tokens, width = block.shape
        whole = jnp.zeros((tokens, width * self.devices), block.dtype)
        column = {0: block}
        for z in (1, 2):
            column[z] = lax.ppermute(block, "fsdp", self.across(4 * z))
        column[3] = lax.ppermute(after(block, column[1]), "fsdp", self.across(12))
        for z in range(4):
            for y in range(2):
                part = lax.ppermute(column[z], "fsdp", self.across(2)) if y else column[z]
                whole = place(whole, part, self.owner(device, 2 * z + y, 0))
                part = lax.ppermute(part, "fsdp", self.sibling)
                whole = place(whole, part, self.owner(device, 2 * z + y, 1))
        return whole

    def scatter_sum(self, keep, other):
        over_y = {}
        mine = {}
        sent = None
        for z in self.FAR_FIRST:
            pair = slice(2 * z, 2 * z + 2)
            part = lax.ppermute(other[pair], "fsdp", self.sibling)
            if sent is not None:
                part = after(part, sent)
            part = keep[pair] + part
            sent = part[1].astype(BF16)
            mine[z] = part[0]
            over_y[z] = lax.ppermute(sent, "fsdp", self.across(2))
        arrived = []
        sent = None
        for z in self.FAR_FIRST:
            part = over_y[z] if sent is None else after(over_y[z], sent)
            total = mine[z] + part.astype(F32)
            if z:
                sent = total.astype(BF16)
                arrived.append(lax.ppermute(sent, "fsdp", self.across(4 * z)))
        for part in arrived:
            total = total + part.astype(F32)
        return total


def kept_rows(kept_index, device, parent_rows):
    local = kept_index[:, None] - device * parent_rows
    kept = jnp.any(local == jnp.arange(parent_rows)[None, :], axis=0)
    return kept.astype(F32).reshape(1, parent_rows)


def routing(kept_index, tile_owner, device, devices, parent_rows, stride):
    tile_count = tile_owner.shape[0]
    tile_rows = kept_index.shape[0] // tile_count
    slots = devices * stride
    layout = kept_index.reshape(tile_count, tile_rows)
    local = layout - device * parent_rows
    mine = (local >= 0) & (local < parent_rows)
    earlier = jnp.arange(tile_rows)[:, None] < jnp.arange(tile_rows)[None, :]
    position = dot(mine.astype(BF16), earlier.astype(BF16)).astype(jnp.int32)
    slot = jnp.where(mine, tile_owner[:, None] * stride + position, -1).reshape(-1)
    at_slot = (slot[None, :] == jnp.arange(slots)[:, None]).astype(BF16)
    at_row = (local.reshape(-1)[:, None] == jnp.arange(parent_rows)[None, :]).astype(BF16)
    send = dot(at_slot, at_row).astype(BF16)
    tile = jnp.sum(jnp.where((tile_owner == device)[:, None], layout, 0), axis=0)
    source = jnp.where(tile >= 0, tile // parent_rows, -1)
    same = (source[:, None] == source[None, :]) & earlier.T
    rank = jnp.sum(same.astype(jnp.int32), axis=1)
    slot = jnp.where(tile >= 0, source * stride + rank, -slots)
    find = (slot[:, None] == jnp.arange(slots)[None, :]).astype(BF16)
    return send, find


def forward_kernel(
    ring,
    hidden,
    parent_gain,
    child_gain,
    gate,
    up,
    down,
    kept,
    scale,
    child_gate,
    child_up,
    child_hid,
    keep,
    send,
):
    tokens, features = hidden.shape
    width = features // ring.devices
    pieces = 16
    piece = features // pieces
    cuts = [slice(k * piece, (k + 1) * piece) for k in range(pieces)]
    squares = jnp.zeros((tokens, piece), F32)
    for cols in cuts:
        h = hidden[:, cols].astype(F32)
        squares = squares + h * h
    mean = jnp.sum(squares, axis=1, keepdims=True) / features
    inverse = 1.0 / jnp.sqrt(mean + 1e-05)
    scale[...] = jnp.broadcast_to(inverse, scale.shape)
    gate_both = jnp.zeros((2 * tokens, gate.shape[0]), F32)
    up_both = jnp.zeros((2 * tokens, gate.shape[0]), F32)
    for cols in cuts:
        normed = hidden[:, cols].astype(F32) * inverse
        parent = (normed * parent_gain[:, cols]).astype(BF16)
        child = (normed * child_gain[:, cols]).astype(BF16)
        both = jnp.concatenate([parent, child], axis=0)
        gate_both = gate_both + dot_nt(both, gate[:, cols])
        up_both = up_both + dot_nt(both, up[:, cols])
    hid = gate_both * jax.nn.sigmoid(gate_both) * up_both
    child_gate[...] = gate_both[tokens:]
    child_up[...] = up_both[tokens:]
    child = jnp.where(kept[...] > 0, hid[tokens:], 0.0).astype(BF16)
    child_hid[...] = child
    both_hid = jnp.concatenate([child, -hid[:tokens].astype(BF16)], axis=0)
    device = lax.axis_index("fsdp")
    for core, target in ((1, send), (0, keep)):
        for distance in range(ring.chips):
            start = ring.owner(device, distance, core) * width
            out = dot(both_hid, down[:, pl.ds(pl.multiple_of(start, width), width)])
            target[distance] = out[:tokens] + out[tokens:]


def backward_kernel(
    per_pair,
    slope,
    hidden,
    gate,
    up,
    down,
    kept,
    scale,
    child_gate,
    child_up,
    child_hid,
    select,
    sent,
    message,
):
    devices, stride, _ = message.shape
    tokens = slope.shape[0]
    width = slope.shape[1] // devices
    child_slope = dot_nt(slope[...], down[...])
    g, u = child_gate[...], child_up[...]
    sig = jax.nn.sigmoid(g)
    live = kept[...] > 0
    gate_back = child_slope * u * sig * (1.0 + g * (1.0 - sig))
    gate_back = jnp.where(live, gate_back, 0.0).astype(BF16)
    up_back = jnp.where(live, child_slope * g * sig, 0.0).astype(BF16)
    rows = dot_nt(select[0], gate_back) + dot_nt(select[1], up_back)
    rows = rows + dot_nt(select[2], child_hid[...])
    message[...] = rows.reshape(devices, stride, tokens)
    inverse = scale[...][:, :1]
    high_at, gain_rows = 3 * per_pair, width // 128
    for k in range(devices):
        cols = slice(k * width, (k + 1) * width)
        input_slope = dot(gate_back, gate[:, cols]) + dot(up_back, up[:, cols])
        normed = hidden[:, cols].astype(F32) * inverse
        part = jnp.sum(input_slope * normed, axis=0, keepdims=True)
        high = part.astype(BF16).astype(F32)
        for r in range(gain_rows):
            lanes = slice(r * 128, (r + 1) * 128)
            at = high_at + r
            message[k, at : at + 1, :] = high[:, lanes]
            at = at + gain_rows
            message[k, at : at + 1, :] = (part - high)[:, lanes]
    sent[...] = message[...].astype(BF16)


def rows_kernel(
    per_pair,
    received,
    places,
    hidden,
    scale,
    child_gain,
    slope,
    grad_gate,
    grad_up,
    grad_down,
    gain,
    loss,
    made,
    done,
):
    rows, features = grad_gate.shape
    devices, stride, tokens = received.shape
    message = received[...].reshape(devices * stride, tokens)
    tiles = [dot(places[kind], message).astype(BF16) for kind in range(3)]
    both = jnp.concatenate(tiles[:2], axis=0)
    inverse = scale[...][:, :1]
    cut = min(features, 1024)
    copies = []
    squares = jnp.zeros((slope.shape[0], cut), F32)
    for k in range(features // cut):
        cols = slice(k * cut, (k + 1) * cut)
        difference = slope[:, cols]
        squares = squares + difference.astype(F32) * difference.astype(F32)
        made[2, :, cols] = dot(tiles[2], difference).astype(BF16)
        child = (hidden[:, cols].astype(F32) * inverse * child_gain[:, cols]).astype(BF16)
        out = dot(both, child).astype(BF16)
        made[0, :, cols] = out[:rows]
        made[1, :, cols] = out[rows:]
        for kind, grad in enumerate((grad_gate, grad_up, grad_down)):
            copy = pltpu.make_async_copy(made.at[kind, :, cols], grad.at[:, cols], done.at[kind, k])
            copy.start()
            copies.append(copy)
    squares = jnp.sum(jnp.sum(squares, axis=0, keepdims=True), axis=1, keepdims=True)
    loss[...] = 0.5 * squares / (slope.shape[0] * features)
    total = jnp.sum(message.astype(F32).reshape(devices, stride, tokens), axis=0)
    gain_rows = gain.shape[1] // 128
    for r in range(gain_rows):
        at = 3 * per_pair + r
        gain[:, r * 128 : (r + 1) * 128] = (
            total[at : at + 1, :] + total[at + gain_rows : at + gain_rows + 1, :]
        )
    for copy in copies:
        copy.wait()


VMEM = pl.BlockSpec(memory_space=pltpu.VMEM)
MIB = 1024 * 1024


def call(kernel, outs, operands, limit, name, scratch=(), specs=None):
    return pl.pallas_call(
        kernel,
        out_shape=[jax.ShapeDtypeStruct(shape, dtype) for shape, dtype in outs],
        in_specs=[VMEM] * len(operands),
        out_specs=specs or [VMEM] * len(outs),
        scratch_shapes=list(scratch),
        compiler_params=pltpu.CompilerParams(vmem_limit_bytes=limit * MIB),
        name=name,
    )(*operands)


def shards(
    hidden, parent_gain, child_gain, gate_weight, up_weight, down_weight, kept_index, tile_owner
):
    devices = lax.axis_size("fsdp")
    device = lax.axis_index("fsdp")
    ring = Grid(devices) if devices == 16 else Ring(devices)
    chips = ring.chips
    parent_rows = gate_weight.shape[0]
    tokens, width = hidden.shape
    features = width * devices
    per_pair = kept_index.shape[0] // tile_owner.shape[0] // devices
    stride = -(-(3 * per_pair + 2 * (width // 128)) // 8) * 8
    kept = kept_rows(kept_index, device, parent_rows)

    square = ((tokens, parent_rows), F32)
    gains = [parent_gain.reshape(1, features), child_gain.reshape(1, features)]
    hidden_all = ring.gather(hidden, device)
    scale, child_gate, child_up, child_hid, keep, other = call(
        functools.partial(forward_kernel, ring),
        [
            ((tokens, 128), F32),
            square,
            square,
            ((tokens, parent_rows), BF16),
            ((chips, tokens, width), F32),
            ((chips, tokens, width), F32),
        ],
        [
            hidden_all,
            *gains,
            gate_weight,
            up_weight,
            down_weight,
            kept,
        ],
        limit=12,
        name="forward",
    )
    difference = ring.scatter_sum(keep, other)
    slope_all = ring.gather(difference.astype(BF16), device)

    send, find = routing(
        after(kept_index, child_hid), tile_owner, device, devices, parent_rows, stride
    )
    select = jnp.stack([jnp.roll(send, kind * per_pair, axis=0) for kind in range(3)])
    places = jnp.stack([jnp.roll(find, kind * per_pair, axis=1) for kind in range(3)])
    message = (devices, stride, tokens)
    (sent,) = call(
        functools.partial(backward_kernel, per_pair),
        [(message, BF16)],
        [
            slope_all,
            hidden_all,
            gate_weight,
            up_weight,
            down_weight,
            kept,
            scale,
            child_gate,
            child_up,
            child_hid,
            select,
        ],
        limit=8,
        name="backward",
        scratch=[pltpu.VMEM(message, F32)],
    )
    received = lax.all_to_all(sent, "fsdp", 0, 0, tiled=True)
    anywhere = pl.BlockSpec(memory_space=pl.ANY)
    grad = ((parent_rows, features), BF16)
    *grads, gain_grad, loss_value = call(
        functools.partial(rows_kernel, per_pair),
        [grad, grad, grad, ((1, width), F32), ((1, 1), F32)],
        [received, places, hidden_all, scale, gains[1], slope_all],
        limit=16,
        name="rows",
        scratch=[
            pltpu.VMEM((3, parent_rows, features), BF16),
            pltpu.SemaphoreType.DMA((3, features // min(features, 1024))),
        ],
        specs=[anywhere] * 3 + [VMEM] * 2,
    )
    return (*grads, gain_grad.reshape(width), loss_value.reshape(1))


def solution(mesh):
    placed = (
        P("groups", "fsdp"),
        P("groups"),
        P("groups"),
        P(("groups", "fsdp"), None),
        P(("groups", "fsdp"), None),
        P(("groups", "fsdp"), None),
        P("groups"),
        P("groups"),
    )
    return jax.shard_map(
        shards,
        mesh=mesh,
        in_specs=placed,
        out_specs=(
            P(("groups", "fsdp"), None),
            P(("groups", "fsdp"), None),
            P(("groups", "fsdp"), None),
            P(("groups", "fsdp")),
            P("groups"),
        ),
        check_vma=False,
    )
```

time: 114 us -> 99.8 us (0.88)
  waiting for transfers between devices: 47.3 us -> 37.6 us
  local copies, waits for them, and re-layouts: 9.83 us -> 4.77 us
  starting transfers between devices: 36.3 us -> 39 us
  between operations: 3.42 us -> 1.58 us
  other arithmetic: 2.3 us -> 3.61 us
  Pallas kernels: 13 us -> 11.8 us
    ppermute x40 -> x41, waiting for transfers between devices: 46.6 us -> 30.2 us  [the longest x8 9.51 us: gather(): part = lax.ppermute(column[z], 'fsdp', self.across(2)) if y else column[z]]
    ppermute x40 -> x41, starting transfers between devices: 26.9 us -> 35.3 us  [the longest x4 8.8 us: gather(): column[z] = lax.ppermute(block, 'fsdp', self.across(4 * z))]
    all_to_all x2 -> x1, waiting for transfers between devices: 0.68 us -> 7.44 us  [shards(): received = lax.all_to_all(sent, 'fsdp', 0, 0, tiled=True)]
    all_to_all x2 -> x1, starting transfers between devices: 9.46 us -> 3.69 us  [shards(): received = lax.all_to_all(sent, 'fsdp', 0, 0, tiled=True)]
    pallas_call x1 -> x0, Pallas kernels: 5.3 us -> none  [shards(): pl.pallas_call(rows_kernel, out_shape=[jax.ShapeDtypeStruct((parent_rows,...]
    pallas_call x3, Pallas kernels: 7.67 us -> 11.8 us  [call(): pl.pallas_call(kernel, out_shape=[jax.ShapeDtypeStruct(shape, dtype) for...]
    unnamed x32 -> x22, local copies, waits for them, and re-layouts: 7.51 us -> 3.47 us
  transfers between devices with their start and end apart: 42 -> 42, of which waited for: 19 -> 14; matrix products, arithmetic and copies ran while one was open for 3% -> 5% of each run, Pallas kernels for 6% -> 0%
where the time goes in v3:
time: 99.8 us; the launch traced here: 99.5 us
  starting transfers between devices  39 us (39%)
  waiting for transfers between devices  37.6 us (38%)
  Pallas kernels  11.8 us (12%)
  local copies, waits for them, and re-layouts  4.77 us (5%)
  other arithmetic  3.61 us (4%)
  between operations  1.58 us (2%)
  matrix products  1.09 us (1%)
    pallas_call x3, Pallas kernels, call(): pl.pallas_call(kernel, out_shape=[jax.ShapeDtypeStruct(shape, dtype) for...  11.8 us
    ppermute x8, waiting for transfers between devices, gather(): part = lax.ppermute(column[z], 'fsdp', self.across(2)) if y else column[z]  9.51 us
    ppermute x4, starting transfers between devices, gather(): column[z] = lax.ppermute(block, 'fsdp', self.across(4 * z))  8.8 us
    ppermute x3, starting transfers between devices, scatter_sum(): arrived.append(lax.ppermute(sent, 'fsdp', self.across(4 * z)))  8.55 us
    ppermute x8, starting transfers between devices, gather(): part = lax.ppermute(column[z], 'fsdp', self.across(2)) if y else column[z]  8.27 us
    all_to_all x1, waiting for transfers between devices, shards(): received = lax.all_to_all(sent, 'fsdp', 0, 0, tiled=True)  7.44 us
    ppermute x3, waiting for transfers between devices, scatter_sum(): arrived.append(lax.ppermute(sent, 'fsdp', self.across(4 * z)))  6.11 us
    ppermute x4, waiting for transfers between devices, gather(): column[z] = lax.ppermute(block, 'fsdp', self.across(4 * z))  5.51 us
  transfers between devices with their start and end apart: 42, of which 14 were waited for; matrix products, arithmetic and copies ran while one was open for 5% of the time, Pallas kernels for 0%

profile of v3, /device:TPU:0, one launch (start us, length us, event | category | flops | bytes accessed | tf_op | source)
XLA Modules:
  0.0 99.5 jit_solution(15457056799785796482)
XLA Ops:
  0.6 3.1 %collective-permute-start.3 = (bf16[128,512]{1,0:T(8,128)(2,1)}, bf16[128,512]{1,0:T(8,128)(2,1)S(1)}, u32[]{:S(2)}, u32[]{:S(2)}) collective-permute-start(bf16[128,512]{1,0:T(8,128)(2,1)} %param.8), channel_id=1, source_target_pairs={{0,4},{1,5},{2,6},{3,7},{4,0},{5,1},{6,2},{7,3},{8,12},{9,13},{10,... | collective-permute-start | bytes 393224 | tf_op jit(solution)/shard_map/ppermute | solution.py:99
  3.7 1.5 %collective-permute-start.1 = (bf16[128,512]{1,0:T(8,128)(2,1)}, bf16[128,512]{1,0:T(8,128)(2,1)S(1)}, u32[]{:S(2)}, u32[]{:S(2)}) collective-permute-start(bf16[128,512]{1,0:T(8,128)(2,1)} %param.8), channel_id=1, source_target_pairs={{0,2},{1,3},{2,0},{3,1},{4,6},{5,7},{6,4},{7,5},{8,10},{9,11},{10,... | collective-permute-start | bytes 393224 | tf_op jit(solution)/shard_map/ppermute | solution.py:103
  5.3 2.6 %collective-permute-start.7 = (bf16[128,512]{1,0:T(8,128)(2,1)}, bf16[128,512]{1,0:T(8,128)(2,1)S(1)}, u32[]{:S(2)}, u32[]{:S(2)}) collective-permute-start(bf16[128,512]{1,0:T(8,128)(2,1)} %param.8), channel_id=1, source_target_pairs={{0,8},{1,9},{2,10},{3,11},{4,12},{5,13},{6,14},{7,15},{8,0},{9,1},... | collective-permute-start | bytes 393224 | tf_op jit(solution)/shard_map/ppermute | solution.py:99
  7.8 0.7 broadcast_multiply_fusion
  8.5 0.7 broadcast_compare_fusion
  9.2 0.7 broadcast_subtract_fusion.1
  10.6 0.6 collective-permute-start.11
  11.2 2.6 %collective-permute-start.5 = (bf16[128,512]{1,0:T(8,128)(2,1)S(1)}, bf16[128,512]{1,0:T(8,128)(2,1)S(1)}, u32[]{:S(2)}, u32[]{:S(2)}) collective-permute-start(bf16[128,512]{1,0:T(8,128)(2,1)S(1)} %collective-permute-done.3), channel_id=1, source_target_pairs={{0,2},{1,3},{2,0},{3,1},{4,6},{5,7},{6,4},{7,5},{8,10},{9,11},{10,... | collective-permute-start | bytes 393224 | tf_op jit(solution)/shard_map/ppermute | solution.py:103
  13.8 0.5 collective-permute-start.2
  14.3 1.0 %collective-permute-done.7 = bf16[128,512]{1,0:T(8,128)(2,1)S(1)} collective-permute-done((bf16[128,512]{1,0:T(8,128)(2,1)}, bf16[128,512]{1,0:T(8,128)(2,1)S(1)}, u32[]{:S(2)}, u32[]{:S(2)}) %collective-permute-start.7) | collective-permute-done | bytes 131104 | tf_op jit(solution)/shard_map/ppermute | solution.py:99
  15.3 0.5 collective-permute-start.9
  15.9 2.4 %collective-permute-done.11 = bf16[128,512]{1,0:T(8,128)(2,1)S(1)} collective-permute-done((bf16[128,512]{1,0:T(8,128)(2,1)S(1)}, bf16[128,512]{1,0:T(8,128)(2,1)S(1)}, u32[]{:S(2)}, u32[]{:S(2)}) %collective-permute-start.11) | collective-permute-done | bytes 131104 | tf_op jit(solution)/shard_map/ppermute | solution.py:100
  18.2 0.5 collective-permute-start.13
  19.4 0.9 collective-permute-done.9
  20.4 3.8 %collective-permute-done.13 = bf16[128,512]{1,0:T(8,128)(2,1)S(1)} collective-permute-done((bf16[128,512]{1,0:T(8,128)(2,1)S(1)}, bf16[128,512]{1,0:T(8,128)(2,1)S(1)}, u32[]{:S(2)}, u32[]{:S(2)}) %collective-permute-start.13) | collective-permute-done | bytes 131104 | tf_op jit(solution)/shard_map/ppermute | solution.py:103
  24.4 1.1 %collective-permute-done.14 = bf16[128,512]{1,0:T(8,128)(2,1)S(1)} collective-permute-done((bf16[128,512]{1,0:T(8,128)(2,1)S(1)}, bf16[128,512]{1,0:T(8,128)(2,1)S(1)}, u32[]{:S(2)}, u32[]{:S(2)}) %collective-permute-start.14) | collective-permute-done | bytes 131104 | tf_op jit(solution)/shard_map/ppermute | solution.py:105
  25.6 4.0 %forward.1 = (f32[128,128]{1,0:T(8,128)S(1)}, f32[128,128]{1,0:T(8,128)S(1)}, f32[128,128]{1,0:T(8,128)S(1)}, bf16[128,128]{1,0:T(8,128)(2,1)S(1)}, f32[8,128,51...) custom-call(bf16[128,8192]{1,0:T(8,128)(2,1)S(1)} %constant_dynamic-update-slice_fusion.16.hidden, f32[1,8192]{1,0:T(1,128)S(1)} %bitcast.71, ...), custom_call_target="tpu_custom_call" | custom-call | tf_op jit(solution)/shard_map/forward/pallas_call | solution.py:316
  29.8 0.5 copy-done.10
  30.8 0.4 collective-permute-start.17
  31.3 1.0 %fusion.2 = bf16[512,128]{1,0:T(8,128)(2,1)S(1)} fusion(s32[2048]{0:T(1024)S(1)} %fusion.5, s32[2048]{0:T(1024)S(1)} %broadcast_subtract_fusion), kind=kOutput, calls=%fused_computation.3 | convolution fusion | flops 269811712 | bytes 147456 | tf_op jit(solution)/shard_map/dot_general | solution.py:16
  33.0 0.6 collective-permute-start.22
  33.7 1.6 %collective-permute-start.21 = (bf16[128,512]{1,0:T(8,128)(2,1)S(1)}, bf16[128,512]{1,0:T(8,128)(2,1)S(1)}, u32[]{:S(2)}, u32[]{:S(2)}) collective-permute-start(bf16[128,512]{1,0:T(8,128)(2,1)S(1)} %fusion.22), channel_id=1, source_target_pairs={{0,2},{1,3},{2,0},{3,1},{4,6},{5,7},{6,4},{7,5},{8,10},{9,11},{10,... | collective-permute-start | bytes 393224 | tf_op jit(solution)/shard_map/ppermute | solution.py:121
  35.4 0.6 collective-permute-start.20
  36.1 1.6 %collective-permute-start.19 = (bf16[128,512]{1,0:T(8,128)(2,1)S(1)}, bf16[128,512]{1,0:T(8,128)(2,1)S(1)}, u32[]{:S(2)}, u32[]{:S(2)}) collective-permute-start(bf16[128,512]{1,0:T(8,128)(2,1)S(1)} %fusion.24), channel_id=1, source_target_pairs={{0,2},{1,3},{2,0},{3,1},{4,6},{5,7},{6,4},{7,5},{8,10},{9,11},{10,... | collective-permute-start | bytes 393224 | tf_op jit(solution)/shard_map/ppermute | solution.py:121
  37.7 1.7 %collective-permute-done.22 = bf16[128,512]{1,0:T(8,128)(2,1)S(1)} collective-permute-done((bf16[128,512]{1,0:T(8,128)(2,1)S(1)}, bf16[128,512]{1,0:T(8,128)(2,1)S(1)}, u32[]{:S(2)}, u32[]{:S(2)}) %collective-permute-start.22) | collective-permute-done | bytes 131104 | tf_op jit(solution)/shard_map/ppermute | solution.py:121
  39.5 4.4 %collective-permute-start.23 = (bf16[128,512]{1,0:T(8,128)(2,1)S(1)}, bf16[128,512]{1,0:T(8,128)(2,1)S(1)}, u32[]{:S(2)}, u32[]{:S(2)}) collective-permute-start(bf16[128,512]{1,0:T(8,128)(2,1)S(1)} %fusion.9), channel_id=1, source_target_pairs={{0,12},{1,13},{2,14},{3,15},{4,8},{5,9},{6,10},{7,11},{8,4},{9,5},... | collective-permute-start | bytes 393224 | tf_op jit(solution)/shard_map/ppermute | solution.py:129
  44.0 2.4 %collective-permute-start.24 = (bf16[128,512]{1,0:T(8,128)(2,1)S(1)}, bf16[128,512]{1,0:T(8,128)(2,1)S(1)}, u32[]{:S(2)}, u32[]{:S(2)}) collective-permute-start(bf16[128,512]{1,0:T(8,128)(2,1)S(1)} %fusion.11), channel_id=1, source_target_pairs={{0,8},{1,9},{2,10},{3,11},{4,12},{5,13},{6,14},{7,15},{8,0},{9,1},... | collective-permute-start | bytes 393224 | tf_op jit(solution)/shard_map/ppermute | solution.py:129
  46.4 1.7 %collective-permute-start.25 = (bf16[128,512]{1,0:T(8,128)(2,1)S(1)}, bf16[128,512]{1,0:T(8,128)(2,1)S(1)}, u32[]{:S(2)}, u32[]{:S(2)}) collective-permute-start(bf16[128,512]{1,0:T(8,128)(2,1)S(1)} %fusion.13), channel_id=1, source_target_pairs={{0,4},{1,5},{2,6},{3,7},{4,0},{5,1},{6,2},{7,3},{8,12},{9,13},{10,... | collective-permute-start | bytes 393224 | tf_op jit(solution)/shard_map/ppermute | solution.py:129
  48.2 6.1 %collective-permute-done.24 = bf16[128,512]{1,0:T(8,128)(2,1)S(1)} collective-permute-done((bf16[128,512]{1,0:T(8,128)(2,1)S(1)}, bf16[128,512]{1,0:T(8,128)(2,1)S(1)}, u32[]{:S(2)}, u32[]{:S(2)}) %collective-permute-start.24) | collective-permute-done | bytes 131104 | tf_op jit(solution)/shard_map/ppermute | solution.py:129
  54.7 3.1 %collective-permute-start.29 = (bf16[128,512]{1,0:T(8,128)(2,1)S(1)}, bf16[128,512]{1,0:T(8,128)(2,1)S(1)}, u32[]{:S(2)}, u32[]{:S(2)}) collective-permute-start(bf16[128,512]{1,0:T(8,128)(2,1)S(1)} %get-tuple-element.34), channel_id=1, source_target_pairs={{0,4},{1,5},{2,6},{3,7},{4,0},{5,1},{6,2},{7,3},{8,12},{9,13},{10,... | collective-permute-start | bytes 393224 | tf_op jit(solution)/shard_map/ppermute | solution.py:99
  57.8 0.6 collective-permute-start.27
  58.5 4.5 %collective-permute-done.29 = bf16[128,512]{1,0:T(8,128)(2,1)S(1)} collective-permute-done((bf16[128,512]{1,0:T(8,128)(2,1)S(1)}, bf16[128,512]{1,0:T(8,128)(2,1)S(1)}, u32[]{:S(2)}, u32[]{:S(2)}) %collective-permute-start.29) | collective-permute-done | bytes 131104 | tf_op jit(solution)/shard_map/ppermute | solution.py:99
  63.0 1.8 %collective-permute-start.37 = (bf16[128,512]{1,0:T(8,128)(2,1)S(1)}, bf16[128,512]{1,0:T(8,128)(2,1)S(1)}, u32[]{:S(2)}, u32[]{:S(2)}) collective-permute-start(bf16[128,512]{1,0:T(8,128)(2,1)S(1)} %get-tuple-element.34), channel_id=1, source_target_pairs={{0,12},{1,13},{2,14},{3,15},{4,8},{5,9},{6,10},{7,11},{8,4},{9,5},... | collective-permute-start | bytes 393224 | tf_op jit(solution)/shard_map/ppermute | solution.py:100
  64.8 0.6 collective-permute-start.35
  65.4 1.5 %collective-permute-start.31 = (bf16[128,512]{1,0:T(8,128)(2,1)S(1)}, bf16[128,512]{1,0:T(8,128)(2,1)S(1)}, u32[]{:S(2)}, u32[]{:S(2)}) collective-permute-start(bf16[128,512]{1,0:T(8,128)(2,1)S(1)} %collective-permute-done.29), channel_id=1, source_target_pairs={{0,2},{1,3},{2,0},{3,1},{4,6},{5,7},{6,4},{7,5},{8,10},{9,11},{10,... | collective-permute-start | bytes 393224 | tf_op jit(solution)/shard_map/ppermute | solution.py:103
  67.1 2.6 %collective-permute-done.37 = bf16[128,512]{1,0:T(8,128)(2,1)S(1)} collective-permute-done((bf16[128,512]{1,0:T(8,128)(2,1)S(1)}, bf16[128,512]{1,0:T(8,128)(2,1)S(1)}, u32[]{:S(2)}, u32[]{:S(2)}) %collective-permute-start.37) | collective-permute-done | bytes 131104 | tf_op jit(solution)/shard_map/ppermute | solution.py:100
  69.8 0.5 collective-permute-start.39
  70.3 0.7 collective-permute-done.35
  71.1 1.5 %collective-permute-done.31 = bf16[128,512]{1,0:T(8,128)(2,1)S(1)} collective-permute-done((bf16[128,512]{1,0:T(8,128)(2,1)S(1)}, bf16[128,512]{1,0:T(8,128)(2,1)S(1)}, u32[]{:S(2)}, u32[]{:S(2)}) %collective-permute-start.31) | collective-permute-done | bytes 131104 | tf_op jit(solution)/shard_map/ppermute | solution.py:103
  72.6 0.5 collective-permute-start.32
  73.1 2.5 %collective-permute-done.39 = bf16[128,512]{1,0:T(8,128)(2,1)S(1)} collective-permute-done((bf16[128,512]{1,0:T(8,128)(2,1)S(1)}, bf16[128,512]{1,0:T(8,128)(2,1)S(1)}, u32[]{:S(2)}, u32[]{:S(2)}) %collective-permute-start.39) | collective-permute-done | bytes 131104 | tf_op jit(solution)/shard_map/ppermute | solution.py:103
  75.9 1.1 %collective-permute-done.40 = bf16[128,512]{1,0:T(8,128)(2,1)S(1)} collective-permute-done((bf16[128,512]{1,0:T(8,128)(2,1)S(1)}, bf16[128,512]{1,0:T(8,128)(2,1)S(1)}, u32[]{:S(2)}, u32[]{:S(2)}) %collective-permute-start.40) | collective-permute-done | bytes 131104 | tf_op jit(solution)/shard_map/ppermute | solution.py:105
  77.0 3.8 %backward.1 = bf16[16,32,128]{2,1,0:T(8,128)(2,1)} custom-call(bf16[128,8192]{1,0:T(8,128)(2,1)S(1)} %constant_dynamic-update-slice_fusion.slope, bf16[128,8192]{1,0:T(8,128)(2,1)S(1)} %constant_dynamic-update-slice_fusion.16.hidden, bf16[128,8192]{1,0:T(8,128)(2,1)S(1)} %copy-done.2, bf16[128,8192]{1,0:T(8,128)(2,1)S(1)} %copy-done.3, ...), custom_call_target="tpu_custom_call" | custom-call | tf_op jit(solution)/shard_map/backward/pallas_call | solution.py:316
  80.8 1.3 %copy-done = bf16[128,8192]{1,0:T(8,128)(2,1)} copy-done((bf16[128,8192]{1,0:T(8,128)(2,1)}, bf16[128,8192]{1,0:T(8,128)(2,1)S(1)}, u32[]{:S(2)}) %copy-start) | copy-done | bytes 2097176
  82.1 3.7 %all-to-all-start = ((bf16[16,32,128]{2,1,0:T(8,128)(2,1)}), bf16[16,32,128]{2,1,0:T(8,128)(2,1)S(1)}, u32[]{:S(2)}, u32[]{:S(2)}) async-start(bf16[16,32,128]{2,1,0:T(8,128)(2,1)} %backward.1), calls=%async_computation | async-start | bytes 262144 | tf_op jit(solution)/shard_map/all_to_all | solution.py:394
  86.3 7.4 %all-to-all-done.received = bf16[16,32,128]{2,1,0:T(8,128)(2,1)S(1)} async-done(((bf16[16,32,128]{2,1,0:T(8,128)(2,1)}), bf16[16,32,128]{2,1,0:T(8,128)(2,1)S(1)}, u32[]{:S(2)}, u32[]{:S(2)}) %all-to-all-start) | async-done | bytes 131104 | tf_op jit(solution)/shard_map/all_to_all | solution.py:394
  93.7 1.6 %copy-done.1 = bf16[128,8192]{1,0:T(8,128)(2,1)S(1)} copy-done((bf16[128,8192]{1,0:T(8,128)(2,1)S(1)}, bf16[128,8192]{1,0:T(8,128)(2,1)}, u32[]{:S(2)}) %copy-start.1) | copy-done | bytes 2097176
  95.3 4.0 %rows.1 = (bf16[128,8192]{1,0:T(8,128)(2,1)}, bf16[128,8192]{1,0:T(8,128)(2,1)}, bf16[128,8192]{1,0:T(8,128)(2,1)}, f32[1,512]{1,0:T(1,128)}, f32[1,1]{1,0:T(1,128)}) custom-call(bf16[16,32,128]{2,1,0:T(8,128)(2,1)S(1)} %all-to-all-done.received, bf16[3,128,512]{2,1,0:T(8,128)(2,1)S(1)} %pad_maximum_fusion.1.places, ...), custom_call_target="tpu_custom_call" | custom-call | tf_op jit(solution)/shard_map/rows/pallas_call | solution.py:316
  (135 shorter events, 4.8 us)
Async XLA Ops:
  0.6 10.0 %collective-permute-start.3 = (bf16[128,512]{1,0:T(8,128)(2,1)}, bf16[128,512]{1,0:T(8,128)(2,1)S(1)}, u32[]{:S(2)}, u32[]{:S(2)}) collective-permute-start(bf16[128,512]{1,0:T(8,128)(2,1)} %param.8), channel_id=1, source_target_pairs={{0,4},{1,5},{2,6},{3,7},{4,0},{5,1},{6,2},{7,3},{8,12},{9,13},{10,... | collective-permute-start | bytes 393224 | tf_op jit(solution)/shard_map/ppermute | solution.py:99
  3.7 10.1 %collective-permute-start.1 = (bf16[128,512]{1,0:T(8,128)(2,1)}, bf16[128,512]{1,0:T(8,128)(2,1)S(1)}, u32[]{:S(2)}, u32[]{:S(2)}) collective-permute-start(bf16[128,512]{1,0:T(8,128)(2,1)} %param.8), channel_id=1, source_target_pairs={{0,2},{1,3},{2,0},{3,1},{4,6},{5,7},{6,4},{7,5},{8,10},{9,11},{10,... | collective-permute-start | bytes 393224 | tf_op jit(solution)/shard_map/ppermute | solution.py:103
  5.2 8.6 %collective-permute-start = (bf16[128,512]{1,0:T(8,128)(2,1)}, bf16[128,512]{1,0:T(8,128)(2,1)S(1)}, u32[]{:S(2)}, u32[]{:S(2)}) collective-permute-start(bf16[128,512]{1,0:T(8,128)(2,1)} %param.8), channel_id=1, source_target_pairs={{0,1},{1,0},{2,3},{3,2},{4,5},{5,4},{6,7},{7,6},{8,9},{9,8},{10,11... | collective-permute-start | bytes 393224 | tf_op jit(solution)/shard_map/ppermute | solution.py:105
  5.3 10.1 %collective-permute-start.7 = (bf16[128,512]{1,0:T(8,128)(2,1)}, bf16[128,512]{1,0:T(8,128)(2,1)S(1)}, u32[]{:S(2)}, u32[]{:S(2)}) collective-permute-start(bf16[128,512]{1,0:T(8,128)(2,1)} %param.8), channel_id=1, source_target_pairs={{0,8},{1,9},{2,10},{3,11},{4,12},{5,13},{6,14},{7,15},{8,0},{9,1},... | collective-permute-start | bytes 393224 | tf_op jit(solution)/shard_map/ppermute | solution.py:99
  10.3 15.3 %copy-start.6 = (f32[8192]{0:T(1024)S(1)}, f32[8192]{0:T(1024)}, u32[]{:S(2)}) copy-start(f32[8192]{0:T(1024)} %param.9) | copy-start | bytes 98308
  10.3 15.2 %copy-start.5 = (f32[8192]{0:T(1024)S(1)}, f32[8192]{0:T(1024)}, u32[]{:S(2)}) copy-start(f32[8192]{0:T(1024)} %param.10) | copy-start | bytes 98308
  10.6 7.6 %collective-permute-start.11 = (bf16[128,512]{1,0:T(8,128)(2,1)S(1)}, bf16[128,512]{1,0:T(8,128)(2,1)S(1)}, u32[]{:S(2)}, u32[]{:S(2)}) collective-permute-start(bf16[128,512]{1,0:T(8,128)(2,1)S(1)} %copy-done.9), channel_id=1, source_target_pairs={{0,12},{1,13},{2,14},{3,15},{4,8},{5,9},{6,10},{7,11},{8,4},{9,5},... | collective-permute-start | bytes 393224 | tf_op jit(solution)/shard_map/ppermute | solution.py:100
  11.2 7.6 %collective-permute-start.5 = (bf16[128,512]{1,0:T(8,128)(2,1)S(1)}, bf16[128,512]{1,0:T(8,128)(2,1)S(1)}, u32[]{:S(2)}, u32[]{:S(2)}) collective-permute-start(bf16[128,512]{1,0:T(8,128)(2,1)S(1)} %collective-permute-done.3), channel_id=1, source_target_pairs={{0,2},{1,3},{2,0},{3,1},{4,6},{5,7},{6,4},{7,5},{8,10},{9,11},{10,... | collective-permute-start | bytes 393224 | tf_op jit(solution)/shard_map/ppermute | solution.py:103
  13.8 5.3 %collective-permute-start.4 = (bf16[128,512]{1,0:T(8,128)(2,1)S(1)}, bf16[128,512]{1,0:T(8,128)(2,1)S(1)}, u32[]{:S(2)}, u32[]{:S(2)}) collective-permute-start(bf16[128,512]{1,0:T(8,128)(2,1)S(1)} %collective-permute-done.3), channel_id=1, source_target_pairs={{0,1},{1,0},{2,3},{3,2},{4,5},{5,4},{6,7},{7,6},{8,9},{9,8},{10,11... | collective-permute-start | bytes 393224 | tf_op jit(solution)/shard_map/ppermute | solution.py:105
  13.8 4.4 %collective-permute-start.2 = (bf16[128,512]{1,0:T(8,128)(2,1)S(1)}, bf16[128,512]{1,0:T(8,128)(2,1)S(1)}, u32[]{:S(2)}, u32[]{:S(2)}) collective-permute-start(bf16[128,512]{1,0:T(8,128)(2,1)S(1)} %collective-permute-done.1), channel_id=1, source_target_pairs={{0,1},{1,0},{2,3},{3,2},{4,5},{5,4},{6,7},{7,6},{8,9},{9,8},{10,11... | collective-permute-start | bytes 393224 | tf_op jit(solution)/shard_map/ppermute | solution.py:105
  15.3 5.0 %collective-permute-start.9 = (bf16[128,512]{1,0:T(8,128)(2,1)S(1)}, bf16[128,512]{1,0:T(8,128)(2,1)S(1)}, u32[]{:S(2)}, u32[]{:S(2)}) collective-permute-start(bf16[128,512]{1,0:T(8,128)(2,1)S(1)} %collective-permute-done.7), channel_id=1, source_target_pairs={{0,2},{1,3},{2,0},{3,1},{4,6},{5,7},{6,4},{7,5},{8,10},{9,11},{10,... | collective-permute-start | bytes 393224 | tf_op jit(solution)/shard_map/ppermute | solution.py:103
  18.2 6.0 %collective-permute-start.8 = (bf16[128,512]{1,0:T(8,128)(2,1)S(1)}, bf16[128,512]{1,0:T(8,128)(2,1)S(1)}, u32[]{:S(2)}, u32[]{:S(2)}) collective-permute-start(bf16[128,512]{1,0:T(8,128)(2,1)S(1)} %collective-permute-done.7), channel_id=1, source_target_pairs={{0,1},{1,0},{2,3},{3,2},{4,5},{5,4},{6,7},{7,6},{8,9},{9,8},{10,11... | collective-permute-start | bytes 393224 | tf_op jit(solution)/shard_map/ppermute | solution.py:105
  18.2 5.9 %collective-permute-start.13 = (bf16[128,512]{1,0:T(8,128)(2,1)S(1)}, bf16[128,512]{1,0:T(8,128)(2,1)S(1)}, u32[]{:S(2)}, u32[]{:S(2)}) collective-permute-start(bf16[128,512]{1,0:T(8,128)(2,1)S(1)} %collective-permute-done.11), channel_id=1, source_target_pairs={{0,2},{1,3},{2,0},{3,1},{4,6},{5,7},{6,4},{7,5},{8,10},{9,11},{10,... | collective-permute-start | bytes 393224 | tf_op jit(solution)/shard_map/ppermute | solution.py:103
  18.8 5.5 %collective-permute-start.12 = (bf16[128,512]{1,0:T(8,128)(2,1)S(1)}, bf16[128,512]{1,0:T(8,128)(2,1)S(1)}, u32[]{:S(2)}, u32[]{:S(2)}) collective-permute-start(bf16[128,512]{1,0:T(8,128)(2,1)S(1)} %collective-permute-done.11), channel_id=1, source_target_pairs={{0,1},{1,0},{2,3},{3,2},{4,5},{5,4},{6,7},{7,6},{8,9},{9,8},{10,11... | collective-permute-start | bytes 393224 | tf_op jit(solution)/shard_map/ppermute | solution.py:105
  19.1 5.1 %collective-permute-start.6 = (bf16[128,512]{1,0:T(8,128)(2,1)S(1)}, bf16[128,512]{1,0:T(8,128)(2,1)S(1)}, u32[]{:S(2)}, u32[]{:S(2)}) collective-permute-start(bf16[128,512]{1,0:T(8,128)(2,1)S(1)} %collective-permute-done.5), channel_id=1, source_target_pairs={{0,1},{1,0},{2,3},{3,2},{4,5},{5,4},{6,7},{7,6},{8,9},{9,8},{10,11... | collective-permute-start | bytes 393224 | tf_op jit(solution)/shard_map/ppermute | solution.py:105
  20.3 4.0 %collective-permute-start.10 = (bf16[128,512]{1,0:T(8,128)(2,1)S(1)}, bf16[128,512]{1,0:T(8,128)(2,1)S(1)}, u32[]{:S(2)}, u32[]{:S(2)}) collective-permute-start(bf16[128,512]{1,0:T(8,128)(2,1)S(1)} %collective-permute-done.9), channel_id=1, source_target_pairs={{0,1},{1,0},{2,3},{3,2},{4,5},{5,4},{6,7},{7,6},{8,9},{9,8},{10,11... | collective-permute-start | bytes 393224 | tf_op jit(solution)/shard_map/ppermute | solution.py:105
  24.2 1.3 %collective-permute-start.14 = (bf16[128,512]{1,0:T(8,128)(2,1)S(1)}, bf16[128,512]{1,0:T(8,128)(2,1)S(1)}, u32[]{:S(2)}, u32[]{:S(2)}) collective-permute-start(bf16[128,512]{1,0:T(8,128)(2,1)S(1)} %collective-permute-done.13), channel_id=1, source_target_pairs={{0,1},{1,0},{2,3},{3,2},{4,5},{5,4},{6,7},{7,6},{8,9},{9,8},{10,11... | collective-permute-start | bytes 393224 | tf_op jit(solution)/shard_map/ppermute | solution.py:105
  30.6 2.3 %collective-permute-start.18 = (f32[2,128,512]{2,1,0:T(8,128)S(1)}, f32[2,128,512]{2,1,0:T(8,128)S(1)}, u32[]{:S(2)}, u32[]{:S(2)}) collective-permute-start(f32[2,128,512]{2,1,0:T(8,128)S(1)} %get-tuple-element.48), channel_id=1, source_target_pairs={{0,1},{1,0},{2,3},{3,2},{4,5},{5,4},{6,7},{7,6},{8,9},{9,8},{10,11... | collective-permute-start | bytes 1572872 | tf_op jit(solution)/shard_map/ppermute | solution.py:115
  30.8 2.8 %collective-permute-start.17 = (f32[2,128,512]{2,1,0:T(8,128)S(1)}, f32[2,128,512]{2,1,0:T(8,128)S(1)}, u32[]{:S(2)}, u32[]{:S(2)}) collective-permute-start(f32[2,128,512]{2,1,0:T(8,128)S(1)} %get-tuple-element.49), channel_id=1, source_target_pairs={{0,1},{1,0},{2,3},{3,2},{4,5},{5,4},{6,7},{7,6},{8,9},{9,8},{10,11... | collective-permute-start | bytes 1572872 | tf_op jit(solution)/shard_map/ppermute | solution.py:115
  32.3 3.7 %collective-permute-start.15 = (f32[2,128,512]{2,1,0:T(8,128)S(1)}, f32[2,128,512]{2,1,0:T(8,128)S(1)}, u32[]{:S(2)}, u32[]{:S(2)}) collective-permute-start(f32[2,128,512]{2,1,0:T(8,128)S(1)} %get-tuple-element.47), channel_id=1, source_target_pairs={{0,1},{1,0},{2,3},{3,2},{4,5},{5,4},{6,7},{7,6},{8,9},{9,8},{10,11... | collective-permute-start | bytes 1572872 | tf_op jit(solution)/shard_map/ppermute | solution.py:115
  32.5 2.8 %collective-permute-start.16 = (f32[2,128,512]{2,1,0:T(8,128)S(1)}, f32[2,128,512]{2,1,0:T(8,128)S(1)}, u32[]{:S(2)}, u32[]{:S(2)}) collective-permute-start(f32[2,128,512]{2,1,0:T(8,128)S(1)} %get-tuple-element.50), channel_id=1, source_target_pairs={{0,1},{1,0},{2,3},{3,2},{4,5},{5,4},{6,7},{7,6},{8,9},{9,8},{10,11... | collective-permute-start | bytes 1572872 | tf_op jit(solution)/shard_map/ppermute | solution.py:115
  33.0 6.4 %collective-permute-start.22 = (bf16[128,512]{1,0:T(8,128)(2,1)S(1)}, bf16[128,512]{1,0:T(8,128)(2,1)S(1)}, u32[]{:S(2)}, u32[]{:S(2)}) collective-permute-start(bf16[128,512]{1,0:T(8,128)(2,1)S(1)} %fusion.21), channel_id=1, source_target_pairs={{0,2},{1,3},{2,0},{3,1},{4,6},{5,7},{6,4},{7,5},{8,10},{9,11},{10,... | collective-permute-start | bytes 393224 | tf_op jit(solution)/shard_map/ppermute | solution.py:121
  33.7 10.2 %collective-permute-start.21 = (bf16[128,512]{1,0:T(8,128)(2,1)S(1)}, bf16[128,512]{1,0:T(8,128)(2,1)S(1)}, u32[]{:S(2)}, u32[]{:S(2)}) collective-permute-start(bf16[128,512]{1,0:T(8,128)(2,1)S(1)} %fusion.22), channel_id=1, source_target_pairs={{0,2},{1,3},{2,0},{3,1},{4,6},{5,7},{6,4},{7,5},{8,10},{9,11},{10,... | collective-permute-start | bytes 393224 | tf_op jit(solution)/shard_map/ppermute | solution.py:121
  35.4 11.0 %collective-permute-start.20 = (bf16[128,512]{1,0:T(8,128)(2,1)S(1)}, bf16[128,512]{1,0:T(8,128)(2,1)S(1)}, u32[]{:S(2)}, u32[]{:S(2)}) collective-permute-start(bf16[128,512]{1,0:T(8,128)(2,1)S(1)} %fusion.23), channel_id=1, source_target_pairs={{0,2},{1,3},{2,0},{3,1},{4,6},{5,7},{6,4},{7,5},{8,10},{9,11},{10,... | collective-permute-start | bytes 393224 | tf_op jit(solution)/shard_map/ppermute | solution.py:121
  36.1 12.1 %collective-permute-start.19 = (bf16[128,512]{1,0:T(8,128)(2,1)S(1)}, bf16[128,512]{1,0:T(8,128)(2,1)S(1)}, u32[]{:S(2)}, u32[]{:S(2)}) collective-permute-start(bf16[128,512]{1,0:T(8,128)(2,1)S(1)} %fusion.24), channel_id=1, source_target_pairs={{0,2},{1,3},{2,0},{3,1},{4,6},{5,7},{6,4},{7,5},{8,10},{9,11},{10,... | collective-permute-start | bytes 393224 | tf_op jit(solution)/shard_map/ppermute | solution.py:121
  39.4 18.9 %slice-start = ((bf16[512,128]{1,0:T(8,128)(2,1)}), bf16[8,128]{1,0:T(8,128)(2,1)S(1)}, s32[]{:S(2)}) async-start(bf16[512,128]{1,0:T(8,128)(2,1)} %copy-done.7), calls=%async_computation.1 | async-start | bytes 4096 | tf_op jit(solution)/shard_map/jit(_roll_static)/slice | solution.py:371
  39.4 18.9 %slice-start.1 = ((bf16[512,128]{1,0:T(8,128)(2,1)}), bf16[16,128]{1,0:T(8,128)(2,1)S(1)}, s32[]{:S(2)}) async-start(bf16[512,128]{1,0:T(8,128)(2,1)} %copy-done.7), calls=%async_computation.2 | async-start | bytes 8192 | tf_op jit(solution)/shard_map/jit(_roll_static)/slice | solution.py:371
  39.5 18.9 %slice-start.2 = ((bf16[512,128]{1,0:T(8,128)(2,1)}), bf16[496,128]{1,0:T(8,128)(2,1)S(1)}, s32[]{:S(2)}) async-start(bf16[512,128]{1,0:T(8,128)(2,1)} %copy-done.7), calls=%async_computation.3 | async-start | bytes 253952 | tf_op jit(solution)/shard_map/jit(_roll_static)/slice | solution.py:371
  39.5 18.9 %slice-start.3 = ((bf16[512,128]{1,0:T(8,128)(2,1)}), bf16[504,128]{1,0:T(8,128)(2,1)S(1)}, s32[]{:S(2)}) async-start(bf16[512,128]{1,0:T(8,128)(2,1)} %copy-done.7), calls=%async_computation.4 | async-start | bytes 258048 | tf_op jit(solution)/shard_map/jit(_roll_static)/slice | solution.py:371
  39.5 8.7 %collective-permute-start.23 = (bf16[128,512]{1,0:T(8,128)(2,1)S(1)}, bf16[128,512]{1,0:T(8,128)(2,1)S(1)}, u32[]{:S(2)}, u32[]{:S(2)}) collective-permute-start(bf16[128,512]{1,0:T(8,128)(2,1)S(1)} %fusion.9), channel_id=1, source_target_pairs={{0,12},{1,13},{2,14},{3,15},{4,8},{5,9},{6,10},{7,11},{8,4},{9,5},... | collective-permute-start | bytes 393224 | tf_op jit(solution)/shard_map/ppermute | solution.py:129
  44.0 10.4 %collective-permute-start.24 = (bf16[128,512]{1,0:T(8,128)(2,1)S(1)}, bf16[128,512]{1,0:T(8,128)(2,1)S(1)}, u32[]{:S(2)}, u32[]{:S(2)}) collective-permute-start(bf16[128,512]{1,0:T(8,128)(2,1)S(1)} %fusion.11), channel_id=1, source_target_pairs={{0,8},{1,9},{2,10},{3,11},{4,12},{5,13},{6,14},{7,15},{8,0},{9,1},... | collective-permute-start | bytes 393224 | tf_op jit(solution)/shard_map/ppermute | solution.py:129
  46.4 7.9 %collective-permute-start.25 = (bf16[128,512]{1,0:T(8,128)(2,1)S(1)}, bf16[128,512]{1,0:T(8,128)(2,1)S(1)}, u32[]{:S(2)}, u32[]{:S(2)}) collective-permute-start(bf16[128,512]{1,0:T(8,128)(2,1)S(1)} %fusion.13), channel_id=1, source_target_pairs={{0,4},{1,5},{2,6},{3,7},{4,0},{5,1},{6,2},{7,3},{8,12},{9,13},{10,... | collective-permute-start | bytes 393224 | tf_op jit(solution)/shard_map/ppermute | solution.py:129
  54.6 10.2 %collective-permute-start.33 = (bf16[128,512]{1,0:T(8,128)(2,1)S(1)}, bf16[128,512]{1,0:T(8,128)(2,1)S(1)}, u32[]{:S(2)}, u32[]{:S(2)}) collective-permute-start(bf16[128,512]{1,0:T(8,128)(2,1)S(1)} %get-tuple-element.34), channel_id=1, source_target_pairs={{0,8},{1,9},{2,10},{3,11},{4,12},{5,13},{6,14},{7,15},{8,0},{9,1},... | collective-permute-start | bytes 393224 | tf_op jit(solution)/shard_map/ppermute | solution.py:99
  54.7 8.3 %collective-permute-start.29 = (bf16[128,512]{1,0:T(8,128)(2,1)S(1)}, bf16[128,512]{1,0:T(8,128)(2,1)S(1)}, u32[]{:S(2)}, u32[]{:S(2)}) collective-permute-start(bf16[128,512]{1,0:T(8,128)(2,1)S(1)} %get-tuple-element.34), channel_id=1, source_target_pairs={{0,4},{1,5},{2,6},{3,7},{4,0},{5,1},{6,2},{7,3},{8,12},{9,13},{10,... | collective-permute-start | bytes 393224 | tf_op jit(solution)/shard_map/ppermute | solution.py:99
  57.8 7.6 %collective-permute-start.27 = (bf16[128,512]{1,0:T(8,128)(2,1)S(1)}, bf16[128,512]{1,0:T(8,128)(2,1)S(1)}, u32[]{:S(2)}, u32[]{:S(2)}) collective-permute-start(bf16[128,512]{1,0:T(8,128)(2,1)S(1)} %get-tuple-element.34), channel_id=1, source_target_pairs={{0,2},{1,3},{2,0},{3,1},{4,6},{5,7},{6,4},{7,5},{8,10},{9,11},{10,... | collective-permute-start | bytes 393224 | tf_op jit(solution)/shard_map/ppermute | solution.py:103
  58.3 8.5 %collective-permute-start.26 = (bf16[128,512]{1,0:T(8,128)(2,1)S(1)}, bf16[128,512]{1,0:T(8,128)(2,1)S(1)}, u32[]{:S(2)}, u32[]{:S(2)}) collective-permute-start(bf16[128,512]{1,0:T(8,128)(2,1)S(1)} %get-tuple-element.34), channel_id=1, source_target_pairs={{0,1},{1,0},{2,3},{3,2},{4,5},{5,4},{6,7},{7,6},{8,9},{9,8},{10,11... | collective-permute-start | bytes 393224 | tf_op jit(solution)/shard_map/ppermute | solution.py:105
  63.0 6.8 %collective-permute-start.37 = (bf16[128,512]{1,0:T(8,128)(2,1)S(1)}, bf16[128,512]{1,0:T(8,128)(2,1)S(1)}, u32[]{:S(2)}, u32[]{:S(2)}) collective-permute-start(bf16[128,512]{1,0:T(8,128)(2,1)S(1)} %get-tuple-element.34), channel_id=1, source_target_pairs={{0,12},{1,13},{2,14},{3,15},{4,8},{5,9},{6,10},{7,11},{8,4},{9,5},... | collective-permute-start | bytes 393224 | tf_op jit(solution)/shard_map/ppermute | solution.py:100
  64.8 6.3 %collective-permute-start.35 = (bf16[128,512]{1,0:T(8,128)(2,1)S(1)}, bf16[128,512]{1,0:T(8,128)(2,1)S(1)}, u32[]{:S(2)}, u32[]{:S(2)}) collective-permute-start(bf16[128,512]{1,0:T(8,128)(2,1)S(1)} %collective-permute-done.33), channel_id=1, source_target_pairs={{0,2},{1,3},{2,0},{3,1},{4,6},{5,7},{6,4},{7,5},{8,10},{9,11},{10,... | collective-permute-start | bytes 393224 | tf_op jit(solution)/shard_map/ppermute | solution.py:103
  65.4 10.3 %collective-permute-start.34 = (bf16[128,512]{1,0:T(8,128)(2,1)S(1)}, bf16[128,512]{1,0:T(8,128)(2,1)S(1)}, u32[]{:S(2)}, u32[]{:S(2)}) collective-permute-start(bf16[128,512]{1,0:T(8,128)(2,1)S(1)} %collective-permute-done.33), channel_id=1, source_target_pairs={{0,1},{1,0},{2,3},{3,2},{4,5},{5,4},{6,7},{7,6},{8,9},{9,8},{10,11... | collective-permute-start | bytes 393224 | tf_op jit(solution)/shard_map/ppermute | solution.py:105
  65.4 7.2 %collective-permute-start.31 = (bf16[128,512]{1,0:T(8,128)(2,1)S(1)}, bf16[128,512]{1,0:T(8,128)(2,1)S(1)}, u32[]{:S(2)}, u32[]{:S(2)}) collective-permute-start(bf16[128,512]{1,0:T(8,128)(2,1)S(1)} %collective-permute-done.29), channel_id=1, source_target_pairs={{0,2},{1,3},{2,0},{3,1},{4,6},{5,7},{6,4},{7,5},{8,10},{9,11},{10,... | collective-permute-start | bytes 393224 | tf_op jit(solution)/shard_map/ppermute | solution.py:103
  66.8 2.9 %collective-permute-start.28 = (bf16[128,512]{1,0:T(8,128)(2,1)S(1)}, bf16[128,512]{1,0:T(8,128)(2,1)S(1)}, u32[]{:S(2)}, u32[]{:S(2)}) collective-permute-start(bf16[128,512]{1,0:T(8,128)(2,1)S(1)} %collective-permute-done.27), channel_id=1, source_target_pairs={{0,1},{1,0},{2,3},{3,2},{4,5},{5,4},{6,7},{7,6},{8,9},{9,8},{10,11... | collective-permute-start | bytes 393224 | tf_op jit(solution)/shard_map/ppermute | solution.py:105
  69.7 2.8 %collective-permute-start.30 = (bf16[128,512]{1,0:T(8,128)(2,1)S(1)}, bf16[128,512]{1,0:T(8,128)(2,1)S(1)}, u32[]{:S(2)}, u32[]{:S(2)}) collective-permute-start(bf16[128,512]{1,0:T(8,128)(2,1)S(1)} %collective-permute-done.29), channel_id=1, source_target_pairs={{0,1},{1,0},{2,3},{3,2},{4,5},{5,4},{6,7},{7,6},{8,9},{9,8},{10,11... | collective-permute-start | bytes 393224 | tf_op jit(solution)/shard_map/ppermute | solution.py:105
  69.8 5.9 %collective-permute-start.39 = (bf16[128,512]{1,0:T(8,128)(2,1)S(1)}, bf16[128,512]{1,0:T(8,128)(2,1)S(1)}, u32[]{:S(2)}, u32[]{:S(2)}) collective-permute-start(bf16[128,512]{1,0:T(8,128)(2,1)S(1)} %collective-permute-done.37), channel_id=1, source_target_pairs={{0,2},{1,3},{2,0},{3,1},{4,6},{5,7},{6,4},{7,5},{8,10},{9,11},{10,... | collective-permute-start | bytes 393224 | tf_op jit(solution)/shard_map/ppermute | solution.py:103
  71.1 4.8 %collective-permute-start.38 = (bf16[128,512]{1,0:T(8,128)(2,1)S(1)}, bf16[128,512]{1,0:T(8,128)(2,1)S(1)}, u32[]{:S(2)}, u32[]{:S(2)}) collective-permute-start(bf16[128,512]{1,0:T(8,128)(2,1)S(1)} %collective-permute-done.37), channel_id=1, source_target_pairs={{0,1},{1,0},{2,3},{3,2},{4,5},{5,4},{6,7},{7,6},{8,9},{9,8},{10,11... | collective-permute-start | bytes 393224 | tf_op jit(solution)/shard_map/ppermute | solution.py:105
  72.6 3.2 %collective-permute-start.36 = (bf16[128,512]{1,0:T(8,128)(2,1)S(1)}, bf16[128,512]{1,0:T(8,128)(2,1)S(1)}, u32[]{:S(2)}, u32[]{:S(2)}) collective-permute-start(bf16[128,512]{1,0:T(8,128)(2,1)S(1)} %collective-permute-done.35), channel_id=1, source_target_pairs={{0,1},{1,0},{2,3},{3,2},{4,5},{5,4},{6,7},{7,6},{8,9},{9,8},{10,11... | collective-permute-start | bytes 393224 | tf_op jit(solution)/shard_map/ppermute | solution.py:105
  72.6 3.1 %collective-permute-start.32 = (bf16[128,512]{1,0:T(8,128)(2,1)S(1)}, bf16[128,512]{1,0:T(8,128)(2,1)S(1)}, u32[]{:S(2)}, u32[]{:S(2)}) collective-permute-start(bf16[128,512]{1,0:T(8,128)(2,1)S(1)} %collective-permute-done.31), channel_id=1, source_target_pairs={{0,1},{1,0},{2,3},{3,2},{4,5},{5,4},{6,7},{7,6},{8,9},{9,8},{10,11... | collective-permute-start | bytes 393224 | tf_op jit(solution)/shard_map/ppermute | solution.py:105
  75.7 1.3 %collective-permute-start.40 = (bf16[128,512]{1,0:T(8,128)(2,1)S(1)}, bf16[128,512]{1,0:T(8,128)(2,1)S(1)}, u32[]{:S(2)}, u32[]{:S(2)}) collective-permute-start(bf16[128,512]{1,0:T(8,128)(2,1)S(1)} %collective-permute-done.39), channel_id=1, source_target_pairs={{0,1},{1,0},{2,3},{3,2},{4,5},{5,4},{6,7},{7,6},{8,9},{9,8},{10,11... | collective-permute-start | bytes 393224 | tf_op jit(solution)/shard_map/ppermute | solution.py:105
  82.1 11.6 %all-to-all-start = ((bf16[16,32,128]{2,1,0:T(8,128)(2,1)}), bf16[16,32,128]{2,1,0:T(8,128)(2,1)S(1)}, u32[]{:S(2)}, u32[]{:S(2)}) async-start(bf16[16,32,128]{2,1,0:T(8,128)(2,1)} %backward.1), calls=%async_computation | async-start | bytes 262144 | tf_op jit(solution)/shard_map/all_to_all | solution.py:394
  (9 other events, 74.5 us)

commit v4 on v3

--- a/solution.py
+++ b/solution.py
@@ -60,7 +60,7 @@
             whole = put(whole, up, self.chips - step)
             if step <= self.down_steps:
                 whole = put(whole, down, step)
-        return whole
+        return whole, block
 
     def scatter_sum(self, keep, other):
         swapped = lax.ppermute(other, "fsdp", self.sibling)
@@ -79,7 +79,7 @@
             if step < self.down_steps:
                 down = down + term(self.up_steps + 1 + step)
         total = term(0) + up
-        return total + down if self.down_steps else total
+        return (total + down if self.down_steps else total), keep
 
 
 class Grid(Ring):
@@ -104,7 +104,7 @@
                 whole = place(whole, part, self.owner(device, 2 * z + y, 0))
                 part = lax.ppermute(part, "fsdp", self.sibling)
                 whole = place(whole, part, self.owner(device, 2 * z + y, 1))
-        return whole
+        return whole, column[1]
 
     def scatter_sum(self, keep, other):
         over_y = {}
@@ -129,7 +129,7 @@
                 arrived.append(lax.ppermute(sent, "fsdp", self.across(4 * z)))
         for part in arrived:
             total = total + part.astype(F32)
-        return total
+        return total, sent
 
 
 def kept_rows(kept_index, device, parent_rows):
@@ -257,19 +257,31 @@
     sent[...] = message[...].astype(BF16)
 
 
+def prepare_kernel(hidden, scale, child_gain, slope, child_in, loss):
+    tokens, features = hidden.shape
+    inverse = scale[...][:, :1]
+    cut = min(features, 512)
+    squares = jnp.zeros((tokens, cut), F32)
+    for k in range(features // cut):
+        cols = slice(k * cut, (k + 1) * cut)
+        difference = slope[:, cols].astype(F32)
+        squares = squares + difference * difference
+        child = hidden[:, cols].astype(F32) * inverse * child_gain[:, cols]
+        child_in[:, cols] = child.astype(BF16)
+    squares = jnp.sum(jnp.sum(squares, axis=0, keepdims=True), axis=1, keepdims=True)
+    loss[...] = 0.5 * squares / (tokens * features)
+
+
 def rows_kernel(
     per_pair,
     received,
     places,
-    hidden,
-    scale,
-    child_gain,
+    child_in,
     slope,
     grad_gate,
     grad_up,
     grad_down,
     gain,
-    loss,
     made,
     done,
 ):
@@ -278,25 +290,18 @@
     message = received[...].reshape(devices * stride, tokens)
     tiles = [dot(places[kind], message).astype(BF16) for kind in range(3)]
     both = jnp.concatenate(tiles[:2], axis=0)
-    inverse = scale[...][:, :1]
     cut = min(features, 1024)
     copies = []
-    squares = jnp.zeros((slope.shape[0], cut), F32)
     for k in range(features // cut):
         cols = slice(k * cut, (k + 1) * cut)
-        difference = slope[:, cols]
-        squares = squares + difference.astype(F32) * difference.astype(F32)
-        made[2, :, cols] = dot(tiles[2], difference).astype(BF16)
-        child = (hidden[:, cols].astype(F32) * inverse * child_gain[:, cols]).astype(BF16)
-        out = dot(both, child).astype(BF16)
+        made[2, :, cols] = dot(tiles[2], slope[:, cols]).astype(BF16)
+        out = dot(both, child_in[:, cols]).astype(BF16)
         made[0, :, cols] = out[:rows]
         made[1, :, cols] = out[rows:]
         for kind, grad in enumerate((grad_gate, grad_up, grad_down)):
             copy = pltpu.make_async_copy(made.at[kind, :, cols], grad.at[:, cols], done.at[kind, k])
             copy.start()
             copies.append(copy)
-    squares = jnp.sum(jnp.sum(squares, axis=0, keepdims=True), axis=1, keepdims=True)
-    loss[...] = 0.5 * squares / (slope.shape[0] * features)
     total = jnp.sum(message.astype(F32).reshape(devices, stride, tokens), axis=0)
     gain_rows = gain.shape[1] // 128
     for r in range(gain_rows):
@@ -336,11 +341,10 @@
     features = width * devices
     per_pair = kept_index.shape[0] // tile_owner.shape[0] // devices
     stride = -(-(3 * per_pair + 2 * (width // 128)) // 8) * 8
-    kept = kept_rows(kept_index, device, parent_rows)
-
     square = ((tokens, parent_rows), F32)
     gains = [parent_gain.reshape(1, features), child_gain.reshape(1, features)]
-    hidden_all = ring.gather(hidden, device)
+    hidden_all, early = ring.gather(hidden, device)
+    kept = kept_rows(after(kept_index, early), device, parent_rows)
     scale, child_gate, child_up, child_hid, keep, other = call(
         functools.partial(forward_kernel, ring),
         [
@@ -359,15 +363,14 @@
             down_weight,
             kept,
         ],
-        limit=12,
+        limit=6,
         name="forward",
     )
-    difference = ring.scatter_sum(keep, other)
-    slope_all = ring.gather(difference.astype(BF16), device)
-
-    send, find = routing(
-        after(kept_index, child_hid), tile_owner, device, devices, parent_rows, stride
-    )
+    difference, last_sent = ring.scatter_sum(keep, other)
+    slope_all, _ = ring.gather(difference.astype(BF16), device)
+
+    kept_index, tile_owner, _ = lax.optimization_barrier((kept_index, tile_owner, last_sent))
+    send, find = routing(kept_index, tile_owner, device, devices, parent_rows, stride)
     select = jnp.stack([jnp.roll(send, kind * per_pair, axis=0) for kind in range(3)])
     places = jnp.stack([jnp.roll(find, kind * per_pair, axis=1) for kind in range(3)])
     message = (devices, stride, tokens)
@@ -387,24 +390,31 @@
             child_hid,
             select,
         ],
-        limit=8,
+        limit=6,
         name="backward",
         scratch=[pltpu.VMEM(message, F32)],
     )
     received = lax.all_to_all(sent, "fsdp", 0, 0, tiled=True)
     anywhere = pl.BlockSpec(memory_space=pl.ANY)
     grad = ((parent_rows, features), BF16)
-    *grads, gain_grad, loss_value = call(
+    child_in, loss_value = call(
+        prepare_kernel,
+        [((tokens, features), BF16), ((1, 1), F32)],
+        [after(hidden_all, sent), scale, gains[1], slope_all],
+        limit=6,
+        name="prepare",
+    )
+    *grads, gain_grad = call(
         functools.partial(rows_kernel, per_pair),
-        [grad, grad, grad, ((1, width), F32), ((1, 1), F32)],
-        [received, places, hidden_all, scale, gains[1], slope_all],
-        limit=16,
+        [grad, grad, grad, ((1, width), F32)],
+        [received, places, child_in, slope_all],
+        limit=8,
         name="rows",
         scratch=[
             pltpu.VMEM((3, parent_rows, features), BF16),
             pltpu.SemaphoreType.DMA((3, features // min(features, 1024))),
         ],
-        specs=[anywhere] * 3 + [VMEM] * 2,
+        specs=[anywhere] * 3 + [VMEM],
     )
     return (*grads, gain_grad.reshape(width), loss_value.reshape(1))
 

time: 99.8 us -> 97.3 us (0.975)
  waiting for transfers between devices: 37.6 us -> 33.4 us
  Pallas kernels: 11.8 us -> 13.7 us
  other arithmetic: 3.61 us -> 2.44 us
  local copies, waits for them, and re-layouts: 4.77 us -> 5.84 us
    all_to_all x1, waiting for transfers between devices: 7.44 us -> 2.57 us  [shards(): received = lax.all_to_all(sent, 'fsdp', 0, 0, tiled=True)]
    ppermute x3, starting transfers between devices: 8.55 us -> 6.23 us  [scatter_sum(): arrived.append(lax.ppermute(sent, 'fsdp', self.across(4 * z)))]
    pallas_call x3 -> x4, Pallas kernels: 11.8 us -> 13.7 us  [call(): pl.pallas_call(kernel, out_shape=[jax.ShapeDtypeStruct(shape, dtype) for...]
    ppermute x2, starting transfers between devices: 2.4 us -> 3.49 us  [gather(): column[3] = lax.ppermute(after(block, column[1]), 'fsdp', self.across(12))]
    unnamed x22 -> x24, local copies, waits for them, and re-layouts: 3.47 us -> 4.54 us
    ppermute x2, waiting for transfers between devices: 4.99 us -> 3.95 us  [gather(): column[3] = lax.ppermute(after(block, column[1]), 'fsdp', self.across(12))]
  transfers between devices with their start and end apart: 42 -> 42, of which waited for: 14 -> 16; matrix products, arithmetic and copies ran while one was open for 5% -> 4% of each run, Pallas kernels for 0% -> 2%
where the time goes in v4:
time: 97.3 us; the launch traced here: 97 us
  starting transfers between devices  38.9 us (40%)
  waiting for transfers between devices  33.4 us (34%)
  Pallas kernels  13.7 us (14%)
  local copies, waits for them, and re-layouts  5.84 us (6%)
  other arithmetic  2.44 us (3%)
  between operations  1.5 us (2%)
  matrix products  1.1 us (1%)
    pallas_call x4, Pallas kernels, call(): pl.pallas_call(kernel, out_shape=[jax.ShapeDtypeStruct(shape, dtype) for...  13.7 us
    ppermute x8, waiting for transfers between devices, gather(): part = lax.ppermute(column[z], 'fsdp', self.across(2)) if y else column[z]  9.4 us
    ppermute x8, starting transfers between devices, gather(): part = lax.ppermute(column[z], 'fsdp', self.across(2)) if y else column[z]  9.2 us
    ppermute x4, starting transfers between devices, gather(): column[z] = lax.ppermute(block, 'fsdp', self.across(4 * z))  8.76 us
    ppermute x4, waiting for transfers between devices, gather(): column[z] = lax.ppermute(block, 'fsdp', self.across(4 * z))  6.5 us
    ppermute x3, starting transfers between devices, scatter_sum(): arrived.append(lax.ppermute(sent, 'fsdp', self.across(4 * z)))  6.23 us
    ppermute x3, waiting for transfers between devices, scatter_sum(): arrived.append(lax.ppermute(sent, 'fsdp', self.across(4 * z)))  5.46 us
    unnamed x24, local copies, waits for them, and re-layouts  4.54 us
  transfers between devices with their start and end apart: 42, of which 16 were waited for; matrix products, arithmetic and copies ran while one was open for 4% of the time, Pallas kernels for 2%

profile of v4, /device:TPU:0, one launch (start us, length us, event | category | flops | bytes accessed | tf_op | source)
XLA Modules:
  0.0 97.0 jit_solution(10881515377123523616)
XLA Ops:
  0.6 3.1 %collective-permute-start.3 = (bf16[128,512]{1,0:T(8,128)(2,1)}, bf16[128,512]{1,0:T(8,128)(2,1)S(1)}, u32[]{:S(2)}, u32[]{:S(2)}) collective-permute-start(bf16[128,512]{1,0:T(8,128)(2,1)} %param.8), channel_id=1, source_target_pairs={{0,4},{1,5},{2,6},{3,7},{4,0},{5,1},{6,2},{7,3},{8,12},{9,13},{10,... | collective-permute-start | bytes 393224 | tf_op jit(solution)/shard_map/ppermute | solution.py:99
  3.7 1.5 %collective-permute-start.1 = (bf16[128,512]{1,0:T(8,128)(2,1)}, bf16[128,512]{1,0:T(8,128)(2,1)S(1)}, u32[]{:S(2)}, u32[]{:S(2)}) collective-permute-start(bf16[128,512]{1,0:T(8,128)(2,1)} %param.8), channel_id=1, source_target_pairs={{0,2},{1,3},{2,0},{3,1},{4,6},{5,7},{6,4},{7,5},{8,10},{9,11},{10,... | collective-permute-start | bytes 393224 | tf_op jit(solution)/shard_map/ppermute | solution.py:103
  5.3 2.6 %collective-permute-start.7 = (bf16[128,512]{1,0:T(8,128)(2,1)}, bf16[128,512]{1,0:T(8,128)(2,1)S(1)}, u32[]{:S(2)}, u32[]{:S(2)}) collective-permute-start(bf16[128,512]{1,0:T(8,128)(2,1)} %param.8), channel_id=1, source_target_pairs={{0,8},{1,9},{2,10},{3,11},{4,12},{5,13},{6,14},{7,15},{8,0},{9,1},... | collective-permute-start | bytes 393224 | tf_op jit(solution)/shard_map/ppermute | solution.py:99
  8.1 0.9 broadcast_subtract_fusion.1
  9.3 3.0 %collective-permute-start.11 = (bf16[128,512]{1,0:T(8,128)(2,1)S(1)}, bf16[128,512]{1,0:T(8,128)(2,1)S(1)}, u32[]{:S(2)}, u32[]{:S(2)}) collective-permute-start(bf16[128,512]{1,0:T(8,128)(2,1)S(1)} %copy-done.9), channel_id=1, source_target_pairs={{0,12},{1,13},{2,14},{3,15},{4,8},{5,9},{6,10},{7,11},{8,4},{9,5},... | collective-permute-start | bytes 393224 | tf_op jit(solution)/shard_map/ppermute | solution.py:100
  12.3 2.6 %collective-permute-start.5 = (bf16[128,512]{1,0:T(8,128)(2,1)S(1)}, bf16[128,512]{1,0:T(8,128)(2,1)S(1)}, u32[]{:S(2)}, u32[]{:S(2)}) collective-permute-start(bf16[128,512]{1,0:T(8,128)(2,1)S(1)} %collective-permute-done.3), channel_id=1, source_target_pairs={{0,2},{1,3},{2,0},{3,1},{4,6},{5,7},{6,4},{7,5},{8,10},{9,11},{10,... | collective-permute-start | bytes 393224 | tf_op jit(solution)/shard_map/ppermute | solution.py:103
  14.9 0.5 collective-permute-start.2
  15.4 2.7 %collective-permute-done.7 = bf16[128,512]{1,0:T(8,128)(2,1)S(1)} collective-permute-done((bf16[128,512]{1,0:T(8,128)(2,1)}, bf16[128,512]{1,0:T(8,128)(2,1)S(1)}, u32[]{:S(2)}, u32[]{:S(2)}) %collective-permute-start.7) | collective-permute-done | bytes 131104 | tf_op jit(solution)/shard_map/ppermute | solution.py:99
  18.1 0.5 collective-permute-start.9
  18.8 1.6 %collective-permute-start.13 = (bf16[128,512]{1,0:T(8,128)(2,1)S(1)}, bf16[128,512]{1,0:T(8,128)(2,1)S(1)}, u32[]{:S(2)}, u32[]{:S(2)}) collective-permute-start(bf16[128,512]{1,0:T(8,128)(2,1)S(1)} %collective-permute-done.11), channel_id=1, source_target_pairs={{0,2},{1,3},{2,0},{3,1},{4,6},{5,7},{6,4},{7,5},{8,10},{9,11},{10,... | collective-permute-start | bytes 393224 | tf_op jit(solution)/shard_map/ppermute | solution.py:103
  21.0 3.4 %collective-permute-done.9 = bf16[128,512]{1,0:T(8,128)(2,1)S(1)} collective-permute-done((bf16[128,512]{1,0:T(8,128)(2,1)S(1)}, bf16[128,512]{1,0:T(8,128)(2,1)S(1)}, u32[]{:S(2)}, u32[]{:S(2)}) %collective-permute-start.9) | collective-permute-done | bytes 131104 | tf_op jit(solution)/shard_map/ppermute | solution.py:103
  24.4 1.5 %collective-permute-done.13 = bf16[128,512]{1,0:T(8,128)(2,1)S(1)} collective-permute-done((bf16[128,512]{1,0:T(8,128)(2,1)S(1)}, bf16[128,512]{1,0:T(8,128)(2,1)S(1)}, u32[]{:S(2)}, u32[]{:S(2)}) %collective-permute-start.13) | collective-permute-done | bytes 131104 | tf_op jit(solution)/shard_map/ppermute | solution.py:103
  26.1 1.1 %collective-permute-done.14 = bf16[128,512]{1,0:T(8,128)(2,1)S(1)} collective-permute-done((bf16[128,512]{1,0:T(8,128)(2,1)S(1)}, bf16[128,512]{1,0:T(8,128)(2,1)S(1)}, u32[]{:S(2)}, u32[]{:S(2)}) %collective-permute-start.14) | collective-permute-done | bytes 131104 | tf_op jit(solution)/shard_map/ppermute | solution.py:105
  27.4 4.1 %forward.1 = (f32[128,128]{1,0:T(8,128)S(1)}, f32[128,128]{1,0:T(8,128)S(1)}, f32[128,128]{1,0:T(8,128)S(1)}, bf16[128,128]{1,0:T(8,128)(2,1)S(1)}, f32[8,128,51...) custom-call(bf16[128,8192]{1,0:T(8,128)(2,1)S(1)} %constant_dynamic-update-slice_fusion.16.hidden, f32[1,8192]{1,0:T(1,128)S(1)} %bitcast.71, ...), custom_call_target="tpu_custom_call" | custom-call | tf_op jit(solution)/shard_map/forward/pallas_call | solution.py:321
  32.7 0.9 collective-permute-done.18
  33.7 0.6 collective-permute-start.22
  34.4 1.5 %collective-permute-start.21 = (bf16[128,512]{1,0:T(8,128)(2,1)S(1)}, bf16[128,512]{1,0:T(8,128)(2,1)S(1)}, u32[]{:S(2)}, u32[]{:S(2)}) collective-permute-start(bf16[128,512]{1,0:T(8,128)(2,1)S(1)} %fusion.22), channel_id=1, source_target_pairs={{0,2},{1,3},{2,0},{3,1},{4,6},{5,7},{6,4},{7,5},{8,10},{9,11},{10,... | collective-permute-start | bytes 393224 | tf_op jit(solution)/shard_map/ppermute | solution.py:121
  36.1 0.6 collective-permute-start.20
  36.8 1.5 %collective-permute-start.19 = (bf16[128,512]{1,0:T(8,128)(2,1)S(1)}, bf16[128,512]{1,0:T(8,128)(2,1)S(1)}, u32[]{:S(2)}, u32[]{:S(2)}) collective-permute-start(bf16[128,512]{1,0:T(8,128)(2,1)S(1)} %fusion.24), channel_id=1, source_target_pairs={{0,2},{1,3},{2,0},{3,1},{4,6},{5,7},{6,4},{7,5},{8,10},{9,11},{10,... | collective-permute-start | bytes 393224 | tf_op jit(solution)/shard_map/ppermute | solution.py:121
  38.4 1.7 %collective-permute-done.22 = bf16[128,512]{1,0:T(8,128)(2,1)S(1)} collective-permute-done((bf16[128,512]{1,0:T(8,128)(2,1)S(1)}, bf16[128,512]{1,0:T(8,128)(2,1)S(1)}, u32[]{:S(2)}, u32[]{:S(2)}) %collective-permute-start.22) | collective-permute-done | bytes 131104 | tf_op jit(solution)/shard_map/ppermute | solution.py:121
  40.1 2.6 %collective-permute-start.23 = (bf16[128,512]{1,0:T(8,128)(2,1)S(1)}, bf16[128,512]{1,0:T(8,128)(2,1)S(1)}, u32[]{:S(2)}, u32[]{:S(2)}) collective-permute-start(bf16[128,512]{1,0:T(8,128)(2,1)S(1)} %fusion.9), channel_id=1, source_target_pairs={{0,12},{1,13},{2,14},{3,15},{4,8},{5,9},{6,10},{7,11},{8,4},{9,5},... | collective-permute-start | bytes 393224 | tf_op jit(solution)/shard_map/ppermute | solution.py:129
  42.9 2.3 %collective-permute-start.24 = (bf16[128,512]{1,0:T(8,128)(2,1)S(1)}, bf16[128,512]{1,0:T(8,128)(2,1)S(1)}, u32[]{:S(2)}, u32[]{:S(2)}) collective-permute-start(bf16[128,512]{1,0:T(8,128)(2,1)S(1)} %fusion.11), channel_id=1, source_target_pairs={{0,8},{1,9},{2,10},{3,11},{4,12},{5,13},{6,14},{7,15},{8,0},{9,1},... | collective-permute-start | bytes 393224 | tf_op jit(solution)/shard_map/ppermute | solution.py:129
  45.3 0.4 collective-permute-done.20
  45.9 1.0 %fusion.2 = bf16[512,128]{1,0:T(8,128)(2,1)S(1)} fusion(s32[2048]{0:T(1024)S(1)} %fusion.5, s32[2048]{0:T(1024)S(1)} %broadcast_subtract_fusion), kind=kOutput, calls=%fused_computation.3 | convolution fusion | flops 269811712 | bytes 147456 | tf_op jit(solution)/shard_map/dot_general | solution.py:16
  47.0 1.3 %collective-permute-start.25 = (bf16[128,512]{1,0:T(8,128)(2,1)S(1)}, bf16[128,512]{1,0:T(8,128)(2,1)S(1)}, u32[]{:S(2)}, u32[]{:S(2)}) collective-permute-start(bf16[128,512]{1,0:T(8,128)(2,1)S(1)} %fusion.13), channel_id=1, source_target_pairs={{0,4},{1,5},{2,6},{3,7},{4,0},{5,1},{6,2},{7,3},{8,12},{9,13},{10,... | collective-permute-start | bytes 393224 | tf_op jit(solution)/shard_map/ppermute | solution.py:129
  48.7 4.7 %collective-permute-done.24 = bf16[128,512]{1,0:T(8,128)(2,1)S(1)} collective-permute-done((bf16[128,512]{1,0:T(8,128)(2,1)S(1)}, bf16[128,512]{1,0:T(8,128)(2,1)S(1)}, u32[]{:S(2)}, u32[]{:S(2)}) %collective-permute-start.24) | collective-permute-done | bytes 131104 | tf_op jit(solution)/shard_map/ppermute | solution.py:129
  53.3 0.8 collective-permute-done.25
  54.4 0.6 collective-permute-start.33
  55.0 2.5 %collective-permute-start.29 = (bf16[128,512]{1,0:T(8,128)(2,1)S(1)}, bf16[128,512]{1,0:T(8,128)(2,1)S(1)}, u32[]{:S(2)}, u32[]{:S(2)}) collective-permute-start(bf16[128,512]{1,0:T(8,128)(2,1)S(1)} %get-tuple-element.39), channel_id=1, source_target_pairs={{0,4},{1,5},{2,6},{3,7},{4,0},{5,1},{6,2},{7,3},{8,12},{9,13},{10,... | collective-permute-start | bytes 393224 | tf_op jit(solution)/shard_map/ppermute | solution.py:99
  57.5 0.5 collective-permute-start.27
  58.0 3.8 %collective-permute-done.29 = bf16[128,512]{1,0:T(8,128)(2,1)S(1)} collective-permute-done((bf16[128,512]{1,0:T(8,128)(2,1)S(1)}, bf16[128,512]{1,0:T(8,128)(2,1)S(1)}, u32[]{:S(2)}, u32[]{:S(2)}) %collective-permute-start.29) | collective-permute-done | bytes 131104 | tf_op jit(solution)/shard_map/ppermute | solution.py:99
  61.9 0.5 collective-permute-start.37
  62.4 0.6 collective-permute-start.35
  63.0 1.4 %collective-permute-start.31 = (bf16[128,512]{1,0:T(8,128)(2,1)S(1)}, bf16[128,512]{1,0:T(8,128)(2,1)S(1)}, u32[]{:S(2)}, u32[]{:S(2)}) collective-permute-start(bf16[128,512]{1,0:T(8,128)(2,1)S(1)} %collective-permute-done.29), channel_id=1, source_target_pairs={{0,2},{1,3},{2,0},{3,1},{4,6},{5,7},{6,4},{7,5},{8,10},{9,11},{10,... | collective-permute-start | bytes 393224 | tf_op jit(solution)/shard_map/ppermute | solution.py:103
  64.7 3.9 %collective-permute-done.37 = bf16[128,512]{1,0:T(8,128)(2,1)S(1)} collective-permute-done((bf16[128,512]{1,0:T(8,128)(2,1)S(1)}, bf16[128,512]{1,0:T(8,128)(2,1)S(1)}, u32[]{:S(2)}, u32[]{:S(2)}) %collective-permute-start.37) | collective-permute-done | bytes 131104 | tf_op jit(solution)/shard_map/ppermute | solution.py:100
  68.6 0.5 collective-permute-start.39
  69.5 0.7 collective-permute-done.31
  70.2 0.5 collective-permute-start.32
  70.7 3.8 %collective-permute-done.39 = bf16[128,512]{1,0:T(8,128)(2,1)S(1)} collective-permute-done((bf16[128,512]{1,0:T(8,128)(2,1)S(1)}, bf16[128,512]{1,0:T(8,128)(2,1)S(1)}, u32[]{:S(2)}, u32[]{:S(2)}) %collective-permute-start.39) | collective-permute-done | bytes 131104 | tf_op jit(solution)/shard_map/ppermute | solution.py:103
  74.8 1.1 %collective-permute-done.40 = bf16[128,512]{1,0:T(8,128)(2,1)S(1)} collective-permute-done((bf16[128,512]{1,0:T(8,128)(2,1)S(1)}, bf16[128,512]{1,0:T(8,128)(2,1)S(1)}, u32[]{:S(2)}, u32[]{:S(2)}) %collective-permute-start.40) | collective-permute-done | bytes 131104 | tf_op jit(solution)/shard_map/ppermute | solution.py:105
  75.9 3.7 %backward.1 = bf16[16,32,128]{2,1,0:T(8,128)(2,1)} custom-call(bf16[128,8192]{1,0:T(8,128)(2,1)S(1)} %constant_dynamic-update-slice_fusion.slope, bf16[128,8192]{1,0:T(8,128)(2,1)S(1)} %constant_dynamic-update-slice_fusion.16.hidden, bf16[128,8192]{1,0:T(8,128)(2,1)S(1)} %copy-done.2, bf16[128,8192]{1,0:T(8,128)(2,1)S(1)} %copy-done.3, ...), custom_call_target="tpu_custom_call" | custom-call | tf_op jit(solution)/shard_map/backward/pallas_call | solution.py:321
  79.7 3.7 %all-to-all-start = ((bf16[16,32,128]{2,1,0:T(8,128)(2,1)}), bf16[16,32,128]{2,1,0:T(8,128)(2,1)S(1)}, u32[]{:S(2)}, u32[]{:S(2)}) async-start(bf16[16,32,128]{2,1,0:T(8,128)(2,1)} %backward.1), calls=%async_computation | async-start | bytes 262144 | tf_op jit(solution)/shard_map/all_to_all | solution.py:397
  83.8 1.6 %copy-done.1 = bf16[128,8192]{1,0:T(8,128)(2,1)S(1)} copy-done((bf16[128,8192]{1,0:T(8,128)(2,1)S(1)}, bf16[128,8192]{1,0:T(8,128)(2,1)}, u32[]{:S(2)}) %copy-start.1) | copy-done | bytes 2097176
  85.4 2.0 %prepare.1 = (bf16[128,8192]{1,0:T(8,128)(2,1)S(1)}, f32[1,1]{1,0:T(1,128)}) custom-call(bf16[128,8192]{1,0:T(8,128)(2,1)S(1)} %copy-done.1, f32[128,128]{1,0:T(8,128)S(1)} %get-tuple-element.40.scale, f32[1,8192]{1,0:T(1,128)S(1)} %bitcast.70, bf16[128,8192]{1,0:T(8,128)(2,1)S(1)} %constant_dynamic-update-slice_fusion.slope), custom_call_target="tpu_custom_call" | custom-call | tf_op jit(solution)/shard_map/prepare/pallas_call | solution.py:321
  87.4 1.3 %copy-done.5 = bf16[128,8192]{1,0:T(8,128)(2,1)} copy-done((bf16[128,8192]{1,0:T(8,128)(2,1)}, bf16[128,8192]{1,0:T(8,128)(2,1)S(1)}, u32[]{:S(2)}) %copy-start.5) | copy-done | bytes 2097176
  88.7 2.6 %all-to-all-done.received = bf16[16,32,128]{2,1,0:T(8,128)(2,1)S(1)} async-done(((bf16[16,32,128]{2,1,0:T(8,128)(2,1)}), bf16[16,32,128]{2,1,0:T(8,128)(2,1)S(1)}, u32[]{:S(2)}, u32[]{:S(2)}) %all-to-all-start) | async-done | bytes 131104 | tf_op jit(solution)/shard_map/all_to_all | solution.py:397
  91.3 1.6 %copy-done.6 = bf16[128,8192]{1,0:T(8,128)(2,1)S(1)} copy-done((bf16[128,8192]{1,0:T(8,128)(2,1)S(1)}, bf16[128,8192]{1,0:T(8,128)(2,1)}, u32[]{:S(2)}) %copy-start.6) | copy-done | bytes 2097176
  92.9 4.0 %rows.1 = (bf16[128,8192]{1,0:T(8,128)(2,1)}, bf16[128,8192]{1,0:T(8,128)(2,1)}, bf16[128,8192]{1,0:T(8,128)(2,1)}, f32[1,512]{1,0:T(1,128)}) custom-call(bf16[16,32,128]{2,1,0:T(8,128)(2,1)S(1)} %all-to-all-done.received, bf16[3,128,512]{2,1,0:T(8,128)(2,1)S(1)} %pad_maximum_fusion.1.places, bf16[128,8192]{1,0:T(8,128)(2,1)S(1)} %copy-done.6, ...), custom_call_target="tpu_custom_call" | custom-call | tf_op jit(solution)/shard_map/rows/pallas_call | solution.py:321
  (134 shorter events, 5.6 us)
Async XLA Ops:
  0.6 7.5 %collective-permute-start.3 = (bf16[128,512]{1,0:T(8,128)(2,1)}, bf16[128,512]{1,0:T(8,128)(2,1)S(1)}, u32[]{:S(2)}, u32[]{:S(2)}) collective-permute-start(bf16[128,512]{1,0:T(8,128)(2,1)} %param.8), channel_id=1, source_target_pairs={{0,4},{1,5},{2,6},{3,7},{4,0},{5,1},{6,2},{7,3},{8,12},{9,13},{10,... | collective-permute-start | bytes 393224 | tf_op jit(solution)/shard_map/ppermute | solution.py:99
  3.7 11.2 %collective-permute-start.1 = (bf16[128,512]{1,0:T(8,128)(2,1)}, bf16[128,512]{1,0:T(8,128)(2,1)S(1)}, u32[]{:S(2)}, u32[]{:S(2)}) collective-permute-start(bf16[128,512]{1,0:T(8,128)(2,1)} %param.8), channel_id=1, source_target_pairs={{0,2},{1,3},{2,0},{3,1},{4,6},{5,7},{6,4},{7,5},{8,10},{9,11},{10,... | collective-permute-start | bytes 393224 | tf_op jit(solution)/shard_map/ppermute | solution.py:103
  5.2 9.7 %collective-permute-start = (bf16[128,512]{1,0:T(8,128)(2,1)}, bf16[128,512]{1,0:T(8,128)(2,1)S(1)}, u32[]{:S(2)}, u32[]{:S(2)}) collective-permute-start(bf16[128,512]{1,0:T(8,128)(2,1)} %param.8), channel_id=1, source_target_pairs={{0,1},{1,0},{2,3},{3,2},{4,5},{5,4},{6,7},{7,6},{8,9},{9,8},{10,11... | collective-permute-start | bytes 393224 | tf_op jit(solution)/shard_map/ppermute | solution.py:105
  5.3 12.9 %collective-permute-start.7 = (bf16[128,512]{1,0:T(8,128)(2,1)}, bf16[128,512]{1,0:T(8,128)(2,1)S(1)}, u32[]{:S(2)}, u32[]{:S(2)}) collective-permute-start(bf16[128,512]{1,0:T(8,128)(2,1)} %param.8), channel_id=1, source_target_pairs={{0,8},{1,9},{2,10},{3,11},{4,12},{5,13},{6,14},{7,15},{8,0},{9,1},... | collective-permute-start | bytes 393224 | tf_op jit(solution)/shard_map/ppermute | solution.py:99
  7.8 19.5 %copy-start.8 = (f32[8192]{0:T(1024)S(1)}, f32[8192]{0:T(1024)}, u32[]{:S(2)}) copy-start(f32[8192]{0:T(1024)} %param.9) | copy-start | bytes 98308
  7.8 19.5 %copy-start.4 = (bf16[128,8192]{1,0:T(8,128)(2,1)S(1)}, bf16[128,8192]{1,0:T(8,128)(2,1)}, u32[]{:S(2)}) copy-start(bf16[128,8192]{1,0:T(8,128)(2,1)} %down.3) | copy-start | bytes 6291460
  8.1 19.3 %copy-start.2 = (bf16[128,8192]{1,0:T(8,128)(2,1)S(1)}, bf16[128,8192]{1,0:T(8,128)(2,1)}, u32[]{:S(2)}) copy-start(bf16[128,8192]{1,0:T(8,128)(2,1)} %gate.3) | copy-start | bytes 6291460
  8.1 19.3 %copy-start.3 = (bf16[128,8192]{1,0:T(8,128)(2,1)S(1)}, bf16[128,8192]{1,0:T(8,128)(2,1)}, u32[]{:S(2)}) copy-start(bf16[128,8192]{1,0:T(8,128)(2,1)} %up.3) | copy-start | bytes 6291460
  8.1 19.3 %copy-start.7 = (f32[8192]{0:T(1024)S(1)}, f32[8192]{0:T(1024)}, u32[]{:S(2)}) copy-start(f32[8192]{0:T(1024)} %param.10) | copy-start | bytes 98308
  9.3 9.3 %collective-permute-start.11 = (bf16[128,512]{1,0:T(8,128)(2,1)S(1)}, bf16[128,512]{1,0:T(8,128)(2,1)S(1)}, u32[]{:S(2)}, u32[]{:S(2)}) collective-permute-start(bf16[128,512]{1,0:T(8,128)(2,1)S(1)} %copy-done.9), channel_id=1, source_target_pairs={{0,12},{1,13},{2,14},{3,15},{4,8},{5,9},{6,10},{7,11},{8,4},{9,5},... | collective-permute-start | bytes 393224 | tf_op jit(solution)/shard_map/ppermute | solution.py:100
  12.3 8.1 %collective-permute-start.5 = (bf16[128,512]{1,0:T(8,128)(2,1)S(1)}, bf16[128,512]{1,0:T(8,128)(2,1)S(1)}, u32[]{:S(2)}, u32[]{:S(2)}) collective-permute-start(bf16[128,512]{1,0:T(8,128)(2,1)S(1)} %collective-permute-done.3), channel_id=1, source_target_pairs={{0,2},{1,3},{2,0},{3,1},{4,6},{5,7},{6,4},{7,5},{8,10},{9,11},{10,... | collective-permute-start | bytes 393224 | tf_op jit(solution)/shard_map/ppermute | solution.py:103
  14.9 5.7 %collective-permute-start.4 = (bf16[128,512]{1,0:T(8,128)(2,1)S(1)}, bf16[128,512]{1,0:T(8,128)(2,1)S(1)}, u32[]{:S(2)}, u32[]{:S(2)}) collective-permute-start(bf16[128,512]{1,0:T(8,128)(2,1)S(1)} %collective-permute-done.3), channel_id=1, source_target_pairs={{0,1},{1,0},{2,3},{3,2},{4,5},{5,4},{6,7},{7,6},{8,9},{9,8},{10,11... | collective-permute-start | bytes 393224 | tf_op jit(solution)/shard_map/ppermute | solution.py:105
  14.9 3.8 %collective-permute-start.2 = (bf16[128,512]{1,0:T(8,128)(2,1)S(1)}, bf16[128,512]{1,0:T(8,128)(2,1)S(1)}, u32[]{:S(2)}, u32[]{:S(2)}) collective-permute-start(bf16[128,512]{1,0:T(8,128)(2,1)S(1)} %collective-permute-done.1), channel_id=1, source_target_pairs={{0,1},{1,0},{2,3},{3,2},{4,5},{5,4},{6,7},{7,6},{8,9},{9,8},{10,11... | collective-permute-start | bytes 393224 | tf_op jit(solution)/shard_map/ppermute | solution.py:105
  18.1 6.2 %collective-permute-start.9 = (bf16[128,512]{1,0:T(8,128)(2,1)S(1)}, bf16[128,512]{1,0:T(8,128)(2,1)S(1)}, u32[]{:S(2)}, u32[]{:S(2)}) collective-permute-start(bf16[128,512]{1,0:T(8,128)(2,1)S(1)} %collective-permute-done.7), channel_id=1, source_target_pairs={{0,2},{1,3},{2,0},{3,1},{4,6},{5,7},{6,4},{7,5},{8,10},{9,11},{10,... | collective-permute-start | bytes 393224 | tf_op jit(solution)/shard_map/ppermute | solution.py:103
  18.7 7.3 %collective-permute-start.8 = (bf16[128,512]{1,0:T(8,128)(2,1)S(1)}, bf16[128,512]{1,0:T(8,128)(2,1)S(1)}, u32[]{:S(2)}, u32[]{:S(2)}) collective-permute-start(bf16[128,512]{1,0:T(8,128)(2,1)S(1)} %collective-permute-done.7), channel_id=1, source_target_pairs={{0,1},{1,0},{2,3},{3,2},{4,5},{5,4},{6,7},{7,6},{8,9},{9,8},{10,11... | collective-permute-start | bytes 393224 | tf_op jit(solution)/shard_map/ppermute | solution.py:105
  18.8 7.1 %collective-permute-start.13 = (bf16[128,512]{1,0:T(8,128)(2,1)S(1)}, bf16[128,512]{1,0:T(8,128)(2,1)S(1)}, u32[]{:S(2)}, u32[]{:S(2)}) collective-permute-start(bf16[128,512]{1,0:T(8,128)(2,1)S(1)} %collective-permute-done.11), channel_id=1, source_target_pairs={{0,2},{1,3},{2,0},{3,1},{4,6},{5,7},{6,4},{7,5},{8,10},{9,11},{10,... | collective-permute-start | bytes 393224 | tf_op jit(solution)/shard_map/ppermute | solution.py:103
  20.4 5.7 %collective-permute-start.12 = (bf16[128,512]{1,0:T(8,128)(2,1)S(1)}, bf16[128,512]{1,0:T(8,128)(2,1)S(1)}, u32[]{:S(2)}, u32[]{:S(2)}) collective-permute-start(bf16[128,512]{1,0:T(8,128)(2,1)S(1)} %collective-permute-done.11), channel_id=1, source_target_pairs={{0,1},{1,0},{2,3},{3,2},{4,5},{5,4},{6,7},{7,6},{8,9},{9,8},{10,11... | collective-permute-start | bytes 393224 | tf_op jit(solution)/shard_map/ppermute | solution.py:105
  20.6 5.3 %collective-permute-start.6 = (bf16[128,512]{1,0:T(8,128)(2,1)S(1)}, bf16[128,512]{1,0:T(8,128)(2,1)S(1)}, u32[]{:S(2)}, u32[]{:S(2)}) collective-permute-start(bf16[128,512]{1,0:T(8,128)(2,1)S(1)} %collective-permute-done.5), channel_id=1, source_target_pairs={{0,1},{1,0},{2,3},{3,2},{4,5},{5,4},{6,7},{7,6},{8,9},{9,8},{10,11... | collective-permute-start | bytes 393224 | tf_op jit(solution)/shard_map/ppermute | solution.py:105
  24.4 1.7 %collective-permute-start.10 = (bf16[128,512]{1,0:T(8,128)(2,1)S(1)}, bf16[128,512]{1,0:T(8,128)(2,1)S(1)}, u32[]{:S(2)}, u32[]{:S(2)}) collective-permute-start(bf16[128,512]{1,0:T(8,128)(2,1)S(1)} %collective-permute-done.9), channel_id=1, source_target_pairs={{0,1},{1,0},{2,3},{3,2},{4,5},{5,4},{6,7},{7,6},{8,9},{9,8},{10,11... | collective-permute-start | bytes 393224 | tf_op jit(solution)/shard_map/ppermute | solution.py:105
  25.9 1.3 %collective-permute-start.14 = (bf16[128,512]{1,0:T(8,128)(2,1)S(1)}, bf16[128,512]{1,0:T(8,128)(2,1)S(1)}, u32[]{:S(2)}, u32[]{:S(2)}) collective-permute-start(bf16[128,512]{1,0:T(8,128)(2,1)S(1)} %collective-permute-done.13), channel_id=1, source_target_pairs={{0,1},{1,0},{2,3},{3,2},{4,5},{5,4},{6,7},{7,6},{8,9},{9,8},{10,11... | collective-permute-start | bytes 393224 | tf_op jit(solution)/shard_map/ppermute | solution.py:105
  27.3 48.6 %copy-start = (bf16[128,8192]{1,0:T(8,128)(2,1)}, bf16[128,8192]{1,0:T(8,128)(2,1)S(1)}, u32[]{:S(2)}) copy-start(bf16[128,8192]{1,0:T(8,128)(2,1)S(1)} %constant_dynamic-update-slice_fusion.16.hidden) | copy-start | bytes 6291460
  31.6 2.0 %collective-permute-start.18 = (f32[2,128,512]{2,1,0:T(8,128)S(1)}, f32[2,128,512]{2,1,0:T(8,128)S(1)}, u32[]{:S(2)}, u32[]{:S(2)}) collective-permute-start(f32[2,128,512]{2,1,0:T(8,128)S(1)} %get-tuple-element.56), channel_id=1, source_target_pairs={{0,1},{1,0},{2,3},{3,2},{4,5},{5,4},{6,7},{7,6},{8,9},{9,8},{10,11... | collective-permute-start | bytes 1572872 | tf_op jit(solution)/shard_map/ppermute | solution.py:115
  31.8 2.5 %collective-permute-start.17 = (f32[2,128,512]{2,1,0:T(8,128)S(1)}, f32[2,128,512]{2,1,0:T(8,128)S(1)}, u32[]{:S(2)}, u32[]{:S(2)}) collective-permute-start(f32[2,128,512]{2,1,0:T(8,128)S(1)} %get-tuple-element.57), channel_id=1, source_target_pairs={{0,1},{1,0},{2,3},{3,2},{4,5},{5,4},{6,7},{7,6},{8,9},{9,8},{10,11... | collective-permute-start | bytes 1572872 | tf_op jit(solution)/shard_map/ppermute | solution.py:115
  32.2 4.6 %collective-permute-start.15 = (f32[2,128,512]{2,1,0:T(8,128)S(1)}, f32[2,128,512]{2,1,0:T(8,128)S(1)}, u32[]{:S(2)}, u32[]{:S(2)}) collective-permute-start(f32[2,128,512]{2,1,0:T(8,128)S(1)} %get-tuple-element.55), channel_id=1, source_target_pairs={{0,1},{1,0},{2,3},{3,2},{4,5},{5,4},{6,7},{7,6},{8,9},{9,8},{10,11... | collective-permute-start | bytes 1572872 | tf_op jit(solution)/shard_map/ppermute | solution.py:115
  32.3 3.6 %collective-permute-start.16 = (f32[2,128,512]{2,1,0:T(8,128)S(1)}, f32[2,128,512]{2,1,0:T(8,128)S(1)}, u32[]{:S(2)}, u32[]{:S(2)}) collective-permute-start(f32[2,128,512]{2,1,0:T(8,128)S(1)} %get-tuple-element.58), channel_id=1, source_target_pairs={{0,1},{1,0},{2,3},{3,2},{4,5},{5,4},{6,7},{7,6},{8,9},{9,8},{10,11... | collective-permute-start | bytes 1572872 | tf_op jit(solution)/shard_map/ppermute | solution.py:115
  33.7 6.4 %collective-permute-start.22 = (bf16[128,512]{1,0:T(8,128)(2,1)S(1)}, bf16[128,512]{1,0:T(8,128)(2,1)S(1)}, u32[]{:S(2)}, u32[]{:S(2)}) collective-permute-start(bf16[128,512]{1,0:T(8,128)(2,1)S(1)} %fusion.21), channel_id=1, source_target_pairs={{0,2},{1,3},{2,0},{3,1},{4,6},{5,7},{6,4},{7,5},{8,10},{9,11},{10,... | collective-permute-start | bytes 393224 | tf_op jit(solution)/shard_map/ppermute | solution.py:121
  34.4 8.5 %collective-permute-start.21 = (bf16[128,512]{1,0:T(8,128)(2,1)S(1)}, bf16[128,512]{1,0:T(8,128)(2,1)S(1)}, u32[]{:S(2)}, u32[]{:S(2)}) collective-permute-start(bf16[128,512]{1,0:T(8,128)(2,1)S(1)} %fusion.22), channel_id=1, source_target_pairs={{0,2},{1,3},{2,0},{3,1},{4,6},{5,7},{6,4},{7,5},{8,10},{9,11},{10,... | collective-permute-start | bytes 393224 | tf_op jit(solution)/shard_map/ppermute | solution.py:121
  36.1 9.6 %collective-permute-start.20 = (bf16[128,512]{1,0:T(8,128)(2,1)S(1)}, bf16[128,512]{1,0:T(8,128)(2,1)S(1)}, u32[]{:S(2)}, u32[]{:S(2)}) collective-permute-start(bf16[128,512]{1,0:T(8,128)(2,1)S(1)} %fusion.23), channel_id=1, source_target_pairs={{0,2},{1,3},{2,0},{3,1},{4,6},{5,7},{6,4},{7,5},{8,10},{9,11},{10,... | collective-permute-start | bytes 393224 | tf_op jit(solution)/shard_map/ppermute | solution.py:121
  36.8 11.5 %collective-permute-start.19 = (bf16[128,512]{1,0:T(8,128)(2,1)S(1)}, bf16[128,512]{1,0:T(8,128)(2,1)S(1)}, u32[]{:S(2)}, u32[]{:S(2)}) collective-permute-start(bf16[128,512]{1,0:T(8,128)(2,1)S(1)} %fusion.24), channel_id=1, source_target_pairs={{0,2},{1,3},{2,0},{3,1},{4,6},{5,7},{6,4},{7,5},{8,10},{9,11},{10,... | collective-permute-start | bytes 393224 | tf_op jit(solution)/shard_map/ppermute | solution.py:121
  40.1 8.5 %collective-permute-start.23 = (bf16[128,512]{1,0:T(8,128)(2,1)S(1)}, bf16[128,512]{1,0:T(8,128)(2,1)S(1)}, u32[]{:S(2)}, u32[]{:S(2)}) collective-permute-start(bf16[128,512]{1,0:T(8,128)(2,1)S(1)} %fusion.9), channel_id=1, source_target_pairs={{0,12},{1,13},{2,14},{3,15},{4,8},{5,9},{6,10},{7,11},{8,4},{9,5},... | collective-permute-start | bytes 393224 | tf_op jit(solution)/shard_map/ppermute | solution.py:129
  42.9 10.4 %collective-permute-start.24 = (bf16[128,512]{1,0:T(8,128)(2,1)S(1)}, bf16[128,512]{1,0:T(8,128)(2,1)S(1)}, u32[]{:S(2)}, u32[]{:S(2)}) collective-permute-start(bf16[128,512]{1,0:T(8,128)(2,1)S(1)} %fusion.11), channel_id=1, source_target_pairs={{0,8},{1,9},{2,10},{3,11},{4,12},{5,13},{6,14},{7,15},{8,0},{9,1},... | collective-permute-start | bytes 393224 | tf_op jit(solution)/shard_map/ppermute | solution.py:129
  47.0 7.2 %collective-permute-start.25 = (bf16[128,512]{1,0:T(8,128)(2,1)S(1)}, bf16[128,512]{1,0:T(8,128)(2,1)S(1)}, u32[]{:S(2)}, u32[]{:S(2)}) collective-permute-start(bf16[128,512]{1,0:T(8,128)(2,1)S(1)} %fusion.13), channel_id=1, source_target_pairs={{0,4},{1,5},{2,6},{3,7},{4,0},{5,1},{6,2},{7,3},{8,12},{9,13},{10,... | collective-permute-start | bytes 393224 | tf_op jit(solution)/shard_map/ppermute | solution.py:129
  54.4 7.9 %collective-permute-start.33 = (bf16[128,512]{1,0:T(8,128)(2,1)S(1)}, bf16[128,512]{1,0:T(8,128)(2,1)S(1)}, u32[]{:S(2)}, u32[]{:S(2)}) collective-permute-start(bf16[128,512]{1,0:T(8,128)(2,1)S(1)} %get-tuple-element.39), channel_id=1, source_target_pairs={{0,8},{1,9},{2,10},{3,11},{4,12},{5,13},{6,14},{7,15},{8,0},{9,1},... | collective-permute-start | bytes 393224 | tf_op jit(solution)/shard_map/ppermute | solution.py:99
  55.0 6.8 %collective-permute-start.29 = (bf16[128,512]{1,0:T(8,128)(2,1)S(1)}, bf16[128,512]{1,0:T(8,128)(2,1)S(1)}, u32[]{:S(2)}, u32[]{:S(2)}) collective-permute-start(bf16[128,512]{1,0:T(8,128)(2,1)S(1)} %get-tuple-element.39), channel_id=1, source_target_pairs={{0,4},{1,5},{2,6},{3,7},{4,0},{5,1},{6,2},{7,3},{8,12},{9,13},{10,... | collective-permute-start | bytes 393224 | tf_op jit(solution)/shard_map/ppermute | solution.py:99
  57.5 5.5 %collective-permute-start.27 = (bf16[128,512]{1,0:T(8,128)(2,1)S(1)}, bf16[128,512]{1,0:T(8,128)(2,1)S(1)}, u32[]{:S(2)}, u32[]{:S(2)}) collective-permute-start(bf16[128,512]{1,0:T(8,128)(2,1)S(1)} %get-tuple-element.39), channel_id=1, source_target_pairs={{0,2},{1,3},{2,0},{3,1},{4,6},{5,7},{6,4},{7,5},{8,10},{9,11},{10,... | collective-permute-start | bytes 393224 | tf_op jit(solution)/shard_map/ppermute | solution.py:103
  58.0 6.4 %collective-permute-start.26 = (bf16[128,512]{1,0:T(8,128)(2,1)S(1)}, bf16[128,512]{1,0:T(8,128)(2,1)S(1)}, u32[]{:S(2)}, u32[]{:S(2)}) collective-permute-start(bf16[128,512]{1,0:T(8,128)(2,1)S(1)} %get-tuple-element.39), channel_id=1, source_target_pairs={{0,1},{1,0},{2,3},{3,2},{4,5},{5,4},{6,7},{7,6},{8,9},{9,8},{10,11... | collective-permute-start | bytes 393224 | tf_op jit(solution)/shard_map/ppermute | solution.py:105
  61.9 6.8 %collective-permute-start.37 = (bf16[128,512]{1,0:T(8,128)(2,1)S(1)}, bf16[128,512]{1,0:T(8,128)(2,1)S(1)}, u32[]{:S(2)}, u32[]{:S(2)}) collective-permute-start(bf16[128,512]{1,0:T(8,128)(2,1)S(1)} %get-tuple-element.39), channel_id=1, source_target_pairs={{0,12},{1,13},{2,14},{3,15},{4,8},{5,9},{6,10},{7,11},{8,4},{9,5},... | collective-permute-start | bytes 393224 | tf_op jit(solution)/shard_map/ppermute | solution.py:100
  62.4 6.8 %collective-permute-start.35 = (bf16[128,512]{1,0:T(8,128)(2,1)S(1)}, bf16[128,512]{1,0:T(8,128)(2,1)S(1)}, u32[]{:S(2)}, u32[]{:S(2)}) collective-permute-start(bf16[128,512]{1,0:T(8,128)(2,1)S(1)} %collective-permute-done.33), channel_id=1, source_target_pairs={{0,2},{1,3},{2,0},{3,1},{4,6},{5,7},{6,4},{7,5},{8,10},{9,11},{10,... | collective-permute-start | bytes 393224 | tf_op jit(solution)/shard_map/ppermute | solution.py:103
  63.0 11.6 %collective-permute-start.34 = (bf16[128,512]{1,0:T(8,128)(2,1)S(1)}, bf16[128,512]{1,0:T(8,128)(2,1)S(1)}, u32[]{:S(2)}, u32[]{:S(2)}) collective-permute-start(bf16[128,512]{1,0:T(8,128)(2,1)S(1)} %collective-permute-done.33), channel_id=1, source_target_pairs={{0,1},{1,0},{2,3},{3,2},{4,5},{5,4},{6,7},{7,6},{8,9},{9,8},{10,11... | collective-permute-start | bytes 393224 | tf_op jit(solution)/shard_map/ppermute | solution.py:105
  63.0 7.2 %collective-permute-start.31 = (bf16[128,512]{1,0:T(8,128)(2,1)S(1)}, bf16[128,512]{1,0:T(8,128)(2,1)S(1)}, u32[]{:S(2)}, u32[]{:S(2)}) collective-permute-start(bf16[128,512]{1,0:T(8,128)(2,1)S(1)} %collective-permute-done.29), channel_id=1, source_target_pairs={{0,2},{1,3},{2,0},{3,1},{4,6},{5,7},{6,4},{7,5},{8,10},{9,11},{10,... | collective-permute-start | bytes 393224 | tf_op jit(solution)/shard_map/ppermute | solution.py:103
  64.4 4.2 %collective-permute-start.28 = (bf16[128,512]{1,0:T(8,128)(2,1)S(1)}, bf16[128,512]{1,0:T(8,128)(2,1)S(1)}, u32[]{:S(2)}, u32[]{:S(2)}) collective-permute-start(bf16[128,512]{1,0:T(8,128)(2,1)S(1)} %collective-permute-done.27), channel_id=1, source_target_pairs={{0,1},{1,0},{2,3},{3,2},{4,5},{5,4},{6,7},{7,6},{8,9},{9,8},{10,11... | collective-permute-start | bytes 393224 | tf_op jit(solution)/shard_map/ppermute | solution.py:105
  68.6 1.5 %collective-permute-start.30 = (bf16[128,512]{1,0:T(8,128)(2,1)S(1)}, bf16[128,512]{1,0:T(8,128)(2,1)S(1)}, u32[]{:S(2)}, u32[]{:S(2)}) collective-permute-start(bf16[128,512]{1,0:T(8,128)(2,1)S(1)} %collective-permute-done.29), channel_id=1, source_target_pairs={{0,1},{1,0},{2,3},{3,2},{4,5},{5,4},{6,7},{7,6},{8,9},{9,8},{10,11... | collective-permute-start | bytes 393224 | tf_op jit(solution)/shard_map/ppermute | solution.py:105
  68.6 5.9 %collective-permute-start.39 = (bf16[128,512]{1,0:T(8,128)(2,1)S(1)}, bf16[128,512]{1,0:T(8,128)(2,1)S(1)}, u32[]{:S(2)}, u32[]{:S(2)}) collective-permute-start(bf16[128,512]{1,0:T(8,128)(2,1)S(1)} %collective-permute-done.37), channel_id=1, source_target_pairs={{0,2},{1,3},{2,0},{3,1},{4,6},{5,7},{6,4},{7,5},{8,10},{9,11},{10,... | collective-permute-start | bytes 393224 | tf_op jit(solution)/shard_map/ppermute | solution.py:103
  69.2 5.5 %collective-permute-start.38 = (bf16[128,512]{1,0:T(8,128)(2,1)S(1)}, bf16[128,512]{1,0:T(8,128)(2,1)S(1)}, u32[]{:S(2)}, u32[]{:S(2)}) collective-permute-start(bf16[128,512]{1,0:T(8,128)(2,1)S(1)} %collective-permute-done.37), channel_id=1, source_target_pairs={{0,1},{1,0},{2,3},{3,2},{4,5},{5,4},{6,7},{7,6},{8,9},{9,8},{10,11... | collective-permute-start | bytes 393224 | tf_op jit(solution)/shard_map/ppermute | solution.py:105
  70.2 4.5 %collective-permute-start.36 = (bf16[128,512]{1,0:T(8,128)(2,1)S(1)}, bf16[128,512]{1,0:T(8,128)(2,1)S(1)}, u32[]{:S(2)}, u32[]{:S(2)}) collective-permute-start(bf16[128,512]{1,0:T(8,128)(2,1)S(1)} %collective-permute-done.35), channel_id=1, source_target_pairs={{0,1},{1,0},{2,3},{3,2},{4,5},{5,4},{6,7},{7,6},{8,9},{9,8},{10,11... | collective-permute-start | bytes 393224 | tf_op jit(solution)/shard_map/ppermute | solution.py:105
  70.2 4.4 %collective-permute-start.32 = (bf16[128,512]{1,0:T(8,128)(2,1)S(1)}, bf16[128,512]{1,0:T(8,128)(2,1)S(1)}, u32[]{:S(2)}, u32[]{:S(2)}) collective-permute-start(bf16[128,512]{1,0:T(8,128)(2,1)S(1)} %collective-permute-done.31), channel_id=1, source_target_pairs={{0,1},{1,0},{2,3},{3,2},{4,5},{5,4},{6,7},{7,6},{8,9},{9,8},{10,11... | collective-permute-start | bytes 393224 | tf_op jit(solution)/shard_map/ppermute | solution.py:105
  74.5 1.3 %collective-permute-start.40 = (bf16[128,512]{1,0:T(8,128)(2,1)S(1)}, bf16[128,512]{1,0:T(8,128)(2,1)S(1)}, u32[]{:S(2)}, u32[]{:S(2)}) collective-permute-start(bf16[128,512]{1,0:T(8,128)(2,1)S(1)} %collective-permute-done.39), channel_id=1, source_target_pairs={{0,1},{1,0},{2,3},{3,2},{4,5},{5,4},{6,7},{7,6},{8,9},{9,8},{10,11... | collective-permute-start | bytes 393224 | tf_op jit(solution)/shard_map/ppermute | solution.py:105
  79.7 11.6 %all-to-all-start = ((bf16[16,32,128]{2,1,0:T(8,128)(2,1)}), bf16[16,32,128]{2,1,0:T(8,128)(2,1)S(1)}, u32[]{:S(2)}, u32[]{:S(2)}) async-start(bf16[16,32,128]{2,1,0:T(8,128)(2,1)} %backward.1), calls=%async_computation | async-start | bytes 262144 | tf_op jit(solution)/shard_map/all_to_all | solution.py:397
  (6 other events, 31.3 us)

commit v5 on v4

--- a/solution.py
+++ b/solution.py
@@ -62,11 +62,11 @@
                 whole = put(whole, down, step)
         return whole, block
 
-    def scatter_sum(self, keep, other):
-        swapped = lax.ppermute(other, "fsdp", self.sibling)
+    def scatter_sum(self, product):
+        keep = product([], list(range(self.chips)), None)
 
         def term(distance):
-            return keep[distance] + swapped[distance]
+            return keep[distance]
 
         up = term(self.up_steps)
         down = term(self.up_steps + 1) if self.down_steps else None
@@ -79,7 +79,7 @@
             if step < self.down_steps:
                 down = down + term(self.up_steps + 1 + step)
         total = term(0) + up
-        return (total + down if self.down_steps else total), keep
+        return (total + down if self.down_steps else total), keep[0]
 
 
 class Grid(Ring):
@@ -106,18 +106,12 @@
                 whole = place(whole, part, self.owner(device, 2 * z + y, 1))
         return whole, column[1]
 
-    def scatter_sum(self, keep, other):
+    def scatter_sum(self, product):
         over_y = {}
         mine = {}
         sent = None
         for z in self.FAR_FIRST:
-            pair = slice(2 * z, 2 * z + 2)
-            part = lax.ppermute(other[pair], "fsdp", self.sibling)
-            if sent is not None:
-                part = after(part, sent)
-            part = keep[pair] + part
-            sent = part[1].astype(BF16)
-            mine[z] = part[0]
+            sent, mine[z] = product([2 * z + 1], [2 * z], sent)
             over_y[z] = lax.ppermute(sent, "fsdp", self.across(2))
         arrived = []
         sent = None
@@ -161,23 +155,9 @@
 
 
 def forward_kernel(
-    ring,
-    hidden,
-    parent_gain,
-    child_gain,
-    gate,
-    up,
-    down,
-    kept,
-    scale,
-    child_gate,
-    child_up,
-    child_hid,
-    keep,
-    send,
+    hidden, parent_gain, child_gain, gate, up, kept, scale, child_gate, child_up, both_hid
 ):
     tokens, features = hidden.shape
-    width = features // ring.devices
     pieces = 16
     piece = features // pieces
     cuts = [slice(k * piece, (k + 1) * piece) for k in range(pieces)]
@@ -188,27 +168,35 @@
     mean = jnp.sum(squares, axis=1, keepdims=True) / features
     inverse = 1.0 / jnp.sqrt(mean + 1e-05)
     scale[...] = jnp.broadcast_to(inverse, scale.shape)
-    gate_both = jnp.zeros((2 * tokens, gate.shape[0]), F32)
-    up_both = jnp.zeros((2 * tokens, gate.shape[0]), F32)
+    rows = gate.shape[0]
+    products = jnp.zeros((2 * tokens, 2 * rows), F32)
     for cols in cuts:
         normed = hidden[:, cols].astype(F32) * inverse
         parent = (normed * parent_gain[:, cols]).astype(BF16)
         child = (normed * child_gain[:, cols]).astype(BF16)
         both = jnp.concatenate([parent, child], axis=0)
-        gate_both = gate_both + dot_nt(both, gate[:, cols])
-        up_both = up_both + dot_nt(both, up[:, cols])
+        weights = jnp.concatenate([gate[:, cols], up[:, cols]], axis=0)
+        products = products + dot_nt(both, weights)
+    gate_both, up_both = products[:, :rows], products[:, rows:]
     hid = gate_both * jax.nn.sigmoid(gate_both) * up_both
     child_gate[...] = gate_both[tokens:]
     child_up[...] = up_both[tokens:]
     child = jnp.where(kept[...] > 0, hid[tokens:], 0.0).astype(BF16)
-    child_hid[...] = child
-    both_hid = jnp.concatenate([child, -hid[:tokens].astype(BF16)], axis=0)
+    both_hid[:tokens, :] = child
+    both_hid[tokens:, :] = -hid[:tokens].astype(BF16)
+
+
+def difference_kernel(ring, distances, hid, other_hid, down, other_down, *parts):
+    tokens = hid.shape[0] // 2
+    width = down.shape[1] // ring.devices
     device = lax.axis_index("fsdp")
-    for core, target in ((1, send), (0, keep)):
-        for distance in range(ring.chips):
-            start = ring.owner(device, distance, core) * width
-            out = dot(both_hid, down[:, pl.ds(pl.multiple_of(start, width), width)])
-            target[distance] = out[:tokens] + out[tokens:]
+    left = jnp.concatenate([hid[...], other_hid[...]], axis=1)
+    for distance, part in zip(distances, parts):
+        start = ring.owner(device, distance, 0) * width
+        cols = pl.ds(pl.multiple_of(start, width), width)
+        right = jnp.concatenate([down[:, cols], other_down[:, cols]], axis=0)
+        out = dot(left, right)
+        part[...] = (out[:tokens] + out[tokens:]).astype(part.dtype)
 
 
 def backward_kernel(
@@ -222,7 +210,7 @@
     scale,
     child_gate,
     child_up,
-    child_hid,
+    both_hid,
     select,
     sent,
     message,
@@ -238,13 +226,15 @@
     gate_back = jnp.where(live, gate_back, 0.0).astype(BF16)
     up_back = jnp.where(live, child_slope * g * sig, 0.0).astype(BF16)
     rows = dot_nt(select[0], gate_back) + dot_nt(select[1], up_back)
-    rows = rows + dot_nt(select[2], child_hid[...])
+    rows = rows + dot_nt(select[2], both_hid[:tokens, :])
     message[...] = rows.reshape(devices, stride, tokens)
+    both_back = jnp.concatenate([gate_back, up_back], axis=1)
     inverse = scale[...][:, :1]
     high_at, gain_rows = 3 * per_pair, width // 128
     for k in range(devices):
         cols = slice(k * width, (k + 1) * width)
-        input_slope = dot(gate_back, gate[:, cols]) + dot(up_back, up[:, cols])
+        weights = jnp.concatenate([gate[:, cols], up[:, cols]], axis=0)
+        input_slope = dot(both_back, weights)
         normed = hidden[:, cols].astype(F32) * inverse
         part = jnp.sum(input_slope * normed, axis=0, keepdims=True)
         high = part.astype(BF16).astype(F32)
@@ -345,28 +335,28 @@
     gains = [parent_gain.reshape(1, features), child_gain.reshape(1, features)]
     hidden_all, early = ring.gather(hidden, device)
     kept = kept_rows(after(kept_index, early), device, parent_rows)
-    scale, child_gate, child_up, child_hid, keep, other = call(
-        functools.partial(forward_kernel, ring),
-        [
-            ((tokens, 128), F32),
-            square,
-            square,
-            ((tokens, parent_rows), BF16),
-            ((chips, tokens, width), F32),
-            ((chips, tokens, width), F32),
-        ],
-        [
-            hidden_all,
-            *gains,
-            gate_weight,
-            up_weight,
-            down_weight,
-            kept,
-        ],
+    scale, child_gate, child_up, both_hid = call(
+        forward_kernel,
+        [((tokens, 128), F32), square, square, ((2 * tokens, parent_rows), BF16)],
+        [hidden_all, *gains, gate_weight, up_weight, kept],
         limit=6,
         name="forward",
     )
-    difference, last_sent = ring.scatter_sum(keep, other)
+    other_down = lax.ppermute(down_weight, "fsdp", ring.sibling)
+    other_hid = lax.ppermute(both_hid, "fsdp", ring.sibling)
+
+    def product(rounded, exact, previous):
+        block = (tokens, width)
+        hid = both_hid if previous is None else after(both_hid, previous)
+        return call(
+            functools.partial(difference_kernel, ring, rounded + exact),
+            [(block, BF16)] * len(rounded) + [(block, F32)] * len(exact),
+            [hid, other_hid, down_weight, other_down],
+            limit=6,
+            name="difference",
+        )
+
+    difference, last_sent = ring.scatter_sum(product)
     slope_all, _ = ring.gather(difference.astype(BF16), device)
 
     kept_index, tile_owner, _ = lax.optimization_barrier((kept_index, tile_owner, last_sent))
@@ -387,7 +377,7 @@
             scale,
             child_gate,
             child_up,
-            child_hid,
+            both_hid,
             select,
         ],
         limit=6,

time: 97.3 us -> 95.4 us (0.980)
  waiting for transfers between devices: 33.4 us -> 36.5 us
  starting transfers between devices: 38.9 us -> 36.6 us
  other arithmetic: 2.44 us -> 1.29 us
  Pallas kernels: 13.7 us -> 12.6 us
    ppermute x3, starting transfers between devices: 6.23 us -> 4.67 us  [scatter_sum(): arrived.append(lax.ppermute(sent, 'fsdp', self.across(4 * z)))]
    ppermute x8, waiting for transfers between devices: 9.4 us -> 10.8 us  [gather(): part = lax.ppermute(column[z], 'fsdp', self.across(2)) if y else column[z]]
    pallas_call x4 -> x8, Pallas kernels: 13.7 us -> 12.6 us  [call(): pl.pallas_call(kernel, out_shape=[jax.ShapeDtypeStruct(shape, dtype) for...]
    ppermute x4, waiting for transfers between devices: 6.5 us -> 7.52 us  [gather(): column[z] = lax.ppermute(block, 'fsdp', self.across(4 * z))]
  transfers between devices with their start and end apart: 42 -> 40, of which waited for: 16 -> 18; matrix products, arithmetic and copies ran while one was open for 4% -> 3% of each run, Pallas kernels for 2% -> 5%
where the time goes in v5:
time: 95.4 us; the launch traced here: 95.1 us
  starting transfers between devices  36.6 us (38%)
  waiting for transfers between devices  36.5 us (38%)
  Pallas kernels  12.6 us (13%)
  local copies, waits for them, and re-layouts  5.59 us (6%)
  between operations  1.43 us (1%)
  other arithmetic  1.29 us (1%)
  matrix products  1.1 us (1%)
    pallas_call x8, Pallas kernels, call(): pl.pallas_call(kernel, out_shape=[jax.ShapeDtypeStruct(shape, dtype) for...  12.6 us
    ppermute x8, waiting for transfers between devices, gather(): part = lax.ppermute(column[z], 'fsdp', self.across(2)) if y else column[z]  10.8 us
    ppermute x8, starting transfers between devices, gather(): part = lax.ppermute(column[z], 'fsdp', self.across(2)) if y else column[z]  9.31 us
    ppermute x4, starting transfers between devices, gather(): column[z] = lax.ppermute(block, 'fsdp', self.across(4 * z))  8.73 us
    ppermute x4, waiting for transfers between devices, gather(): column[z] = lax.ppermute(block, 'fsdp', self.across(4 * z))  7.52 us
    ppermute x3, waiting for transfers between devices, scatter_sum(): arrived.append(lax.ppermute(sent, 'fsdp', self.across(4 * z)))  6.1 us
    ppermute x3, starting transfers between devices, scatter_sum(): arrived.append(lax.ppermute(sent, 'fsdp', self.across(4 * z)))  4.67 us
    unnamed x24, local copies, waits for them, and re-layouts  4.55 us
  transfers between devices with their start and end apart: 40, of which 18 were waited for; matrix products, arithmetic and copies ran while one was open for 3% of the time, Pallas kernels for 5%

profile of v5, /device:TPU:0, one launch (start us, length us, event | category | flops | bytes accessed | tf_op | source)
XLA Modules:
  0.0 95.1 jit_solution(12733750683960439914)
XLA Ops:
  0.7 3.1 %collective-permute-start.3 = (bf16[128,512]{1,0:T(8,128)(2,1)}, bf16[128,512]{1,0:T(8,128)(2,1)S(1)}, u32[]{:S(2)}, u32[]{:S(2)}) collective-permute-start(bf16[128,512]{1,0:T(8,128)(2,1)} %param.8), channel_id=1, source_target_pairs={{0,4},{1,5},{2,6},{3,7},{4,0},{5,1},{6,2},{7,3},{8,12},{9,13},{10,... | collective-permute-start | bytes 393224 | tf_op jit(solution)/shard_map/ppermute | solution.py:99
  3.7 1.5 %collective-permute-start.1 = (bf16[128,512]{1,0:T(8,128)(2,1)}, bf16[128,512]{1,0:T(8,128)(2,1)S(1)}, u32[]{:S(2)}, u32[]{:S(2)}) collective-permute-start(bf16[128,512]{1,0:T(8,128)(2,1)} %param.8), channel_id=1, source_target_pairs={{0,2},{1,3},{2,0},{3,1},{4,6},{5,7},{6,4},{7,5},{8,10},{9,11},{10,... | collective-permute-start | bytes 393224 | tf_op jit(solution)/shard_map/ppermute | solution.py:103
  5.3 2.6 %collective-permute-start.7 = (bf16[128,512]{1,0:T(8,128)(2,1)}, bf16[128,512]{1,0:T(8,128)(2,1)S(1)}, u32[]{:S(2)}, u32[]{:S(2)}) collective-permute-start(bf16[128,512]{1,0:T(8,128)(2,1)} %param.8), channel_id=1, source_target_pairs={{0,8},{1,9},{2,10},{3,11},{4,12},{5,13},{6,14},{7,15},{8,0},{9,1},... | collective-permute-start | bytes 393224 | tf_op jit(solution)/shard_map/ppermute | solution.py:99
  8.4 2.8 %collective-permute-start.11 = (bf16[128,512]{1,0:T(8,128)(2,1)S(1)}, bf16[128,512]{1,0:T(8,128)(2,1)S(1)}, u32[]{:S(2)}, u32[]{:S(2)}) collective-permute-start(bf16[128,512]{1,0:T(8,128)(2,1)S(1)} %copy-done.9), channel_id=1, source_target_pairs={{0,12},{1,13},{2,14},{3,15},{4,8},{5,9},{6,10},{7,11},{8,4},{9,5},... | collective-permute-start | bytes 393224 | tf_op jit(solution)/shard_map/ppermute | solution.py:100
  11.6 2.7 %collective-permute-start.5 = (bf16[128,512]{1,0:T(8,128)(2,1)S(1)}, bf16[128,512]{1,0:T(8,128)(2,1)S(1)}, u32[]{:S(2)}, u32[]{:S(2)}) collective-permute-start(bf16[128,512]{1,0:T(8,128)(2,1)S(1)} %collective-permute-done.3), channel_id=1, source_target_pairs={{0,2},{1,3},{2,0},{3,1},{4,6},{5,7},{6,4},{7,5},{8,10},{9,11},{10,... | collective-permute-start | bytes 393224 | tf_op jit(solution)/shard_map/ppermute | solution.py:103
  14.3 3.8 %collective-permute-done.7 = bf16[128,512]{1,0:T(8,128)(2,1)S(1)} collective-permute-done((bf16[128,512]{1,0:T(8,128)(2,1)}, bf16[128,512]{1,0:T(8,128)(2,1)S(1)}, u32[]{:S(2)}, u32[]{:S(2)}) %collective-permute-start.7) | collective-permute-done | bytes 131104 | tf_op jit(solution)/shard_map/ppermute | solution.py:99
  18.1 0.5 collective-permute-start.9
  19.0 1.5 %collective-permute-start.13 = (bf16[128,512]{1,0:T(8,128)(2,1)S(1)}, bf16[128,512]{1,0:T(8,128)(2,1)S(1)}, u32[]{:S(2)}, u32[]{:S(2)}) collective-permute-start(bf16[128,512]{1,0:T(8,128)(2,1)S(1)} %collective-permute-done.11), channel_id=1, source_target_pairs={{0,2},{1,3},{2,0},{3,1},{4,6},{5,7},{6,4},{7,5},{8,10},{9,11},{10,... | collective-permute-start | bytes 393224 | tf_op jit(solution)/shard_map/ppermute | solution.py:103
  20.6 3.9 %collective-permute-done.9 = bf16[128,512]{1,0:T(8,128)(2,1)S(1)} collective-permute-done((bf16[128,512]{1,0:T(8,128)(2,1)S(1)}, bf16[128,512]{1,0:T(8,128)(2,1)S(1)}, u32[]{:S(2)}, u32[]{:S(2)}) %collective-permute-start.9) | collective-permute-done | bytes 131104 | tf_op jit(solution)/shard_map/ppermute | solution.py:103
  24.4 2.4 %collective-permute-done.13 = bf16[128,512]{1,0:T(8,128)(2,1)S(1)} collective-permute-done((bf16[128,512]{1,0:T(8,128)(2,1)S(1)}, bf16[128,512]{1,0:T(8,128)(2,1)S(1)}, u32[]{:S(2)}, u32[]{:S(2)}) %collective-permute-start.13) | collective-permute-done | bytes 131104 | tf_op jit(solution)/shard_map/ppermute | solution.py:103
  26.9 0.5 collective-permute-start.14
  27.5 0.7 collective-permute-done.10
  28.5 2.2 %forward.1 = (f32[128,128]{1,0:T(8,128)S(1)}, f32[128,128]{1,0:T(8,128)S(1)}, f32[128,128]{1,0:T(8,128)S(1)}, bf16[256,128]{1,0:T(8,128)(2,1)S(1)}) custom-call(bf16[128,8192]{1,0:T(8,128)(2,1)S(1)} %constant_dynamic-update-slice_fusion.16.hidden, f32[1,8192]{1,0:T(1,128)S(1)} %bitcast.32, f32[1,8192]{1,0:T(1,128)S(1)} %bitcast.30, ...), custom_call_target="tpu_custom_call" | custom-call | tf_op jit(solution)/shard_map/forward/pallas_call | solution.py:311
  30.7 0.4 collective-permute-start.15
  31.1 0.9 collective-permute-done.15.other_hid
  32.3 0.6 collective-permute-start.20
  33.2 1.6 %collective-permute-start.19 = (bf16[128,512]{1,0:T(8,128)(2,1)S(1)}, bf16[128,512]{1,0:T(8,128)(2,1)S(1)}, u32[]{:S(2)}, u32[]{:S(2)}) collective-permute-start(bf16[128,512]{1,0:T(8,128)(2,1)S(1)} %get-tuple-element.40), channel_id=1, source_target_pairs={{0,2},{1,3},{2,0},{3,1},{4,6},{5,7},{6,4},{7,5},{8,10},{9,11},{10,... | collective-permute-start | bytes 393224 | tf_op jit(solution)/shard_map/ppermute | solution.py:115
  35.1 0.6 collective-permute-start.18
  36.0 1.6 %collective-permute-start.17 = (bf16[128,512]{1,0:T(8,128)(2,1)S(1)}, bf16[128,512]{1,0:T(8,128)(2,1)S(1)}, u32[]{:S(2)}, u32[]{:S(2)}) collective-permute-start(bf16[128,512]{1,0:T(8,128)(2,1)S(1)} %get-tuple-element.45), channel_id=1, source_target_pairs={{0,2},{1,3},{2,0},{3,1},{4,6},{5,7},{6,4},{7,5},{8,10},{9,11},{10,... | collective-permute-start | bytes 393224 | tf_op jit(solution)/shard_map/ppermute | solution.py:115
  37.6 1.1 %collective-permute-done.20 = bf16[128,512]{1,0:T(8,128)(2,1)S(1)} collective-permute-done((bf16[128,512]{1,0:T(8,128)(2,1)S(1)}, bf16[128,512]{1,0:T(8,128)(2,1)S(1)}, u32[]{:S(2)}, u32[]{:S(2)}) %collective-permute-start.20) | collective-permute-done | bytes 131104 | tf_op jit(solution)/shard_map/ppermute | solution.py:115
  38.7 2.7 %collective-permute-start.21 = (bf16[128,512]{1,0:T(8,128)(2,1)S(1)}, bf16[128,512]{1,0:T(8,128)(2,1)S(1)}, u32[]{:S(2)}, u32[]{:S(2)}) collective-permute-start(bf16[128,512]{1,0:T(8,128)(2,1)S(1)} %add_convert_fusion.3), channel_id=1, source_target_pairs={{0,12},{1,13},{2,14},{3,15},{4,8},{5,9},{6,10},{7,11},{8,4},{9,5},... | collective-permute-start | bytes 393224 | tf_op jit(solution)/shard_map/ppermute | solution.py:123
  41.5 1.4 %collective-permute-start.22 = (bf16[128,512]{1,0:T(8,128)(2,1)S(1)}, bf16[128,512]{1,0:T(8,128)(2,1)S(1)}, u32[]{:S(2)}, u32[]{:S(2)}) collective-permute-start(bf16[128,512]{1,0:T(8,128)(2,1)S(1)} %add_convert_fusion.2), channel_id=1, source_target_pairs={{0,8},{1,9},{2,10},{3,11},{4,12},{5,13},{6,14},{7,15},{8,0},{9,1},... | collective-permute-start | bytes 393224 | tf_op jit(solution)/shard_map/ppermute | solution.py:123
  42.9 1.4 %collective-permute-done.18 = bf16[128,512]{1,0:T(8,128)(2,1)S(1)} collective-permute-done((bf16[128,512]{1,0:T(8,128)(2,1)S(1)}, bf16[128,512]{1,0:T(8,128)(2,1)S(1)}, u32[]{:S(2)}, u32[]{:S(2)}) %collective-permute-start.18) | collective-permute-done | bytes 131104 | tf_op jit(solution)/shard_map/ppermute | solution.py:115
  44.5 1.0 %fusion.2 = bf16[512,128]{1,0:T(8,128)(2,1)S(1)} fusion(s32[2048]{0:T(1024)S(1)} %fusion.5, s32[2048]{0:T(1024)S(1)} %broadcast_subtract_fusion), kind=kOutput, calls=%fused_computation.3 | convolution fusion | flops 269811712 | bytes 147456 | tf_op jit(solution)/shard_map/dot_general | solution.py:16
  45.5 0.6 collective-permute-start.23
  46.9 5.2 %collective-permute-done.22 = bf16[128,512]{1,0:T(8,128)(2,1)S(1)} collective-permute-done((bf16[128,512]{1,0:T(8,128)(2,1)S(1)}, bf16[128,512]{1,0:T(8,128)(2,1)S(1)}, u32[]{:S(2)}, u32[]{:S(2)}) %collective-permute-start.22) | collective-permute-done | bytes 131104 | tf_op jit(solution)/shard_map/ppermute | solution.py:123
  52.0 0.9 collective-permute-done.23
  53.3 0.6 collective-permute-start.31
  53.8 2.5 %collective-permute-start.27 = (bf16[128,512]{1,0:T(8,128)(2,1)S(1)}, bf16[128,512]{1,0:T(8,128)(2,1)S(1)}, u32[]{:S(2)}, u32[]{:S(2)}) collective-permute-start(bf16[128,512]{1,0:T(8,128)(2,1)S(1)} %get-tuple-element.52), channel_id=1, source_target_pairs={{0,4},{1,5},{2,6},{3,7},{4,0},{5,1},{6,2},{7,3},{8,12},{9,13},{10,... | collective-permute-start | bytes 393224 | tf_op jit(solution)/shard_map/ppermute | solution.py:99
  56.3 0.5 collective-permute-start.25
  56.9 3.7 %collective-permute-done.27 = bf16[128,512]{1,0:T(8,128)(2,1)S(1)} collective-permute-done((bf16[128,512]{1,0:T(8,128)(2,1)S(1)}, bf16[128,512]{1,0:T(8,128)(2,1)S(1)}, u32[]{:S(2)}, u32[]{:S(2)}) %collective-permute-start.27) | collective-permute-done | bytes 131104 | tf_op jit(solution)/shard_map/ppermute | solution.py:99
  60.6 0.5 collective-permute-start.35
  61.2 0.5 collective-permute-start.33
  61.7 1.5 %collective-permute-start.29 = (bf16[128,512]{1,0:T(8,128)(2,1)S(1)}, bf16[128,512]{1,0:T(8,128)(2,1)S(1)}, u32[]{:S(2)}, u32[]{:S(2)}) collective-permute-start(bf16[128,512]{1,0:T(8,128)(2,1)S(1)} %collective-permute-done.27), channel_id=1, source_target_pairs={{0,2},{1,3},{2,0},{3,1},{4,6},{5,7},{6,4},{7,5},{8,10},{9,11},{10,... | collective-permute-start | bytes 393224 | tf_op jit(solution)/shard_map/ppermute | solution.py:103
  63.5 3.9 %collective-permute-done.35 = bf16[128,512]{1,0:T(8,128)(2,1)S(1)} collective-permute-done((bf16[128,512]{1,0:T(8,128)(2,1)S(1)}, bf16[128,512]{1,0:T(8,128)(2,1)S(1)}, u32[]{:S(2)}, u32[]{:S(2)}) %collective-permute-start.35) | collective-permute-done | bytes 131104 | tf_op jit(solution)/shard_map/ppermute | solution.py:100
  67.4 0.5 collective-permute-start.37
  68.3 0.7 collective-permute-done.29
  68.9 0.5 collective-permute-start.30
  69.5 3.8 %collective-permute-done.37 = bf16[128,512]{1,0:T(8,128)(2,1)S(1)} collective-permute-done((bf16[128,512]{1,0:T(8,128)(2,1)S(1)}, bf16[128,512]{1,0:T(8,128)(2,1)S(1)}, u32[]{:S(2)}, u32[]{:S(2)}) %collective-permute-start.37) | collective-permute-done | bytes 131104 | tf_op jit(solution)/shard_map/ppermute | solution.py:103
  73.5 1.1 %collective-permute-done.38 = bf16[128,512]{1,0:T(8,128)(2,1)S(1)} collective-permute-done((bf16[128,512]{1,0:T(8,128)(2,1)S(1)}, bf16[128,512]{1,0:T(8,128)(2,1)S(1)}, u32[]{:S(2)}, u32[]{:S(2)}) %collective-permute-start.38) | collective-permute-done | bytes 131104 | tf_op jit(solution)/shard_map/ppermute | solution.py:105
  74.7 3.3 %backward.1 = bf16[16,32,128]{2,1,0:T(8,128)(2,1)} custom-call(bf16[128,8192]{1,0:T(8,128)(2,1)S(1)} %constant_dynamic-update-slice_fusion.slope, bf16[128,8192]{1,0:T(8,128)(2,1)S(1)} %constant_dynamic-update-slice_fusion.16.hidden, bf16[128,8192]{1,0:T(8,128)(2,1)S(1)} %copy-done.3, bf16[128,8192]{1,0:T(8,128)(2,1)S(1)} %copy-done.4, ...), custom_call_target="tpu_custom_call" | custom-call | tf_op jit(solution)/shard_map/backward/pallas_call | solution.py:311
  78.0 3.7 %all-to-all-start = ((bf16[16,32,128]{2,1,0:T(8,128)(2,1)}), bf16[16,32,128]{2,1,0:T(8,128)(2,1)S(1)}, u32[]{:S(2)}, u32[]{:S(2)}) async-start(bf16[16,32,128]{2,1,0:T(8,128)(2,1)} %backward.1), calls=%async_computation | async-start | bytes 262144 | tf_op jit(solution)/shard_map/all_to_all | solution.py:387
  82.1 1.6 %copy-done.2 = bf16[128,8192]{1,0:T(8,128)(2,1)S(1)} copy-done((bf16[128,8192]{1,0:T(8,128)(2,1)S(1)}, bf16[128,8192]{1,0:T(8,128)(2,1)}, u32[]{:S(2)}) %copy-start.2) | copy-done | bytes 2097176
  83.7 2.0 %prepare.1 = (bf16[128,8192]{1,0:T(8,128)(2,1)S(1)}, f32[1,1]{1,0:T(1,128)}) custom-call(bf16[128,8192]{1,0:T(8,128)(2,1)S(1)} %copy-done.2, f32[128,128]{1,0:T(8,128)S(1)} %get-tuple-element.53.scale, f32[1,8192]{1,0:T(1,128)S(1)} %bitcast.31, bf16[128,8192]{1,0:T(8,128)(2,1)S(1)} %constant_dynamic-update-slice_fusion.slope), custom_call_target="tpu_custom_call" | custom-call | tf_op jit(solution)/shard_map/prepare/pallas_call | solution.py:311
  85.7 1.3 %copy-done.5 = bf16[128,8192]{1,0:T(8,128)(2,1)} copy-done((bf16[128,8192]{1,0:T(8,128)(2,1)}, bf16[128,8192]{1,0:T(8,128)(2,1)S(1)}, u32[]{:S(2)}) %copy-start.5) | copy-done | bytes 2097176
  87.0 2.4 %all-to-all-done.received = bf16[16,32,128]{2,1,0:T(8,128)(2,1)S(1)} async-done(((bf16[16,32,128]{2,1,0:T(8,128)(2,1)}), bf16[16,32,128]{2,1,0:T(8,128)(2,1)S(1)}, u32[]{:S(2)}, u32[]{:S(2)}) %all-to-all-start) | async-done | bytes 131104 | tf_op jit(solution)/shard_map/all_to_all | solution.py:387
  89.4 1.6 %copy-done.6 = bf16[128,8192]{1,0:T(8,128)(2,1)S(1)} copy-done((bf16[128,8192]{1,0:T(8,128)(2,1)S(1)}, bf16[128,8192]{1,0:T(8,128)(2,1)}, u32[]{:S(2)}) %copy-start.6) | copy-done | bytes 2097176
  91.0 4.0 %rows.1 = (bf16[128,8192]{1,0:T(8,128)(2,1)}, bf16[128,8192]{1,0:T(8,128)(2,1)}, bf16[128,8192]{1,0:T(8,128)(2,1)}, f32[1,512]{1,0:T(1,128)}) custom-call(bf16[16,32,128]{2,1,0:T(8,128)(2,1)S(1)} %all-to-all-done.received, bf16[3,128,512]{2,1,0:T(8,128)(2,1)S(1)} %pad_maximum_fusion.1.places, bf16[128,8192]{1,0:T(8,128)(2,1)S(1)} %copy-done.6, ...), custom_call_target="tpu_custom_call" | custom-call | tf_op jit(solution)/shard_map/rows/pallas_call | solution.py:311
  (125 shorter events, 5.3 us)
Async XLA Ops:
  0.6 7.7 %copy-start.9 = (bf16[128,512]{1,0:T(8,128)(2,1)S(1)}, bf16[128,512]{1,0:T(8,128)(2,1)}, u32[]{:S(2)}) copy-start(bf16[128,512]{1,0:T(8,128)(2,1)} %param.8) | copy-start | bytes 393220
  0.6 10.6 %copy-start.10 = (s32[2048]{0:T(1024)S(1)}, s32[2048]{0:T(1024)}, u32[]{:S(2)}) copy-start(s32[2048]{0:T(1024)} %param.14) | copy-start | bytes 24580
  0.7 7.7 %collective-permute-start.3 = (bf16[128,512]{1,0:T(8,128)(2,1)}, bf16[128,512]{1,0:T(8,128)(2,1)S(1)}, u32[]{:S(2)}, u32[]{:S(2)}) collective-permute-start(bf16[128,512]{1,0:T(8,128)(2,1)} %param.8), channel_id=1, source_target_pairs={{0,4},{1,5},{2,6},{3,7},{4,0},{5,1},{6,2},{7,3},{8,12},{9,13},{10,... | collective-permute-start | bytes 393224 | tf_op jit(solution)/shard_map/ppermute | solution.py:99
  3.7 7.8 %collective-permute-start.1 = (bf16[128,512]{1,0:T(8,128)(2,1)}, bf16[128,512]{1,0:T(8,128)(2,1)S(1)}, u32[]{:S(2)}, u32[]{:S(2)}) collective-permute-start(bf16[128,512]{1,0:T(8,128)(2,1)} %param.8), channel_id=1, source_target_pairs={{0,2},{1,3},{2,0},{3,1},{4,6},{5,7},{6,4},{7,5},{8,10},{9,11},{10,... | collective-permute-start | bytes 393224 | tf_op jit(solution)/shard_map/ppermute | solution.py:103
  5.3 9.0 %collective-permute-start = (bf16[128,512]{1,0:T(8,128)(2,1)}, bf16[128,512]{1,0:T(8,128)(2,1)S(1)}, u32[]{:S(2)}, u32[]{:S(2)}) collective-permute-start(bf16[128,512]{1,0:T(8,128)(2,1)} %param.8), channel_id=1, source_target_pairs={{0,1},{1,0},{2,3},{3,2},{4,5},{5,4},{6,7},{7,6},{8,9},{9,8},{10,11... | collective-permute-start | bytes 393224 | tf_op jit(solution)/shard_map/ppermute | solution.py:105
  5.3 12.9 %collective-permute-start.7 = (bf16[128,512]{1,0:T(8,128)(2,1)}, bf16[128,512]{1,0:T(8,128)(2,1)S(1)}, u32[]{:S(2)}, u32[]{:S(2)}) collective-permute-start(bf16[128,512]{1,0:T(8,128)(2,1)} %param.8), channel_id=1, source_target_pairs={{0,8},{1,9},{2,10},{3,11},{4,12},{5,13},{6,14},{7,15},{8,0},{9,1},... | collective-permute-start | bytes 393224 | tf_op jit(solution)/shard_map/ppermute | solution.py:99
  7.9 24.1 %collective-permute-start.16 = (bf16[128,8192]{1,0:T(8,128)(2,1)}, bf16[128,8192]{1,0:T(8,128)(2,1)S(1)}, u32[]{:S(2)}, u32[]{:S(2)}) collective-permute-start(bf16[128,8192]{1,0:T(8,128)(2,1)} %down.9), channel_id=1, source_target_pairs={{0,1},{1,0},{2,3},{3,2},{4,5},{5,4},{6,7},{7,6},{8,9},{9,8},{10,11... | collective-permute-start | bytes 6291464 | tf_op jit(solution)/shard_map/ppermute | solution.py:345
  8.1 20.3 %copy-start.8 = (f32[8192]{0:T(1024)S(1)}, f32[8192]{0:T(1024)}, u32[]{:S(2)}) copy-start(f32[8192]{0:T(1024)} %param.9) | copy-start | bytes 98308
  8.3 20.1 %copy-start.3 = (bf16[128,8192]{1,0:T(8,128)(2,1)S(1)}, bf16[128,8192]{1,0:T(8,128)(2,1)}, u32[]{:S(2)}) copy-start(bf16[128,8192]{1,0:T(8,128)(2,1)} %gate.3) | copy-start | bytes 6291460
  8.3 20.1 %copy-start.4 = (bf16[128,8192]{1,0:T(8,128)(2,1)S(1)}, bf16[128,8192]{1,0:T(8,128)(2,1)}, u32[]{:S(2)}) copy-start(bf16[128,8192]{1,0:T(8,128)(2,1)} %up.3) | copy-start | bytes 6291460
  8.3 20.1 %copy-start.7 = (f32[8192]{0:T(1024)S(1)}, f32[8192]{0:T(1024)}, u32[]{:S(2)}) copy-start(f32[8192]{0:T(1024)} %param.10) | copy-start | bytes 98308
  8.4 10.3 %collective-permute-start.11 = (bf16[128,512]{1,0:T(8,128)(2,1)S(1)}, bf16[128,512]{1,0:T(8,128)(2,1)S(1)}, u32[]{:S(2)}, u32[]{:S(2)}) collective-permute-start(bf16[128,512]{1,0:T(8,128)(2,1)S(1)} %copy-done.9), channel_id=1, source_target_pairs={{0,12},{1,13},{2,14},{3,15},{4,8},{5,9},{6,10},{7,11},{8,4},{9,5},... | collective-permute-start | bytes 393224 | tf_op jit(solution)/shard_map/ppermute | solution.py:100
  11.6 7.4 %collective-permute-start.5 = (bf16[128,512]{1,0:T(8,128)(2,1)S(1)}, bf16[128,512]{1,0:T(8,128)(2,1)S(1)}, u32[]{:S(2)}, u32[]{:S(2)}) collective-permute-start(bf16[128,512]{1,0:T(8,128)(2,1)S(1)} %collective-permute-done.3), channel_id=1, source_target_pairs={{0,2},{1,3},{2,0},{3,1},{4,6},{5,7},{6,4},{7,5},{8,10},{9,11},{10,... | collective-permute-start | bytes 393224 | tf_op jit(solution)/shard_map/ppermute | solution.py:103
  14.3 3.9 %collective-permute-start.2 = (bf16[128,512]{1,0:T(8,128)(2,1)S(1)}, bf16[128,512]{1,0:T(8,128)(2,1)S(1)}, u32[]{:S(2)}, u32[]{:S(2)}) collective-permute-start(bf16[128,512]{1,0:T(8,128)(2,1)S(1)} %collective-permute-done.1), channel_id=1, source_target_pairs={{0,1},{1,0},{2,3},{3,2},{4,5},{5,4},{6,7},{7,6},{8,9},{9,8},{10,11... | collective-permute-start | bytes 393224 | tf_op jit(solution)/shard_map/ppermute | solution.py:105
  18.1 2.4 %collective-permute-start.4 = (bf16[128,512]{1,0:T(8,128)(2,1)S(1)}, bf16[128,512]{1,0:T(8,128)(2,1)S(1)}, u32[]{:S(2)}, u32[]{:S(2)}) collective-permute-start(bf16[128,512]{1,0:T(8,128)(2,1)S(1)} %collective-permute-done.3), channel_id=1, source_target_pairs={{0,1},{1,0},{2,3},{3,2},{4,5},{5,4},{6,7},{7,6},{8,9},{9,8},{10,11... | collective-permute-start | bytes 393224 | tf_op jit(solution)/shard_map/ppermute | solution.py:105
  18.1 6.3 %collective-permute-start.9 = (bf16[128,512]{1,0:T(8,128)(2,1)S(1)}, bf16[128,512]{1,0:T(8,128)(2,1)S(1)}, u32[]{:S(2)}, u32[]{:S(2)}) collective-permute-start(bf16[128,512]{1,0:T(8,128)(2,1)S(1)} %collective-permute-done.7), channel_id=1, source_target_pairs={{0,2},{1,3},{2,0},{3,1},{4,6},{5,7},{6,4},{7,5},{8,10},{9,11},{10,... | collective-permute-start | bytes 393224 | tf_op jit(solution)/shard_map/ppermute | solution.py:103
  18.7 8.7 %collective-permute-start.8 = (bf16[128,512]{1,0:T(8,128)(2,1)S(1)}, bf16[128,512]{1,0:T(8,128)(2,1)S(1)}, u32[]{:S(2)}, u32[]{:S(2)}) collective-permute-start(bf16[128,512]{1,0:T(8,128)(2,1)S(1)} %collective-permute-done.7), channel_id=1, source_target_pairs={{0,1},{1,0},{2,3},{3,2},{4,5},{5,4},{6,7},{7,6},{8,9},{9,8},{10,11... | collective-permute-start | bytes 393224 | tf_op jit(solution)/shard_map/ppermute | solution.py:105
  19.0 7.9 %collective-permute-start.13 = (bf16[128,512]{1,0:T(8,128)(2,1)S(1)}, bf16[128,512]{1,0:T(8,128)(2,1)S(1)}, u32[]{:S(2)}, u32[]{:S(2)}) collective-permute-start(bf16[128,512]{1,0:T(8,128)(2,1)S(1)} %collective-permute-done.11), channel_id=1, source_target_pairs={{0,2},{1,3},{2,0},{3,1},{4,6},{5,7},{6,4},{7,5},{8,10},{9,11},{10,... | collective-permute-start | bytes 393224 | tf_op jit(solution)/shard_map/ppermute | solution.py:103
  20.5 6.3 %collective-permute-start.6 = (bf16[128,512]{1,0:T(8,128)(2,1)S(1)}, bf16[128,512]{1,0:T(8,128)(2,1)S(1)}, u32[]{:S(2)}, u32[]{:S(2)}) collective-permute-start(bf16[128,512]{1,0:T(8,128)(2,1)S(1)} %collective-permute-done.5), channel_id=1, source_target_pairs={{0,1},{1,0},{2,3},{3,2},{4,5},{5,4},{6,7},{7,6},{8,9},{9,8},{10,11... | collective-permute-start | bytes 393224 | tf_op jit(solution)/shard_map/ppermute | solution.py:105
  24.4 3.8 %collective-permute-start.12 = (bf16[128,512]{1,0:T(8,128)(2,1)S(1)}, bf16[128,512]{1,0:T(8,128)(2,1)S(1)}, u32[]{:S(2)}, u32[]{:S(2)}) collective-permute-start(bf16[128,512]{1,0:T(8,128)(2,1)S(1)} %collective-permute-done.11), channel_id=1, source_target_pairs={{0,1},{1,0},{2,3},{3,2},{4,5},{5,4},{6,7},{7,6},{8,9},{9,8},{10,11... | collective-permute-start | bytes 393224 | tf_op jit(solution)/shard_map/ppermute | solution.py:105
  26.9 1.3 %collective-permute-start.10 = (bf16[128,512]{1,0:T(8,128)(2,1)S(1)}, bf16[128,512]{1,0:T(8,128)(2,1)S(1)}, u32[]{:S(2)}, u32[]{:S(2)}) collective-permute-start(bf16[128,512]{1,0:T(8,128)(2,1)S(1)} %collective-permute-done.9), channel_id=1, source_target_pairs={{0,1},{1,0},{2,3},{3,2},{4,5},{5,4},{6,7},{7,6},{8,9},{9,8},{10,11... | collective-permute-start | bytes 393224 | tf_op jit(solution)/shard_map/ppermute | solution.py:105
  26.9 1.5 %collective-permute-start.14 = (bf16[128,512]{1,0:T(8,128)(2,1)S(1)}, bf16[128,512]{1,0:T(8,128)(2,1)S(1)}, u32[]{:S(2)}, u32[]{:S(2)}) collective-permute-start(bf16[128,512]{1,0:T(8,128)(2,1)S(1)} %collective-permute-done.13), channel_id=1, source_target_pairs={{0,1},{1,0},{2,3},{3,2},{4,5},{5,4},{6,7},{7,6},{8,9},{9,8},{10,11... | collective-permute-start | bytes 393224 | tf_op jit(solution)/shard_map/ppermute | solution.py:105
  28.4 46.3 %copy-start.1 = (bf16[128,8192]{1,0:T(8,128)(2,1)}, bf16[128,8192]{1,0:T(8,128)(2,1)S(1)}, u32[]{:S(2)}) copy-start(bf16[128,8192]{1,0:T(8,128)(2,1)S(1)} %constant_dynamic-update-slice_fusion.16.hidden) | copy-start | bytes 6291460
  30.7 1.3 %collective-permute-start.15 = (bf16[256,128]{1,0:T(8,128)(2,1)S(1)}, bf16[256,128]{1,0:T(8,128)(2,1)S(1)}, u32[]{:S(2)}, u32[]{:S(2)}) collective-permute-start(bf16[256,128]{1,0:T(8,128)(2,1)S(1)} %get-tuple-element.43.hid.both_hid), channel_id=1, source_target_pairs={{0,1},{1,0},{2,3},{3,2},{4,5},{5,4},{6,7},{7,6},{8,9},{9,8},{10,11... | collective-permute-start | bytes 196616 | tf_op jit(solution)/shard_map/ppermute | solution.py:346
  32.3 6.4 %collective-permute-start.20 = (bf16[128,512]{1,0:T(8,128)(2,1)S(1)}, bf16[128,512]{1,0:T(8,128)(2,1)S(1)}, u32[]{:S(2)}, u32[]{:S(2)}) collective-permute-start(bf16[128,512]{1,0:T(8,128)(2,1)S(1)} %get-tuple-element.38), channel_id=1, source_target_pairs={{0,2},{1,3},{2,0},{3,1},{4,6},{5,7},{6,4},{7,5},{8,10},{9,11},{10,... | collective-permute-start | bytes 393224 | tf_op jit(solution)/shard_map/ppermute | solution.py:115
  33.2 8.3 %collective-permute-start.19 = (bf16[128,512]{1,0:T(8,128)(2,1)S(1)}, bf16[128,512]{1,0:T(8,128)(2,1)S(1)}, u32[]{:S(2)}, u32[]{:S(2)}) collective-permute-start(bf16[128,512]{1,0:T(8,128)(2,1)S(1)} %get-tuple-element.40), channel_id=1, source_target_pairs={{0,2},{1,3},{2,0},{3,1},{4,6},{5,7},{6,4},{7,5},{8,10},{9,11},{10,... | collective-permute-start | bytes 393224 | tf_op jit(solution)/shard_map/ppermute | solution.py:115
  35.1 9.3 %copy-start.11 = (s32[16]{0:T(128)S(1)}, s32[16]{0:T(128)}, u32[]{:S(2)}) copy-start(s32[16]{0:T(128)} %param.15) | copy-start | bytes 196
  35.1 9.2 %collective-permute-start.18 = (bf16[128,512]{1,0:T(8,128)(2,1)S(1)}, bf16[128,512]{1,0:T(8,128)(2,1)S(1)}, u32[]{:S(2)}, u32[]{:S(2)}) collective-permute-start(bf16[128,512]{1,0:T(8,128)(2,1)S(1)} %get-tuple-element.42), channel_id=1, source_target_pairs={{0,2},{1,3},{2,0},{3,1},{4,6},{5,7},{6,4},{7,5},{8,10},{9,11},{10,... | collective-permute-start | bytes 393224 | tf_op jit(solution)/shard_map/ppermute | solution.py:115
  36.0 10.6 %collective-permute-start.17 = (bf16[128,512]{1,0:T(8,128)(2,1)S(1)}, bf16[128,512]{1,0:T(8,128)(2,1)S(1)}, u32[]{:S(2)}, u32[]{:S(2)}) collective-permute-start(bf16[128,512]{1,0:T(8,128)(2,1)S(1)} %get-tuple-element.45), channel_id=1, source_target_pairs={{0,2},{1,3},{2,0},{3,1},{4,6},{5,7},{6,4},{7,5},{8,10},{9,11},{10,... | collective-permute-start | bytes 393224 | tf_op jit(solution)/shard_map/ppermute | solution.py:115
  38.7 8.1 %collective-permute-start.21 = (bf16[128,512]{1,0:T(8,128)(2,1)S(1)}, bf16[128,512]{1,0:T(8,128)(2,1)S(1)}, u32[]{:S(2)}, u32[]{:S(2)}) collective-permute-start(bf16[128,512]{1,0:T(8,128)(2,1)S(1)} %add_convert_fusion.3), channel_id=1, source_target_pairs={{0,12},{1,13},{2,14},{3,15},{4,8},{5,9},{6,10},{7,11},{8,4},{9,5},... | collective-permute-start | bytes 393224 | tf_op jit(solution)/shard_map/ppermute | solution.py:123
  41.5 10.5 %collective-permute-start.22 = (bf16[128,512]{1,0:T(8,128)(2,1)S(1)}, bf16[128,512]{1,0:T(8,128)(2,1)S(1)}, u32[]{:S(2)}, u32[]{:S(2)}) collective-permute-start(bf16[128,512]{1,0:T(8,128)(2,1)S(1)} %add_convert_fusion.2), channel_id=1, source_target_pairs={{0,8},{1,9},{2,10},{3,11},{4,12},{5,13},{6,14},{7,15},{8,0},{9,1},... | collective-permute-start | bytes 393224 | tf_op jit(solution)/shard_map/ppermute | solution.py:123
  45.5 7.4 %collective-permute-start.23 = (bf16[128,512]{1,0:T(8,128)(2,1)S(1)}, bf16[128,512]{1,0:T(8,128)(2,1)S(1)}, u32[]{:S(2)}, u32[]{:S(2)}) collective-permute-start(bf16[128,512]{1,0:T(8,128)(2,1)S(1)} %add_convert_fusion.1), channel_id=1, source_target_pairs={{0,4},{1,5},{2,6},{3,7},{4,0},{5,1},{6,2},{7,3},{8,12},{9,13},{10,... | collective-permute-start | bytes 393224 | tf_op jit(solution)/shard_map/ppermute | solution.py:123
  53.3 7.9 %collective-permute-start.31 = (bf16[128,512]{1,0:T(8,128)(2,1)S(1)}, bf16[128,512]{1,0:T(8,128)(2,1)S(1)}, u32[]{:S(2)}, u32[]{:S(2)}) collective-permute-start(bf16[128,512]{1,0:T(8,128)(2,1)S(1)} %get-tuple-element.52), channel_id=1, source_target_pairs={{0,8},{1,9},{2,10},{3,11},{4,12},{5,13},{6,14},{7,15},{8,0},{9,1},... | collective-permute-start | bytes 393224 | tf_op jit(solution)/shard_map/ppermute | solution.py:99
  53.8 6.8 %collective-permute-start.27 = (bf16[128,512]{1,0:T(8,128)(2,1)S(1)}, bf16[128,512]{1,0:T(8,128)(2,1)S(1)}, u32[]{:S(2)}, u32[]{:S(2)}) collective-permute-start(bf16[128,512]{1,0:T(8,128)(2,1)S(1)} %get-tuple-element.52), channel_id=1, source_target_pairs={{0,4},{1,5},{2,6},{3,7},{4,0},{5,1},{6,2},{7,3},{8,12},{9,13},{10,... | collective-permute-start | bytes 393224 | tf_op jit(solution)/shard_map/ppermute | solution.py:99
  56.3 5.4 %collective-permute-start.25 = (bf16[128,512]{1,0:T(8,128)(2,1)S(1)}, bf16[128,512]{1,0:T(8,128)(2,1)S(1)}, u32[]{:S(2)}, u32[]{:S(2)}) collective-permute-start(bf16[128,512]{1,0:T(8,128)(2,1)S(1)} %get-tuple-element.52), channel_id=1, source_target_pairs={{0,2},{1,3},{2,0},{3,1},{4,6},{5,7},{6,4},{7,5},{8,10},{9,11},{10,... | collective-permute-start | bytes 393224 | tf_op jit(solution)/shard_map/ppermute | solution.py:103
  56.9 6.3 %collective-permute-start.24 = (bf16[128,512]{1,0:T(8,128)(2,1)S(1)}, bf16[128,512]{1,0:T(8,128)(2,1)S(1)}, u32[]{:S(2)}, u32[]{:S(2)}) collective-permute-start(bf16[128,512]{1,0:T(8,128)(2,1)S(1)} %get-tuple-element.52), channel_id=1, source_target_pairs={{0,1},{1,0},{2,3},{3,2},{4,5},{5,4},{6,7},{7,6},{8,9},{9,8},{10,11... | collective-permute-start | bytes 393224 | tf_op jit(solution)/shard_map/ppermute | solution.py:105
  60.6 6.8 %collective-permute-start.35 = (bf16[128,512]{1,0:T(8,128)(2,1)S(1)}, bf16[128,512]{1,0:T(8,128)(2,1)S(1)}, u32[]{:S(2)}, u32[]{:S(2)}) collective-permute-start(bf16[128,512]{1,0:T(8,128)(2,1)S(1)} %get-tuple-element.52), channel_id=1, source_target_pairs={{0,12},{1,13},{2,14},{3,15},{4,8},{5,9},{6,10},{7,11},{8,4},{9,5},... | collective-permute-start | bytes 393224 | tf_op jit(solution)/shard_map/ppermute | solution.py:100
  61.2 6.8 %collective-permute-start.33 = (bf16[128,512]{1,0:T(8,128)(2,1)S(1)}, bf16[128,512]{1,0:T(8,128)(2,1)S(1)}, u32[]{:S(2)}, u32[]{:S(2)}) collective-permute-start(bf16[128,512]{1,0:T(8,128)(2,1)S(1)} %collective-permute-done.31), channel_id=1, source_target_pairs={{0,2},{1,3},{2,0},{3,1},{4,6},{5,7},{6,4},{7,5},{8,10},{9,11},{10,... | collective-permute-start | bytes 393224 | tf_op jit(solution)/shard_map/ppermute | solution.py:103
  61.7 11.7 %collective-permute-start.32 = (bf16[128,512]{1,0:T(8,128)(2,1)S(1)}, bf16[128,512]{1,0:T(8,128)(2,1)S(1)}, u32[]{:S(2)}, u32[]{:S(2)}) collective-permute-start(bf16[128,512]{1,0:T(8,128)(2,1)S(1)} %collective-permute-done.31), channel_id=1, source_target_pairs={{0,1},{1,0},{2,3},{3,2},{4,5},{5,4},{6,7},{7,6},{8,9},{9,8},{10,11... | collective-permute-start | bytes 393224 | tf_op jit(solution)/shard_map/ppermute | solution.py:105
  61.7 7.3 %collective-permute-start.29 = (bf16[128,512]{1,0:T(8,128)(2,1)S(1)}, bf16[128,512]{1,0:T(8,128)(2,1)S(1)}, u32[]{:S(2)}, u32[]{:S(2)}) collective-permute-start(bf16[128,512]{1,0:T(8,128)(2,1)S(1)} %collective-permute-done.27), channel_id=1, source_target_pairs={{0,2},{1,3},{2,0},{3,1},{4,6},{5,7},{6,4},{7,5},{8,10},{9,11},{10,... | collective-permute-start | bytes 393224 | tf_op jit(solution)/shard_map/ppermute | solution.py:103
  63.2 4.2 %collective-permute-start.26 = (bf16[128,512]{1,0:T(8,128)(2,1)S(1)}, bf16[128,512]{1,0:T(8,128)(2,1)S(1)}, u32[]{:S(2)}, u32[]{:S(2)}) collective-permute-start(bf16[128,512]{1,0:T(8,128)(2,1)S(1)} %collective-permute-done.25), channel_id=1, source_target_pairs={{0,1},{1,0},{2,3},{3,2},{4,5},{5,4},{6,7},{7,6},{8,9},{9,8},{10,11... | collective-permute-start | bytes 393224 | tf_op jit(solution)/shard_map/ppermute | solution.py:105
  67.4 1.5 %collective-permute-start.28 = (bf16[128,512]{1,0:T(8,128)(2,1)S(1)}, bf16[128,512]{1,0:T(8,128)(2,1)S(1)}, u32[]{:S(2)}, u32[]{:S(2)}) collective-permute-start(bf16[128,512]{1,0:T(8,128)(2,1)S(1)} %collective-permute-done.27), channel_id=1, source_target_pairs={{0,1},{1,0},{2,3},{3,2},{4,5},{5,4},{6,7},{7,6},{8,9},{9,8},{10,11... | collective-permute-start | bytes 393224 | tf_op jit(solution)/shard_map/ppermute | solution.py:105
  67.4 5.9 %collective-permute-start.37 = (bf16[128,512]{1,0:T(8,128)(2,1)S(1)}, bf16[128,512]{1,0:T(8,128)(2,1)S(1)}, u32[]{:S(2)}, u32[]{:S(2)}) collective-permute-start(bf16[128,512]{1,0:T(8,128)(2,1)S(1)} %collective-permute-done.35), channel_id=1, source_target_pairs={{0,2},{1,3},{2,0},{3,1},{4,6},{5,7},{6,4},{7,5},{8,10},{9,11},{10,... | collective-permute-start | bytes 393224 | tf_op jit(solution)/shard_map/ppermute | solution.py:103
  68.0 5.5 %collective-permute-start.36 = (bf16[128,512]{1,0:T(8,128)(2,1)S(1)}, bf16[128,512]{1,0:T(8,128)(2,1)S(1)}, u32[]{:S(2)}, u32[]{:S(2)}) collective-permute-start(bf16[128,512]{1,0:T(8,128)(2,1)S(1)} %collective-permute-done.35), channel_id=1, source_target_pairs={{0,1},{1,0},{2,3},{3,2},{4,5},{5,4},{6,7},{7,6},{8,9},{9,8},{10,11... | collective-permute-start | bytes 393224 | tf_op jit(solution)/shard_map/ppermute | solution.py:105
  68.9 4.5 %collective-permute-start.34 = (bf16[128,512]{1,0:T(8,128)(2,1)S(1)}, bf16[128,512]{1,0:T(8,128)(2,1)S(1)}, u32[]{:S(2)}, u32[]{:S(2)}) collective-permute-start(bf16[128,512]{1,0:T(8,128)(2,1)S(1)} %collective-permute-done.33), channel_id=1, source_target_pairs={{0,1},{1,0},{2,3},{3,2},{4,5},{5,4},{6,7},{7,6},{8,9},{9,8},{10,11... | collective-permute-start | bytes 393224 | tf_op jit(solution)/shard_map/ppermute | solution.py:105
  68.9 4.4 %collective-permute-start.30 = (bf16[128,512]{1,0:T(8,128)(2,1)S(1)}, bf16[128,512]{1,0:T(8,128)(2,1)S(1)}, u32[]{:S(2)}, u32[]{:S(2)}) collective-permute-start(bf16[128,512]{1,0:T(8,128)(2,1)S(1)} %collective-permute-done.29), channel_id=1, source_target_pairs={{0,1},{1,0},{2,3},{3,2},{4,5},{5,4},{6,7},{7,6},{8,9},{9,8},{10,11... | collective-permute-start | bytes 393224 | tf_op jit(solution)/shard_map/ppermute | solution.py:105
  73.3 1.3 %collective-permute-start.38 = (bf16[128,512]{1,0:T(8,128)(2,1)S(1)}, bf16[128,512]{1,0:T(8,128)(2,1)S(1)}, u32[]{:S(2)}, u32[]{:S(2)}) collective-permute-start(bf16[128,512]{1,0:T(8,128)(2,1)S(1)} %collective-permute-done.37), channel_id=1, source_target_pairs={{0,1},{1,0},{2,3},{3,2},{4,5},{5,4},{6,7},{7,6},{8,9},{9,8},{10,11... | collective-permute-start | bytes 393224 | tf_op jit(solution)/shard_map/ppermute | solution.py:105
  78.0 11.4 %all-to-all-start = ((bf16[16,32,128]{2,1,0:T(8,128)(2,1)}), bf16[16,32,128]{2,1,0:T(8,128)(2,1)S(1)}, u32[]{:S(2)}, u32[]{:S(2)}) async-start(bf16[16,32,128]{2,1,0:T(8,128)(2,1)} %backward.1), calls=%async_computation | async-start | bytes 262144 | tf_op jit(solution)/shard_map/all_to_all | solution.py:387
  (4 other events, 8.0 us)

commit v6 on v5

--- a/solution.py
+++ b/solution.py
@@ -29,12 +29,16 @@
 
 
 class Ring:
+    EARLY = 1
+
     def __init__(self, devices):
         self.devices = devices
         self.chips = devices // 2
         self.up_steps = self.chips // 2
         self.down_steps = self.chips - 1 - self.up_steps
         self.sibling = [(i, i ^ 1) for i in range(devices)]
+        at = [(j, core) for j in range(self.chips) for core in (0, 1)]
+        self.first_at, self.late_at = at[: self.EARLY], at[self.EARLY :]
 
     def owner(self, device, distance, core):
         return 2 * ((device // 2 + distance) % self.chips) + (device % 2 + core) % 2
@@ -60,7 +64,7 @@
             whole = put(whole, up, self.chips - step)
             if step <= self.down_steps:
                 whole = put(whole, down, step)
-        return whole, block
+        return whole, [block], block
 
     def scatter_sum(self, product):
         keep = product([], list(range(self.chips)), None)
@@ -84,6 +88,7 @@
 
 class Grid(Ring):
     FAR_FIRST = (3, 2, 1, 0)
+    EARLY = 12
 
     def across(self, bits):
         return [(i, i ^ bits) for i in range(self.devices)]
@@ -92,6 +97,7 @@
         return jnp.bitwise_xor(device, 2 * distance + core)
 
     def gather(self, block, device):
+        first = []
         tokens, width = block.shape
         whole = jnp.zeros((tokens, width * self.devices), block.dtype)
         column = {0: block}
@@ -102,9 +108,11 @@
             for y in range(2):
                 part = lax.ppermute(column[z], "fsdp", self.across(2)) if y else column[z]
                 whole = place(whole, part, self.owner(device, 2 * z + y, 0))
-                part = lax.ppermute(part, "fsdp", self.sibling)
-                whole = place(whole, part, self.owner(device, 2 * z + y, 1))
-        return whole, column[1]
+                other = lax.ppermute(part, "fsdp", self.sibling)
+                whole = place(whole, other, self.owner(device, 2 * z + y, 1))
+                if z < 3:
+                    first += [part, other]
+        return whole, first, column[1]
 
     def scatter_sum(self, product):
         over_y = {}
@@ -154,18 +162,30 @@
     return send, find
 
 
+def squares_kernel(*refs):
+    blocks, squares = refs[:-1], refs[-1]
+    total = jnp.zeros(blocks[0].shape, F32)
+    for block in blocks:
+        h = block[...].astype(F32)
+        total = total + h * h
+    squares[...] = jnp.broadcast_to(jnp.sum(total, axis=1, keepdims=True), squares.shape)
+
+
 def forward_kernel(
-    hidden, parent_gain, child_gain, gate, up, kept, scale, child_gate, child_up, both_hid
+    ring, early, hidden, parent_gain, child_gain, gate, up, kept, scale, child_gate, child_up, both_hid
 ):
     tokens, features = hidden.shape
     pieces = 16
     piece = features // pieces
     cuts = [slice(k * piece, (k + 1) * piece) for k in range(pieces)]
-    squares = jnp.zeros((tokens, piece), F32)
-    for cols in cuts:
-        h = hidden[:, cols].astype(F32)
+    width = features // ring.devices
+    device = lax.axis_index("fsdp")
+    squares = jnp.zeros((tokens, width), F32)
+    for at in ring.late_at:
+        start = ring.owner(device, *at) * width
+        h = hidden[:, pl.ds(pl.multiple_of(start, width), width)].astype(F32)
         squares = squares + h * h
-    mean = jnp.sum(squares, axis=1, keepdims=True) / features
+    mean = (early[...][:, :1] + jnp.sum(squares, axis=1, keepdims=True)) / features
     inverse = 1.0 / jnp.sqrt(mean + 1e-05)
     scale[...] = jnp.broadcast_to(inverse, scale.shape)
     rows = gate.shape[0]
@@ -199,8 +219,22 @@
         part[...] = (out[:tokens] + out[tokens:]).astype(part.dtype)
 
 
+def early_kernel(ring, *refs):
+    blocks, (down, partial) = refs[:-2], refs[-2:]
+    tokens, width = blocks[0].shape
+    device = lax.axis_index("fsdp")
+    total = jnp.zeros(partial.shape, F32)
+    for block, at in zip(blocks, ring.first_at):
+        start = ring.owner(device, *at) * width
+        cols = pl.ds(pl.multiple_of(start, width), width)
+        total = total + dot_nt(block[...], down[:, cols])
+    partial[...] = total
+
+
 def backward_kernel(
     per_pair,
+    ring,
+    partial,
     slope,
     hidden,
     gate,
@@ -218,7 +252,12 @@
     devices, stride, _ = message.shape
     tokens = slope.shape[0]
     width = slope.shape[1] // devices
-    child_slope = dot_nt(slope[...], down[...])
+    device = lax.axis_index("fsdp")
+    child_slope = partial[...]
+    for at in ring.late_at:
+        start = ring.owner(device, *at) * width
+        cols = pl.ds(pl.multiple_of(start, width), width)
+        child_slope = child_slope + dot_nt(slope[:, cols], down[:, cols])
     g, u = child_gate[...], child_up[...]
     sig = jax.nn.sigmoid(g)
     live = kept[...] > 0
@@ -279,15 +318,23 @@
     devices, stride, tokens = received.shape
     message = received[...].reshape(devices * stride, tokens)
     tiles = [dot(places[kind], message).astype(BF16) for kind in range(3)]
-    both = jnp.concatenate(tiles[:2], axis=0)
+    empty = jnp.zeros_like(tiles[0])
+    left = jnp.concatenate(
+        [
+            jnp.concatenate([tiles[0], empty], axis=1),
+            jnp.concatenate([tiles[1], empty], axis=1),
+            jnp.concatenate([empty, tiles[2]], axis=1),
+        ],
+        axis=0,
+    )
     cut = min(features, 1024)
     copies = []
     for k in range(features // cut):
         cols = slice(k * cut, (k + 1) * cut)
-        made[2, :, cols] = dot(tiles[2], slope[:, cols]).astype(BF16)
-        out = dot(both, child_in[:, cols]).astype(BF16)
-        made[0, :, cols] = out[:rows]
-        made[1, :, cols] = out[rows:]
+        right = jnp.concatenate([child_in[:, cols], slope[:, cols]], axis=0)
+        out = dot(left, right).astype(BF16)
+        for kind in range(3):
+            made[kind, :, cols] = out[kind * rows : (kind + 1) * rows]
         for kind, grad in enumerate((grad_gate, grad_up, grad_down)):
             copy = pltpu.make_async_copy(made.at[kind, :, cols], grad.at[:, cols], done.at[kind, k])
             copy.start()
@@ -333,12 +380,15 @@
     stride = -(-(3 * per_pair + 2 * (width // 128)) // 8) * 8
     square = ((tokens, parent_rows), F32)
     gains = [parent_gain.reshape(1, features), child_gain.reshape(1, features)]
-    hidden_all, early = ring.gather(hidden, device)
+    hidden_all, first, early = ring.gather(hidden, device)
     kept = kept_rows(after(kept_index, early), device, parent_rows)
+    (early_squares,) = call(
+        squares_kernel, [((tokens, 128), F32)], first, limit=6, name="squares"
+    )
     scale, child_gate, child_up, both_hid = call(
-        forward_kernel,
+        functools.partial(forward_kernel, ring),
         [((tokens, 128), F32), square, square, ((2 * tokens, parent_rows), BF16)],
-        [hidden_all, *gains, gate_weight, up_weight, kept],
+        [early_squares, hidden_all, *gains, gate_weight, up_weight, kept],
         limit=6,
         name="forward",
     )
@@ -357,17 +407,25 @@
         )
 
     difference, last_sent = ring.scatter_sum(product)
-    slope_all, _ = ring.gather(difference.astype(BF16), device)
+    slope_all, first_slope, _ = ring.gather(difference.astype(BF16), device)
 
     kept_index, tile_owner, _ = lax.optimization_barrier((kept_index, tile_owner, last_sent))
     send, find = routing(kept_index, tile_owner, device, devices, parent_rows, stride)
     select = jnp.stack([jnp.roll(send, kind * per_pair, axis=0) for kind in range(3)])
     places = jnp.stack([jnp.roll(find, kind * per_pair, axis=1) for kind in range(3)])
     message = (devices, stride, tokens)
+    (partial,) = call(
+        functools.partial(early_kernel, ring),
+        [square],
+        [*first_slope, down_weight],
+        limit=6,
+        name="early",
+    )
     (sent,) = call(
-        functools.partial(backward_kernel, per_pair),
+        functools.partial(backward_kernel, per_pair, ring),
         [(message, BF16)],
         [
+            partial,
             slope_all,
             hidden_all,
             gate_weight,

time: 95.4 us -> 91.9 us (0.963)
  waiting for transfers between devices: 36.5 us -> 31.9 us
  starting transfers between devices: 36.6 us -> 38 us
    ppermute x4, waiting for transfers between devices: 7.52 us -> 3.42 us  [gather(): column[z] = lax.ppermute(block, 'fsdp', self.across(4 * z))]
    ppermute x8, waiting for transfers between devices: 10.8 us -> 9.4 us  [gather(): part = lax.ppermute(column[z], 'fsdp', self.across(2)) if y else column[z]]
    ppermute x8, starting transfers between devices: 9.31 us -> 10.4 us  [gather(): part = lax.ppermute(column[z], 'fsdp', self.across(2)) if y else column[z]]
    pallas_call x8 -> x10, Pallas kernels: 12.6 us -> 12.3 us  [call(): pl.pallas_call(kernel, out_shape=[jax.ShapeDtypeStruct(shape, dtype) for...]
  transfers between devices with their start and end apart: 40 -> 40, of which waited for: 18 -> 18; matrix products, arithmetic and copies ran while one was open for 3% -> 3% of each run, Pallas kernels for 5% -> 6%
where the time goes in v6:
time: 91.9 us; the launch traced here: 91.7 us
  starting transfers between devices  38 us (41%)
  waiting for transfers between devices  31.9 us (35%)
  Pallas kernels  12.3 us (13%)
  local copies, waits for them, and re-layouts  5.59 us (6%)
  between operations  1.46 us (2%)
  other arithmetic  1.29 us (1%)
  matrix products  1.09 us (1%)
    pallas_call x10, Pallas kernels, call(): pl.pallas_call(kernel, out_shape=[jax.ShapeDtypeStruct(shape, dtype) for...  12.3 us
    ppermute x8, starting transfers between devices, gather(): part = lax.ppermute(column[z], 'fsdp', self.across(2)) if y else column[z]  10.4 us
    ppermute x8, waiting for transfers between devices, gather(): part = lax.ppermute(column[z], 'fsdp', self.across(2)) if y else column[z]  9.4 us
    ppermute x4, starting transfers between devices, gather(): column[z] = lax.ppermute(block, 'fsdp', self.across(4 * z))  8.44 us
    ppermute x3, waiting for transfers between devices, scatter_sum(): arrived.append(lax.ppermute(sent, 'fsdp', self.across(4 * z)))  5.96 us
    unnamed x24, local copies, waits for them, and re-layouts  4.55 us
    ppermute x4, starting transfers between devices, scatter_sum(): over_y[z] = lax.ppermute(sent, 'fsdp', self.across(2))  4.31 us
    ppermute x2, starting transfers between devices, gather(): column[3] = lax.ppermute(after(block, column[1]), 'fsdp', self.across(12))  4.18 us
  transfers between devices with their start and end apart: 40, of which 18 were waited for; matrix products, arithmetic and copies ran while one was open for 3% of the time, Pallas kernels for 6%

profile of v6, /device:TPU:0, one launch (start us, length us, event | category | flops | bytes accessed | tf_op | source)
XLA Modules:
  0.0 91.7 jit_solution(940863208649794683)
XLA Ops:
  0.7 3.1 %collective-permute-start.3 = (bf16[128,512]{1,0:T(8,128)(2,1)}, bf16[128,512]{1,0:T(8,128)(2,1)S(1)}, u32[]{:S(2)}, u32[]{:S(2)}) collective-permute-start(bf16[128,512]{1,0:T(8,128)(2,1)} %refs_0_.1), channel_id=1, source_target_pairs={{0,4},{1,5},{2,6},{3,7},{4,0},{5,1},{6,2},{7,3},{8,12},{9,13},{10,... | collective-permute-start | bytes 393224 | tf_op jit(solution)/shard_map/ppermute | solution.py:105
  3.7 2.6 %collective-permute-start.7 = (bf16[128,512]{1,0:T(8,128)(2,1)}, bf16[128,512]{1,0:T(8,128)(2,1)S(1)}, u32[]{:S(2)}, u32[]{:S(2)}) collective-permute-start(bf16[128,512]{1,0:T(8,128)(2,1)} %refs_0_.1), channel_id=1, source_target_pairs={{0,8},{1,9},{2,10},{3,11},{4,12},{5,13},{6,14},{7,15},{8,0},{9,1},... | collective-permute-start | bytes 393224 | tf_op jit(solution)/shard_map/ppermute | solution.py:105
  6.3 1.5 %collective-permute-start.1 = (bf16[128,512]{1,0:T(8,128)(2,1)}, bf16[128,512]{1,0:T(8,128)(2,1)S(1)}, u32[]{:S(2)}, u32[]{:S(2)}) collective-permute-start(bf16[128,512]{1,0:T(8,128)(2,1)} %refs_0_.1), channel_id=1, source_target_pairs={{0,2},{1,3},{2,0},{3,1},{4,6},{5,7},{6,4},{7,5},{8,10},{9,11},{10,... | collective-permute-start | bytes 393224 | tf_op jit(solution)/shard_map/ppermute | solution.py:109
  7.9 0.5 collective-permute-start.16
  8.6 0.7 collective-permute-done.3.refs_4_
  9.3 3.5 %collective-permute-start.11 = (bf16[128,512]{1,0:T(8,128)(2,1)S(1)}, bf16[128,512]{1,0:T(8,128)(2,1)S(1)}, u32[]{:S(2)}, u32[]{:S(2)}) collective-permute-start(bf16[128,512]{1,0:T(8,128)(2,1)S(1)} %copy-done.7), channel_id=1, source_target_pairs={{0,12},{1,13},{2,14},{3,15},{4,8},{5,9},{6,10},{7,11},{8,4},{9,5},... | collective-permute-start | bytes 393224 | tf_op jit(solution)/shard_map/ppermute | solution.py:106
  13.2 1.6 %collective-permute-start.5 = (bf16[128,512]{1,0:T(8,128)(2,1)S(1)}, bf16[128,512]{1,0:T(8,128)(2,1)S(1)}, u32[]{:S(2)}, u32[]{:S(2)}) collective-permute-start(bf16[128,512]{1,0:T(8,128)(2,1)S(1)} %collective-permute-done.3.refs_4_), channel_id=1, source_target_pairs={{0,2},{1,3},{2,0},{3,1},{4,6},{5,7},{6,4},{7,5},{8,10},{9,11},{10,... | collective-permute-start | bytes 393224 | tf_op jit(solution)/shard_map/ppermute | solution.py:109
  14.8 0.6 collective-permute-start.4
  15.4 0.7 collective-permute-done.2.refs_3_
  16.7 1.5 %collective-permute-done.5.refs_6_ = bf16[128,512]{1,0:T(8,128)(2,1)S(1)} collective-permute-done((bf16[128,512]{1,0:T(8,128)(2,1)S(1)}, bf16[128,512]{1,0:T(8,128)(2,1)S(1)}, u32[]{:S(2)}, u32[]{:S(2)}) %collective-permute-start.5) | collective-permute-done | bytes 131104 | tf_op jit(solution)/shard_map/ppermute | solution.py:109
  18.2 1.9 %collective-permute-start.13 = (bf16[128,512]{1,0:T(8,128)(2,1)S(1)}, bf16[128,512]{1,0:T(8,128)(2,1)S(1)}, u32[]{:S(2)}, u32[]{:S(2)}) collective-permute-start(bf16[128,512]{1,0:T(8,128)(2,1)S(1)} %collective-permute-done.11), channel_id=1, source_target_pairs={{0,2},{1,3},{2,0},{3,1},{4,6},{5,7},{6,4},{7,5},{8,10},{9,11},{10,... | collective-permute-start | bytes 393224 | tf_op jit(solution)/shard_map/ppermute | solution.py:109
  20.2 2.3 %collective-permute-done.9.refs_10_ = bf16[128,512]{1,0:T(8,128)(2,1)S(1)} collective-permute-done((bf16[128,512]{1,0:T(8,128)(2,1)S(1)}, bf16[128,512]{1,0:T(8,128)(2,1)S(1)}, u32[]{:S(2)}, u32[]{:S(2)}) %collective-permute-start.9) | collective-permute-done | bytes 131104 | tf_op jit(solution)/shard_map/ppermute | solution.py:109
  22.4 2.0 %collective-permute-done.13 = bf16[128,512]{1,0:T(8,128)(2,1)S(1)} collective-permute-done((bf16[128,512]{1,0:T(8,128)(2,1)S(1)}, bf16[128,512]{1,0:T(8,128)(2,1)S(1)}, u32[]{:S(2)}, u32[]{:S(2)}) %collective-permute-start.13) | collective-permute-done | bytes 131104 | tf_op jit(solution)/shard_map/ppermute | solution.py:109
  24.5 0.5 collective-permute-start.14
  25.1 0.7 collective-permute-done.10.refs_11_
  26.4 2.0 %forward.1 = (f32[128,128]{1,0:T(8,128)S(1)}, f32[128,128]{1,0:T(8,128)S(1)}, f32[128,128]{1,0:T(8,128)S(1)}, bf16[256,128]{1,0:T(8,128)(2,1)S(1)}) custom-call(f32[128,128]{1,0:T(8,128)S(1)} %squares.1.early, bf16[128,8192]{1,0:T(8,128)(2,1)S(1)} %constant_dynamic-update-slice_fusion.16.hidden, f32[1,8192]{1,0:T(1,128)S(1)} %bitcast.32, ...), custom_call_target="tpu_custom_call" | custom-call | tf_op jit(solution)/shard_map/forward/pallas_call | solution.py:358
  28.6 1.1 %collective-permute-done.15.other_hid = bf16[256,128]{1,0:T(8,128)(2,1)S(1)} collective-permute-done((bf16[256,128]{1,0:T(8,128)(2,1)S(1)}, bf16[256,128]{1,0:T(8,128)(2,1)S(1)}, u32[]{:S(2)}, u32[]{:S(2)}) %collective-permute-start.15) | collective-permute-done | bytes 65568 | tf_op jit(solution)/shard_map/ppermute | solution.py:396
  30.0 0.9 %collective-permute-start.20 = (bf16[128,512]{1,0:T(8,128)(2,1)S(1)}, bf16[128,512]{1,0:T(8,128)(2,1)S(1)}, u32[]{:S(2)}, u32[]{:S(2)}) collective-permute-start(bf16[128,512]{1,0:T(8,128)(2,1)S(1)} %get-tuple-element.38), channel_id=1, source_target_pairs={{0,2},{1,3},{2,0},{3,1},{4,6},{5,7},{6,4},{7,5},{8,10},{9,11},{10,... | collective-permute-start | bytes 393224 | tf_op jit(solution)/shard_map/ppermute | solution.py:123
  31.3 1.2 %collective-permute-start.19 = (bf16[128,512]{1,0:T(8,128)(2,1)S(1)}, bf16[128,512]{1,0:T(8,128)(2,1)S(1)}, u32[]{:S(2)}, u32[]{:S(2)}) collective-permute-start(bf16[128,512]{1,0:T(8,128)(2,1)S(1)} %get-tuple-element.40), channel_id=1, source_target_pairs={{0,2},{1,3},{2,0},{3,1},{4,6},{5,7},{6,4},{7,5},{8,10},{9,11},{10,... | collective-permute-start | bytes 393224 | tf_op jit(solution)/shard_map/ppermute | solution.py:123
  32.8 0.9 %collective-permute-start.18 = (bf16[128,512]{1,0:T(8,128)(2,1)S(1)}, bf16[128,512]{1,0:T(8,128)(2,1)S(1)}, u32[]{:S(2)}, u32[]{:S(2)}) collective-permute-start(bf16[128,512]{1,0:T(8,128)(2,1)S(1)} %get-tuple-element.42), channel_id=1, source_target_pairs={{0,2},{1,3},{2,0},{3,1},{4,6},{5,7},{6,4},{7,5},{8,10},{9,11},{10,... | collective-permute-start | bytes 393224 | tf_op jit(solution)/shard_map/ppermute | solution.py:123
  34.0 1.2 %collective-permute-start.17 = (bf16[128,512]{1,0:T(8,128)(2,1)S(1)}, bf16[128,512]{1,0:T(8,128)(2,1)S(1)}, u32[]{:S(2)}, u32[]{:S(2)}) collective-permute-start(bf16[128,512]{1,0:T(8,128)(2,1)S(1)} %get-tuple-element.45), channel_id=1, source_target_pairs={{0,2},{1,3},{2,0},{3,1},{4,6},{5,7},{6,4},{7,5},{8,10},{9,11},{10,... | collective-permute-start | bytes 393224 | tf_op jit(solution)/shard_map/ppermute | solution.py:123
  35.3 1.2 %collective-permute-done.20 = bf16[128,512]{1,0:T(8,128)(2,1)S(1)} collective-permute-done((bf16[128,512]{1,0:T(8,128)(2,1)S(1)}, bf16[128,512]{1,0:T(8,128)(2,1)S(1)}, u32[]{:S(2)}, u32[]{:S(2)}) %collective-permute-start.20) | collective-permute-done | bytes 131104 | tf_op jit(solution)/shard_map/ppermute | solution.py:123
  36.5 2.1 %collective-permute-start.21 = (bf16[128,512]{1,0:T(8,128)(2,1)S(1)}, bf16[128,512]{1,0:T(8,128)(2,1)S(1)}, u32[]{:S(2)}, u32[]{:S(2)}) collective-permute-start(bf16[128,512]{1,0:T(8,128)(2,1)S(1)} %add_convert_fusion.3), channel_id=1, source_target_pairs={{0,12},{1,13},{2,14},{3,15},{4,8},{5,9},{6,10},{7,11},{8,4},{9,5},... | collective-permute-start | bytes 393224 | tf_op jit(solution)/shard_map/ppermute | solution.py:131
  38.6 0.7 collective-permute-done.19
  39.3 1.4 %collective-permute-start.22 = (bf16[128,512]{1,0:T(8,128)(2,1)S(1)}, bf16[128,512]{1,0:T(8,128)(2,1)S(1)}, u32[]{:S(2)}, u32[]{:S(2)}) collective-permute-start(bf16[128,512]{1,0:T(8,128)(2,1)S(1)} %add_convert_fusion.2), channel_id=1, source_target_pairs={{0,8},{1,9},{2,10},{3,11},{4,12},{5,13},{6,14},{7,15},{8,0},{9,1},... | collective-permute-start | bytes 393224 | tf_op jit(solution)/shard_map/ppermute | solution.py:131
  40.6 1.4 %collective-permute-done.18 = bf16[128,512]{1,0:T(8,128)(2,1)S(1)} collective-permute-done((bf16[128,512]{1,0:T(8,128)(2,1)S(1)}, bf16[128,512]{1,0:T(8,128)(2,1)S(1)}, u32[]{:S(2)}, u32[]{:S(2)}) %collective-permute-start.18) | collective-permute-done | bytes 131104 | tf_op jit(solution)/shard_map/ppermute | solution.py:123
  42.2 1.0 %fusion.2 = bf16[512,128]{1,0:T(8,128)(2,1)S(1)} fusion(s32[2048]{0:T(1024)S(1)} %fusion.5, s32[2048]{0:T(1024)S(1)} %broadcast_subtract_fusion), kind=kOutput, calls=%fused_computation.3 | convolution fusion | flops 269811712 | bytes 147456 | tf_op jit(solution)/shard_map/dot_general | solution.py:16
  44.4 5.0 %collective-permute-done.22 = bf16[128,512]{1,0:T(8,128)(2,1)S(1)} collective-permute-done((bf16[128,512]{1,0:T(8,128)(2,1)S(1)}, bf16[128,512]{1,0:T(8,128)(2,1)S(1)}, u32[]{:S(2)}, u32[]{:S(2)}) %collective-permute-start.22) | collective-permute-done | bytes 131104 | tf_op jit(solution)/shard_map/ppermute | solution.py:131
  49.4 0.9 %collective-permute-done.23 = bf16[128,512]{1,0:T(8,128)(2,1)S(1)} collective-permute-done((bf16[128,512]{1,0:T(8,128)(2,1)S(1)}, bf16[128,512]{1,0:T(8,128)(2,1)S(1)}, u32[]{:S(2)}, u32[]{:S(2)}) %collective-permute-start.23) | collective-permute-done | bytes 131104 | tf_op jit(solution)/shard_map/ppermute | solution.py:131
  50.9 2.5 %collective-permute-start.27 = (bf16[128,512]{1,0:T(8,128)(2,1)S(1)}, bf16[128,512]{1,0:T(8,128)(2,1)S(1)}, u32[]{:S(2)}, u32[]{:S(2)}) collective-permute-start(bf16[128,512]{1,0:T(8,128)(2,1)S(1)} %get-tuple-element.52.refs_0_), channel_id=1, source_target_pairs={{0,4},{1,5},{2,6},{3,7},{4,0},{5,1},{6,2},{7,3},{8,12},{9,13},{10,... | collective-permute-start | bytes 393224 | tf_op jit(solution)/shard_map/ppermute | solution.py:105
  53.4 1.5 %collective-permute-start.25 = (bf16[128,512]{1,0:T(8,128)(2,1)S(1)}, bf16[128,512]{1,0:T(8,128)(2,1)S(1)}, u32[]{:S(2)}, u32[]{:S(2)}) collective-permute-start(bf16[128,512]{1,0:T(8,128)(2,1)S(1)} %get-tuple-element.52.refs_0_), channel_id=1, source_target_pairs={{0,2},{1,3},{2,0},{3,1},{4,6},{5,7},{6,4},{7,5},{8,10},{9,11},{10,... | collective-permute-start | bytes 393224 | tf_op jit(solution)/shard_map/ppermute | solution.py:109
  55.0 2.8 %collective-permute-done.27.refs_4_ = bf16[128,512]{1,0:T(8,128)(2,1)S(1)} collective-permute-done((bf16[128,512]{1,0:T(8,128)(2,1)S(1)}, bf16[128,512]{1,0:T(8,128)(2,1)S(1)}, u32[]{:S(2)}, u32[]{:S(2)}) %collective-permute-start.27) | collective-permute-done | bytes 131104 | tf_op jit(solution)/shard_map/ppermute | solution.py:105
  57.8 0.7 collective-permute-start.35
  58.4 1.4 %collective-permute-start.33 = (bf16[128,512]{1,0:T(8,128)(2,1)S(1)}, bf16[128,512]{1,0:T(8,128)(2,1)S(1)}, u32[]{:S(2)}, u32[]{:S(2)}) collective-permute-start(bf16[128,512]{1,0:T(8,128)(2,1)S(1)} %collective-permute-done.31.refs_8_), channel_id=1, source_target_pairs={{0,2},{1,3},{2,0},{3,1},{4,6},{5,7},{6,4},{7,5},{8,10},{9,11},{10,... | collective-permute-start | bytes 393224 | tf_op jit(solution)/shard_map/ppermute | solution.py:109
  59.8 0.7 collective-permute-start.29
  60.7 3.8 %collective-permute-done.35 = bf16[128,512]{1,0:T(8,128)(2,1)S(1)} collective-permute-done((bf16[128,512]{1,0:T(8,128)(2,1)S(1)}, bf16[128,512]{1,0:T(8,128)(2,1)S(1)}, u32[]{:S(2)}, u32[]{:S(2)}) %collective-permute-start.35) | collective-permute-done | bytes 131104 | tf_op jit(solution)/shard_map/ppermute | solution.py:106
  64.5 1.4 %collective-permute-start.37 = (bf16[128,512]{1,0:T(8,128)(2,1)S(1)}, bf16[128,512]{1,0:T(8,128)(2,1)S(1)}, u32[]{:S(2)}, u32[]{:S(2)}) collective-permute-start(bf16[128,512]{1,0:T(8,128)(2,1)S(1)} %collective-permute-done.35), channel_id=1, source_target_pairs={{0,2},{1,3},{2,0},{3,1},{4,6},{5,7},{6,4},{7,5},{8,10},{9,11},{10,... | collective-permute-start | bytes 393224 | tf_op jit(solution)/shard_map/ppermute | solution.py:109
  66.8 3.6 %collective-permute-done.37 = bf16[128,512]{1,0:T(8,128)(2,1)S(1)} collective-permute-done((bf16[128,512]{1,0:T(8,128)(2,1)S(1)}, bf16[128,512]{1,0:T(8,128)(2,1)S(1)}, u32[]{:S(2)}, u32[]{:S(2)}) %collective-permute-start.37) | collective-permute-done | bytes 131104 | tf_op jit(solution)/shard_map/ppermute | solution.py:109
  70.7 0.6 early.1.partial
  71.3 0.5 collective-permute-done.38
  71.8 2.3 %backward.1 = bf16[16,32,128]{2,1,0:T(8,128)(2,1)} custom-call(f32[128,128]{1,0:T(8,128)S(1)} %early.1.partial, bf16[128,8192]{1,0:T(8,128)(2,1)S(1)} %constant_dynamic-update-slice_fusion.slope, bf16[128,8192]{1,0:T(8,128)(2,1)S(1)} %constant_dynamic-update-slice_fusion.16.hidden, bf16[128,8192]{1,0:T(8,128)(2,1)S(1)} %copy-done.3, ...), custom_call_target="tpu_custom_call" | custom-call | tf_op jit(solution)/shard_map/backward/pallas_call | solution.py:358
  74.2 3.9 %all-to-all-start = ((bf16[16,32,128]{2,1,0:T(8,128)(2,1)}), bf16[16,32,128]{2,1,0:T(8,128)(2,1)S(1)}, u32[]{:S(2)}, u32[]{:S(2)}) async-start(bf16[16,32,128]{2,1,0:T(8,128)(2,1)} %backward.1), calls=%async_computation | async-start | bytes 262144 | tf_op jit(solution)/shard_map/all_to_all | solution.py:445
  78.6 1.6 %copy-done.2 = bf16[128,8192]{1,0:T(8,128)(2,1)S(1)} copy-done((bf16[128,8192]{1,0:T(8,128)(2,1)S(1)}, bf16[128,8192]{1,0:T(8,128)(2,1)}, u32[]{:S(2)}) %copy-start.2) | copy-done | bytes 2097176
  80.2 2.0 %prepare.1 = (bf16[128,8192]{1,0:T(8,128)(2,1)S(1)}, f32[1,1]{1,0:T(1,128)}) custom-call(bf16[128,8192]{1,0:T(8,128)(2,1)S(1)} %copy-done.2, f32[128,128]{1,0:T(8,128)S(1)} %get-tuple-element.53.scale, f32[1,8192]{1,0:T(1,128)S(1)} %bitcast.31, bf16[128,8192]{1,0:T(8,128)(2,1)S(1)} %constant_dynamic-update-slice_fusion.slope), custom_call_target="tpu_custom_call" | custom-call | tf_op jit(solution)/shard_map/prepare/pallas_call | solution.py:358
  82.1 1.3 %copy-done.5 = bf16[128,8192]{1,0:T(8,128)(2,1)} copy-done((bf16[128,8192]{1,0:T(8,128)(2,1)}, bf16[128,8192]{1,0:T(8,128)(2,1)S(1)}, u32[]{:S(2)}) %copy-start.5) | copy-done | bytes 2097176
  83.4 2.6 %all-to-all-done.received = bf16[16,32,128]{2,1,0:T(8,128)(2,1)S(1)} async-done(((bf16[16,32,128]{2,1,0:T(8,128)(2,1)}), bf16[16,32,128]{2,1,0:T(8,128)(2,1)S(1)}, u32[]{:S(2)}, u32[]{:S(2)}) %all-to-all-start) | async-done | bytes 131104 | tf_op jit(solution)/shard_map/all_to_all | solution.py:445
  86.0 1.6 %copy-done.6 = bf16[128,8192]{1,0:T(8,128)(2,1)S(1)} copy-done((bf16[128,8192]{1,0:T(8,128)(2,1)S(1)}, bf16[128,8192]{1,0:T(8,128)(2,1)}, u32[]{:S(2)}) %copy-start.6) | copy-done | bytes 2097176
  87.6 3.9 %rows.1 = (bf16[128,8192]{1,0:T(8,128)(2,1)}, bf16[128,8192]{1,0:T(8,128)(2,1)}, bf16[128,8192]{1,0:T(8,128)(2,1)}, f32[1,512]{1,0:T(1,128)}) custom-call(bf16[16,32,128]{2,1,0:T(8,128)(2,1)S(1)} %all-to-all-done.received, bf16[3,128,512]{2,1,0:T(8,128)(2,1)S(1)} %pad_maximum_fusion.1.places, bf16[128,8192]{1,0:T(8,128)(2,1)S(1)} %copy-done.6, ...), custom_call_target="tpu_custom_call" | custom-call | tf_op jit(solution)/shard_map/rows/pallas_call | solution.py:358
  (127 shorter events, 6.9 us)
Async XLA Ops:
  0.6 7.9 %copy-start.7 = (bf16[128,512]{1,0:T(8,128)(2,1)S(1)}, bf16[128,512]{1,0:T(8,128)(2,1)}, u32[]{:S(2)}) copy-start(bf16[128,512]{1,0:T(8,128)(2,1)} %refs_0_.1) | copy-start | bytes 393220
  0.6 12.1 %copy-start.10 = (s32[2048]{0:T(1024)S(1)}, s32[2048]{0:T(1024)}, u32[]{:S(2)}) copy-start(s32[2048]{0:T(1024)} %param.14) | copy-start | bytes 24580
  0.7 8.6 %collective-permute-start.3 = (bf16[128,512]{1,0:T(8,128)(2,1)}, bf16[128,512]{1,0:T(8,128)(2,1)S(1)}, u32[]{:S(2)}, u32[]{:S(2)}) collective-permute-start(bf16[128,512]{1,0:T(8,128)(2,1)} %refs_0_.1), channel_id=1, source_target_pairs={{0,4},{1,5},{2,6},{3,7},{4,0},{5,1},{6,2},{7,3},{8,12},{9,13},{10,... | collective-permute-start | bytes 393224 | tf_op jit(solution)/shard_map/ppermute | solution.py:105
  3.7 11.1 %collective-permute-start.7 = (bf16[128,512]{1,0:T(8,128)(2,1)}, bf16[128,512]{1,0:T(8,128)(2,1)S(1)}, u32[]{:S(2)}, u32[]{:S(2)}) collective-permute-start(bf16[128,512]{1,0:T(8,128)(2,1)} %refs_0_.1), channel_id=1, source_target_pairs={{0,8},{1,9},{2,10},{3,11},{4,12},{5,13},{6,14},{7,15},{8,0},{9,1},... | collective-permute-start | bytes 393224 | tf_op jit(solution)/shard_map/ppermute | solution.py:105
  6.3 6.8 %collective-permute-start.1 = (bf16[128,512]{1,0:T(8,128)(2,1)}, bf16[128,512]{1,0:T(8,128)(2,1)S(1)}, u32[]{:S(2)}, u32[]{:S(2)}) collective-permute-start(bf16[128,512]{1,0:T(8,128)(2,1)} %refs_0_.1), channel_id=1, source_target_pairs={{0,2},{1,3},{2,0},{3,1},{4,6},{5,7},{6,4},{7,5},{8,10},{9,11},{10,... | collective-permute-start | bytes 393224 | tf_op jit(solution)/shard_map/ppermute | solution.py:109
  7.8 6.9 %collective-permute-start = (bf16[128,512]{1,0:T(8,128)(2,1)}, bf16[128,512]{1,0:T(8,128)(2,1)S(1)}, u32[]{:S(2)}, u32[]{:S(2)}) collective-permute-start(bf16[128,512]{1,0:T(8,128)(2,1)} %refs_0_.1), channel_id=1, source_target_pairs={{0,1},{1,0},{2,3},{3,2},{4,5},{5,4},{6,7},{7,6},{8,9},{9,8},{10,11... | collective-permute-start | bytes 393224 | tf_op jit(solution)/shard_map/ppermute | solution.py:111
  7.9 21.9 %collective-permute-start.16 = (bf16[128,8192]{1,0:T(8,128)(2,1)}, bf16[128,8192]{1,0:T(8,128)(2,1)S(1)}, u32[]{:S(2)}, u32[]{:S(2)}) collective-permute-start(bf16[128,8192]{1,0:T(8,128)(2,1)} %down.9), channel_id=1, source_target_pairs={{0,1},{1,0},{2,3},{3,2},{4,5},{5,4},{6,7},{7,6},{8,9},{9,8},{10,11... | collective-permute-start | bytes 6291464 | tf_op jit(solution)/shard_map/ppermute | solution.py:395
  9.3 7.4 %collective-permute-start.11 = (bf16[128,512]{1,0:T(8,128)(2,1)S(1)}, bf16[128,512]{1,0:T(8,128)(2,1)S(1)}, u32[]{:S(2)}, u32[]{:S(2)}) collective-permute-start(bf16[128,512]{1,0:T(8,128)(2,1)S(1)} %copy-done.7), channel_id=1, source_target_pairs={{0,12},{1,13},{2,14},{3,15},{4,8},{5,9},{6,10},{7,11},{8,4},{9,5},... | collective-permute-start | bytes 393224 | tf_op jit(solution)/shard_map/ppermute | solution.py:106
  13.2 5.0 %collective-permute-start.5 = (bf16[128,512]{1,0:T(8,128)(2,1)S(1)}, bf16[128,512]{1,0:T(8,128)(2,1)S(1)}, u32[]{:S(2)}, u32[]{:S(2)}) collective-permute-start(bf16[128,512]{1,0:T(8,128)(2,1)S(1)} %collective-permute-done.3.refs_4_), channel_id=1, source_target_pairs={{0,2},{1,3},{2,0},{3,1},{4,6},{5,7},{6,4},{7,5},{8,10},{9,11},{10,... | collective-permute-start | bytes 393224 | tf_op jit(solution)/shard_map/ppermute | solution.py:109
  14.8 1.3 %collective-permute-start.2 = (bf16[128,512]{1,0:T(8,128)(2,1)S(1)}, bf16[128,512]{1,0:T(8,128)(2,1)S(1)}, u32[]{:S(2)}, u32[]{:S(2)}) collective-permute-start(bf16[128,512]{1,0:T(8,128)(2,1)S(1)} %collective-permute-done.1.refs_2_), channel_id=1, source_target_pairs={{0,1},{1,0},{2,3},{3,2},{4,5},{5,4},{6,7},{7,6},{8,9},{9,8},{10,11... | collective-permute-start | bytes 393224 | tf_op jit(solution)/shard_map/ppermute | solution.py:111
  14.8 5.3 %collective-permute-start.4 = (bf16[128,512]{1,0:T(8,128)(2,1)S(1)}, bf16[128,512]{1,0:T(8,128)(2,1)S(1)}, u32[]{:S(2)}, u32[]{:S(2)}) collective-permute-start(bf16[128,512]{1,0:T(8,128)(2,1)S(1)} %collective-permute-done.3.refs_4_), channel_id=1, source_target_pairs={{0,1},{1,0},{2,3},{3,2},{4,5},{5,4},{6,7},{7,6},{8,9},{9,8},{10,11... | collective-permute-start | bytes 393224 | tf_op jit(solution)/shard_map/ppermute | solution.py:111
  16.1 6.3 %collective-permute-start.9 = (bf16[128,512]{1,0:T(8,128)(2,1)S(1)}, bf16[128,512]{1,0:T(8,128)(2,1)S(1)}, u32[]{:S(2)}, u32[]{:S(2)}) collective-permute-start(bf16[128,512]{1,0:T(8,128)(2,1)S(1)} %collective-permute-done.7.refs_8_), channel_id=1, source_target_pairs={{0,2},{1,3},{2,0},{3,1},{4,6},{5,7},{6,4},{7,5},{8,10},{9,11},{10,... | collective-permute-start | bytes 393224 | tf_op jit(solution)/shard_map/ppermute | solution.py:109
  16.7 8.4 %collective-permute-start.8 = (bf16[128,512]{1,0:T(8,128)(2,1)S(1)}, bf16[128,512]{1,0:T(8,128)(2,1)S(1)}, u32[]{:S(2)}, u32[]{:S(2)}) collective-permute-start(bf16[128,512]{1,0:T(8,128)(2,1)S(1)} %collective-permute-done.7.refs_8_), channel_id=1, source_target_pairs={{0,1},{1,0},{2,3},{3,2},{4,5},{5,4},{6,7},{7,6},{8,9},{9,8},{10,11... | collective-permute-start | bytes 393224 | tf_op jit(solution)/shard_map/ppermute | solution.py:111
  18.2 6.3 %collective-permute-start.13 = (bf16[128,512]{1,0:T(8,128)(2,1)S(1)}, bf16[128,512]{1,0:T(8,128)(2,1)S(1)}, u32[]{:S(2)}, u32[]{:S(2)}) collective-permute-start(bf16[128,512]{1,0:T(8,128)(2,1)S(1)} %collective-permute-done.11), channel_id=1, source_target_pairs={{0,2},{1,3},{2,0},{3,1},{4,6},{5,7},{6,4},{7,5},{8,10},{9,11},{10,... | collective-permute-start | bytes 393224 | tf_op jit(solution)/shard_map/ppermute | solution.py:109
  20.1 4.4 %collective-permute-start.6 = (bf16[128,512]{1,0:T(8,128)(2,1)S(1)}, bf16[128,512]{1,0:T(8,128)(2,1)S(1)}, u32[]{:S(2)}, u32[]{:S(2)}) collective-permute-start(bf16[128,512]{1,0:T(8,128)(2,1)S(1)} %collective-permute-done.5.refs_6_), channel_id=1, source_target_pairs={{0,1},{1,0},{2,3},{3,2},{4,5},{5,4},{6,7},{7,6},{8,9},{9,8},{10,11... | collective-permute-start | bytes 393224 | tf_op jit(solution)/shard_map/ppermute | solution.py:111
  20.1 6.2 %copy-start.3 = (bf16[128,8192]{1,0:T(8,128)(2,1)S(1)}, bf16[128,8192]{1,0:T(8,128)(2,1)}, u32[]{:S(2)}) copy-start(bf16[128,8192]{1,0:T(8,128)(2,1)} %gate.3) | copy-start | bytes 6291460
  20.1 6.2 %copy-start.4 = (bf16[128,8192]{1,0:T(8,128)(2,1)S(1)}, bf16[128,8192]{1,0:T(8,128)(2,1)}, u32[]{:S(2)}) copy-start(bf16[128,8192]{1,0:T(8,128)(2,1)} %up.3) | copy-start | bytes 6291460
  20.1 6.2 %copy-start.8 = (f32[8192]{0:T(1024)S(1)}, f32[8192]{0:T(1024)}, u32[]{:S(2)}) copy-start(f32[8192]{0:T(1024)} %param.10) | copy-start | bytes 98308
  20.1 6.2 %copy-start.9 = (f32[8192]{0:T(1024)S(1)}, f32[8192]{0:T(1024)}, u32[]{:S(2)}) copy-start(f32[8192]{0:T(1024)} %param.9) | copy-start | bytes 98308
  22.4 3.4 %collective-permute-start.12 = (bf16[128,512]{1,0:T(8,128)(2,1)S(1)}, bf16[128,512]{1,0:T(8,128)(2,1)S(1)}, u32[]{:S(2)}, u32[]{:S(2)}) collective-permute-start(bf16[128,512]{1,0:T(8,128)(2,1)S(1)} %collective-permute-done.11), channel_id=1, source_target_pairs={{0,1},{1,0},{2,3},{3,2},{4,5},{5,4},{6,7},{7,6},{8,9},{9,8},{10,11... | collective-permute-start | bytes 393224 | tf_op jit(solution)/shard_map/ppermute | solution.py:111
  24.5 1.3 %collective-permute-start.10 = (bf16[128,512]{1,0:T(8,128)(2,1)S(1)}, bf16[128,512]{1,0:T(8,128)(2,1)S(1)}, u32[]{:S(2)}, u32[]{:S(2)}) collective-permute-start(bf16[128,512]{1,0:T(8,128)(2,1)S(1)} %collective-permute-done.9.refs_10_), channel_id=1, source_target_pairs={{0,1},{1,0},{2,3},{3,2},{4,5},{5,4},{6,7},{7,6},{8,9},{9,8},{10,11... | collective-permute-start | bytes 393224 | tf_op jit(solution)/shard_map/ppermute | solution.py:111
  24.5 1.8 %collective-permute-start.14 = (bf16[128,512]{1,0:T(8,128)(2,1)S(1)}, bf16[128,512]{1,0:T(8,128)(2,1)S(1)}, u32[]{:S(2)}, u32[]{:S(2)}) collective-permute-start(bf16[128,512]{1,0:T(8,128)(2,1)S(1)} %collective-permute-done.13), channel_id=1, source_target_pairs={{0,1},{1,0},{2,3},{3,2},{4,5},{5,4},{6,7},{7,6},{8,9},{9,8},{10,11... | collective-permute-start | bytes 393224 | tf_op jit(solution)/shard_map/ppermute | solution.py:111
  26.3 45.5 %copy-start.1 = (bf16[128,8192]{1,0:T(8,128)(2,1)}, bf16[128,8192]{1,0:T(8,128)(2,1)S(1)}, u32[]{:S(2)}) copy-start(bf16[128,8192]{1,0:T(8,128)(2,1)S(1)} %constant_dynamic-update-slice_fusion.16.hidden) | copy-start | bytes 6291460
  28.4 1.3 %collective-permute-start.15 = (bf16[256,128]{1,0:T(8,128)(2,1)S(1)}, bf16[256,128]{1,0:T(8,128)(2,1)S(1)}, u32[]{:S(2)}, u32[]{:S(2)}) collective-permute-start(bf16[256,128]{1,0:T(8,128)(2,1)S(1)} %get-tuple-element.43.hid.both_hid), channel_id=1, source_target_pairs={{0,1},{1,0},{2,3},{3,2},{4,5},{5,4},{6,7},{7,6},{8,9},{9,8},{10,11... | collective-permute-start | bytes 196616 | tf_op jit(solution)/shard_map/ppermute | solution.py:396
  30.0 6.4 %collective-permute-start.20 = (bf16[128,512]{1,0:T(8,128)(2,1)S(1)}, bf16[128,512]{1,0:T(8,128)(2,1)S(1)}, u32[]{:S(2)}, u32[]{:S(2)}) collective-permute-start(bf16[128,512]{1,0:T(8,128)(2,1)S(1)} %get-tuple-element.38), channel_id=1, source_target_pairs={{0,2},{1,3},{2,0},{3,1},{4,6},{5,7},{6,4},{7,5},{8,10},{9,11},{10,... | collective-permute-start | bytes 393224 | tf_op jit(solution)/shard_map/ppermute | solution.py:123
  31.3 8.0 %collective-permute-start.19 = (bf16[128,512]{1,0:T(8,128)(2,1)S(1)}, bf16[128,512]{1,0:T(8,128)(2,1)S(1)}, u32[]{:S(2)}, u32[]{:S(2)}) collective-permute-start(bf16[128,512]{1,0:T(8,128)(2,1)S(1)} %get-tuple-element.40), channel_id=1, source_target_pairs={{0,2},{1,3},{2,0},{3,1},{4,6},{5,7},{6,4},{7,5},{8,10},{9,11},{10,... | collective-permute-start | bytes 393224 | tf_op jit(solution)/shard_map/ppermute | solution.py:123
  32.8 9.3 %copy-start.11 = (s32[16]{0:T(128)S(1)}, s32[16]{0:T(128)}, u32[]{:S(2)}) copy-start(s32[16]{0:T(128)} %param.15) | copy-start | bytes 196
  32.8 9.2 %collective-permute-start.18 = (bf16[128,512]{1,0:T(8,128)(2,1)S(1)}, bf16[128,512]{1,0:T(8,128)(2,1)S(1)}, u32[]{:S(2)}, u32[]{:S(2)}) collective-permute-start(bf16[128,512]{1,0:T(8,128)(2,1)S(1)} %get-tuple-element.42), channel_id=1, source_target_pairs={{0,2},{1,3},{2,0},{3,1},{4,6},{5,7},{6,4},{7,5},{8,10},{9,11},{10,... | collective-permute-start | bytes 393224 | tf_op jit(solution)/shard_map/ppermute | solution.py:123
  34.0 10.0 %collective-permute-start.17 = (bf16[128,512]{1,0:T(8,128)(2,1)S(1)}, bf16[128,512]{1,0:T(8,128)(2,1)S(1)}, u32[]{:S(2)}, u32[]{:S(2)}) collective-permute-start(bf16[128,512]{1,0:T(8,128)(2,1)S(1)} %get-tuple-element.45), channel_id=1, source_target_pairs={{0,2},{1,3},{2,0},{3,1},{4,6},{5,7},{6,4},{7,5},{8,10},{9,11},{10,... | collective-permute-start | bytes 393224 | tf_op jit(solution)/shard_map/ppermute | solution.py:123
  36.5 7.9 %collective-permute-start.21 = (bf16[128,512]{1,0:T(8,128)(2,1)S(1)}, bf16[128,512]{1,0:T(8,128)(2,1)S(1)}, u32[]{:S(2)}, u32[]{:S(2)}) collective-permute-start(bf16[128,512]{1,0:T(8,128)(2,1)S(1)} %add_convert_fusion.3), channel_id=1, source_target_pairs={{0,12},{1,13},{2,14},{3,15},{4,8},{5,9},{6,10},{7,11},{8,4},{9,5},... | collective-permute-start | bytes 393224 | tf_op jit(solution)/shard_map/ppermute | solution.py:131
  39.3 10.1 %collective-permute-start.22 = (bf16[128,512]{1,0:T(8,128)(2,1)S(1)}, bf16[128,512]{1,0:T(8,128)(2,1)S(1)}, u32[]{:S(2)}, u32[]{:S(2)}) collective-permute-start(bf16[128,512]{1,0:T(8,128)(2,1)S(1)} %add_convert_fusion.2), channel_id=1, source_target_pairs={{0,8},{1,9},{2,10},{3,11},{4,12},{5,13},{6,14},{7,15},{8,0},{9,1},... | collective-permute-start | bytes 393224 | tf_op jit(solution)/shard_map/ppermute | solution.py:131
  43.3 7.1 %collective-permute-start.23 = (bf16[128,512]{1,0:T(8,128)(2,1)S(1)}, bf16[128,512]{1,0:T(8,128)(2,1)S(1)}, u32[]{:S(2)}, u32[]{:S(2)}) collective-permute-start(bf16[128,512]{1,0:T(8,128)(2,1)S(1)} %add_convert_fusion.1), channel_id=1, source_target_pairs={{0,4},{1,5},{2,6},{3,7},{4,0},{5,1},{6,2},{7,3},{8,12},{9,13},{10,... | collective-permute-start | bytes 393224 | tf_op jit(solution)/shard_map/ppermute | solution.py:131
  50.7 7.8 %collective-permute-start.31 = (bf16[128,512]{1,0:T(8,128)(2,1)S(1)}, bf16[128,512]{1,0:T(8,128)(2,1)S(1)}, u32[]{:S(2)}, u32[]{:S(2)}) collective-permute-start(bf16[128,512]{1,0:T(8,128)(2,1)S(1)} %get-tuple-element.52.refs_0_), channel_id=1, source_target_pairs={{0,8},{1,9},{2,10},{3,11},{4,12},{5,13},{6,14},{7,15},{8,0},{9,1},... | collective-permute-start | bytes 393224 | tf_op jit(solution)/shard_map/ppermute | solution.py:105
  50.9 6.8 %collective-permute-start.27 = (bf16[128,512]{1,0:T(8,128)(2,1)S(1)}, bf16[128,512]{1,0:T(8,128)(2,1)S(1)}, u32[]{:S(2)}, u32[]{:S(2)}) collective-permute-start(bf16[128,512]{1,0:T(8,128)(2,1)S(1)} %get-tuple-element.52.refs_0_), channel_id=1, source_target_pairs={{0,4},{1,5},{2,6},{3,7},{4,0},{5,1},{6,2},{7,3},{8,12},{9,13},{10,... | collective-permute-start | bytes 393224 | tf_op jit(solution)/shard_map/ppermute | solution.py:105
  53.4 6.4 %collective-permute-start.25 = (bf16[128,512]{1,0:T(8,128)(2,1)S(1)}, bf16[128,512]{1,0:T(8,128)(2,1)S(1)}, u32[]{:S(2)}, u32[]{:S(2)}) collective-permute-start(bf16[128,512]{1,0:T(8,128)(2,1)S(1)} %get-tuple-element.52.refs_0_), channel_id=1, source_target_pairs={{0,2},{1,3},{2,0},{3,1},{4,6},{5,7},{6,4},{7,5},{8,10},{9,11},{10,... | collective-permute-start | bytes 393224 | tf_op jit(solution)/shard_map/ppermute | solution.py:109
  54.9 5.5 %collective-permute-start.24 = (bf16[128,512]{1,0:T(8,128)(2,1)S(1)}, bf16[128,512]{1,0:T(8,128)(2,1)S(1)}, u32[]{:S(2)}, u32[]{:S(2)}) collective-permute-start(bf16[128,512]{1,0:T(8,128)(2,1)S(1)} %get-tuple-element.52.refs_0_), channel_id=1, source_target_pairs={{0,1},{1,0},{2,3},{3,2},{4,5},{5,4},{6,7},{7,6},{8,9},{9,8},{10,11... | collective-permute-start | bytes 393224 | tf_op jit(solution)/shard_map/ppermute | solution.py:111
  57.8 6.8 %collective-permute-start.35 = (bf16[128,512]{1,0:T(8,128)(2,1)S(1)}, bf16[128,512]{1,0:T(8,128)(2,1)S(1)}, u32[]{:S(2)}, u32[]{:S(2)}) collective-permute-start(bf16[128,512]{1,0:T(8,128)(2,1)S(1)} %get-tuple-element.52.refs_0_), channel_id=1, source_target_pairs={{0,12},{1,13},{2,14},{3,15},{4,8},{5,9},{6,10},{7,11},{8,4},{9,5},... | collective-permute-start | bytes 393224 | tf_op jit(solution)/shard_map/ppermute | solution.py:106
  58.4 7.5 %collective-permute-start.33 = (bf16[128,512]{1,0:T(8,128)(2,1)S(1)}, bf16[128,512]{1,0:T(8,128)(2,1)S(1)}, u32[]{:S(2)}, u32[]{:S(2)}) collective-permute-start(bf16[128,512]{1,0:T(8,128)(2,1)S(1)} %collective-permute-done.31.refs_8_), channel_id=1, source_target_pairs={{0,2},{1,3},{2,0},{3,1},{4,6},{5,7},{6,4},{7,5},{8,10},{9,11},{10,... | collective-permute-start | bytes 393224 | tf_op jit(solution)/shard_map/ppermute | solution.py:109
  59.8 10.7 %collective-permute-start.32 = (bf16[128,512]{1,0:T(8,128)(2,1)S(1)}, bf16[128,512]{1,0:T(8,128)(2,1)S(1)}, u32[]{:S(2)}, u32[]{:S(2)}) collective-permute-start(bf16[128,512]{1,0:T(8,128)(2,1)S(1)} %collective-permute-done.31.refs_8_), channel_id=1, source_target_pairs={{0,1},{1,0},{2,3},{3,2},{4,5},{5,4},{6,7},{7,6},{8,9},{9,8},{10,11... | collective-permute-start | bytes 393224 | tf_op jit(solution)/shard_map/ppermute | solution.py:111
  59.8 6.4 %collective-permute-start.29 = (bf16[128,512]{1,0:T(8,128)(2,1)S(1)}, bf16[128,512]{1,0:T(8,128)(2,1)S(1)}, u32[]{:S(2)}, u32[]{:S(2)}) collective-permute-start(bf16[128,512]{1,0:T(8,128)(2,1)S(1)} %collective-permute-done.27.refs_4_), channel_id=1, source_target_pairs={{0,2},{1,3},{2,0},{3,1},{4,6},{5,7},{6,4},{7,5},{8,10},{9,11},{10,... | collective-permute-start | bytes 393224 | tf_op jit(solution)/shard_map/ppermute | solution.py:109
  60.5 4.1 %collective-permute-start.26 = (bf16[128,512]{1,0:T(8,128)(2,1)S(1)}, bf16[128,512]{1,0:T(8,128)(2,1)S(1)}, u32[]{:S(2)}, u32[]{:S(2)}) collective-permute-start(bf16[128,512]{1,0:T(8,128)(2,1)S(1)} %collective-permute-done.25.refs_2_), channel_id=1, source_target_pairs={{0,1},{1,0},{2,3},{3,2},{4,5},{5,4},{6,7},{7,6},{8,9},{9,8},{10,11... | collective-permute-start | bytes 393224 | tf_op jit(solution)/shard_map/ppermute | solution.py:111
  64.5 2.0 %collective-permute-start.28 = (bf16[128,512]{1,0:T(8,128)(2,1)S(1)}, bf16[128,512]{1,0:T(8,128)(2,1)S(1)}, u32[]{:S(2)}, u32[]{:S(2)}) collective-permute-start(bf16[128,512]{1,0:T(8,128)(2,1)S(1)} %collective-permute-done.27.refs_4_), channel_id=1, source_target_pairs={{0,1},{1,0},{2,3},{3,2},{4,5},{5,4},{6,7},{7,6},{8,9},{9,8},{10,11... | collective-permute-start | bytes 393224 | tf_op jit(solution)/shard_map/ppermute | solution.py:111
  64.5 5.9 %collective-permute-start.37 = (bf16[128,512]{1,0:T(8,128)(2,1)S(1)}, bf16[128,512]{1,0:T(8,128)(2,1)S(1)}, u32[]{:S(2)}, u32[]{:S(2)}) collective-permute-start(bf16[128,512]{1,0:T(8,128)(2,1)S(1)} %collective-permute-done.35), channel_id=1, source_target_pairs={{0,2},{1,3},{2,0},{3,1},{4,6},{5,7},{6,4},{7,5},{8,10},{9,11},{10,... | collective-permute-start | bytes 393224 | tf_op jit(solution)/shard_map/ppermute | solution.py:109
  66.0 4.7 %collective-permute-start.36 = (bf16[128,512]{1,0:T(8,128)(2,1)S(1)}, bf16[128,512]{1,0:T(8,128)(2,1)S(1)}, u32[]{:S(2)}, u32[]{:S(2)}) collective-permute-start(bf16[128,512]{1,0:T(8,128)(2,1)S(1)} %collective-permute-done.35), channel_id=1, source_target_pairs={{0,1},{1,0},{2,3},{3,2},{4,5},{5,4},{6,7},{7,6},{8,9},{9,8},{10,11... | collective-permute-start | bytes 393224 | tf_op jit(solution)/shard_map/ppermute | solution.py:111
  66.3 4.3 %collective-permute-start.34 = (bf16[128,512]{1,0:T(8,128)(2,1)S(1)}, bf16[128,512]{1,0:T(8,128)(2,1)S(1)}, u32[]{:S(2)}, u32[]{:S(2)}) collective-permute-start(bf16[128,512]{1,0:T(8,128)(2,1)S(1)} %collective-permute-done.33.refs_10_), channel_id=1, source_target_pairs={{0,1},{1,0},{2,3},{3,2},{4,5},{5,4},{6,7},{7,6},{8,9},{9,8},{10,11... | collective-permute-start | bytes 393224 | tf_op jit(solution)/shard_map/ppermute | solution.py:111
  66.6 3.9 %collective-permute-start.30 = (bf16[128,512]{1,0:T(8,128)(2,1)S(1)}, bf16[128,512]{1,0:T(8,128)(2,1)S(1)}, u32[]{:S(2)}, u32[]{:S(2)}) collective-permute-start(bf16[128,512]{1,0:T(8,128)(2,1)S(1)} %collective-permute-done.29.refs_6_), channel_id=1, source_target_pairs={{0,1},{1,0},{2,3},{3,2},{4,5},{5,4},{6,7},{7,6},{8,9},{9,8},{10,11... | collective-permute-start | bytes 393224 | tf_op jit(solution)/shard_map/ppermute | solution.py:111
  70.5 1.3 %collective-permute-start.38 = (bf16[128,512]{1,0:T(8,128)(2,1)S(1)}, bf16[128,512]{1,0:T(8,128)(2,1)S(1)}, u32[]{:S(2)}, u32[]{:S(2)}) collective-permute-start(bf16[128,512]{1,0:T(8,128)(2,1)S(1)} %collective-permute-done.37), channel_id=1, source_target_pairs={{0,1},{1,0},{2,3},{3,2},{4,5},{5,4},{6,7},{7,6},{8,9},{9,8},{10,11... | collective-permute-start | bytes 393224 | tf_op jit(solution)/shard_map/ppermute | solution.py:111
  74.2 11.9 %all-to-all-start = ((bf16[16,32,128]{2,1,0:T(8,128)(2,1)}), bf16[16,32,128]{2,1,0:T(8,128)(2,1)S(1)}, u32[]{:S(2)}, u32[]{:S(2)}) async-start(bf16[16,32,128]{2,1,0:T(8,128)(2,1)} %backward.1), calls=%async_computation | async-start | bytes 262144 | tf_op jit(solution)/shard_map/all_to_all | solution.py:445
  (4 other events, 7.9 us)

commit v7 on v6

--- a/solution.py
+++ b/solution.py
@@ -88,7 +88,7 @@
 
 class Grid(Ring):
     FAR_FIRST = (3, 2, 1, 0)
-    EARLY = 12
+    EARLY = 14
 
     def across(self, bits):
         return [(i, i ^ bits) for i in range(self.devices)]
@@ -110,7 +110,7 @@
                 whole = place(whole, part, self.owner(device, 2 * z + y, 0))
                 other = lax.ppermute(part, "fsdp", self.sibling)
                 whole = place(whole, other, self.owner(device, 2 * z + y, 1))
-                if z < 3:
+                if 2 * z + y < 7:
                     first += [part, other]
         return whole, first, column[1]
 

time: 91.9 us -> 91.8 us (level)
  no operation moved by 1% of the time
where the time goes in v7:
time: 91.8 us; the launch traced here: 91.5 us
  starting transfers between devices  38 us (41%)
  waiting for transfers between devices  31.8 us (35%)
  Pallas kernels  12.2 us (13%)
  local copies, waits for them, and re-layouts  5.59 us (6%)
  between operations  1.46 us (2%)
  other arithmetic  1.29 us (1%)
  matrix products  1.11 us (1%)
    pallas_call x10, Pallas kernels, call(): pl.pallas_call(kernel, out_shape=[jax.ShapeDtypeStruct(shape, dtype) for...  12.2 us
    ppermute x8, starting transfers between devices, gather(): part = lax.ppermute(column[z], 'fsdp', self.across(2)) if y else column[z]  10.4 us
    ppermute x8, waiting for transfers between devices, gather(): part = lax.ppermute(column[z], 'fsdp', self.across(2)) if y else column[z]  9.41 us
    ppermute x4, starting transfers between devices, gather(): column[z] = lax.ppermute(block, 'fsdp', self.across(4 * z))  8.43 us
    ppermute x3, waiting for transfers between devices, scatter_sum(): arrived.append(lax.ppermute(sent, 'fsdp', self.across(4 * z)))  5.97 us
    unnamed x24, local copies, waits for them, and re-layouts  4.55 us
    ppermute x4, starting transfers between devices, scatter_sum(): over_y[z] = lax.ppermute(sent, 'fsdp', self.across(2))  4.31 us
    ppermute x2, starting transfers between devices, gather(): column[3] = lax.ppermute(after(block, column[1]), 'fsdp', self.across(12))  4.19 us
  transfers between devices with their start and end apart: 40, of which 18 were waited for; matrix products, arithmetic and copies ran while one was open for 3% of the time, Pallas kernels for 6%

profile of v7, /device:TPU:0, one launch (start us, length us, event | category | flops | bytes accessed | tf_op | source)
XLA Modules:
  0.0 91.5 jit_solution(7037229643165827225)
XLA Ops:
  0.7 3.1 %collective-permute-start.3 = (bf16[128,512]{1,0:T(8,128)(2,1)}, bf16[128,512]{1,0:T(8,128)(2,1)S(1)}, u32[]{:S(2)}, u32[]{:S(2)}) collective-permute-start(bf16[128,512]{1,0:T(8,128)(2,1)} %refs_0_.1), channel_id=1, source_target_pairs={{0,4},{1,5},{2,6},{3,7},{4,0},{5,1},{6,2},{7,3},{8,12},{9,13},{10,... | collective-permute-start | bytes 393224 | tf_op jit(solution)/shard_map/ppermute | solution.py:105
  3.7 2.6 %collective-permute-start.7 = (bf16[128,512]{1,0:T(8,128)(2,1)}, bf16[128,512]{1,0:T(8,128)(2,1)S(1)}, u32[]{:S(2)}, u32[]{:S(2)}) collective-permute-start(bf16[128,512]{1,0:T(8,128)(2,1)} %refs_0_.1), channel_id=1, source_target_pairs={{0,8},{1,9},{2,10},{3,11},{4,12},{5,13},{6,14},{7,15},{8,0},{9,1},... | collective-permute-start | bytes 393224 | tf_op jit(solution)/shard_map/ppermute | solution.py:105
  6.3 1.5 %collective-permute-start.1 = (bf16[128,512]{1,0:T(8,128)(2,1)}, bf16[128,512]{1,0:T(8,128)(2,1)S(1)}, u32[]{:S(2)}, u32[]{:S(2)}) collective-permute-start(bf16[128,512]{1,0:T(8,128)(2,1)} %refs_0_.1), channel_id=1, source_target_pairs={{0,2},{1,3},{2,0},{3,1},{4,6},{5,7},{6,4},{7,5},{8,10},{9,11},{10,... | collective-permute-start | bytes 393224 | tf_op jit(solution)/shard_map/ppermute | solution.py:109
  7.9 0.5 collective-permute-start.16
  8.6 0.7 collective-permute-done.3.refs_4_
  9.3 3.5 %collective-permute-start.11 = (bf16[128,512]{1,0:T(8,128)(2,1)S(1)}, bf16[128,512]{1,0:T(8,128)(2,1)S(1)}, u32[]{:S(2)}, u32[]{:S(2)}) collective-permute-start(bf16[128,512]{1,0:T(8,128)(2,1)S(1)} %copy-done.7), channel_id=1, source_target_pairs={{0,12},{1,13},{2,14},{3,15},{4,8},{5,9},{6,10},{7,11},{8,4},{9,5},... | collective-permute-start | bytes 393224 | tf_op jit(solution)/shard_map/ppermute | solution.py:106
  13.2 1.6 %collective-permute-start.5 = (bf16[128,512]{1,0:T(8,128)(2,1)S(1)}, bf16[128,512]{1,0:T(8,128)(2,1)S(1)}, u32[]{:S(2)}, u32[]{:S(2)}) collective-permute-start(bf16[128,512]{1,0:T(8,128)(2,1)S(1)} %collective-permute-done.3.refs_4_), channel_id=1, source_target_pairs={{0,2},{1,3},{2,0},{3,1},{4,6},{5,7},{6,4},{7,5},{8,10},{9,11},{10,... | collective-permute-start | bytes 393224 | tf_op jit(solution)/shard_map/ppermute | solution.py:109
  14.8 0.6 collective-permute-start.4
  15.4 0.7 collective-permute-done.2.refs_3_
  16.1 0.5 collective-permute-start.9
  16.7 1.5 %collective-permute-done.5.refs_6_ = bf16[128,512]{1,0:T(8,128)(2,1)S(1)} collective-permute-done((bf16[128,512]{1,0:T(8,128)(2,1)S(1)}, bf16[128,512]{1,0:T(8,128)(2,1)S(1)}, u32[]{:S(2)}, u32[]{:S(2)}) %collective-permute-start.5) | collective-permute-done | bytes 131104 | tf_op jit(solution)/shard_map/ppermute | solution.py:109
  18.2 1.9 %collective-permute-start.13 = (bf16[128,512]{1,0:T(8,128)(2,1)S(1)}, bf16[128,512]{1,0:T(8,128)(2,1)S(1)}, u32[]{:S(2)}, u32[]{:S(2)}) collective-permute-start(bf16[128,512]{1,0:T(8,128)(2,1)S(1)} %collective-permute-done.11.refs_12_), channel_id=1, source_target_pairs={{0,2},{1,3},{2,0},{3,1},{4,6},{5,7},{6,4},{7,5},{8,10},{9,11},{10,... | collective-permute-start | bytes 393224 | tf_op jit(solution)/shard_map/ppermute | solution.py:109
  20.2 2.3 %collective-permute-done.9.refs_10_ = bf16[128,512]{1,0:T(8,128)(2,1)S(1)} collective-permute-done((bf16[128,512]{1,0:T(8,128)(2,1)S(1)}, bf16[128,512]{1,0:T(8,128)(2,1)S(1)}, u32[]{:S(2)}, u32[]{:S(2)}) %collective-permute-start.9) | collective-permute-done | bytes 131104 | tf_op jit(solution)/shard_map/ppermute | solution.py:109
  22.4 2.0 %collective-permute-done.13 = bf16[128,512]{1,0:T(8,128)(2,1)S(1)} collective-permute-done((bf16[128,512]{1,0:T(8,128)(2,1)S(1)}, bf16[128,512]{1,0:T(8,128)(2,1)S(1)}, u32[]{:S(2)}, u32[]{:S(2)}) %collective-permute-start.13) | collective-permute-done | bytes 131104 | tf_op jit(solution)/shard_map/ppermute | solution.py:109
  24.5 0.5 collective-permute-start.14
  25.1 0.7 collective-permute-done.10.refs_11_
  26.4 2.0 %forward.1 = (f32[128,128]{1,0:T(8,128)S(1)}, f32[128,128]{1,0:T(8,128)S(1)}, f32[128,128]{1,0:T(8,128)S(1)}, bf16[256,128]{1,0:T(8,128)(2,1)S(1)}) custom-call(f32[128,128]{1,0:T(8,128)S(1)} %squares.1.early, bf16[128,8192]{1,0:T(8,128)(2,1)S(1)} %constant_dynamic-update-slice_fusion.16.hidden, f32[1,8192]{1,0:T(1,128)S(1)} %bitcast.32, ...), custom_call_target="tpu_custom_call" | custom-call | tf_op jit(solution)/shard_map/forward/pallas_call | solution.py:358
  28.6 1.1 %collective-permute-done.15.other_hid = bf16[256,128]{1,0:T(8,128)(2,1)S(1)} collective-permute-done((bf16[256,128]{1,0:T(8,128)(2,1)S(1)}, bf16[256,128]{1,0:T(8,128)(2,1)S(1)}, u32[]{:S(2)}, u32[]{:S(2)}) %collective-permute-start.15) | collective-permute-done | bytes 65568 | tf_op jit(solution)/shard_map/ppermute | solution.py:396
  30.0 0.9 %collective-permute-start.20 = (bf16[128,512]{1,0:T(8,128)(2,1)S(1)}, bf16[128,512]{1,0:T(8,128)(2,1)S(1)}, u32[]{:S(2)}, u32[]{:S(2)}) collective-permute-start(bf16[128,512]{1,0:T(8,128)(2,1)S(1)} %get-tuple-element.38), channel_id=1, source_target_pairs={{0,2},{1,3},{2,0},{3,1},{4,6},{5,7},{6,4},{7,5},{8,10},{9,11},{10,... | collective-permute-start | bytes 393224 | tf_op jit(solution)/shard_map/ppermute | solution.py:123
  31.3 1.2 %collective-permute-start.19 = (bf16[128,512]{1,0:T(8,128)(2,1)S(1)}, bf16[128,512]{1,0:T(8,128)(2,1)S(1)}, u32[]{:S(2)}, u32[]{:S(2)}) collective-permute-start(bf16[128,512]{1,0:T(8,128)(2,1)S(1)} %get-tuple-element.40), channel_id=1, source_target_pairs={{0,2},{1,3},{2,0},{3,1},{4,6},{5,7},{6,4},{7,5},{8,10},{9,11},{10,... | collective-permute-start | bytes 393224 | tf_op jit(solution)/shard_map/ppermute | solution.py:123
  32.8 0.9 %collective-permute-start.18 = (bf16[128,512]{1,0:T(8,128)(2,1)S(1)}, bf16[128,512]{1,0:T(8,128)(2,1)S(1)}, u32[]{:S(2)}, u32[]{:S(2)}) collective-permute-start(bf16[128,512]{1,0:T(8,128)(2,1)S(1)} %get-tuple-element.42), channel_id=1, source_target_pairs={{0,2},{1,3},{2,0},{3,1},{4,6},{5,7},{6,4},{7,5},{8,10},{9,11},{10,... | collective-permute-start | bytes 393224 | tf_op jit(solution)/shard_map/ppermute | solution.py:123
  34.0 1.2 %collective-permute-start.17 = (bf16[128,512]{1,0:T(8,128)(2,1)S(1)}, bf16[128,512]{1,0:T(8,128)(2,1)S(1)}, u32[]{:S(2)}, u32[]{:S(2)}) collective-permute-start(bf16[128,512]{1,0:T(8,128)(2,1)S(1)} %get-tuple-element.45), channel_id=1, source_target_pairs={{0,2},{1,3},{2,0},{3,1},{4,6},{5,7},{6,4},{7,5},{8,10},{9,11},{10,... | collective-permute-start | bytes 393224 | tf_op jit(solution)/shard_map/ppermute | solution.py:123
  35.3 1.2 %collective-permute-done.20 = bf16[128,512]{1,0:T(8,128)(2,1)S(1)} collective-permute-done((bf16[128,512]{1,0:T(8,128)(2,1)S(1)}, bf16[128,512]{1,0:T(8,128)(2,1)S(1)}, u32[]{:S(2)}, u32[]{:S(2)}) %collective-permute-start.20) | collective-permute-done | bytes 131104 | tf_op jit(solution)/shard_map/ppermute | solution.py:123
  36.5 2.1 %collective-permute-start.21 = (bf16[128,512]{1,0:T(8,128)(2,1)S(1)}, bf16[128,512]{1,0:T(8,128)(2,1)S(1)}, u32[]{:S(2)}, u32[]{:S(2)}) collective-permute-start(bf16[128,512]{1,0:T(8,128)(2,1)S(1)} %add_convert_fusion.3), channel_id=1, source_target_pairs={{0,12},{1,13},{2,14},{3,15},{4,8},{5,9},{6,10},{7,11},{8,4},{9,5},... | collective-permute-start | bytes 393224 | tf_op jit(solution)/shard_map/ppermute | solution.py:131
  38.6 0.7 collective-permute-done.19
  39.3 1.4 %collective-permute-start.22 = (bf16[128,512]{1,0:T(8,128)(2,1)S(1)}, bf16[128,512]{1,0:T(8,128)(2,1)S(1)}, u32[]{:S(2)}, u32[]{:S(2)}) collective-permute-start(bf16[128,512]{1,0:T(8,128)(2,1)S(1)} %add_convert_fusion.2), channel_id=1, source_target_pairs={{0,8},{1,9},{2,10},{3,11},{4,12},{5,13},{6,14},{7,15},{8,0},{9,1},... | collective-permute-start | bytes 393224 | tf_op jit(solution)/shard_map/ppermute | solution.py:131
  40.6 1.4 %collective-permute-done.18 = bf16[128,512]{1,0:T(8,128)(2,1)S(1)} collective-permute-done((bf16[128,512]{1,0:T(8,128)(2,1)S(1)}, bf16[128,512]{1,0:T(8,128)(2,1)S(1)}, u32[]{:S(2)}, u32[]{:S(2)}) %collective-permute-start.18) | collective-permute-done | bytes 131104 | tf_op jit(solution)/shard_map/ppermute | solution.py:123
  42.2 1.0 %fusion.2 = bf16[512,128]{1,0:T(8,128)(2,1)S(1)} fusion(s32[2048]{0:T(1024)S(1)} %fusion.5, s32[2048]{0:T(1024)S(1)} %broadcast_subtract_fusion), kind=kOutput, calls=%fused_computation.3 | convolution fusion | flops 269811712 | bytes 147456 | tf_op jit(solution)/shard_map/dot_general | solution.py:16
  44.4 5.0 %collective-permute-done.22 = bf16[128,512]{1,0:T(8,128)(2,1)S(1)} collective-permute-done((bf16[128,512]{1,0:T(8,128)(2,1)S(1)}, bf16[128,512]{1,0:T(8,128)(2,1)S(1)}, u32[]{:S(2)}, u32[]{:S(2)}) %collective-permute-start.22) | collective-permute-done | bytes 131104 | tf_op jit(solution)/shard_map/ppermute | solution.py:131
  49.4 0.9 %collective-permute-done.23 = bf16[128,512]{1,0:T(8,128)(2,1)S(1)} collective-permute-done((bf16[128,512]{1,0:T(8,128)(2,1)S(1)}, bf16[128,512]{1,0:T(8,128)(2,1)S(1)}, u32[]{:S(2)}, u32[]{:S(2)}) %collective-permute-start.23) | collective-permute-done | bytes 131104 | tf_op jit(solution)/shard_map/ppermute | solution.py:131
  50.9 2.5 %collective-permute-start.27 = (bf16[128,512]{1,0:T(8,128)(2,1)S(1)}, bf16[128,512]{1,0:T(8,128)(2,1)S(1)}, u32[]{:S(2)}, u32[]{:S(2)}) collective-permute-start(bf16[128,512]{1,0:T(8,128)(2,1)S(1)} %get-tuple-element.52.refs_0_), channel_id=1, source_target_pairs={{0,4},{1,5},{2,6},{3,7},{4,0},{5,1},{6,2},{7,3},{8,12},{9,13},{10,... | collective-permute-start | bytes 393224 | tf_op jit(solution)/shard_map/ppermute | solution.py:105
  53.4 1.5 %collective-permute-start.25 = (bf16[128,512]{1,0:T(8,128)(2,1)S(1)}, bf16[128,512]{1,0:T(8,128)(2,1)S(1)}, u32[]{:S(2)}, u32[]{:S(2)}) collective-permute-start(bf16[128,512]{1,0:T(8,128)(2,1)S(1)} %get-tuple-element.52.refs_0_), channel_id=1, source_target_pairs={{0,2},{1,3},{2,0},{3,1},{4,6},{5,7},{6,4},{7,5},{8,10},{9,11},{10,... | collective-permute-start | bytes 393224 | tf_op jit(solution)/shard_map/ppermute | solution.py:109
  55.0 2.7 %collective-permute-done.27.refs_4_ = bf16[128,512]{1,0:T(8,128)(2,1)S(1)} collective-permute-done((bf16[128,512]{1,0:T(8,128)(2,1)S(1)}, bf16[128,512]{1,0:T(8,128)(2,1)S(1)}, u32[]{:S(2)}, u32[]{:S(2)}) %collective-permute-start.27) | collective-permute-done | bytes 131104 | tf_op jit(solution)/shard_map/ppermute | solution.py:105
  57.8 0.7 collective-permute-start.35
  58.4 1.4 %collective-permute-start.33 = (bf16[128,512]{1,0:T(8,128)(2,1)S(1)}, bf16[128,512]{1,0:T(8,128)(2,1)S(1)}, u32[]{:S(2)}, u32[]{:S(2)}) collective-permute-start(bf16[128,512]{1,0:T(8,128)(2,1)S(1)} %collective-permute-done.31.refs_8_), channel_id=1, source_target_pairs={{0,2},{1,3},{2,0},{3,1},{4,6},{5,7},{6,4},{7,5},{8,10},{9,11},{10,... | collective-permute-start | bytes 393224 | tf_op jit(solution)/shard_map/ppermute | solution.py:109
  59.8 0.7 collective-permute-start.29
  60.8 3.8 %collective-permute-done.35.refs_12_ = bf16[128,512]{1,0:T(8,128)(2,1)S(1)} collective-permute-done((bf16[128,512]{1,0:T(8,128)(2,1)S(1)}, bf16[128,512]{1,0:T(8,128)(2,1)S(1)}, u32[]{:S(2)}, u32[]{:S(2)}) %collective-permute-start.35) | collective-permute-done | bytes 131104 | tf_op jit(solution)/shard_map/ppermute | solution.py:106
  64.5 1.4 %collective-permute-start.37 = (bf16[128,512]{1,0:T(8,128)(2,1)S(1)}, bf16[128,512]{1,0:T(8,128)(2,1)S(1)}, u32[]{:S(2)}, u32[]{:S(2)}) collective-permute-start(bf16[128,512]{1,0:T(8,128)(2,1)S(1)} %collective-permute-done.35.refs_12_), channel_id=1, source_target_pairs={{0,2},{1,3},{2,0},{3,1},{4,6},{5,7},{6,4},{7,5},{8,10},{9,11},{10,... | collective-permute-start | bytes 393224 | tf_op jit(solution)/shard_map/ppermute | solution.py:109
  66.8 3.6 %collective-permute-done.37 = bf16[128,512]{1,0:T(8,128)(2,1)S(1)} collective-permute-done((bf16[128,512]{1,0:T(8,128)(2,1)S(1)}, bf16[128,512]{1,0:T(8,128)(2,1)S(1)}, u32[]{:S(2)}, u32[]{:S(2)}) %collective-permute-start.37) | collective-permute-done | bytes 131104 | tf_op jit(solution)/shard_map/ppermute | solution.py:109
  70.7 0.6 early.1.partial
  71.8 2.2 %backward.1 = bf16[16,32,128]{2,1,0:T(8,128)(2,1)} custom-call(f32[128,128]{1,0:T(8,128)S(1)} %early.1.partial, bf16[128,8192]{1,0:T(8,128)(2,1)S(1)} %constant_dynamic-update-slice_fusion.slope, bf16[128,8192]{1,0:T(8,128)(2,1)S(1)} %constant_dynamic-update-slice_fusion.16.hidden, bf16[128,8192]{1,0:T(8,128)(2,1)S(1)} %copy-done.3, ...), custom_call_target="tpu_custom_call" | custom-call | tf_op jit(solution)/shard_map/backward/pallas_call | solution.py:358
  74.0 3.9 %all-to-all-start = ((bf16[16,32,128]{2,1,0:T(8,128)(2,1)}), bf16[16,32,128]{2,1,0:T(8,128)(2,1)S(1)}, u32[]{:S(2)}, u32[]{:S(2)}) async-start(bf16[16,32,128]{2,1,0:T(8,128)(2,1)} %backward.1), calls=%async_computation | async-start | bytes 262144 | tf_op jit(solution)/shard_map/all_to_all | solution.py:445
  78.4 1.6 %copy-done.2 = bf16[128,8192]{1,0:T(8,128)(2,1)S(1)} copy-done((bf16[128,8192]{1,0:T(8,128)(2,1)S(1)}, bf16[128,8192]{1,0:T(8,128)(2,1)}, u32[]{:S(2)}) %copy-start.2) | copy-done | bytes 2097176
  80.0 2.0 %prepare.1 = (bf16[128,8192]{1,0:T(8,128)(2,1)S(1)}, f32[1,1]{1,0:T(1,128)}) custom-call(bf16[128,8192]{1,0:T(8,128)(2,1)S(1)} %copy-done.2, f32[128,128]{1,0:T(8,128)S(1)} %get-tuple-element.53.scale, f32[1,8192]{1,0:T(1,128)S(1)} %bitcast.31, bf16[128,8192]{1,0:T(8,128)(2,1)S(1)} %constant_dynamic-update-slice_fusion.slope), custom_call_target="tpu_custom_call" | custom-call | tf_op jit(solution)/shard_map/prepare/pallas_call | solution.py:358
  82.0 1.3 %copy-done.5 = bf16[128,8192]{1,0:T(8,128)(2,1)} copy-done((bf16[128,8192]{1,0:T(8,128)(2,1)}, bf16[128,8192]{1,0:T(8,128)(2,1)S(1)}, u32[]{:S(2)}) %copy-start.5) | copy-done | bytes 2097176
  83.3 2.6 %all-to-all-done.received = bf16[16,32,128]{2,1,0:T(8,128)(2,1)S(1)} async-done(((bf16[16,32,128]{2,1,0:T(8,128)(2,1)}), bf16[16,32,128]{2,1,0:T(8,128)(2,1)S(1)}, u32[]{:S(2)}, u32[]{:S(2)}) %all-to-all-start) | async-done | bytes 131104 | tf_op jit(solution)/shard_map/all_to_all | solution.py:445
  85.9 1.6 %copy-done.6 = bf16[128,8192]{1,0:T(8,128)(2,1)S(1)} copy-done((bf16[128,8192]{1,0:T(8,128)(2,1)S(1)}, bf16[128,8192]{1,0:T(8,128)(2,1)}, u32[]{:S(2)}) %copy-start.6) | copy-done | bytes 2097176
  87.5 3.9 %rows.1 = (bf16[128,8192]{1,0:T(8,128)(2,1)}, bf16[128,8192]{1,0:T(8,128)(2,1)}, bf16[128,8192]{1,0:T(8,128)(2,1)}, f32[1,512]{1,0:T(1,128)}) custom-call(bf16[16,32,128]{2,1,0:T(8,128)(2,1)S(1)} %all-to-all-done.received, bf16[3,128,512]{2,1,0:T(8,128)(2,1)S(1)} %pad_maximum_fusion.1.places, bf16[128,8192]{1,0:T(8,128)(2,1)S(1)} %copy-done.6, ...), custom_call_target="tpu_custom_call" | custom-call | tf_op jit(solution)/shard_map/rows/pallas_call | solution.py:358
  (127 shorter events, 6.9 us)
Async XLA Ops:
  0.6 7.9 %copy-start.7 = (bf16[128,512]{1,0:T(8,128)(2,1)S(1)}, bf16[128,512]{1,0:T(8,128)(2,1)}, u32[]{:S(2)}) copy-start(bf16[128,512]{1,0:T(8,128)(2,1)} %refs_0_.1) | copy-start | bytes 393220
  0.6 12.1 %copy-start.10 = (s32[2048]{0:T(1024)S(1)}, s32[2048]{0:T(1024)}, u32[]{:S(2)}) copy-start(s32[2048]{0:T(1024)} %param.14) | copy-start | bytes 24580
  0.7 8.6 %collective-permute-start.3 = (bf16[128,512]{1,0:T(8,128)(2,1)}, bf16[128,512]{1,0:T(8,128)(2,1)S(1)}, u32[]{:S(2)}, u32[]{:S(2)}) collective-permute-start(bf16[128,512]{1,0:T(8,128)(2,1)} %refs_0_.1), channel_id=1, source_target_pairs={{0,4},{1,5},{2,6},{3,7},{4,0},{5,1},{6,2},{7,3},{8,12},{9,13},{10,... | collective-permute-start | bytes 393224 | tf_op jit(solution)/shard_map/ppermute | solution.py:105
  3.7 11.1 %collective-permute-start.7 = (bf16[128,512]{1,0:T(8,128)(2,1)}, bf16[128,512]{1,0:T(8,128)(2,1)S(1)}, u32[]{:S(2)}, u32[]{:S(2)}) collective-permute-start(bf16[128,512]{1,0:T(8,128)(2,1)} %refs_0_.1), channel_id=1, source_target_pairs={{0,8},{1,9},{2,10},{3,11},{4,12},{5,13},{6,14},{7,15},{8,0},{9,1},... | collective-permute-start | bytes 393224 | tf_op jit(solution)/shard_map/ppermute | solution.py:105
  6.3 6.8 %collective-permute-start.1 = (bf16[128,512]{1,0:T(8,128)(2,1)}, bf16[128,512]{1,0:T(8,128)(2,1)S(1)}, u32[]{:S(2)}, u32[]{:S(2)}) collective-permute-start(bf16[128,512]{1,0:T(8,128)(2,1)} %refs_0_.1), channel_id=1, source_target_pairs={{0,2},{1,3},{2,0},{3,1},{4,6},{5,7},{6,4},{7,5},{8,10},{9,11},{10,... | collective-permute-start | bytes 393224 | tf_op jit(solution)/shard_map/ppermute | solution.py:109
  7.8 6.9 %collective-permute-start = (bf16[128,512]{1,0:T(8,128)(2,1)}, bf16[128,512]{1,0:T(8,128)(2,1)S(1)}, u32[]{:S(2)}, u32[]{:S(2)}) collective-permute-start(bf16[128,512]{1,0:T(8,128)(2,1)} %refs_0_.1), channel_id=1, source_target_pairs={{0,1},{1,0},{2,3},{3,2},{4,5},{5,4},{6,7},{7,6},{8,9},{9,8},{10,11... | collective-permute-start | bytes 393224 | tf_op jit(solution)/shard_map/ppermute | solution.py:111
  7.9 21.9 %collective-permute-start.16 = (bf16[128,8192]{1,0:T(8,128)(2,1)}, bf16[128,8192]{1,0:T(8,128)(2,1)S(1)}, u32[]{:S(2)}, u32[]{:S(2)}) collective-permute-start(bf16[128,8192]{1,0:T(8,128)(2,1)} %down.9), channel_id=1, source_target_pairs={{0,1},{1,0},{2,3},{3,2},{4,5},{5,4},{6,7},{7,6},{8,9},{9,8},{10,11... | collective-permute-start | bytes 6291464 | tf_op jit(solution)/shard_map/ppermute | solution.py:395
  9.3 7.4 %collective-permute-start.11 = (bf16[128,512]{1,0:T(8,128)(2,1)S(1)}, bf16[128,512]{1,0:T(8,128)(2,1)S(1)}, u32[]{:S(2)}, u32[]{:S(2)}) collective-permute-start(bf16[128,512]{1,0:T(8,128)(2,1)S(1)} %copy-done.7), channel_id=1, source_target_pairs={{0,12},{1,13},{2,14},{3,15},{4,8},{5,9},{6,10},{7,11},{8,4},{9,5},... | collective-permute-start | bytes 393224 | tf_op jit(solution)/shard_map/ppermute | solution.py:106
  13.2 5.0 %collective-permute-start.5 = (bf16[128,512]{1,0:T(8,128)(2,1)S(1)}, bf16[128,512]{1,0:T(8,128)(2,1)S(1)}, u32[]{:S(2)}, u32[]{:S(2)}) collective-permute-start(bf16[128,512]{1,0:T(8,128)(2,1)S(1)} %collective-permute-done.3.refs_4_), channel_id=1, source_target_pairs={{0,2},{1,3},{2,0},{3,1},{4,6},{5,7},{6,4},{7,5},{8,10},{9,11},{10,... | collective-permute-start | bytes 393224 | tf_op jit(solution)/shard_map/ppermute | solution.py:109
  14.8 1.3 %collective-permute-start.2 = (bf16[128,512]{1,0:T(8,128)(2,1)S(1)}, bf16[128,512]{1,0:T(8,128)(2,1)S(1)}, u32[]{:S(2)}, u32[]{:S(2)}) collective-permute-start(bf16[128,512]{1,0:T(8,128)(2,1)S(1)} %collective-permute-done.1.refs_2_), channel_id=1, source_target_pairs={{0,1},{1,0},{2,3},{3,2},{4,5},{5,4},{6,7},{7,6},{8,9},{9,8},{10,11... | collective-permute-start | bytes 393224 | tf_op jit(solution)/shard_map/ppermute | solution.py:111
  14.8 5.3 %collective-permute-start.4 = (bf16[128,512]{1,0:T(8,128)(2,1)S(1)}, bf16[128,512]{1,0:T(8,128)(2,1)S(1)}, u32[]{:S(2)}, u32[]{:S(2)}) collective-permute-start(bf16[128,512]{1,0:T(8,128)(2,1)S(1)} %collective-permute-done.3.refs_4_), channel_id=1, source_target_pairs={{0,1},{1,0},{2,3},{3,2},{4,5},{5,4},{6,7},{7,6},{8,9},{9,8},{10,11... | collective-permute-start | bytes 393224 | tf_op jit(solution)/shard_map/ppermute | solution.py:111
  16.1 6.3 %collective-permute-start.9 = (bf16[128,512]{1,0:T(8,128)(2,1)S(1)}, bf16[128,512]{1,0:T(8,128)(2,1)S(1)}, u32[]{:S(2)}, u32[]{:S(2)}) collective-permute-start(bf16[128,512]{1,0:T(8,128)(2,1)S(1)} %collective-permute-done.7.refs_8_), channel_id=1, source_target_pairs={{0,2},{1,3},{2,0},{3,1},{4,6},{5,7},{6,4},{7,5},{8,10},{9,11},{10,... | collective-permute-start | bytes 393224 | tf_op jit(solution)/shard_map/ppermute | solution.py:109
  16.7 8.4 %collective-permute-start.8 = (bf16[128,512]{1,0:T(8,128)(2,1)S(1)}, bf16[128,512]{1,0:T(8,128)(2,1)S(1)}, u32[]{:S(2)}, u32[]{:S(2)}) collective-permute-start(bf16[128,512]{1,0:T(8,128)(2,1)S(1)} %collective-permute-done.7.refs_8_), channel_id=1, source_target_pairs={{0,1},{1,0},{2,3},{3,2},{4,5},{5,4},{6,7},{7,6},{8,9},{9,8},{10,11... | collective-permute-start | bytes 393224 | tf_op jit(solution)/shard_map/ppermute | solution.py:111
  18.2 6.3 %collective-permute-start.13 = (bf16[128,512]{1,0:T(8,128)(2,1)S(1)}, bf16[128,512]{1,0:T(8,128)(2,1)S(1)}, u32[]{:S(2)}, u32[]{:S(2)}) collective-permute-start(bf16[128,512]{1,0:T(8,128)(2,1)S(1)} %collective-permute-done.11.refs_12_), channel_id=1, source_target_pairs={{0,2},{1,3},{2,0},{3,1},{4,6},{5,7},{6,4},{7,5},{8,10},{9,11},{10,... | collective-permute-start | bytes 393224 | tf_op jit(solution)/shard_map/ppermute | solution.py:109
  20.1 4.4 %collective-permute-start.6 = (bf16[128,512]{1,0:T(8,128)(2,1)S(1)}, bf16[128,512]{1,0:T(8,128)(2,1)S(1)}, u32[]{:S(2)}, u32[]{:S(2)}) collective-permute-start(bf16[128,512]{1,0:T(8,128)(2,1)S(1)} %collective-permute-done.5.refs_6_), channel_id=1, source_target_pairs={{0,1},{1,0},{2,3},{3,2},{4,5},{5,4},{6,7},{7,6},{8,9},{9,8},{10,11... | collective-permute-start | bytes 393224 | tf_op jit(solution)/shard_map/ppermute | solution.py:111
  20.1 6.2 %copy-start.3 = (bf16[128,8192]{1,0:T(8,128)(2,1)S(1)}, bf16[128,8192]{1,0:T(8,128)(2,1)}, u32[]{:S(2)}) copy-start(bf16[128,8192]{1,0:T(8,128)(2,1)} %gate.3) | copy-start | bytes 6291460
  20.1 6.2 %copy-start.4 = (bf16[128,8192]{1,0:T(8,128)(2,1)S(1)}, bf16[128,8192]{1,0:T(8,128)(2,1)}, u32[]{:S(2)}) copy-start(bf16[128,8192]{1,0:T(8,128)(2,1)} %up.3) | copy-start | bytes 6291460
  20.1 6.2 %copy-start.8 = (f32[8192]{0:T(1024)S(1)}, f32[8192]{0:T(1024)}, u32[]{:S(2)}) copy-start(f32[8192]{0:T(1024)} %param.10) | copy-start | bytes 98308
  20.2 6.2 %copy-start.9 = (f32[8192]{0:T(1024)S(1)}, f32[8192]{0:T(1024)}, u32[]{:S(2)}) copy-start(f32[8192]{0:T(1024)} %param.9) | copy-start | bytes 98308
  22.4 3.4 %collective-permute-start.12 = (bf16[128,512]{1,0:T(8,128)(2,1)S(1)}, bf16[128,512]{1,0:T(8,128)(2,1)S(1)}, u32[]{:S(2)}, u32[]{:S(2)}) collective-permute-start(bf16[128,512]{1,0:T(8,128)(2,1)S(1)} %collective-permute-done.11.refs_12_), channel_id=1, source_target_pairs={{0,1},{1,0},{2,3},{3,2},{4,5},{5,4},{6,7},{7,6},{8,9},{9,8},{10,11... | collective-permute-start | bytes 393224 | tf_op jit(solution)/shard_map/ppermute | solution.py:111
  24.5 1.3 %collective-permute-start.10 = (bf16[128,512]{1,0:T(8,128)(2,1)S(1)}, bf16[128,512]{1,0:T(8,128)(2,1)S(1)}, u32[]{:S(2)}, u32[]{:S(2)}) collective-permute-start(bf16[128,512]{1,0:T(8,128)(2,1)S(1)} %collective-permute-done.9.refs_10_), channel_id=1, source_target_pairs={{0,1},{1,0},{2,3},{3,2},{4,5},{5,4},{6,7},{7,6},{8,9},{9,8},{10,11... | collective-permute-start | bytes 393224 | tf_op jit(solution)/shard_map/ppermute | solution.py:111
  24.5 1.8 %collective-permute-start.14 = (bf16[128,512]{1,0:T(8,128)(2,1)S(1)}, bf16[128,512]{1,0:T(8,128)(2,1)S(1)}, u32[]{:S(2)}, u32[]{:S(2)}) collective-permute-start(bf16[128,512]{1,0:T(8,128)(2,1)S(1)} %collective-permute-done.13), channel_id=1, source_target_pairs={{0,1},{1,0},{2,3},{3,2},{4,5},{5,4},{6,7},{7,6},{8,9},{9,8},{10,11... | collective-permute-start | bytes 393224 | tf_op jit(solution)/shard_map/ppermute | solution.py:111
  26.3 45.5 %copy-start.1 = (bf16[128,8192]{1,0:T(8,128)(2,1)}, bf16[128,8192]{1,0:T(8,128)(2,1)S(1)}, u32[]{:S(2)}) copy-start(bf16[128,8192]{1,0:T(8,128)(2,1)S(1)} %constant_dynamic-update-slice_fusion.16.hidden) | copy-start | bytes 6291460
  28.4 1.3 %collective-permute-start.15 = (bf16[256,128]{1,0:T(8,128)(2,1)S(1)}, bf16[256,128]{1,0:T(8,128)(2,1)S(1)}, u32[]{:S(2)}, u32[]{:S(2)}) collective-permute-start(bf16[256,128]{1,0:T(8,128)(2,1)S(1)} %get-tuple-element.43.hid.both_hid), channel_id=1, source_target_pairs={{0,1},{1,0},{2,3},{3,2},{4,5},{5,4},{6,7},{7,6},{8,9},{9,8},{10,11... | collective-permute-start | bytes 196616 | tf_op jit(solution)/shard_map/ppermute | solution.py:396
  30.0 6.4 %collective-permute-start.20 = (bf16[128,512]{1,0:T(8,128)(2,1)S(1)}, bf16[128,512]{1,0:T(8,128)(2,1)S(1)}, u32[]{:S(2)}, u32[]{:S(2)}) collective-permute-start(bf16[128,512]{1,0:T(8,128)(2,1)S(1)} %get-tuple-element.38), channel_id=1, source_target_pairs={{0,2},{1,3},{2,0},{3,1},{4,6},{5,7},{6,4},{7,5},{8,10},{9,11},{10,... | collective-permute-start | bytes 393224 | tf_op jit(solution)/shard_map/ppermute | solution.py:123
  31.3 8.0 %collective-permute-start.19 = (bf16[128,512]{1,0:T(8,128)(2,1)S(1)}, bf16[128,512]{1,0:T(8,128)(2,1)S(1)}, u32[]{:S(2)}, u32[]{:S(2)}) collective-permute-start(bf16[128,512]{1,0:T(8,128)(2,1)S(1)} %get-tuple-element.40), channel_id=1, source_target_pairs={{0,2},{1,3},{2,0},{3,1},{4,6},{5,7},{6,4},{7,5},{8,10},{9,11},{10,... | collective-permute-start | bytes 393224 | tf_op jit(solution)/shard_map/ppermute | solution.py:123
  32.8 9.3 %copy-start.11 = (s32[16]{0:T(128)S(1)}, s32[16]{0:T(128)}, u32[]{:S(2)}) copy-start(s32[16]{0:T(128)} %param.15) | copy-start | bytes 196
  32.8 9.2 %collective-permute-start.18 = (bf16[128,512]{1,0:T(8,128)(2,1)S(1)}, bf16[128,512]{1,0:T(8,128)(2,1)S(1)}, u32[]{:S(2)}, u32[]{:S(2)}) collective-permute-start(bf16[128,512]{1,0:T(8,128)(2,1)S(1)} %get-tuple-element.42), channel_id=1, source_target_pairs={{0,2},{1,3},{2,0},{3,1},{4,6},{5,7},{6,4},{7,5},{8,10},{9,11},{10,... | collective-permute-start | bytes 393224 | tf_op jit(solution)/shard_map/ppermute | solution.py:123
  34.0 10.0 %collective-permute-start.17 = (bf16[128,512]{1,0:T(8,128)(2,1)S(1)}, bf16[128,512]{1,0:T(8,128)(2,1)S(1)}, u32[]{:S(2)}, u32[]{:S(2)}) collective-permute-start(bf16[128,512]{1,0:T(8,128)(2,1)S(1)} %get-tuple-element.45), channel_id=1, source_target_pairs={{0,2},{1,3},{2,0},{3,1},{4,6},{5,7},{6,4},{7,5},{8,10},{9,11},{10,... | collective-permute-start | bytes 393224 | tf_op jit(solution)/shard_map/ppermute | solution.py:123
  36.5 7.9 %collective-permute-start.21 = (bf16[128,512]{1,0:T(8,128)(2,1)S(1)}, bf16[128,512]{1,0:T(8,128)(2,1)S(1)}, u32[]{:S(2)}, u32[]{:S(2)}) collective-permute-start(bf16[128,512]{1,0:T(8,128)(2,1)S(1)} %add_convert_fusion.3), channel_id=1, source_target_pairs={{0,12},{1,13},{2,14},{3,15},{4,8},{5,9},{6,10},{7,11},{8,4},{9,5},... | collective-permute-start | bytes 393224 | tf_op jit(solution)/shard_map/ppermute | solution.py:131
  39.3 10.1 %collective-permute-start.22 = (bf16[128,512]{1,0:T(8,128)(2,1)S(1)}, bf16[128,512]{1,0:T(8,128)(2,1)S(1)}, u32[]{:S(2)}, u32[]{:S(2)}) collective-permute-start(bf16[128,512]{1,0:T(8,128)(2,1)S(1)} %add_convert_fusion.2), channel_id=1, source_target_pairs={{0,8},{1,9},{2,10},{3,11},{4,12},{5,13},{6,14},{7,15},{8,0},{9,1},... | collective-permute-start | bytes 393224 | tf_op jit(solution)/shard_map/ppermute | solution.py:131
  43.3 7.1 %collective-permute-start.23 = (bf16[128,512]{1,0:T(8,128)(2,1)S(1)}, bf16[128,512]{1,0:T(8,128)(2,1)S(1)}, u32[]{:S(2)}, u32[]{:S(2)}) collective-permute-start(bf16[128,512]{1,0:T(8,128)(2,1)S(1)} %add_convert_fusion.1), channel_id=1, source_target_pairs={{0,4},{1,5},{2,6},{3,7},{4,0},{5,1},{6,2},{7,3},{8,12},{9,13},{10,... | collective-permute-start | bytes 393224 | tf_op jit(solution)/shard_map/ppermute | solution.py:131
  50.7 7.8 %collective-permute-start.31 = (bf16[128,512]{1,0:T(8,128)(2,1)S(1)}, bf16[128,512]{1,0:T(8,128)(2,1)S(1)}, u32[]{:S(2)}, u32[]{:S(2)}) collective-permute-start(bf16[128,512]{1,0:T(8,128)(2,1)S(1)} %get-tuple-element.52.refs_0_), channel_id=1, source_target_pairs={{0,8},{1,9},{2,10},{3,11},{4,12},{5,13},{6,14},{7,15},{8,0},{9,1},... | collective-permute-start | bytes 393224 | tf_op jit(solution)/shard_map/ppermute | solution.py:105
  50.9 6.8 %collective-permute-start.27 = (bf16[128,512]{1,0:T(8,128)(2,1)S(1)}, bf16[128,512]{1,0:T(8,128)(2,1)S(1)}, u32[]{:S(2)}, u32[]{:S(2)}) collective-permute-start(bf16[128,512]{1,0:T(8,128)(2,1)S(1)} %get-tuple-element.52.refs_0_), channel_id=1, source_target_pairs={{0,4},{1,5},{2,6},{3,7},{4,0},{5,1},{6,2},{7,3},{8,12},{9,13},{10,... | collective-permute-start | bytes 393224 | tf_op jit(solution)/shard_map/ppermute | solution.py:105
  53.4 6.4 %collective-permute-start.25 = (bf16[128,512]{1,0:T(8,128)(2,1)S(1)}, bf16[128,512]{1,0:T(8,128)(2,1)S(1)}, u32[]{:S(2)}, u32[]{:S(2)}) collective-permute-start(bf16[128,512]{1,0:T(8,128)(2,1)S(1)} %get-tuple-element.52.refs_0_), channel_id=1, source_target_pairs={{0,2},{1,3},{2,0},{3,1},{4,6},{5,7},{6,4},{7,5},{8,10},{9,11},{10,... | collective-permute-start | bytes 393224 | tf_op jit(solution)/shard_map/ppermute | solution.py:109
  55.0 5.5 %collective-permute-start.24 = (bf16[128,512]{1,0:T(8,128)(2,1)S(1)}, bf16[128,512]{1,0:T(8,128)(2,1)S(1)}, u32[]{:S(2)}, u32[]{:S(2)}) collective-permute-start(bf16[128,512]{1,0:T(8,128)(2,1)S(1)} %get-tuple-element.52.refs_0_), channel_id=1, source_target_pairs={{0,1},{1,0},{2,3},{3,2},{4,5},{5,4},{6,7},{7,6},{8,9},{9,8},{10,11... | collective-permute-start | bytes 393224 | tf_op jit(solution)/shard_map/ppermute | solution.py:111
  57.8 6.8 %collective-permute-start.35 = (bf16[128,512]{1,0:T(8,128)(2,1)S(1)}, bf16[128,512]{1,0:T(8,128)(2,1)S(1)}, u32[]{:S(2)}, u32[]{:S(2)}) collective-permute-start(bf16[128,512]{1,0:T(8,128)(2,1)S(1)} %get-tuple-element.52.refs_0_), channel_id=1, source_target_pairs={{0,12},{1,13},{2,14},{3,15},{4,8},{5,9},{6,10},{7,11},{8,4},{9,5},... | collective-permute-start | bytes 393224 | tf_op jit(solution)/shard_map/ppermute | solution.py:106
  58.4 7.5 %collective-permute-start.33 = (bf16[128,512]{1,0:T(8,128)(2,1)S(1)}, bf16[128,512]{1,0:T(8,128)(2,1)S(1)}, u32[]{:S(2)}, u32[]{:S(2)}) collective-permute-start(bf16[128,512]{1,0:T(8,128)(2,1)S(1)} %collective-permute-done.31.refs_8_), channel_id=1, source_target_pairs={{0,2},{1,3},{2,0},{3,1},{4,6},{5,7},{6,4},{7,5},{8,10},{9,11},{10,... | collective-permute-start | bytes 393224 | tf_op jit(solution)/shard_map/ppermute | solution.py:109
  59.8 10.7 %collective-permute-start.32 = (bf16[128,512]{1,0:T(8,128)(2,1)S(1)}, bf16[128,512]{1,0:T(8,128)(2,1)S(1)}, u32[]{:S(2)}, u32[]{:S(2)}) collective-permute-start(bf16[128,512]{1,0:T(8,128)(2,1)S(1)} %collective-permute-done.31.refs_8_), channel_id=1, source_target_pairs={{0,1},{1,0},{2,3},{3,2},{4,5},{5,4},{6,7},{7,6},{8,9},{9,8},{10,11... | collective-permute-start | bytes 393224 | tf_op jit(solution)/shard_map/ppermute | solution.py:111
  59.8 6.4 %collective-permute-start.29 = (bf16[128,512]{1,0:T(8,128)(2,1)S(1)}, bf16[128,512]{1,0:T(8,128)(2,1)S(1)}, u32[]{:S(2)}, u32[]{:S(2)}) collective-permute-start(bf16[128,512]{1,0:T(8,128)(2,1)S(1)} %collective-permute-done.27.refs_4_), channel_id=1, source_target_pairs={{0,2},{1,3},{2,0},{3,1},{4,6},{5,7},{6,4},{7,5},{8,10},{9,11},{10,... | collective-permute-start | bytes 393224 | tf_op jit(solution)/shard_map/ppermute | solution.py:109
  60.5 4.1 %collective-permute-start.26 = (bf16[128,512]{1,0:T(8,128)(2,1)S(1)}, bf16[128,512]{1,0:T(8,128)(2,1)S(1)}, u32[]{:S(2)}, u32[]{:S(2)}) collective-permute-start(bf16[128,512]{1,0:T(8,128)(2,1)S(1)} %collective-permute-done.25.refs_2_), channel_id=1, source_target_pairs={{0,1},{1,0},{2,3},{3,2},{4,5},{5,4},{6,7},{7,6},{8,9},{9,8},{10,11... | collective-permute-start | bytes 393224 | tf_op jit(solution)/shard_map/ppermute | solution.py:111
  64.5 2.0 %collective-permute-start.28 = (bf16[128,512]{1,0:T(8,128)(2,1)S(1)}, bf16[128,512]{1,0:T(8,128)(2,1)S(1)}, u32[]{:S(2)}, u32[]{:S(2)}) collective-permute-start(bf16[128,512]{1,0:T(8,128)(2,1)S(1)} %collective-permute-done.27.refs_4_), channel_id=1, source_target_pairs={{0,1},{1,0},{2,3},{3,2},{4,5},{5,4},{6,7},{7,6},{8,9},{9,8},{10,11... | collective-permute-start | bytes 393224 | tf_op jit(solution)/shard_map/ppermute | solution.py:111
  64.5 5.9 %collective-permute-start.37 = (bf16[128,512]{1,0:T(8,128)(2,1)S(1)}, bf16[128,512]{1,0:T(8,128)(2,1)S(1)}, u32[]{:S(2)}, u32[]{:S(2)}) collective-permute-start(bf16[128,512]{1,0:T(8,128)(2,1)S(1)} %collective-permute-done.35.refs_12_), channel_id=1, source_target_pairs={{0,2},{1,3},{2,0},{3,1},{4,6},{5,7},{6,4},{7,5},{8,10},{9,11},{10,... | collective-permute-start | bytes 393224 | tf_op jit(solution)/shard_map/ppermute | solution.py:109
  66.0 4.7 %collective-permute-start.36 = (bf16[128,512]{1,0:T(8,128)(2,1)S(1)}, bf16[128,512]{1,0:T(8,128)(2,1)S(1)}, u32[]{:S(2)}, u32[]{:S(2)}) collective-permute-start(bf16[128,512]{1,0:T(8,128)(2,1)S(1)} %collective-permute-done.35.refs_12_), channel_id=1, source_target_pairs={{0,1},{1,0},{2,3},{3,2},{4,5},{5,4},{6,7},{7,6},{8,9},{9,8},{10,11... | collective-permute-start | bytes 393224 | tf_op jit(solution)/shard_map/ppermute | solution.py:111
  66.3 4.3 %collective-permute-start.34 = (bf16[128,512]{1,0:T(8,128)(2,1)S(1)}, bf16[128,512]{1,0:T(8,128)(2,1)S(1)}, u32[]{:S(2)}, u32[]{:S(2)}) collective-permute-start(bf16[128,512]{1,0:T(8,128)(2,1)S(1)} %collective-permute-done.33.refs_10_), channel_id=1, source_target_pairs={{0,1},{1,0},{2,3},{3,2},{4,5},{5,4},{6,7},{7,6},{8,9},{9,8},{10,11... | collective-permute-start | bytes 393224 | tf_op jit(solution)/shard_map/ppermute | solution.py:111
  66.5 3.9 %collective-permute-start.30 = (bf16[128,512]{1,0:T(8,128)(2,1)S(1)}, bf16[128,512]{1,0:T(8,128)(2,1)S(1)}, u32[]{:S(2)}, u32[]{:S(2)}) collective-permute-start(bf16[128,512]{1,0:T(8,128)(2,1)S(1)} %collective-permute-done.29.refs_6_), channel_id=1, source_target_pairs={{0,1},{1,0},{2,3},{3,2},{4,5},{5,4},{6,7},{7,6},{8,9},{9,8},{10,11... | collective-permute-start | bytes 393224 | tf_op jit(solution)/shard_map/ppermute | solution.py:111
  70.5 1.3 %collective-permute-start.38 = (bf16[128,512]{1,0:T(8,128)(2,1)S(1)}, bf16[128,512]{1,0:T(8,128)(2,1)S(1)}, u32[]{:S(2)}, u32[]{:S(2)}) collective-permute-start(bf16[128,512]{1,0:T(8,128)(2,1)S(1)} %collective-permute-done.37), channel_id=1, source_target_pairs={{0,1},{1,0},{2,3},{3,2},{4,5},{5,4},{6,7},{7,6},{8,9},{9,8},{10,11... | collective-permute-start | bytes 393224 | tf_op jit(solution)/shard_map/ppermute | solution.py:111
  74.0 11.8 %all-to-all-start = ((bf16[16,32,128]{2,1,0:T(8,128)(2,1)}), bf16[16,32,128]{2,1,0:T(8,128)(2,1)S(1)}, u32[]{:S(2)}, u32[]{:S(2)}) async-start(bf16[16,32,128]{2,1,0:T(8,128)(2,1)} %backward.1), calls=%async_computation | async-start | bytes 262144 | tf_op jit(solution)/shard_map/all_to_all | solution.py:445
  (4 other events, 7.8 us)

commit v8 on v7

--- a/solution.py
+++ b/solution.py
@@ -301,44 +301,26 @@
     loss[...] = 0.5 * squares / (tokens * features)
 
 
-def rows_kernel(
-    per_pair,
-    received,
-    places,
-    child_in,
-    slope,
-    grad_gate,
-    grad_up,
-    grad_down,
-    gain,
-    made,
-    done,
-):
-    rows, features = grad_gate.shape
-    devices, stride, tokens = received.shape
-    message = received[...].reshape(devices * stride, tokens)
-    tiles = [dot(places[kind], message).astype(BF16) for kind in range(3)]
-    empty = jnp.zeros_like(tiles[0])
-    left = jnp.concatenate(
-        [
-            jnp.concatenate([tiles[0], empty], axis=1),
-            jnp.concatenate([tiles[1], empty], axis=1),
-            jnp.concatenate([empty, tiles[2]], axis=1),
-        ],
-        axis=0,
-    )
+def write_rows(tile, source, grads, made, done):
+    rows, features = grads[0].shape
     cut = min(features, 1024)
     copies = []
     for k in range(features // cut):
         cols = slice(k * cut, (k + 1) * cut)
-        right = jnp.concatenate([child_in[:, cols], slope[:, cols]], axis=0)
-        out = dot(left, right).astype(BF16)
-        for kind in range(3):
+        out = dot(tile, source[:, cols]).astype(BF16)
+        for kind, grad in enumerate(grads):
             made[kind, :, cols] = out[kind * rows : (kind + 1) * rows]
-        for kind, grad in enumerate((grad_gate, grad_up, grad_down)):
             copy = pltpu.make_async_copy(made.at[kind, :, cols], grad.at[:, cols], done.at[kind, k])
             copy.start()
             copies.append(copy)
+    return copies
+
+
+def down_kernel(per_pair, received, places, slope, grad_down, gain, made, done):
+    devices, stride, tokens = received.shape
+    message = received[...].reshape(devices * stride, tokens)
+    tile = dot(places[2], message).astype(BF16)
+    copies = write_rows(tile, slope, [grad_down], made, done)
     total = jnp.sum(message.astype(F32).reshape(devices, stride, tokens), axis=0)
     gain_rows = gain.shape[1] // 128
     for r in range(gain_rows):
@@ -347,6 +329,15 @@
             total[at : at + 1, :] + total[at + gain_rows : at + gain_rows + 1, :]
         )
     for copy in copies:
+        copy.wait()
+
+
+def rows_kernel(received, places, child_in, grad_gate, grad_up, made, done):
+    devices, stride, tokens = received.shape
+    message = received[...].reshape(devices * stride, tokens)
+    tiles = [dot(places[kind], message).astype(BF16) for kind in range(2)]
+    both = jnp.concatenate(tiles, axis=0)
+    for copy in write_rows(both, child_in, [grad_gate, grad_up], made, done):
         copy.wait()
 
 
@@ -452,19 +443,32 @@
         limit=6,
         name="prepare",
     )
-    *grads, gain_grad = call(
-        functools.partial(rows_kernel, per_pair),
-        [grad, grad, grad, ((1, width), F32)],
-        [received, places, child_in, slope_all],
+    cuts = features // min(features, 1024)
+    grad_down, gain_grad = call(
+        functools.partial(down_kernel, per_pair),
+        [grad, ((1, width), F32)],
+        [received, places, slope_all],
+        limit=6,
+        name="down",
+        scratch=[
+            pltpu.VMEM((1, parent_rows, features), BF16),
+            pltpu.SemaphoreType.DMA((1, cuts)),
+        ],
+        specs=[anywhere, VMEM],
+    )
+    grad_gate, grad_up = call(
+        rows_kernel,
+        [grad, grad],
+        [after(received, gain_grad), places, child_in],
         limit=8,
         name="rows",
         scratch=[
-            pltpu.VMEM((3, parent_rows, features), BF16),
-            pltpu.SemaphoreType.DMA((3, features // min(features, 1024))),
+            pltpu.VMEM((2, parent_rows, features), BF16),
+            pltpu.SemaphoreType.DMA((2, cuts)),
         ],
-        specs=[anywhere] * 3 + [VMEM],
-    )
-    return (*grads, gain_grad.reshape(width), loss_value.reshape(1))
+        specs=[anywhere] * 2,
+    )
+    return (grad_gate, grad_up, grad_down, gain_grad.reshape(width), loss_value.reshape(1))
 
 
 def solution(mesh):

time: 91.8 us -> 107 us (1.17)
  waiting for transfers between devices: 31.8 us -> 45.1 us
  starting transfers between devices: 38 us -> 40.4 us
  local copies, waits for them, and re-layouts: 5.59 us -> 4.01 us
    ppermute x4, waiting for transfers between devices: 3.41 us -> 11.6 us  [gather(): column[z] = lax.ppermute(block, 'fsdp', self.across(4 * z))]
    ppermute x8, waiting for transfers between devices: 9.41 us -> 13.5 us  [gather(): part = lax.ppermute(column[z], 'fsdp', self.across(2)) if y else column[z]]
    all_to_all x1, starting transfers between devices: 3.91 us -> 7.28 us  [shards(): received = lax.all_to_all(sent, 'fsdp', 0, 0, tiled=True)]
    ppermute x2, waiting for transfers between devices: 3.79 us -> 0.57 us  [gather(): column[3] = lax.ppermute(after(block, column[1]), 'fsdp', self.across(12))]
    ppermute x4, waiting for transfers between devices: 3.55 us -> 6.72 us  [scatter_sum(): over_y[z] = lax.ppermute(sent, 'fsdp', self.across(2))]
    ppermute x3, waiting for transfers between devices: 5.97 us -> 7.67 us  [scatter_sum(): arrived.append(lax.ppermute(sent, 'fsdp', self.across(4 * z)))]
    unnamed x24, local copies, waits for them, and re-layouts: 4.55 us -> 2.96 us
    ppermute x8, starting transfers between devices: 10.4 us -> 9.28 us  [gather(): part = lax.ppermute(column[z], 'fsdp', self.across(2)) if y else column[z]]
  transfers between devices with their start and end apart: 40 -> 40, of which waited for: 18 -> 19; matrix products, arithmetic and copies ran while one was open for 3% -> 3% of each run, Pallas kernels for 6% -> 6%
where the time goes in v8:
time: 107 us
  waiting for transfers between devices  45.1 us (42%)
  starting transfers between devices  40.4 us (38%)
  Pallas kernels  13.2 us (12%)
  local copies, waits for them, and re-layouts  4.01 us (4%)
  between operations  1.49 us (1%)
  other arithmetic  1.3 us (1%)
  matrix products  1.09 us (1%)
    ppermute x8, waiting for transfers between devices, gather(): part = lax.ppermute(column[z], 'fsdp', self.across(2)) if y else column[z]  13.5 us
    pallas_call x11, Pallas kernels, call(): pl.pallas_call(kernel, out_shape=[jax.ShapeDtypeStruct(shape, dtype) for...  13.2 us
    ppermute x4, waiting for transfers between devices, gather(): column[z] = lax.ppermute(block, 'fsdp', self.across(4 * z))  11.6 us
    ppermute x8, starting transfers between devices, gather(): part = lax.ppermute(column[z], 'fsdp', self.across(2)) if y else column[z]  9.28 us
    ppermute x4, starting transfers between devices, gather(): column[z] = lax.ppermute(block, 'fsdp', self.across(4 * z))  8.73 us
    ppermute x3, waiting for transfers between devices, scatter_sum(): arrived.append(lax.ppermute(sent, 'fsdp', self.across(4 * z)))  7.67 us
    all_to_all x1, starting transfers between devices, shards(): received = lax.all_to_all(sent, 'fsdp', 0, 0, tiled=True)  7.28 us
    ppermute x4, waiting for transfers between devices, scatter_sum(): over_y[z] = lax.ppermute(sent, 'fsdp', self.across(2))  6.72 us
  transfers between devices with their start and end apart: 40, of which 19 were waited for; matrix products, arithmetic and copies ran while one was open for 3% of the time, Pallas kernels for 6%

profile of v8, /device:TPU:0, one launch (start us, length us, event | category | flops | bytes accessed | tf_op | source)
XLA Modules:
  0.0 106.6 jit_solution(8053968923492626795)
XLA Ops:
  0.7 3.1 %collective-permute-start.3 = (bf16[128,512]{1,0:T(8,128)(2,1)}, bf16[128,512]{1,0:T(8,128)(2,1)S(1)}, u32[]{:S(2)}, u32[]{:S(2)}) collective-permute-start(bf16[128,512]{1,0:T(8,128)(2,1)} %refs_0_.1), channel_id=1, source_target_pairs={{0,4},{1,5},{2,6},{3,7},{4,0},{5,1},{6,2},{7,3},{8,12},{9,13},{10,... | collective-permute-start | bytes 393224 | tf_op jit(solution)/shard_map/ppermute | solution.py:105
  3.7 1.5 %collective-permute-start.1 = (bf16[128,512]{1,0:T(8,128)(2,1)}, bf16[128,512]{1,0:T(8,128)(2,1)S(1)}, u32[]{:S(2)}, u32[]{:S(2)}) collective-permute-start(bf16[128,512]{1,0:T(8,128)(2,1)} %refs_0_.1), channel_id=1, source_target_pairs={{0,2},{1,3},{2,0},{3,1},{4,6},{5,7},{6,4},{7,5},{8,10},{9,11},{10,... | collective-permute-start | bytes 393224 | tf_op jit(solution)/shard_map/ppermute | solution.py:109
  5.3 2.6 %collective-permute-start.7 = (bf16[128,512]{1,0:T(8,128)(2,1)}, bf16[128,512]{1,0:T(8,128)(2,1)S(1)}, u32[]{:S(2)}, u32[]{:S(2)}) collective-permute-start(bf16[128,512]{1,0:T(8,128)(2,1)} %refs_0_.1), channel_id=1, source_target_pairs={{0,8},{1,9},{2,10},{3,11},{4,12},{5,13},{6,14},{7,15},{8,0},{9,1},... | collective-permute-start | bytes 393224 | tf_op jit(solution)/shard_map/ppermute | solution.py:105
  8.1 3.1 %collective-permute-start.11 = (bf16[128,512]{1,0:T(8,128)(2,1)S(1)}, bf16[128,512]{1,0:T(8,128)(2,1)S(1)}, u32[]{:S(2)}, u32[]{:S(2)}) collective-permute-start(bf16[128,512]{1,0:T(8,128)(2,1)S(1)} %copy-done.7), channel_id=1, source_target_pairs={{0,12},{1,13},{2,14},{3,15},{4,8},{5,9},{6,10},{7,11},{8,4},{9,5},... | collective-permute-start | bytes 393224 | tf_op jit(solution)/shard_map/ppermute | solution.py:106
  11.7 0.5 collective-permute-start.2
  12.2 5.7 %collective-permute-done.7.refs_8_ = bf16[128,512]{1,0:T(8,128)(2,1)S(1)} collective-permute-done((bf16[128,512]{1,0:T(8,128)(2,1)}, bf16[128,512]{1,0:T(8,128)(2,1)S(1)}, u32[]{:S(2)}, u32[]{:S(2)}) %collective-permute-start.7) | collective-permute-done | bytes 131104 | tf_op jit(solution)/shard_map/ppermute | solution.py:105
  17.9 0.7 collective-permute-start.5
  18.7 1.4 %collective-permute-start.9 = (bf16[128,512]{1,0:T(8,128)(2,1)S(1)}, bf16[128,512]{1,0:T(8,128)(2,1)S(1)}, u32[]{:S(2)}, u32[]{:S(2)}) collective-permute-start(bf16[128,512]{1,0:T(8,128)(2,1)S(1)} %collective-permute-done.7.refs_8_), channel_id=1, source_target_pairs={{0,2},{1,3},{2,0},{3,1},{4,6},{5,7},{6,4},{7,5},{8,10},{9,11},{10,... | collective-permute-start | bytes 393224 | tf_op jit(solution)/shard_map/ppermute | solution.py:109
  20.1 4.0 %collective-permute-done.5.refs_6_ = bf16[128,512]{1,0:T(8,128)(2,1)S(1)} collective-permute-done((bf16[128,512]{1,0:T(8,128)(2,1)S(1)}, bf16[128,512]{1,0:T(8,128)(2,1)S(1)}, u32[]{:S(2)}, u32[]{:S(2)}) %collective-permute-start.5) | collective-permute-done | bytes 131104 | tf_op jit(solution)/shard_map/ppermute | solution.py:109
  24.1 1.6 %collective-permute-done.9.refs_10_ = bf16[128,512]{1,0:T(8,128)(2,1)S(1)} collective-permute-done((bf16[128,512]{1,0:T(8,128)(2,1)S(1)}, bf16[128,512]{1,0:T(8,128)(2,1)S(1)}, u32[]{:S(2)}, u32[]{:S(2)}) %collective-permute-start.9) | collective-permute-done | bytes 131104 | tf_op jit(solution)/shard_map/ppermute | solution.py:109
  25.7 0.5 collective-permute-start.10
  26.2 3.7 %collective-permute-done.13 = bf16[128,512]{1,0:T(8,128)(2,1)S(1)} collective-permute-done((bf16[128,512]{1,0:T(8,128)(2,1)S(1)}, bf16[128,512]{1,0:T(8,128)(2,1)S(1)}, u32[]{:S(2)}, u32[]{:S(2)}) %collective-permute-start.13) | collective-permute-done | bytes 131104 | tf_op jit(solution)/shard_map/ppermute | solution.py:109
  30.1 0.4 squares.1.early
  30.6 0.7 collective-permute-done.14
  31.4 2.0 %forward.1 = (f32[128,128]{1,0:T(8,128)S(1)}, f32[128,128]{1,0:T(8,128)S(1)}, f32[128,128]{1,0:T(8,128)S(1)}, bf16[256,128]{1,0:T(8,128)(2,1)S(1)}) custom-call(f32[128,128]{1,0:T(8,128)S(1)} %squares.1.early, bf16[128,8192]{1,0:T(8,128)(2,1)S(1)} %constant_dynamic-update-slice_fusion.16.hidden, f32[1,8192]{1,0:T(1,128)S(1)} %bitcast.32, ...), custom_call_target="tpu_custom_call" | custom-call | tf_op jit(solution)/shard_map/forward/pallas_call | solution.py:349
  33.6 1.1 %collective-permute-done.15.other_hid = bf16[256,128]{1,0:T(8,128)(2,1)S(1)} collective-permute-done((bf16[256,128]{1,0:T(8,128)(2,1)S(1)}, bf16[256,128]{1,0:T(8,128)(2,1)S(1)}, u32[]{:S(2)}, u32[]{:S(2)}) %collective-permute-start.15) | collective-permute-done | bytes 65568 | tf_op jit(solution)/shard_map/ppermute | solution.py:387
  35.6 1.8 %collective-permute-start.19 = (bf16[128,512]{1,0:T(8,128)(2,1)S(1)}, bf16[128,512]{1,0:T(8,128)(2,1)S(1)}, u32[]{:S(2)}, u32[]{:S(2)}) collective-permute-start(bf16[128,512]{1,0:T(8,128)(2,1)S(1)} %get-tuple-element.41), channel_id=1, source_target_pairs={{0,2},{1,3},{2,0},{3,1},{4,6},{5,7},{6,4},{7,5},{8,10},{9,11},{10,... | collective-permute-start | bytes 393224 | tf_op jit(solution)/shard_map/ppermute | solution.py:123
  38.4 1.8 %collective-permute-start.17 = (bf16[128,512]{1,0:T(8,128)(2,1)S(1)}, bf16[128,512]{1,0:T(8,128)(2,1)S(1)}, u32[]{:S(2)}, u32[]{:S(2)}) collective-permute-start(bf16[128,512]{1,0:T(8,128)(2,1)S(1)} %get-tuple-element.46), channel_id=1, source_target_pairs={{0,2},{1,3},{2,0},{3,1},{4,6},{5,7},{6,4},{7,5},{8,10},{9,11},{10,... | collective-permute-start | bytes 393224 | tf_op jit(solution)/shard_map/ppermute | solution.py:123
  40.2 1.2 %collective-permute-done.20 = bf16[128,512]{1,0:T(8,128)(2,1)S(1)} collective-permute-done((bf16[128,512]{1,0:T(8,128)(2,1)S(1)}, bf16[128,512]{1,0:T(8,128)(2,1)S(1)}, u32[]{:S(2)}, u32[]{:S(2)}) %collective-permute-start.20) | collective-permute-done | bytes 131104 | tf_op jit(solution)/shard_map/ppermute | solution.py:123
  41.4 2.8 %collective-permute-done.19 = bf16[128,512]{1,0:T(8,128)(2,1)S(1)} collective-permute-done((bf16[128,512]{1,0:T(8,128)(2,1)S(1)}, bf16[128,512]{1,0:T(8,128)(2,1)S(1)}, u32[]{:S(2)}, u32[]{:S(2)}) %collective-permute-start.19) | collective-permute-done | bytes 131104 | tf_op jit(solution)/shard_map/ppermute | solution.py:123
  44.2 2.8 %collective-permute-done.18 = bf16[128,512]{1,0:T(8,128)(2,1)S(1)} collective-permute-done((bf16[128,512]{1,0:T(8,128)(2,1)S(1)}, bf16[128,512]{1,0:T(8,128)(2,1)S(1)}, u32[]{:S(2)}, u32[]{:S(2)}) %collective-permute-start.18) | collective-permute-done | bytes 131104 | tf_op jit(solution)/shard_map/ppermute | solution.py:123
  47.2 1.0 fusion.2
  48.2 0.4 collective-permute-start.23
  48.7 3.1 %collective-permute-start.22 = (bf16[128,512]{1,0:T(8,128)(2,1)S(1)}, bf16[128,512]{1,0:T(8,128)(2,1)S(1)}, u32[]{:S(2)}, u32[]{:S(2)}) collective-permute-start(bf16[128,512]{1,0:T(8,128)(2,1)S(1)} %add_convert_fusion.2), channel_id=1, source_target_pairs={{0,8},{1,9},{2,10},{3,11},{4,12},{5,13},{6,14},{7,15},{8,0},{9,1},... | collective-permute-start | bytes 393224 | tf_op jit(solution)/shard_map/ppermute | solution.py:131
  51.8 0.9 collective-permute-start.21
  53.1 0.7 collective-permute-done.23
  53.8 6.9 %collective-permute-done.22 = bf16[128,512]{1,0:T(8,128)(2,1)S(1)} collective-permute-done((bf16[128,512]{1,0:T(8,128)(2,1)S(1)}, bf16[128,512]{1,0:T(8,128)(2,1)S(1)}, u32[]{:S(2)}, u32[]{:S(2)}) %collective-permute-start.22) | collective-permute-done | bytes 131104 | tf_op jit(solution)/shard_map/ppermute | solution.py:131
  61.5 2.0 %collective-permute-start.27 = (bf16[128,512]{1,0:T(8,128)(2,1)S(1)}, bf16[128,512]{1,0:T(8,128)(2,1)S(1)}, u32[]{:S(2)}, u32[]{:S(2)}) collective-permute-start(bf16[128,512]{1,0:T(8,128)(2,1)S(1)} %get-tuple-element.53.refs_0_), channel_id=1, source_target_pairs={{0,4},{1,5},{2,6},{3,7},{4,0},{5,1},{6,2},{7,3},{8,12},{9,13},{10,... | collective-permute-start | bytes 393224 | tf_op jit(solution)/shard_map/ppermute | solution.py:105
  63.5 1.1 %collective-permute-start.31 = (bf16[128,512]{1,0:T(8,128)(2,1)S(1)}, bf16[128,512]{1,0:T(8,128)(2,1)S(1)}, u32[]{:S(2)}, u32[]{:S(2)}) collective-permute-start(bf16[128,512]{1,0:T(8,128)(2,1)S(1)} %get-tuple-element.53.refs_0_), channel_id=1, source_target_pairs={{0,8},{1,9},{2,10},{3,11},{4,12},{5,13},{6,14},{7,15},{8,0},{9,1},... | collective-permute-start | bytes 393224 | tf_op jit(solution)/shard_map/ppermute | solution.py:105
  64.6 4.9 %collective-permute-done.27.refs_4_ = bf16[128,512]{1,0:T(8,128)(2,1)S(1)} collective-permute-done((bf16[128,512]{1,0:T(8,128)(2,1)S(1)}, bf16[128,512]{1,0:T(8,128)(2,1)S(1)}, u32[]{:S(2)}, u32[]{:S(2)}) %collective-permute-start.27) | collective-permute-done | bytes 131104 | tf_op jit(solution)/shard_map/ppermute | solution.py:105
  69.5 1.4 %collective-permute-start.35 = (bf16[128,512]{1,0:T(8,128)(2,1)S(1)}, bf16[128,512]{1,0:T(8,128)(2,1)S(1)}, u32[]{:S(2)}, u32[]{:S(2)}) collective-permute-start(bf16[128,512]{1,0:T(8,128)(2,1)S(1)} %get-tuple-element.53.refs_0_), channel_id=1, source_target_pairs={{0,12},{1,13},{2,14},{3,15},{4,8},{5,9},{6,10},{7,11},{8,4},{9,5},... | collective-permute-start | bytes 393224 | tf_op jit(solution)/shard_map/ppermute | solution.py:106
  70.9 1.7 %collective-permute-start.29 = (bf16[128,512]{1,0:T(8,128)(2,1)S(1)}, bf16[128,512]{1,0:T(8,128)(2,1)S(1)}, u32[]{:S(2)}, u32[]{:S(2)}) collective-permute-start(bf16[128,512]{1,0:T(8,128)(2,1)S(1)} %collective-permute-done.27.refs_4_), channel_id=1, source_target_pairs={{0,2},{1,3},{2,0},{3,1},{4,6},{5,7},{6,4},{7,5},{8,10},{9,11},{10,... | collective-permute-start | bytes 393224 | tf_op jit(solution)/shard_map/ppermute | solution.py:109
  72.9 1.0 collective-permute-done.31.refs_8_
  74.0 1.8 %collective-permute-start.33 = (bf16[128,512]{1,0:T(8,128)(2,1)S(1)}, bf16[128,512]{1,0:T(8,128)(2,1)S(1)}, u32[]{:S(2)}, u32[]{:S(2)}) collective-permute-start(bf16[128,512]{1,0:T(8,128)(2,1)S(1)} %collective-permute-done.31.refs_8_), channel_id=1, source_target_pairs={{0,2},{1,3},{2,0},{3,1},{4,6},{5,7},{6,4},{7,5},{8,10},{9,11},{10,... | collective-permute-start | bytes 393224 | tf_op jit(solution)/shard_map/ppermute | solution.py:109
  75.8 0.6 collective-permute-done.35.refs_12_
  76.4 1.8 %collective-permute-start.37 = (bf16[128,512]{1,0:T(8,128)(2,1)S(1)}, bf16[128,512]{1,0:T(8,128)(2,1)S(1)}, u32[]{:S(2)}, u32[]{:S(2)}) collective-permute-start(bf16[128,512]{1,0:T(8,128)(2,1)S(1)} %collective-permute-done.35.refs_12_), channel_id=1, source_target_pairs={{0,2},{1,3},{2,0},{3,1},{4,6},{5,7},{6,4},{7,5},{8,10},{9,11},{10,... | collective-permute-start | bytes 393224 | tf_op jit(solution)/shard_map/ppermute | solution.py:109
  78.5 1.8 %collective-permute-done.33.refs_10_ = bf16[128,512]{1,0:T(8,128)(2,1)S(1)} collective-permute-done((bf16[128,512]{1,0:T(8,128)(2,1)S(1)}, bf16[128,512]{1,0:T(8,128)(2,1)S(1)}, u32[]{:S(2)}, u32[]{:S(2)}) %collective-permute-start.33) | collective-permute-done | bytes 131104 | tf_op jit(solution)/shard_map/ppermute | solution.py:109
  80.3 2.5 %collective-permute-done.37 = bf16[128,512]{1,0:T(8,128)(2,1)S(1)} collective-permute-done((bf16[128,512]{1,0:T(8,128)(2,1)S(1)}, bf16[128,512]{1,0:T(8,128)(2,1)S(1)}, u32[]{:S(2)}, u32[]{:S(2)}) %collective-permute-start.37) | collective-permute-done | bytes 131104 | tf_op jit(solution)/shard_map/ppermute | solution.py:109
  83.0 0.6 early.1.partial
  83.7 0.5 collective-permute-done.38
  84.2 2.2 %backward.1 = bf16[16,32,128]{2,1,0:T(8,128)(2,1)} custom-call(f32[128,128]{1,0:T(8,128)S(1)} %early.1.partial, bf16[128,8192]{1,0:T(8,128)(2,1)S(1)} %constant_dynamic-update-slice_fusion.slope, bf16[128,8192]{1,0:T(8,128)(2,1)S(1)} %constant_dynamic-update-slice_fusion.16.hidden, bf16[128,8192]{1,0:T(8,128)(2,1)S(1)} %copy-done.3, ...), custom_call_target="tpu_custom_call" | custom-call | tf_op jit(solution)/shard_map/backward/pallas_call | solution.py:349
  86.3 7.3 %all-to-all-start = ((bf16[16,32,128]{2,1,0:T(8,128)(2,1)}), bf16[16,32,128]{2,1,0:T(8,128)(2,1)S(1)}, u32[]{:S(2)}, u32[]{:S(2)}) async-start(bf16[16,32,128]{2,1,0:T(8,128)(2,1)} %backward.1), calls=%async_computation | async-start | bytes 262144 | tf_op jit(solution)/shard_map/all_to_all | solution.py:436
  94.1 1.6 %copy-done.2 = bf16[128,8192]{1,0:T(8,128)(2,1)S(1)} copy-done((bf16[128,8192]{1,0:T(8,128)(2,1)S(1)}, bf16[128,8192]{1,0:T(8,128)(2,1)}, u32[]{:S(2)}) %copy-start.2) | copy-done | bytes 2097176
  95.7 2.0 %prepare.1 = (bf16[128,8192]{1,0:T(8,128)(2,1)S(1)}, f32[1,1]{1,0:T(1,128)}) custom-call(bf16[128,8192]{1,0:T(8,128)(2,1)S(1)} %copy-done.2, f32[128,128]{1,0:T(8,128)S(1)} %get-tuple-element.54.scale, f32[1,8192]{1,0:T(1,128)S(1)} %bitcast.31, bf16[128,8192]{1,0:T(8,128)(2,1)S(1)} %constant_dynamic-update-slice_fusion.slope), custom_call_target="tpu_custom_call" | custom-call | tf_op jit(solution)/shard_map/prepare/pallas_call | solution.py:349
  97.6 1.3 %copy-done.5 = bf16[128,8192]{1,0:T(8,128)(2,1)} copy-done((bf16[128,8192]{1,0:T(8,128)(2,1)}, bf16[128,8192]{1,0:T(8,128)(2,1)S(1)}, u32[]{:S(2)}) %copy-start.5) | copy-done | bytes 2097176
  99.0 2.6 %all-to-all-done.received = bf16[16,32,128]{2,1,0:T(8,128)(2,1)S(1)} async-done(((bf16[16,32,128]{2,1,0:T(8,128)(2,1)}), bf16[16,32,128]{2,1,0:T(8,128)(2,1)S(1)}, u32[]{:S(2)}, u32[]{:S(2)}) %all-to-all-start) | async-done | bytes 131104 | tf_op jit(solution)/shard_map/all_to_all | solution.py:436
  101.6 2.3 %down.11 = (bf16[128,8192]{1,0:T(8,128)(2,1)}, f32[1,512]{1,0:T(1,128)}) custom-call(bf16[16,32,128]{2,1,0:T(8,128)(2,1)S(1)} %all-to-all-done.received, bf16[3,128,512]{2,1,0:T(8,128)(2,1)S(1)} %pad_maximum_fusion.1.places, bf16[128,8192]{1,0:T(8,128)(2,1)S(1)} %constant_dynamic-update-slice_fusion.slope), custom_call_target="tpu_custom_call" | custom-call | tf_op jit(solution)/shard_map/down/pallas_call | solution.py:349
  103.9 2.5 %rows.1 = (bf16[128,8192]{1,0:T(8,128)(2,1)}, bf16[128,8192]{1,0:T(8,128)(2,1)}) custom-call(bf16[16,32,128]{2,1,0:T(8,128)(2,1)S(1)} %all-to-all-done.received, bf16[3,128,512]{2,1,0:T(8,128)(2,1)S(1)} %pad_maximum_fusion.1.places, bf16[128,8192]{1,0:T(8,128)(2,1)S(1)} %copy-done.6), custom_call_target="tpu_custom_call" | custom-call | tf_op jit(solution)/shard_map/rows/pallas_call | solution.py:349
  (128 shorter events, 5.7 us)
Async XLA Ops:
  0.6 7.4 %copy-start.7 = (bf16[128,512]{1,0:T(8,128)(2,1)S(1)}, bf16[128,512]{1,0:T(8,128)(2,1)}, u32[]{:S(2)}) copy-start(bf16[128,512]{1,0:T(8,128)(2,1)} %refs_0_.1) | copy-start | bytes 393220
  0.6 10.6 %copy-start.10 = (s32[2048]{0:T(1024)S(1)}, s32[2048]{0:T(1024)}, u32[]{:S(2)}) copy-start(s32[2048]{0:T(1024)} %param.14) | copy-start | bytes 24580
  0.7 7.4 %collective-permute-start.3 = (bf16[128,512]{1,0:T(8,128)(2,1)}, bf16[128,512]{1,0:T(8,128)(2,1)S(1)}, u32[]{:S(2)}, u32[]{:S(2)}) collective-permute-start(bf16[128,512]{1,0:T(8,128)(2,1)} %refs_0_.1), channel_id=1, source_target_pairs={{0,4},{1,5},{2,6},{3,7},{4,0},{5,1},{6,2},{7,3},{8,12},{9,13},{10,... | collective-permute-start | bytes 393224 | tf_op jit(solution)/shard_map/ppermute | solution.py:105
  3.7 7.8 %collective-permute-start = (bf16[128,512]{1,0:T(8,128)(2,1)}, bf16[128,512]{1,0:T(8,128)(2,1)S(1)}, u32[]{:S(2)}, u32[]{:S(2)}) collective-permute-start(bf16[128,512]{1,0:T(8,128)(2,1)} %refs_0_.1), channel_id=1, source_target_pairs={{0,1},{1,0},{2,3},{3,2},{4,5},{5,4},{6,7},{7,6},{8,9},{9,8},{10,11... | collective-permute-start | bytes 393224 | tf_op jit(solution)/shard_map/ppermute | solution.py:111
  3.7 7.9 %collective-permute-start.1 = (bf16[128,512]{1,0:T(8,128)(2,1)}, bf16[128,512]{1,0:T(8,128)(2,1)S(1)}, u32[]{:S(2)}, u32[]{:S(2)}) collective-permute-start(bf16[128,512]{1,0:T(8,128)(2,1)} %refs_0_.1), channel_id=1, source_target_pairs={{0,2},{1,3},{2,0},{3,1},{4,6},{5,7},{6,4},{7,5},{8,10},{9,11},{10,... | collective-permute-start | bytes 393224 | tf_op jit(solution)/shard_map/ppermute | solution.py:109
  5.3 12.6 %collective-permute-start.7 = (bf16[128,512]{1,0:T(8,128)(2,1)}, bf16[128,512]{1,0:T(8,128)(2,1)S(1)}, u32[]{:S(2)}, u32[]{:S(2)}) collective-permute-start(bf16[128,512]{1,0:T(8,128)(2,1)} %refs_0_.1), channel_id=1, source_target_pairs={{0,8},{1,9},{2,10},{3,11},{4,12},{5,13},{6,14},{7,15},{8,0},{9,1},... | collective-permute-start | bytes 393224 | tf_op jit(solution)/shard_map/ppermute | solution.py:105
  7.9 26.8 %collective-permute-start.16 = (bf16[128,8192]{1,0:T(8,128)(2,1)}, bf16[128,8192]{1,0:T(8,128)(2,1)S(1)}, u32[]{:S(2)}, u32[]{:S(2)}) collective-permute-start(bf16[128,8192]{1,0:T(8,128)(2,1)} %down.10), channel_id=1, source_target_pairs={{0,1},{1,0},{2,3},{3,2},{4,5},{5,4},{6,7},{7,6},{8,9},{9,8},{10,11... | collective-permute-start | bytes 6291464 | tf_op jit(solution)/shard_map/ppermute | solution.py:386
  8.1 15.9 %collective-permute-start.11 = (bf16[128,512]{1,0:T(8,128)(2,1)S(1)}, bf16[128,512]{1,0:T(8,128)(2,1)S(1)}, u32[]{:S(2)}, u32[]{:S(2)}) collective-permute-start(bf16[128,512]{1,0:T(8,128)(2,1)S(1)} %copy-done.7), channel_id=1, source_target_pairs={{0,12},{1,13},{2,14},{3,15},{4,8},{5,9},{6,10},{7,11},{8,4},{9,5},... | collective-permute-start | bytes 393224 | tf_op jit(solution)/shard_map/ppermute | solution.py:106
  11.6 7.1 %collective-permute-start.4 = (bf16[128,512]{1,0:T(8,128)(2,1)S(1)}, bf16[128,512]{1,0:T(8,128)(2,1)S(1)}, u32[]{:S(2)}, u32[]{:S(2)}) collective-permute-start(bf16[128,512]{1,0:T(8,128)(2,1)S(1)} %collective-permute-done.3.refs_4_), channel_id=1, source_target_pairs={{0,1},{1,0},{2,3},{3,2},{4,5},{5,4},{6,7},{7,6},{8,9},{9,8},{10,11... | collective-permute-start | bytes 393224 | tf_op jit(solution)/shard_map/ppermute | solution.py:111
  11.7 6.9 %collective-permute-start.2 = (bf16[128,512]{1,0:T(8,128)(2,1)S(1)}, bf16[128,512]{1,0:T(8,128)(2,1)S(1)}, u32[]{:S(2)}, u32[]{:S(2)}) collective-permute-start(bf16[128,512]{1,0:T(8,128)(2,1)S(1)} %collective-permute-done.1.refs_2_), channel_id=1, source_target_pairs={{0,1},{1,0},{2,3},{3,2},{4,5},{5,4},{6,7},{7,6},{8,9},{9,8},{10,11... | collective-permute-start | bytes 393224 | tf_op jit(solution)/shard_map/ppermute | solution.py:111
  17.9 6.1 %collective-permute-start.5 = (bf16[128,512]{1,0:T(8,128)(2,1)S(1)}, bf16[128,512]{1,0:T(8,128)(2,1)S(1)}, u32[]{:S(2)}, u32[]{:S(2)}) collective-permute-start(bf16[128,512]{1,0:T(8,128)(2,1)S(1)} %collective-permute-done.3.refs_4_), channel_id=1, source_target_pairs={{0,2},{1,3},{2,0},{3,1},{4,6},{5,7},{6,4},{7,5},{8,10},{9,11},{10,... | collective-permute-start | bytes 393224 | tf_op jit(solution)/shard_map/ppermute | solution.py:109
  18.6 11.4 %collective-permute-start.8 = (bf16[128,512]{1,0:T(8,128)(2,1)S(1)}, bf16[128,512]{1,0:T(8,128)(2,1)S(1)}, u32[]{:S(2)}, u32[]{:S(2)}) collective-permute-start(bf16[128,512]{1,0:T(8,128)(2,1)S(1)} %collective-permute-done.7.refs_8_), channel_id=1, source_target_pairs={{0,1},{1,0},{2,3},{3,2},{4,5},{5,4},{6,7},{7,6},{8,9},{9,8},{10,11... | collective-permute-start | bytes 393224 | tf_op jit(solution)/shard_map/ppermute | solution.py:111
  18.7 7.0 %collective-permute-start.9 = (bf16[128,512]{1,0:T(8,128)(2,1)S(1)}, bf16[128,512]{1,0:T(8,128)(2,1)S(1)}, u32[]{:S(2)}, u32[]{:S(2)}) collective-permute-start(bf16[128,512]{1,0:T(8,128)(2,1)S(1)} %collective-permute-done.7.refs_8_), channel_id=1, source_target_pairs={{0,2},{1,3},{2,0},{3,1},{4,6},{5,7},{6,4},{7,5},{8,10},{9,11},{10,... | collective-permute-start | bytes 393224 | tf_op jit(solution)/shard_map/ppermute | solution.py:109
  24.0 1.7 %collective-permute-start.6 = (bf16[128,512]{1,0:T(8,128)(2,1)S(1)}, bf16[128,512]{1,0:T(8,128)(2,1)S(1)}, u32[]{:S(2)}, u32[]{:S(2)}) collective-permute-start(bf16[128,512]{1,0:T(8,128)(2,1)S(1)} %collective-permute-done.5.refs_6_), channel_id=1, source_target_pairs={{0,1},{1,0},{2,3},{3,2},{4,5},{5,4},{6,7},{7,6},{8,9},{9,8},{10,11... | collective-permute-start | bytes 393224 | tf_op jit(solution)/shard_map/ppermute | solution.py:111
  24.0 5.9 %collective-permute-start.13 = (bf16[128,512]{1,0:T(8,128)(2,1)S(1)}, bf16[128,512]{1,0:T(8,128)(2,1)S(1)}, u32[]{:S(2)}, u32[]{:S(2)}) collective-permute-start(bf16[128,512]{1,0:T(8,128)(2,1)S(1)} %collective-permute-done.11.refs_12_), channel_id=1, source_target_pairs={{0,2},{1,3},{2,0},{3,1},{4,6},{5,7},{6,4},{7,5},{8,10},{9,11},{10,... | collective-permute-start | bytes 393224 | tf_op jit(solution)/shard_map/ppermute | solution.py:109
  24.1 7.2 %copy-start.3 = (bf16[128,8192]{1,0:T(8,128)(2,1)S(1)}, bf16[128,8192]{1,0:T(8,128)(2,1)}, u32[]{:S(2)}) copy-start(bf16[128,8192]{1,0:T(8,128)(2,1)} %gate.3) | copy-start | bytes 6291460
  24.1 7.2 %copy-start.4 = (bf16[128,8192]{1,0:T(8,128)(2,1)S(1)}, bf16[128,8192]{1,0:T(8,128)(2,1)}, u32[]{:S(2)}) copy-start(bf16[128,8192]{1,0:T(8,128)(2,1)} %up.3) | copy-start | bytes 6291460
  24.1 7.2 %copy-start.8 = (f32[8192]{0:T(1024)S(1)}, f32[8192]{0:T(1024)}, u32[]{:S(2)}) copy-start(f32[8192]{0:T(1024)} %param.10) | copy-start | bytes 98308
  24.1 7.2 %copy-start.9 = (f32[8192]{0:T(1024)S(1)}, f32[8192]{0:T(1024)}, u32[]{:S(2)}) copy-start(f32[8192]{0:T(1024)} %param.9) | copy-start | bytes 98308
  25.7 4.4 %collective-permute-start.12 = (bf16[128,512]{1,0:T(8,128)(2,1)S(1)}, bf16[128,512]{1,0:T(8,128)(2,1)S(1)}, u32[]{:S(2)}, u32[]{:S(2)}) collective-permute-start(bf16[128,512]{1,0:T(8,128)(2,1)S(1)} %collective-permute-done.11.refs_12_), channel_id=1, source_target_pairs={{0,1},{1,0},{2,3},{3,2},{4,5},{5,4},{6,7},{7,6},{8,9},{9,8},{10,11... | collective-permute-start | bytes 393224 | tf_op jit(solution)/shard_map/ppermute | solution.py:111
  25.7 4.3 %collective-permute-start.10 = (bf16[128,512]{1,0:T(8,128)(2,1)S(1)}, bf16[128,512]{1,0:T(8,128)(2,1)S(1)}, u32[]{:S(2)}, u32[]{:S(2)}) collective-permute-start(bf16[128,512]{1,0:T(8,128)(2,1)S(1)} %collective-permute-done.9.refs_10_), channel_id=1, source_target_pairs={{0,1},{1,0},{2,3},{3,2},{4,5},{5,4},{6,7},{7,6},{8,9},{9,8},{10,11... | collective-permute-start | bytes 393224 | tf_op jit(solution)/shard_map/ppermute | solution.py:111
  29.9 1.3 %collective-permute-start.14 = (bf16[128,512]{1,0:T(8,128)(2,1)S(1)}, bf16[128,512]{1,0:T(8,128)(2,1)S(1)}, u32[]{:S(2)}, u32[]{:S(2)}) collective-permute-start(bf16[128,512]{1,0:T(8,128)(2,1)S(1)} %collective-permute-done.13), channel_id=1, source_target_pairs={{0,1},{1,0},{2,3},{3,2},{4,5},{5,4},{6,7},{7,6},{8,9},{9,8},{10,11... | collective-permute-start | bytes 393224 | tf_op jit(solution)/shard_map/ppermute | solution.py:111
  31.3 52.9 %copy-start.1 = (bf16[128,8192]{1,0:T(8,128)(2,1)}, bf16[128,8192]{1,0:T(8,128)(2,1)S(1)}, u32[]{:S(2)}) copy-start(bf16[128,8192]{1,0:T(8,128)(2,1)S(1)} %constant_dynamic-update-slice_fusion.16.hidden) | copy-start | bytes 6291460
  33.3 1.3 %collective-permute-start.15 = (bf16[256,128]{1,0:T(8,128)(2,1)S(1)}, bf16[256,128]{1,0:T(8,128)(2,1)S(1)}, u32[]{:S(2)}, u32[]{:S(2)}) collective-permute-start(bf16[256,128]{1,0:T(8,128)(2,1)S(1)} %get-tuple-element.44.hid.both_hid), channel_id=1, source_target_pairs={{0,1},{1,0},{2,3},{3,2},{4,5},{5,4},{6,7},{7,6},{8,9},{9,8},{10,11... | collective-permute-start | bytes 196616 | tf_op jit(solution)/shard_map/ppermute | solution.py:387
  35.0 6.4 %collective-permute-start.20 = (bf16[128,512]{1,0:T(8,128)(2,1)S(1)}, bf16[128,512]{1,0:T(8,128)(2,1)S(1)}, u32[]{:S(2)}, u32[]{:S(2)}) collective-permute-start(bf16[128,512]{1,0:T(8,128)(2,1)S(1)} %get-tuple-element.39), channel_id=1, source_target_pairs={{0,2},{1,3},{2,0},{3,1},{4,6},{5,7},{6,4},{7,5},{8,10},{9,11},{10,... | collective-permute-start | bytes 393224 | tf_op jit(solution)/shard_map/ppermute | solution.py:123
  35.6 8.6 %collective-permute-start.19 = (bf16[128,512]{1,0:T(8,128)(2,1)S(1)}, bf16[128,512]{1,0:T(8,128)(2,1)S(1)}, u32[]{:S(2)}, u32[]{:S(2)}) collective-permute-start(bf16[128,512]{1,0:T(8,128)(2,1)S(1)} %get-tuple-element.41), channel_id=1, source_target_pairs={{0,2},{1,3},{2,0},{3,1},{4,6},{5,7},{6,4},{7,5},{8,10},{9,11},{10,... | collective-permute-start | bytes 393224 | tf_op jit(solution)/shard_map/ppermute | solution.py:123
  37.7 9.3 %copy-start.11 = (s32[16]{0:T(128)S(1)}, s32[16]{0:T(128)}, u32[]{:S(2)}) copy-start(s32[16]{0:T(128)} %param.15) | copy-start | bytes 196
  37.8 9.2 %collective-permute-start.18 = (bf16[128,512]{1,0:T(8,128)(2,1)S(1)}, bf16[128,512]{1,0:T(8,128)(2,1)S(1)}, u32[]{:S(2)}, u32[]{:S(2)}) collective-permute-start(bf16[128,512]{1,0:T(8,128)(2,1)S(1)} %get-tuple-element.43), channel_id=1, source_target_pairs={{0,2},{1,3},{2,0},{3,1},{4,6},{5,7},{6,4},{7,5},{8,10},{9,11},{10,... | collective-permute-start | bytes 393224 | tf_op jit(solution)/shard_map/ppermute | solution.py:123
  38.4 14.3 %collective-permute-start.17 = (bf16[128,512]{1,0:T(8,128)(2,1)S(1)}, bf16[128,512]{1,0:T(8,128)(2,1)S(1)}, u32[]{:S(2)}, u32[]{:S(2)}) collective-permute-start(bf16[128,512]{1,0:T(8,128)(2,1)S(1)} %get-tuple-element.46), channel_id=1, source_target_pairs={{0,2},{1,3},{2,0},{3,1},{4,6},{5,7},{6,4},{7,5},{8,10},{9,11},{10,... | collective-permute-start | bytes 393224 | tf_op jit(solution)/shard_map/ppermute | solution.py:123
  48.2 5.6 %collective-permute-start.23 = (bf16[128,512]{1,0:T(8,128)(2,1)S(1)}, bf16[128,512]{1,0:T(8,128)(2,1)S(1)}, u32[]{:S(2)}, u32[]{:S(2)}) collective-permute-start(bf16[128,512]{1,0:T(8,128)(2,1)S(1)} %add_convert_fusion.1), channel_id=1, source_target_pairs={{0,4},{1,5},{2,6},{3,7},{4,0},{5,1},{6,2},{7,3},{8,12},{9,13},{10,... | collective-permute-start | bytes 393224 | tf_op jit(solution)/shard_map/ppermute | solution.py:131
  48.7 12.1 %collective-permute-start.22 = (bf16[128,512]{1,0:T(8,128)(2,1)S(1)}, bf16[128,512]{1,0:T(8,128)(2,1)S(1)}, u32[]{:S(2)}, u32[]{:S(2)}) collective-permute-start(bf16[128,512]{1,0:T(8,128)(2,1)S(1)} %add_convert_fusion.2), channel_id=1, source_target_pairs={{0,8},{1,9},{2,10},{3,11},{4,12},{5,13},{6,14},{7,15},{8,0},{9,1},... | collective-permute-start | bytes 393224 | tf_op jit(solution)/shard_map/ppermute | solution.py:131
  51.8 9.0 %collective-permute-start.21 = (bf16[128,512]{1,0:T(8,128)(2,1)S(1)}, bf16[128,512]{1,0:T(8,128)(2,1)S(1)}, u32[]{:S(2)}, u32[]{:S(2)}) collective-permute-start(bf16[128,512]{1,0:T(8,128)(2,1)S(1)} %add_convert_fusion.3), channel_id=1, source_target_pairs={{0,12},{1,13},{2,14},{3,15},{4,8},{5,9},{6,10},{7,11},{8,4},{9,5},... | collective-permute-start | bytes 393224 | tf_op jit(solution)/shard_map/ppermute | solution.py:131
  61.1 9.9 %collective-permute-start.24 = (bf16[128,512]{1,0:T(8,128)(2,1)S(1)}, bf16[128,512]{1,0:T(8,128)(2,1)S(1)}, u32[]{:S(2)}, u32[]{:S(2)}) collective-permute-start(bf16[128,512]{1,0:T(8,128)(2,1)S(1)} %get-tuple-element.53.refs_0_), channel_id=1, source_target_pairs={{0,1},{1,0},{2,3},{3,2},{4,5},{5,4},{6,7},{7,6},{8,9},{9,8},{10,11... | collective-permute-start | bytes 393224 | tf_op jit(solution)/shard_map/ppermute | solution.py:111
  61.2 11.5 %collective-permute-start.25 = (bf16[128,512]{1,0:T(8,128)(2,1)S(1)}, bf16[128,512]{1,0:T(8,128)(2,1)S(1)}, u32[]{:S(2)}, u32[]{:S(2)}) collective-permute-start(bf16[128,512]{1,0:T(8,128)(2,1)S(1)} %get-tuple-element.53.refs_0_), channel_id=1, source_target_pairs={{0,2},{1,3},{2,0},{3,1},{4,6},{5,7},{6,4},{7,5},{8,10},{9,11},{10,... | collective-permute-start | bytes 393224 | tf_op jit(solution)/shard_map/ppermute | solution.py:109
  61.5 8.0 %collective-permute-start.27 = (bf16[128,512]{1,0:T(8,128)(2,1)S(1)}, bf16[128,512]{1,0:T(8,128)(2,1)S(1)}, u32[]{:S(2)}, u32[]{:S(2)}) collective-permute-start(bf16[128,512]{1,0:T(8,128)(2,1)S(1)} %get-tuple-element.53.refs_0_), channel_id=1, source_target_pairs={{0,4},{1,5},{2,6},{3,7},{4,0},{5,1},{6,2},{7,3},{8,12},{9,13},{10,... | collective-permute-start | bytes 393224 | tf_op jit(solution)/shard_map/ppermute | solution.py:105
  63.5 10.5 %collective-permute-start.31 = (bf16[128,512]{1,0:T(8,128)(2,1)S(1)}, bf16[128,512]{1,0:T(8,128)(2,1)S(1)}, u32[]{:S(2)}, u32[]{:S(2)}) collective-permute-start(bf16[128,512]{1,0:T(8,128)(2,1)S(1)} %get-tuple-element.53.refs_0_), channel_id=1, source_target_pairs={{0,8},{1,9},{2,10},{3,11},{4,12},{5,13},{6,14},{7,15},{8,0},{9,1},... | collective-permute-start | bytes 393224 | tf_op jit(solution)/shard_map/ppermute | solution.py:105
  69.5 6.9 %collective-permute-start.35 = (bf16[128,512]{1,0:T(8,128)(2,1)S(1)}, bf16[128,512]{1,0:T(8,128)(2,1)S(1)}, u32[]{:S(2)}, u32[]{:S(2)}) collective-permute-start(bf16[128,512]{1,0:T(8,128)(2,1)S(1)} %get-tuple-element.53.refs_0_), channel_id=1, source_target_pairs={{0,12},{1,13},{2,14},{3,15},{4,8},{5,9},{6,10},{7,11},{8,4},{9,5},... | collective-permute-start | bytes 393224 | tf_op jit(solution)/shard_map/ppermute | solution.py:106
  70.9 5.5 %collective-permute-start.28 = (bf16[128,512]{1,0:T(8,128)(2,1)S(1)}, bf16[128,512]{1,0:T(8,128)(2,1)S(1)}, u32[]{:S(2)}, u32[]{:S(2)}) collective-permute-start(bf16[128,512]{1,0:T(8,128)(2,1)S(1)} %collective-permute-done.27.refs_4_), channel_id=1, source_target_pairs={{0,1},{1,0},{2,3},{3,2},{4,5},{5,4},{6,7},{7,6},{8,9},{9,8},{10,11... | collective-permute-start | bytes 393224 | tf_op jit(solution)/shard_map/ppermute | solution.py:111
  70.9 7.3 %collective-permute-start.29 = (bf16[128,512]{1,0:T(8,128)(2,1)S(1)}, bf16[128,512]{1,0:T(8,128)(2,1)S(1)}, u32[]{:S(2)}, u32[]{:S(2)}) collective-permute-start(bf16[128,512]{1,0:T(8,128)(2,1)S(1)} %collective-permute-done.27.refs_4_), channel_id=1, source_target_pairs={{0,2},{1,3},{2,0},{3,1},{4,6},{5,7},{6,4},{7,5},{8,10},{9,11},{10,... | collective-permute-start | bytes 393224 | tf_op jit(solution)/shard_map/ppermute | solution.py:109
  72.7 1.3 %collective-permute-start.26 = (bf16[128,512]{1,0:T(8,128)(2,1)S(1)}, bf16[128,512]{1,0:T(8,128)(2,1)S(1)}, u32[]{:S(2)}, u32[]{:S(2)}) collective-permute-start(bf16[128,512]{1,0:T(8,128)(2,1)S(1)} %collective-permute-done.25.refs_2_), channel_id=1, source_target_pairs={{0,1},{1,0},{2,3},{3,2},{4,5},{5,4},{6,7},{7,6},{8,9},{9,8},{10,11... | collective-permute-start | bytes 393224 | tf_op jit(solution)/shard_map/ppermute | solution.py:111
  73.9 8.9 %collective-permute-start.32 = (bf16[128,512]{1,0:T(8,128)(2,1)S(1)}, bf16[128,512]{1,0:T(8,128)(2,1)S(1)}, u32[]{:S(2)}, u32[]{:S(2)}) collective-permute-start(bf16[128,512]{1,0:T(8,128)(2,1)S(1)} %collective-permute-done.31.refs_8_), channel_id=1, source_target_pairs={{0,1},{1,0},{2,3},{3,2},{4,5},{5,4},{6,7},{7,6},{8,9},{9,8},{10,11... | collective-permute-start | bytes 393224 | tf_op jit(solution)/shard_map/ppermute | solution.py:111
  74.0 6.2 %collective-permute-start.33 = (bf16[128,512]{1,0:T(8,128)(2,1)S(1)}, bf16[128,512]{1,0:T(8,128)(2,1)S(1)}, u32[]{:S(2)}, u32[]{:S(2)}) collective-permute-start(bf16[128,512]{1,0:T(8,128)(2,1)S(1)} %collective-permute-done.31.refs_8_), channel_id=1, source_target_pairs={{0,2},{1,3},{2,0},{3,1},{4,6},{5,7},{6,4},{7,5},{8,10},{9,11},{10,... | collective-permute-start | bytes 393224 | tf_op jit(solution)/shard_map/ppermute | solution.py:109
  76.4 6.6 %collective-permute-start.36 = (bf16[128,512]{1,0:T(8,128)(2,1)S(1)}, bf16[128,512]{1,0:T(8,128)(2,1)S(1)}, u32[]{:S(2)}, u32[]{:S(2)}) collective-permute-start(bf16[128,512]{1,0:T(8,128)(2,1)S(1)} %collective-permute-done.35.refs_12_), channel_id=1, source_target_pairs={{0,1},{1,0},{2,3},{3,2},{4,5},{5,4},{6,7},{7,6},{8,9},{9,8},{10,11... | collective-permute-start | bytes 393224 | tf_op jit(solution)/shard_map/ppermute | solution.py:111
  76.4 6.3 %collective-permute-start.37 = (bf16[128,512]{1,0:T(8,128)(2,1)S(1)}, bf16[128,512]{1,0:T(8,128)(2,1)S(1)}, u32[]{:S(2)}, u32[]{:S(2)}) collective-permute-start(bf16[128,512]{1,0:T(8,128)(2,1)S(1)} %collective-permute-done.35.refs_12_), channel_id=1, source_target_pairs={{0,2},{1,3},{2,0},{3,1},{4,6},{5,7},{6,4},{7,5},{8,10},{9,11},{10,... | collective-permute-start | bytes 393224 | tf_op jit(solution)/shard_map/ppermute | solution.py:109
  78.3 4.5 %collective-permute-start.30 = (bf16[128,512]{1,0:T(8,128)(2,1)S(1)}, bf16[128,512]{1,0:T(8,128)(2,1)S(1)}, u32[]{:S(2)}, u32[]{:S(2)}) collective-permute-start(bf16[128,512]{1,0:T(8,128)(2,1)S(1)} %collective-permute-done.29.refs_6_), channel_id=1, source_target_pairs={{0,1},{1,0},{2,3},{3,2},{4,5},{5,4},{6,7},{7,6},{8,9},{9,8},{10,11... | collective-permute-start | bytes 393224 | tf_op jit(solution)/shard_map/ppermute | solution.py:111
  80.3 2.6 %collective-permute-start.34 = (bf16[128,512]{1,0:T(8,128)(2,1)S(1)}, bf16[128,512]{1,0:T(8,128)(2,1)S(1)}, u32[]{:S(2)}, u32[]{:S(2)}) collective-permute-start(bf16[128,512]{1,0:T(8,128)(2,1)S(1)} %collective-permute-done.33.refs_10_), channel_id=1, source_target_pairs={{0,1},{1,0},{2,3},{3,2},{4,5},{5,4},{6,7},{7,6},{8,9},{9,8},{10,11... | collective-permute-start | bytes 393224 | tf_op jit(solution)/shard_map/ppermute | solution.py:111
  82.8 1.3 %collective-permute-start.38 = (bf16[128,512]{1,0:T(8,128)(2,1)S(1)}, bf16[128,512]{1,0:T(8,128)(2,1)S(1)}, u32[]{:S(2)}, u32[]{:S(2)}) collective-permute-start(bf16[128,512]{1,0:T(8,128)(2,1)S(1)} %collective-permute-done.37), channel_id=1, source_target_pairs={{0,1},{1,0},{2,3},{3,2},{4,5},{5,4},{6,7},{7,6},{8,9},{9,8},{10,11... | collective-permute-start | bytes 393224 | tf_op jit(solution)/shard_map/ppermute | solution.py:111
  86.3 15.2 %all-to-all-start = ((bf16[16,32,128]{2,1,0:T(8,128)(2,1)}), bf16[16,32,128]{2,1,0:T(8,128)(2,1)S(1)}, u32[]{:S(2)}, u32[]{:S(2)}) async-start(bf16[16,32,128]{2,1,0:T(8,128)(2,1)} %backward.1), calls=%async_computation | async-start | bytes 262144 | tf_op jit(solution)/shard_map/all_to_all | solution.py:436
  (4 other events, 8.6 us)
